TPU v7x, 256 devices: a whole 4x4x8 slice. The times are simulated.
256 devices in a mesh: loop: 32 (over x, y, core), tp: 8 (over z).
Axes of the slice: x: 4, y: 4, z: 8, core: 2. Of those that a mesh axis runs over, the one named last changes fastest.
Arguments:
- queries: bfloat16 [8192, 8192], P('loop', 'tp'), may hold values from -8 to 8
- key_values: bfloat16 [8192, 2048], P('loop', 'tp'), may hold values from -8 to 8
- prompt_ids: int32 [8192], P('loop'), may hold values from 0 to 15, never falling along the last dimension, each value on 1 to 2048 neighbouring positions
- out_weight: bfloat16 [8192, 4096], P('tp'), may hold values from -5 to 5
Outputs:
- mixed: bfloat16 [8192, 4096], P('loop', 'tp')
Inputs may be any that keep to these rules, and one draw needn't show every extreme that they name: `prompt_ids`: prompt numbers never fall along the tokens; each prompt holds 1 to 2048 tokens and one holds exactly 2048.
All inputs are finite; a program needn't handle non-finite values.
Results may differ from a plain program's by a relative error of at most 0.018.
Values may be sent and summed in bfloat16 or wider, within the bound.
No kernel may reach another device: no remote copies, remote signals or barrier semaphores. Data moves between devices by JAX's collectives and lax.ppermute only.
A program may use at most 64 MiB of HBM per device.

v0:
```python
import math

import jax
import jax.numpy as jnp
from jax import lax
from jax.sharding import PartitionSpec as P

HD = 128


masked_score = -1e30


def from_behind(value, axis, steps):
    count = lax.axis_size(axis)
    first, last = (max(0, -steps), min(count, count - steps))
    return lax.ppermute(value, axis, [(source, source + steps) for source in range(first, last)])


def per_device(queries, key_values, prompt_ids, out_weight):
    tok_rows = queries.shape[0]
    head_dim = HD
    kv_heads = key_values.shape[1] // (2 * head_dim)
    per_group = queries.shape[1] // (kv_heads * head_dim)
    scaler = 1.0 / math.sqrt(head_dim)
    reach = min(8, lax.axis_size("loop") // 2)
    group_size = max(1, -(-512 // tok_rows))
    query_pos = lax.axis_index("loop") * tok_rows + jnp.arange(tok_rows, dtype=jnp.int32)
    query_heads = queries.reshape(tok_rows, kv_heads, per_group, head_dim)

    def absorb(state_now, pending):
        kv_block = jnp.concatenate([item[0] for item in pending], axis=0)
        id_block = jnp.concatenate([item[1] for item in pending], axis=0)
        key_pos = jnp.concatenate([item[2] for item in pending], axis=0)
        allowed = (
            (prompt_ids[:, None] == id_block[None, :])
            & (key_pos[None, :] <= query_pos[:, None])
            & (key_pos[None, :] >= 0)
        )
        run_max, run_sum, run_acc = state_now
        paired = kv_block.reshape(kv_block.shape[0], kv_heads, 2, head_dim)
        key_rows = paired[:, :, 0, :]
        value_rows = paired[:, :, 1, :]
        scores = (
            jnp.einsum("qhgd,khd->hgqk", query_heads, key_rows, preferred_element_type=jnp.float32)
            * scaler
        )
        scores = jnp.where(allowed, scores, masked_score)
        new_max = jnp.maximum(run_max, jnp.max(scores, axis=-1))
        probs = jnp.where(allowed, jnp.exp(scores - new_max[..., None]), 0.0)
        rescale = jnp.exp(run_max - new_max)
        new_sum = run_sum * rescale + jnp.sum(probs, axis=-1)
        added = jnp.einsum(
            "hgqk,khd->hgqd",
            probs.astype(jnp.bfloat16),
            value_rows,
            preferred_element_type=jnp.float32,
        )
        return (new_max, new_sum, run_acc * rescale[..., None] + added)

    state_now = (
        jnp.full((kv_heads, per_group, tok_rows), masked_score, jnp.float32),
        jnp.zeros((kv_heads, per_group, tok_rows), jnp.float32),
        jnp.zeros((kv_heads, per_group, tok_rows, head_dim), jnp.float32),
    )
    pending = [(key_values, prompt_ids, query_pos)]
    for hop_count in range(1, reach + 1):
        moved_kv, moved_ids = from_behind((key_values, prompt_ids), "loop", hop_count)
        pending.append((moved_kv, moved_ids, query_pos - hop_count * tok_rows))
        if len(pending) >= group_size:
            state_now = absorb(state_now, pending)
            pending = []
    state_now = absorb(state_now, pending)
    run_max, run_sum, run_acc = state_now
    weighted = run_acc / run_sum[..., None]
    attention = (
        jnp.transpose(weighted, (2, 0, 1, 3))
        .reshape(tok_rows, kv_heads * per_group * head_dim)
        .astype(jnp.bfloat16)
    )
    partial_rows = jnp.dot(attention, out_weight, preferred_element_type=jnp.float32)
    return lax.psum_scatter(
        partial_rows.astype(jnp.bfloat16), "tp", scatter_dimension=1, tiled=True
    )


def solution(mesh):
    in_specs = (P("loop", "tp"), P("loop", "tp"), P("loop"), P("tp", None))
    out_specs = P("loop", "tp")
    return jax.shard_map(
        per_device, mesh=mesh, in_specs=in_specs, out_specs=out_specs, check_vma=False
    )
```

profile of v0, /device:TPU:12, one launch (start us, length us, event | category | flops | bytes accessed | tf_op | source)
XLA Modules:
  0.0 133.3 jit_solution(17903144515643174587)
XLA Ops:
  6.5 2.6 %collective-permute-start.11 = (s32[256]{0:T(256)}, s32[256]{0:T(256)S(1)}, u32[]{:S(2)}, u32[]{:S(2)}) collective-permute-start(s32[256]{0:T(256)} %param.6), channel_id=1, source_target_pairs={{0,56},{8,64},{16,72},{24,80},{32,88},{40,96},{48,104},{56,112},{6... | collective-permute-start | bytes 3080 | tf_op jit(solution)/shard_map/ppermute | solution.py:17
  9.1 4.9 %collective-permute-start.10 = (s32[256]{0:T(256)}, s32[256]{0:T(256)S(1)}, u32[]{:S(2)}, u32[]{:S(2)}) collective-permute-start(s32[256]{0:T(256)} %param.6), channel_id=1, source_target_pairs={{0,48},{8,56},{16,64},{24,72},{32,80},{40,88},{48,96},{56,104},{64... | collective-permute-start | bytes 3080 | tf_op jit(solution)/shard_map/ppermute | solution.py:17
  14.0 1.9 %collective-permute-start.7 = (s32[256]{0:T(256)}, s32[256]{0:T(256)S(1)}, u32[]{:S(2)}, u32[]{:S(2)}) collective-permute-start(s32[256]{0:T(256)} %param.6), channel_id=1, source_target_pairs={{0,40},{8,48},{16,56},{24,64},{32,72},{40,80},{48,88},{56,96},{64,... | collective-permute-start | bytes 3080 | tf_op jit(solution)/shard_map/ppermute | solution.py:17
  16.0 1.9 %collective-permute-start.6 = (s32[256]{0:T(256)}, s32[256]{0:T(256)S(1)}, u32[]{:S(2)}, u32[]{:S(2)}) collective-permute-start(s32[256]{0:T(256)} %param.6), channel_id=1, source_target_pairs={{0,32},{8,40},{16,48},{24,56},{32,64},{40,72},{48,80},{56,88},{64,... | collective-permute-start | bytes 3080 | tf_op jit(solution)/shard_map/ppermute | solution.py:17
  17.9 2.0 %collective-permute-start = (s32[256]{0:T(256)}, s32[256]{0:T(256)S(1)}, u32[]{:S(2)}, u32[]{:S(2)}) collective-permute-start(s32[256]{0:T(256)} %param.6), channel_id=1, source_target_pairs={{0,8},{8,16},{16,24},{24,32},{32,40},{40,48},{48,56},{56,64},{64,7... | collective-permute-start | bytes 3080 | tf_op jit(solution)/shard_map/ppermute | solution.py:17
  21.1 1.9 %collective-permute-done = s32[256]{0:T(256)S(1)} collective-permute-done((s32[256]{0:T(256)}, s32[256]{0:T(256)S(1)}, u32[]{:S(2)}, u32[]{:S(2)}) %collective-permute-start) | collective-permute-done | bytes 1056 | tf_op jit(solution)/shard_map/ppermute | solution.py:17
  23.0 1.9 %collective-permute-start.3 = (s32[256]{0:T(256)}, s32[256]{0:T(256)S(1)}, u32[]{:S(2)}, u32[]{:S(2)}) collective-permute-start(s32[256]{0:T(256)} %param.6), channel_id=1, source_target_pairs={{0,24},{8,32},{16,40},{24,48},{32,56},{40,64},{48,72},{56,80},{64,... | collective-permute-start | bytes 3080 | tf_op jit(solution)/shard_map/ppermute | solution.py:17
  25.6 3.4 %collective-permute-start.2 = (s32[256]{0:T(256)}, s32[256]{0:T(256)S(1)}, u32[]{:S(2)}, u32[]{:S(2)}) collective-permute-start(s32[256]{0:T(256)} %param.6), channel_id=1, source_target_pairs={{0,16},{8,24},{16,32},{24,40},{32,48},{40,56},{48,64},{56,72},{64,... | collective-permute-start | bytes 3080 | tf_op jit(solution)/shard_map/ppermute | solution.py:17
  29.0 1.9 %collective-permute-start.14 = (s32[256]{0:T(256)}, s32[256]{0:T(256)S(1)}, u32[]{:S(2)}, u32[]{:S(2)}) collective-permute-start(s32[256]{0:T(256)} %param.6), channel_id=1, source_target_pairs={{0,64},{8,72},{16,80},{24,88},{32,96},{40,104},{48,112},{56,120},{... | collective-permute-start | bytes 3080 | tf_op jit(solution)/shard_map/ppermute | solution.py:17
  31.0 1.9 %collective-permute-start.15 = (bf16[256,256]{0,1:T(8,128)(2,1)S(1)}, bf16[256,256]{0,1:T(8,128)(2,1)S(1)}, u32[]{:S(2)}, u32[]{:S(2)}) collective-permute-start(bf16[256,256]{0,1:T(8,128)(2,1)S(1)} %copy.21), channel_id=1, source_target_pairs={{0,64},{8,72},{16,80},{24,88},{32,96},{40,104},{48,112},{56,120},{... | collective-permute-start | bytes 393224 | tf_op jit(solution)/shard_map/ppermute | solution.py:17
  32.9 1.9 %collective-permute-start.13 = (bf16[256,256]{0,1:T(8,128)(2,1)S(1)}, bf16[256,256]{0,1:T(8,128)(2,1)S(1)}, u32[]{:S(2)}, u32[]{:S(2)}) collective-permute-start(bf16[256,256]{0,1:T(8,128)(2,1)S(1)} %copy.21), channel_id=1, source_target_pairs={{0,56},{8,64},{16,72},{24,80},{32,88},{40,96},{48,104},{56,112},{6... | collective-permute-start | bytes 393224 | tf_op jit(solution)/shard_map/ppermute | solution.py:17
  34.8 1.9 %collective-permute-start.12 = (bf16[256,256]{0,1:T(8,128)(2,1)S(1)}, bf16[256,256]{0,1:T(8,128)(2,1)S(1)}, u32[]{:S(2)}, u32[]{:S(2)}) collective-permute-start(bf16[256,256]{0,1:T(8,128)(2,1)S(1)} %copy.21), channel_id=1, source_target_pairs={{0,48},{8,56},{16,64},{24,72},{32,80},{40,88},{48,96},{56,104},{64... | collective-permute-start | bytes 393224 | tf_op jit(solution)/shard_map/ppermute | solution.py:17
  36.8 3.8 %collective-permute-start.5 = (bf16[256,256]{0,1:T(8,128)(2,1)S(1)}, bf16[256,256]{0,1:T(8,128)(2,1)S(1)}, u32[]{:S(2)}, u32[]{:S(2)}) collective-permute-start(bf16[256,256]{0,1:T(8,128)(2,1)S(1)} %copy.21), channel_id=1, source_target_pairs={{0,24},{8,32},{16,40},{24,48},{32,56},{40,64},{48,72},{56,80},{64,... | collective-permute-start | bytes 393224 | tf_op jit(solution)/shard_map/ppermute | solution.py:17
  40.6 1.9 %and_and_fusion.2 = (pred[256,512]{0,1:T(8,128)(4,1)S(1)}, pred[256,512]{0,1:T(8,128)(4,1)S(1)}, pred[256,512]{0,1:T(8,128)(4,1)S(1)}, pred[256,512]{0,1:T(8,128)(4,1)S(1)}) fusion(s32[256]{0:T(256)S(1)} %get-tuple-element.30, s32[256]{0:T(256)} %param.6, s32[512]{0:T(512)S(1)} %pad_add_fusion.3, s32[512]{0:T(512)S(1)} %pad_add_fusion.2, ...), kind=kLoop, calls=%fused_computation.67 | loop fusion | flops 2097152 | bytes 544768 | tf_op jit(solution)/shard_map/and | solution.py:36
  42.5 1.9 %collective-permute-start.4 = (bf16[256,256]{0,1:T(8,128)(2,1)S(1)}, bf16[256,256]{0,1:T(8,128)(2,1)S(1)}, u32[]{:S(2)}, u32[]{:S(2)}) collective-permute-start(bf16[256,256]{0,1:T(8,128)(2,1)S(1)} %copy.21), channel_id=1, source_target_pairs={{0,16},{8,24},{16,32},{24,40},{32,48},{40,56},{48,64},{56,72},{64,... | collective-permute-start | bytes 393224 | tf_op jit(solution)/shard_map/ppermute | solution.py:17
  45.2 3.6 %collective-permute-done.5 = bf16[256,256]{0,1:T(8,128)(2,1)S(1)} collective-permute-done((bf16[256,256]{0,1:T(8,128)(2,1)S(1)}, bf16[256,256]{0,1:T(8,128)(2,1)S(1)}, u32[]{:S(2)}, u32[]{:S(2)}) %collective-permute-start.5) | collective-permute-done | bytes 131104 | tf_op jit(solution)/shard_map/ppermute | solution.py:17
  48.8 1.9 %collective-permute-start.9 = (bf16[256,256]{0,1:T(8,128)(2,1)S(1)}, bf16[256,256]{0,1:T(8,128)(2,1)S(1)}, u32[]{:S(2)}, u32[]{:S(2)}) collective-permute-start(bf16[256,256]{0,1:T(8,128)(2,1)S(1)} %copy.21), channel_id=1, source_target_pairs={{0,40},{8,48},{16,56},{24,64},{32,72},{40,80},{48,88},{56,96},{64,... | collective-permute-start | bytes 393224 | tf_op jit(solution)/shard_map/ppermute | solution.py:17
  50.8 3.2 %collective-permute-start.8 = (bf16[256,256]{0,1:T(8,128)(2,1)S(1)}, bf16[256,256]{0,1:T(8,128)(2,1)S(1)}, u32[]{:S(2)}, u32[]{:S(2)}) collective-permute-start(bf16[256,256]{0,1:T(8,128)(2,1)S(1)} %copy.21), channel_id=1, source_target_pairs={{0,32},{8,40},{16,48},{24,56},{32,64},{40,72},{48,80},{56,88},{64,... | collective-permute-start | bytes 393224 | tf_op jit(solution)/shard_map/ppermute | solution.py:17
  54.9 1.4 %collective-permute-done.9 = bf16[256,256]{0,1:T(8,128)(2,1)S(1)} collective-permute-done((bf16[256,256]{0,1:T(8,128)(2,1)S(1)}, bf16[256,256]{0,1:T(8,128)(2,1)S(1)}, u32[]{:S(2)}, u32[]{:S(2)}) %collective-permute-start.9) | collective-permute-done | bytes 131104 | tf_op jit(solution)/shard_map/ppermute | solution.py:17
  56.3 3.0 %collective-permute-start.1 = (bf16[256,256]{0,1:T(8,128)(2,1)S(1)}, bf16[256,256]{0,1:T(8,128)(2,1)S(1)}, u32[]{:S(2)}, u32[]{:S(2)}) collective-permute-start(bf16[256,256]{0,1:T(8,128)(2,1)S(1)} %copy.21), channel_id=1, source_target_pairs={{0,8},{8,16},{16,24},{24,32},{32,40},{40,48},{48,56},{56,64},{64,7... | collective-permute-start | bytes 393224 | tf_op jit(solution)/shard_map/ppermute | solution.py:17
  59.3 1.3 %collective-permute-done.8 = bf16[256,256]{0,1:T(8,128)(2,1)S(1)} collective-permute-done((bf16[256,256]{0,1:T(8,128)(2,1)S(1)}, bf16[256,256]{0,1:T(8,128)(2,1)S(1)}, u32[]{:S(2)}, u32[]{:S(2)}) %collective-permute-start.8) | collective-permute-done | bytes 131104 | tf_op jit(solution)/shard_map/ppermute | solution.py:17
  63.0 2.6 %collective-permute-done.1 = bf16[256,256]{0,1:T(8,128)(2,1)S(1)} collective-permute-done((bf16[256,256]{0,1:T(8,128)(2,1)S(1)}, bf16[256,256]{0,1:T(8,128)(2,1)S(1)}, u32[]{:S(2)}, u32[]{:S(2)}) %collective-permute-start.1) | collective-permute-done | bytes 131104 | tf_op jit(solution)/shard_map/ppermute | solution.py:17
  66.5 1.0 fusion.4
  68.0 1.0 fusion.10
  69.1 1.0 fusion.8
  70.1 1.0 fusion.6
  71.1 1.3 fusion.53
  72.4 1.3 fusion.47
  73.8 1.3 fusion.41
  75.1 1.5 %fusion.35 = f32[8,256,128]{1,2,0:T(8,128)S(1)} fusion(f32[8,256,128]{1,2,0:T(8,128)S(1)} %fusion.41, f32[512,256,8]{1,0,2:T(8,128)S(1)} %get-tuple-element.23, f32[8,256]{1,0:T(8,128)S(1)} %get-tuple-element.11, pred[256,512]{0,1:T(8,128)(4,1)S(1)} %get-tuple-element.18, f32[8,256]{1,0:T(8,128)S(1)} %get-tuple-element.6, ...), kind=kOutput, calls=%fused_computation.41 | convolution fusion | flops 274202624 | bytes 6569984 | tf_op jit(solution)/shard_map/hgqk,khd->hgqd/dot_general | solution.py:53
  77.5 3.9 %convolution_convert_fusion = bf16[256,4096]{1,0:T(8,128)(2,1)} fusion(bf16[256,1024]{0,1:T(8,128)(2,1)S(1)} %bitcast.238, bf16[1024,4096]{1,0:T(8,128)(2,1)S(1)} %bitcast.237), kind=kOutput, calls=%fused_computation | convolution fusion | flops 2148532224 | bytes 11010048 | tf_op jit(solution)/shard_map/dot_general | solution.py:81
  81.4 45.0 %reduce-scatter.2.cloned.1.call-done = bf16[256,512]{1,0:T(8,128)(2,1)} async-done(((bf16[256,4096]{1,0:T(8,128)(2,1)}), bf16[256,512]{1,0:T(8,128)(2,1)}) %reduce-scatter.2.cloned.1.call-update) | async-done | bytes 262160 | tf_op jit(solution)/shard_map/reduce_scatter | solution.py:82
  (53 shorter events, 8.2 us)
Async XLA Ops:
  6.5 47.5 %copy-start = (bf16[256,1024]{1,0:T(8,128)(2,1)S(1)}, bf16[256,1024]{1,0:T(8,128)(2,1)}, u32[]{:S(2)}) copy-start(bf16[256,1024]{1,0:T(8,128)(2,1)} %param.4) | copy-start | bytes 1572868
  6.5 119.9 %reduce-scatter.2.cloned.1.call-start = ((), (), s32[]{:S(2)}) async-start(), calls=%async_computation.1 | async-start | bytes 2359296 | tf_op jit(solution)/shard_map/reduce_scatter | solution.py:82
  6.5 19.1 %collective-permute-start.11 = (s32[256]{0:T(256)}, s32[256]{0:T(256)S(1)}, u32[]{:S(2)}, u32[]{:S(2)}) collective-permute-start(s32[256]{0:T(256)} %param.6), channel_id=1, source_target_pairs={{0,56},{8,64},{16,72},{24,80},{32,88},{40,96},{48,104},{56,112},{6... | collective-permute-start | bytes 3080 | tf_op jit(solution)/shard_map/ppermute | solution.py:17
  9.1 19.9 %collective-permute-start.10 = (s32[256]{0:T(256)}, s32[256]{0:T(256)S(1)}, u32[]{:S(2)}, u32[]{:S(2)}) collective-permute-start(s32[256]{0:T(256)} %param.6), channel_id=1, source_target_pairs={{0,48},{8,56},{16,64},{24,72},{32,80},{40,88},{48,96},{56,104},{64... | collective-permute-start | bytes 3080 | tf_op jit(solution)/shard_map/ppermute | solution.py:17
  14.0 16.9 %collective-permute-start.7 = (s32[256]{0:T(256)}, s32[256]{0:T(256)S(1)}, u32[]{:S(2)}, u32[]{:S(2)}) collective-permute-start(s32[256]{0:T(256)} %param.6), channel_id=1, source_target_pairs={{0,40},{8,48},{16,56},{24,64},{32,72},{40,80},{48,88},{56,96},{64,... | collective-permute-start | bytes 3080 | tf_op jit(solution)/shard_map/ppermute | solution.py:17
  16.0 16.9 %collective-permute-start.6 = (s32[256]{0:T(256)}, s32[256]{0:T(256)S(1)}, u32[]{:S(2)}, u32[]{:S(2)}) collective-permute-start(s32[256]{0:T(256)} %param.6), channel_id=1, source_target_pairs={{0,32},{8,40},{16,48},{24,56},{32,64},{40,72},{48,80},{56,88},{64,... | collective-permute-start | bytes 3080 | tf_op jit(solution)/shard_map/ppermute | solution.py:17
  17.9 5.1 %collective-permute-start = (s32[256]{0:T(256)}, s32[256]{0:T(256)S(1)}, u32[]{:S(2)}, u32[]{:S(2)}) collective-permute-start(s32[256]{0:T(256)} %param.6), channel_id=1, source_target_pairs={{0,8},{8,16},{16,24},{24,32},{32,40},{40,48},{48,56},{56,64},{64,7... | collective-permute-start | bytes 3080 | tf_op jit(solution)/shard_map/ppermute | solution.py:17
  23.0 11.8 %collective-permute-start.3 = (s32[256]{0:T(256)}, s32[256]{0:T(256)S(1)}, u32[]{:S(2)}, u32[]{:S(2)}) collective-permute-start(s32[256]{0:T(256)} %param.6), channel_id=1, source_target_pairs={{0,24},{8,32},{16,40},{24,48},{32,56},{40,64},{48,72},{56,80},{64,... | collective-permute-start | bytes 3080 | tf_op jit(solution)/shard_map/ppermute | solution.py:17
  25.6 11.2 %collective-permute-start.2 = (s32[256]{0:T(256)}, s32[256]{0:T(256)S(1)}, u32[]{:S(2)}, u32[]{:S(2)}) collective-permute-start(s32[256]{0:T(256)} %param.6), channel_id=1, source_target_pairs={{0,16},{8,24},{16,32},{24,40},{32,48},{40,56},{48,64},{56,72},{64,... | collective-permute-start | bytes 3080 | tf_op jit(solution)/shard_map/ppermute | solution.py:17
  29.0 13.4 %collective-permute-start.14 = (s32[256]{0:T(256)}, s32[256]{0:T(256)S(1)}, u32[]{:S(2)}, u32[]{:S(2)}) collective-permute-start(s32[256]{0:T(256)} %param.6), channel_id=1, source_target_pairs={{0,64},{8,72},{16,80},{24,88},{32,96},{40,104},{48,112},{56,120},{... | collective-permute-start | bytes 3080 | tf_op jit(solution)/shard_map/ppermute | solution.py:17
  31.0 31.5 %collective-permute-start.15 = (bf16[256,256]{0,1:T(8,128)(2,1)S(1)}, bf16[256,256]{0,1:T(8,128)(2,1)S(1)}, u32[]{:S(2)}, u32[]{:S(2)}) collective-permute-start(bf16[256,256]{0,1:T(8,128)(2,1)S(1)} %copy.21), channel_id=1, source_target_pairs={{0,64},{8,72},{16,80},{24,88},{32,96},{40,104},{48,112},{56,120},{... | collective-permute-start | bytes 393224 | tf_op jit(solution)/shard_map/ppermute | solution.py:17
  32.9 28.6 %collective-permute-start.13 = (bf16[256,256]{0,1:T(8,128)(2,1)S(1)}, bf16[256,256]{0,1:T(8,128)(2,1)S(1)}, u32[]{:S(2)}, u32[]{:S(2)}) collective-permute-start(bf16[256,256]{0,1:T(8,128)(2,1)S(1)} %copy.21), channel_id=1, source_target_pairs={{0,56},{8,64},{16,72},{24,80},{32,88},{40,96},{48,104},{56,112},{6... | collective-permute-start | bytes 393224 | tf_op jit(solution)/shard_map/ppermute | solution.py:17
  34.8 26.7 %collective-permute-start.12 = (bf16[256,256]{0,1:T(8,128)(2,1)S(1)}, bf16[256,256]{0,1:T(8,128)(2,1)S(1)}, u32[]{:S(2)}, u32[]{:S(2)}) collective-permute-start(bf16[256,256]{0,1:T(8,128)(2,1)S(1)} %copy.21), channel_id=1, source_target_pairs={{0,48},{8,56},{16,64},{24,72},{32,80},{40,88},{48,96},{56,104},{64... | collective-permute-start | bytes 393224 | tf_op jit(solution)/shard_map/ppermute | solution.py:17
  36.8 12.0 %collective-permute-start.5 = (bf16[256,256]{0,1:T(8,128)(2,1)S(1)}, bf16[256,256]{0,1:T(8,128)(2,1)S(1)}, u32[]{:S(2)}, u32[]{:S(2)}) collective-permute-start(bf16[256,256]{0,1:T(8,128)(2,1)S(1)} %copy.21), channel_id=1, source_target_pairs={{0,24},{8,32},{16,40},{24,48},{32,56},{40,64},{48,72},{56,80},{64,... | collective-permute-start | bytes 393224 | tf_op jit(solution)/shard_map/ppermute | solution.py:17
  42.5 8.3 %collective-permute-start.4 = (bf16[256,256]{0,1:T(8,128)(2,1)S(1)}, bf16[256,256]{0,1:T(8,128)(2,1)S(1)}, u32[]{:S(2)}, u32[]{:S(2)}) collective-permute-start(bf16[256,256]{0,1:T(8,128)(2,1)S(1)} %copy.21), channel_id=1, source_target_pairs={{0,16},{8,24},{16,32},{24,40},{32,48},{40,56},{48,64},{56,72},{64,... | collective-permute-start | bytes 393224 | tf_op jit(solution)/shard_map/ppermute | solution.py:17
  48.8 7.5 %collective-permute-start.9 = (bf16[256,256]{0,1:T(8,128)(2,1)S(1)}, bf16[256,256]{0,1:T(8,128)(2,1)S(1)}, u32[]{:S(2)}, u32[]{:S(2)}) collective-permute-start(bf16[256,256]{0,1:T(8,128)(2,1)S(1)} %copy.21), channel_id=1, source_target_pairs={{0,40},{8,48},{16,56},{24,64},{32,72},{40,80},{48,88},{56,96},{64,... | collective-permute-start | bytes 393224 | tf_op jit(solution)/shard_map/ppermute | solution.py:17
  50.8 9.9 %collective-permute-start.8 = (bf16[256,256]{0,1:T(8,128)(2,1)S(1)}, bf16[256,256]{0,1:T(8,128)(2,1)S(1)}, u32[]{:S(2)}, u32[]{:S(2)}) collective-permute-start(bf16[256,256]{0,1:T(8,128)(2,1)S(1)} %copy.21), channel_id=1, source_target_pairs={{0,32},{8,40},{16,48},{24,56},{32,64},{40,72},{48,80},{56,88},{64,... | collective-permute-start | bytes 393224 | tf_op jit(solution)/shard_map/ppermute | solution.py:17
  56.3 9.3 %collective-permute-start.1 = (bf16[256,256]{0,1:T(8,128)(2,1)S(1)}, bf16[256,256]{0,1:T(8,128)(2,1)S(1)}, u32[]{:S(2)}, u32[]{:S(2)}) collective-permute-start(bf16[256,256]{0,1:T(8,128)(2,1)S(1)} %copy.21), channel_id=1, source_target_pairs={{0,8},{8,16},{16,24},{24,32},{32,40},{40,48},{48,56},{56,64},{64,7... | collective-permute-start | bytes 393224 | tf_op jit(solution)/shard_map/ppermute | solution.py:17
  73.8 3.6 %slice-start = ((s8[8388608]{0:T(1024)(128)(4,1)}), s8[4194304]{0:T(1024)(128)(4,1)S(1)}, s32[]{:S(2)}) async-start(s8[8388608]{0:T(1024)(128)(4,1)} %bitcast.236), calls=%async_computation.2 | async-start | bytes 8388608
  75.1 2.4 %slice-start.1 = ((s8[8388608]{0:T(1024)(128)(4,1)}), s8[4194304]{0:T(1024)(128)(4,1)S(1)}, s32[]{:S(2)}) async-start(s8[8388608]{0:T(1024)(128)(4,1)} %bitcast.236), calls=%async_computation.3 | async-start | bytes 8388608
Sparse Core Ops, SparseCore 0:
  81.5 44.8 reduce-scatter.1
where the time goes:
time: 134 us; the launch traced here: 133 us
  waiting for transfers between devices  55.8 us (42%)
  starting transfers between devices  40.1 us (30%)
  matrix products  14 us (10%)
  between operations  13.9 us (10%)
  other arithmetic  8.28 us (6%)
    reduce_scatter x1, waiting for transfers between devices, per_device(): lax.psum_scatter(partial_rows.astype(jnp.bfloat16), 'tp', scatter_dimensi...  45 us
    ppermute x16, starting transfers between devices, from_behind(): lax.ppermute(value, axis, [(source, source + steps) for source in range(f...  40.1 us
    ppermute x16, waiting for transfers between devices, from_behind(): lax.ppermute(value, axis, [(source, source + steps) for source in range(f...  10.8 us
    dot_general x5, matrix products, absorb(): jnp.einsum('hgqk,khd->hgqd', probs.astype(jnp.bfloat16), value_rows, pref...  6.18 us
    reduce_sum x5, other arithmetic, absorb(): new_sum = run_sum * rescale + jnp.sum(probs, axis=-1)  4.6 us
    dot_general x5, matrix products, absorb(): jnp.einsum('qhgd,khd->hgqk', query_heads, key_rows, preferred_element_typ...  3.96 us
    dot_general x1, matrix products, per_device(): jnp.dot(attention, out_weight, preferred_element_type=jnp.float32)  3.86 us
    and x2, other arithmetic, absorb(): (prompt_ids[:, None] == id_block[None, :]) & (key_pos[None, :] <= query_p...  2.73 us
  transfers between devices with their start and end apart: 17, of which 6 were waited for; matrix products, arithmetic and copies ran while one was open for 6% of the time, Pallas kernels for 0%

commit v1 on v0

v1 whole, which is shorter than its diff:
```python
import functools
import math

import jax
import jax.numpy as jnp
from jax import lax
from jax.experimental import pallas as pl
from jax.experimental.pallas import tpu as pltpu
from jax.sharding import PartitionSpec as P

HD = 128
HEADS = 8
TOK = 256
PART = 128
ROWS = HEADS * PART
PIECE = TOK + 16
CHUNK = 512
SCALE = 1.0 / math.sqrt(HD)
MASKED = -1e30
F32 = jnp.float32
BF16 = jnp.bfloat16


def attend(valid, queries, ids, pieces, before, after, scores, peak, query_rows, own_first):
    count = len(pieces)
    for head in range(HEADS):
        query_rows[pl.ds(head * PART, PART), :] = queries[:, pl.ds(head * HD, HD)]
    own_ids = ids[...]
    masks = []
    for at, (which, piece) in enumerate(pieces):
        key_ids = piece[TOK:PIECE, :][0:1, :].astype(F32)
        key_ids = jnp.where(valid[which] > 0, key_ids, -1.0)
        allowed = own_ids == key_ids
        if own_first is not None and at == 0:
            rows = lax.broadcasted_iota(jnp.int32, (PART, TOK), 0) + own_first
            allowed = allowed & (lax.broadcasted_iota(jnp.int32, (PART, TOK), 1) <= rows)
        masks.append(allowed)
    for head in range(HEADS):
        rows = pl.ds(head * PART, PART)
        best = None
        for at, (_, piece) in enumerate(pieces):
            found = lax.dot_general(
                query_rows[rows, :],
                piece[0:TOK, 0:HD],
                (((1,), (1,)), ((), ())),
                preferred_element_type=F32,
            )
            found = jnp.where(masks[at], found, MASKED)
            scores[rows, at * TOK : (at + 1) * TOK] = found
            here = jnp.maximum(found[:, :HD], found[:, HD:])
            best = here if best is None else jnp.maximum(best, here)
        peak[rows, :] = best
    ones = jnp.ones((TOK, HD), BF16)
    values = jnp.concatenate(
        [jnp.concatenate([piece[0:TOK, HD:], ones], axis=1) for _, piece in pieces], axis=0
    )
    for head in range(HEADS):
        rows = pl.ds(head * PART, PART)
        top = jnp.broadcast_to(jnp.max(peak[rows, :], axis=1, keepdims=True), (PART, HD))
        if before is not None:
            old = before[0][rows, :]
            top = jnp.maximum(top, old)
        wide = jnp.concatenate([top] * (2 * count), axis=1)
        probs = jnp.exp((scores[rows, 0 : count * TOK] - wide) * SCALE).astype(BF16)
        added = jnp.dot(probs, values, preferred_element_type=F32)
        if before is not None:
            shrink = jnp.exp((old - top) * SCALE)
            added = added + before[1][rows, :] * jnp.concatenate([shrink, shrink], axis=1)
        after(head, rows, top, added)


def early_kernel(parts, which, first, *refs):
    valid, queries, ids = refs[:3]
    pieces = list(zip(which, refs[3 : 3 + len(which)]))
    at = 3 + len(which)
    if not first:
        before = refs[at : at + 2 * parts]
        at += 2 * parts
    after = refs[at : at + 2 * parts]
    scores, peak, query_rows = refs[at + 2 * parts :]
    for part in range(parts):
        tops, sums = after[2 * part : 2 * part + 2]

        def keep(head, rows, top, added):
            tops[rows, :] = top
            sums[rows, :] = added

        attend(
            valid,
            queries.at[pl.ds(part * PART, PART)],
            ids.at[pl.ds(part * PART, PART)],
            pieces,
            None if first else before[2 * part : 2 * part + 2],
            keep,
            scores,
            peak,
            query_rows,
            part * PART if first else None,
        )


def last_kernel(part, which, *refs):
    valid, columns, queries, ids = refs[:4]
    pieces = list(zip(which, refs[4 : 4 + len(which)]))
    tops, sums, weight, attention, product, scores, peak, query_rows = refs[4 + len(which) :]

    def finish(head, rows, top, added):
        share = added[:, :HD] / added[:, HD:]
        attention[:, pl.ds(head * HD, HD)] = share.astype(BF16)

    attend(
        valid,
        queries.at[pl.ds(part * PART, PART)],
        ids.at[pl.ds(part * PART, PART)],
        pieces,
        (tops, sums),
        finish,
        scores,
        peak,
        query_rows,
        None,
    )
    start = pl.multiple_of(columns[0] * CHUNK, CHUNK)
    product[...] = jnp.dot(
        attention[...], weight[:, pl.ds(start, CHUNK)], preferred_element_type=F32
    ).astype(BF16)


def project_kernel(columns, own, mate, weight, *outs):
    both = jnp.concatenate([own[...], mate[...]], axis=0)
    for at, out in enumerate(outs):
        rows = both if out.shape[0] == 2 * PART else own[...]
        start = pl.multiple_of(columns[at + 1] * CHUNK, CHUNK)
        out[...] = jnp.dot(
            rows, weight[:, pl.ds(start, CHUNK)], preferred_element_type=F32
        ).astype(BF16)


VMEM = pl.BlockSpec(memory_space=pltpu.VMEM)
SMEM = pl.BlockSpec(memory_space=pltpu.SMEM)
PARAMS = pltpu.CompilerParams(vmem_limit_bytes=48 << 20)


def scratch(count):
    return [
        pltpu.VMEM((ROWS, count * TOK), F32),
        pltpu.VMEM((ROWS, HD), F32),
        pltpu.VMEM((ROWS, HD), BF16),
    ]


def costs(flops, size):
    return pl.CostEstimate(flops=int(flops), bytes_accessed=int(size), transcendentals=0)


def early(valid, queries, ids, pieces, state):
    which = [item[0] for item in pieces]
    parts = TOK // PART
    shapes = [jax.ShapeDtypeStruct((ROWS, HD), F32), jax.ShapeDtypeStruct((ROWS, 2 * HD), F32)]
    given = [] if state is None else list(state)
    fixed = 3 + len(which)
    return pl.pallas_call(
        functools.partial(early_kernel, parts, which, state is None),
        out_shape=shapes * parts,
        in_specs=[SMEM] + [VMEM] * (2 + len(which) + len(given)),
        out_specs=[VMEM] * (2 * parts),
        scratch_shapes=scratch(len(which)),
        input_output_aliases={fixed + i: i for i in range(len(given))},
        compiler_params=PARAMS,
        cost_estimate=costs(1.2e9 * len(which), 1 << 20),
        name="attend_early",
    )(valid, queries, ids, *[item[1] for item in pieces], *given)


def last(part, valid, columns, queries, ids, pieces, state, weight):
    which = [item[0] for item in pieces]
    return pl.pallas_call(
        functools.partial(last_kernel, part, which),
        out_shape=[
            jax.ShapeDtypeStruct((PART, HEADS * HD), BF16),
            jax.ShapeDtypeStruct((PART, CHUNK), BF16),
        ],
        in_specs=[SMEM, SMEM] + [VMEM] * (5 + len(which)),
        out_specs=[VMEM] * 2,
        scratch_shapes=scratch(len(which)),
        compiler_params=PARAMS,
        cost_estimate=costs(0.6e9 * len(which), 1 << 20),
        name="attend_last",
    )(valid, columns, queries, ids, *[item[1] for item in pieces], *state, weight)


def project(columns, own, mate, weight):
    wide = jax.ShapeDtypeStruct((2 * PART, CHUNK), BF16)
    return pl.pallas_call(
        project_kernel,
        out_shape=[wide, wide, wide, jax.ShapeDtypeStruct((PART, CHUNK), BF16)],
        in_specs=[SMEM] + [VMEM] * 3,
        out_specs=[VMEM] * 4,
        compiler_params=PARAMS,
        cost_estimate=costs(1.0e9, 1 << 20),
        name="project",
    )(columns, own, mate, weight)


def per_device(queries, key_values, prompt_ids, out_weight):
    stretches, ring = lax.axis_size("loop"), lax.axis_size("tp")
    place, tp = lax.axis_index("loop"), lax.axis_index("tp")
    core, chip = place % 2, place // 2

    def to_mate(value):
        return lax.ppermute(value, "loop", [(i, i ^ 1) for i in range(stretches)])

    def from_chip(value, steps):
        pairs = [(i, (i + 2 * steps) % stretches) for i in range(stretches)]
        return lax.ppermute(value, "loop", pairs)

    def along(value):
        pairs = []
        for loop in range(stretches):
            step = 1 if loop % 2 else ring - 1
            for z in range(ring):
                pairs.append((loop * ring + z, loop * ring + (z + step) % ring))
        return lax.ppermute(value, ("loop", "tp"), pairs)

    ids_row = jnp.pad(prompt_ids.astype(BF16)[None, :], ((0, PIECE - TOK - 1), (0, 0)))
    own = jnp.concatenate([key_values, ids_row], axis=0)
    ids = prompt_ids.astype(F32)[:, None]
    far = [4, 1, 2, 3]
    valid = jnp.stack([jnp.int32(1), core] + [(chip >= s).astype(jnp.int32) for s in (1, 2, 3, 4)])
    side = jnp.where(core == 0, 1, -1)
    columns = jnp.stack([tp + 4, tp + 4 + side, tp + 4 + 2 * side, tp + 4 + 3 * side, tp]) % ring

    received = {s: from_chip(own, s) for s in far}
    pairs = {0: [(0, own), (1, to_mate(own))]}
    for s in far:
        pairs[s] = [(1 + s, received[s]), (1 + s, to_mate(received[s]))]

    state = early(valid, queries, ids, pairs[0], None)
    state = early(valid, queries, ids, pairs[far[0]], state)
    state = early(valid, queries, ids, pairs[far[1]] + pairs[far[2]], state)

    outs = []
    for part in range(TOK // PART):
        attention, product = last(
            part, valid, columns, queries, ids, pairs[far[3]], state[2 * part : 2 * part + 2], out_weight
        )
        extra = along(product)
        one, two, three, mine = project(columns, attention, to_mate(attention), out_weight)
        moved = along(jnp.concatenate([one[:PART] + extra, one[PART:]], axis=0))
        moved = along(two + moved)
        moved = along(three + moved)
        other = to_mate(moved[PART:])
        total = mine.astype(F32) + moved[:PART].astype(F32) + other.astype(F32)
        outs.append(total.astype(BF16))
    return jnp.concatenate(outs, axis=0)


def solution(mesh):
    in_specs = (P("loop", "tp"), P("loop", "tp"), P("loop"), P("tp", None))
    out_specs = P("loop", "tp")
    return jax.shard_map(
        per_device, mesh=mesh, in_specs=in_specs, out_specs=out_specs, check_vma=False
    )
```

time: 134 us -> 83.2 us (0.62)
  the two profiles are of different devices: /device:TPU:12 before, /device:TPU:17 now
where the time goes in v1:
time: 83.2 us; the launch traced here: 82.9 us
  Pallas kernels  29.3 us (35%)
  starting transfers between devices  26.8 us (32%)
  waiting for transfers between devices  22.4 us (27%)
  other arithmetic  2.86 us (3%)
  local copies, waits for them, and re-layouts  1.37 us (2%)
    ppermute x9, starting transfers between devices, to_mate(): return lax.ppermute(value, 'loop', [(i, i ^ 1) for i in range(stretches)])  16.3 us
    ppermute x8, waiting for transfers between devices, along(): return lax.ppermute(value, ('loop', 'tp'), pairs)  12.8 us
    pallas_call x3, Pallas kernels, early(): pl.pallas_call(functools.partial(early_kernel, parts, which, state is Non...  10.7 us
    pallas_call x2, Pallas kernels, last(): pl.pallas_call(functools.partial(last_kernel, part, which), out_shape=[ja...  9.56 us
    pallas_call x2, Pallas kernels, project(): pl.pallas_call(project_kernel, out_shape=[wide, wide, wide, jax.ShapeDtyp...  9.05 us
    ppermute x4, waiting for transfers between devices, from_chip(): return lax.ppermute(value, 'loop', pairs)  8.66 us
    ppermute x8, starting transfers between devices, along(): return lax.ppermute(value, ('loop', 'tp'), pairs)  5.57 us
    ppermute x4, starting transfers between devices, from_chip(): return lax.ppermute(value, 'loop', pairs)  4.91 us
  transfers between devices with their start and end apart: 21, of which 9 were waited for; matrix products, arithmetic and copies ran while one was open for 1% of the time, Pallas kernels for 30%

profile of v1, /device:TPU:17, one launch (start us, length us, event | category | flops | bytes accessed | tf_op | source)
XLA Modules:
  0.0 82.9 jit_solution(11034236093318379621)
XLA Ops:
  0.0 0.8 fusion.3
  0.8 0.9 %fusion.1.refs_3_ = bf16[272,256]{1,0:T(8,128)(2,1)S(1)} fusion(bf16[1,256]{1,0:T(2,128)(2,1)S(1)} %broadcast_in_dim.7, bf16[256,256]{1,0:T(8,128)(2,1)} %param.5), kind=kLoop, calls=%fused_computation.7 | loop fusion | flops 417792 | bytes 270848 | tf_op jit(solution)/shard_map/concatenate | solution.py:226
  1.7 0.8 collective-permute-start.8
  2.4 1.2 %collective-permute-start.6 = (bf16[272,256]{1,0:T(8,128)(2,1)S(1)}, bf16[272,256]{1,0:T(8,128)(2,1)S(1)}, u32[]{:S(2)}, u32[]{:S(2)}) collective-permute-start(bf16[272,256]{1,0:T(8,128)(2,1)S(1)} %fusion.1.refs_3_), channel_id=1, source_target_pairs={{0,64},{8,72},{16,80},{24,88},{32,96},{40,104},{48,112},{56,120},{... | collective-permute-start | bytes 417800 | tf_op jit(solution)/shard_map/ppermute | solution.py:215
  3.7 1.0 %collective-permute-start.2 = (bf16[272,256]{1,0:T(8,128)(2,1)S(1)}, bf16[272,256]{1,0:T(8,128)(2,1)S(1)}, u32[]{:S(2)}, u32[]{:S(2)}) collective-permute-start(bf16[272,256]{1,0:T(8,128)(2,1)S(1)} %fusion.1.refs_3_), channel_id=1, source_target_pairs={{0,16},{8,24},{16,32},{24,40},{32,48},{40,56},{48,64},{56,72},{64,... | collective-permute-start | bytes 417800 | tf_op jit(solution)/shard_map/ppermute | solution.py:215
  4.7 1.3 %collective-permute-start.4 = (bf16[272,256]{1,0:T(8,128)(2,1)S(1)}, bf16[272,256]{1,0:T(8,128)(2,1)S(1)}, u32[]{:S(2)}, u32[]{:S(2)}) collective-permute-start(bf16[272,256]{1,0:T(8,128)(2,1)S(1)} %fusion.1.refs_3_), channel_id=1, source_target_pairs={{0,32},{8,40},{16,48},{24,56},{32,64},{40,72},{48,80},{56,88},{64,... | collective-permute-start | bytes 417800 | tf_op jit(solution)/shard_map/ppermute | solution.py:215
  6.0 1.4 %collective-permute-start = (bf16[272,256]{1,0:T(8,128)(2,1)S(1)}, bf16[272,256]{1,0:T(8,128)(2,1)S(1)}, u32[]{:S(2)}, u32[]{:S(2)}) collective-permute-start(bf16[272,256]{1,0:T(8,128)(2,1)S(1)} %fusion.1.refs_3_), channel_id=1, source_target_pairs={{0,48},{8,56},{16,64},{24,72},{32,80},{40,88},{48,96},{56,104},{64... | collective-permute-start | bytes 417800 | tf_op jit(solution)/shard_map/ppermute | solution.py:215
  7.7 1.2 %collective-permute-done.6.refs_3_ = bf16[272,256]{1,0:T(8,128)(2,1)S(1)} collective-permute-done((bf16[272,256]{1,0:T(8,128)(2,1)S(1)}, bf16[272,256]{1,0:T(8,128)(2,1)S(1)}, u32[]{:S(2)}, u32[]{:S(2)}) %collective-permute-start.6) | collective-permute-done | bytes 139296 | tf_op jit(solution)/shard_map/ppermute | solution.py:215
  8.9 1.3 %collective-permute-start.7 = (bf16[272,256]{1,0:T(8,128)(2,1)S(1)}, bf16[272,256]{1,0:T(8,128)(2,1)S(1)}, u32[]{:S(2)}, u32[]{:S(2)}) collective-permute-start(bf16[272,256]{1,0:T(8,128)(2,1)S(1)} %collective-permute-done.6.refs_3_), channel_id=1, source_target_pairs={{0,8},{8,0},{16,24},{24,16},{32,40},{40,32},{48,56},{56,48},{64,72... | collective-permute-start | bytes 417800 | tf_op jit(solution)/shard_map/ppermute | solution.py:211
  10.2 2.5 %collective-permute-start.3 = (bf16[272,256]{1,0:T(8,128)(2,1)S(1)}, bf16[272,256]{1,0:T(8,128)(2,1)S(1)}, u32[]{:S(2)}, u32[]{:S(2)}) collective-permute-start(bf16[272,256]{1,0:T(8,128)(2,1)S(1)} %collective-permute-done.2.refs_3_), channel_id=1, source_target_pairs={{0,8},{8,0},{16,24},{24,16},{32,40},{40,32},{48,56},{56,48},{64,72... | collective-permute-start | bytes 417800 | tf_op jit(solution)/shard_map/ppermute | solution.py:211
  12.8 7.5 %collective-permute-done.refs_4_ = bf16[272,256]{1,0:T(8,128)(2,1)S(1)} collective-permute-done((bf16[272,256]{1,0:T(8,128)(2,1)S(1)}, bf16[272,256]{1,0:T(8,128)(2,1)S(1)}, u32[]{:S(2)}, u32[]{:S(2)}) %collective-permute-start) | collective-permute-done | bytes 139296 | tf_op jit(solution)/shard_map/ppermute | solution.py:215
  20.2 0.9 %collective-permute-start.1 = (bf16[272,256]{1,0:T(8,128)(2,1)S(1)}, bf16[272,256]{1,0:T(8,128)(2,1)S(1)}, u32[]{:S(2)}, u32[]{:S(2)}) collective-permute-start(bf16[272,256]{1,0:T(8,128)(2,1)S(1)} %collective-permute-done.refs_4_), channel_id=1, source_target_pairs={{0,8},{8,0},{16,24},{24,16},{32,40},{40,32},{48,56},{56,48},{64,72... | collective-permute-start | bytes 417800 | tf_op jit(solution)/shard_map/ppermute | solution.py:211
  21.1 1.0 %copy-done = bf16[256,1024]{1,0:T(8,128)(2,1)S(1)} copy-done((bf16[256,1024]{1,0:T(8,128)(2,1)S(1)}, bf16[256,1024]{1,0:T(8,128)(2,1)}, u32[]{:S(2)}) %copy-start) | copy-done | bytes 524312
  22.2 2.5 %attend_early.3 = (f32[1024,128]{1,0:T(8,128)S(1)}, f32[1024,256]{1,0:T(8,128)S(1)}, f32[1024,128]{1,0:T(8,128)S(1)}, f32[1024,256]{1,0:T(8,128)S(1)}) custom-call(s32[6]{0:T(128)S(1)} %stack.63.refs_0_, bf16[256,1024]{1,0:T(8,128)(2,1)S(1)} %copy-done, f32[256,1]{1,0:T(8,128)S(1)} %copy.16.refs_2_.refs_3_, bf16[272,256]{1,0:T(8,128)(2,1)S(1)} %fusion.1.refs_3_, ...), custom_call_target="tpu_custom_call" | custom-call | flops 2400000000 | bytes 1048576 | tf_op jit(solution)/shard_map/attend_early/pallas_call | solution.py:162
  24.7 3.1 %attend_early.4 = (f32[1024,128]{1,0:T(8,128)S(1)}, f32[1024,256]{1,0:T(8,128)S(1)}, f32[1024,128]{1,0:T(8,128)S(1)}, f32[1024,256]{1,0:T(8,128)S(1)}) custom-call(s32[6]{0:T(128)S(1)} %stack.63.refs_0_, bf16[256,1024]{1,0:T(8,128)(2,1)S(1)} %copy-done, ...), custom_call_target="tpu_custom_call", output_to_operand_aliasing={{0}: (5, {}), {1}: (6, {}), {2}: (7, {}), {3}: (8, {})} | custom-call | flops 2400000000 | bytes 1048576 | tf_op jit(solution)/shard_map/attend_early/pallas_call | solution.py:162
  27.9 5.0 %attend_early.5 = (f32[1024,128]{1,0:T(8,128)S(1)}, f32[1024,256]{1,0:T(8,128)S(1)}, f32[1024,128]{1,0:T(8,128)S(1)}, f32[1024,256]{1,0:T(8,128)S(1)}) custom-call(s32[6]{0:T(128)S(1)} %stack.63.refs_0_, bf16[256,1024]{1,0:T(8,128)(2,1)S(1)} %copy-done, ...), custom_call_target="tpu_custom_call", output_to_operand_aliasing={{0}: (7, {}), {1}: (8, {}), {2}: (9, {}), {3}: (10, {})} | custom-call | flops 4800000000 | bytes 1048576 | tf_op jit(solution)/shard_map/attend_early/pallas_call | solution.py:162
  32.9 4.8 %attend_last.2 = (bf16[128,1024]{1,0:T(8,128)(2,1)S(1)}, bf16[128,512]{1,0:T(8,128)(2,1)S(1)}) custom-call(s32[6]{0:T(128)S(1)} %stack.63.refs_0_, s32[5]{0:T(128)S(1)} %and_select_fusion.refs_1_.columns, bf16[256,1024]{1,0:T(8,128)(2,1)S(1)} %copy-done, f32[256,1]{1,0:T(8,128)S(1)} %copy.16.refs_2_.refs_3_, ...), custom_call_target="tpu_custom_call" | custom-call | flops 1200000000 | bytes 1048576 | tf_op jit(solution)/shard_map/attend_last/pallas_call | solution.py:177
  37.8 1.7 %collective-permute-start.10 = (bf16[128,512]{1,0:T(8,128)(2,1)S(1)}, bf16[128,512]{1,0:T(8,128)(2,1)S(1)}, u32[]{:S(2)}, u32[]{:S(2)}) collective-permute-start(bf16[128,512]{1,0:T(8,128)(2,1)S(1)} %get-tuple-element.44), channel_id=1, source_target_pairs={{0,7},{1,0},{2,1},{3,2},{4,3},{5,4},{6,5},{7,6},{8,9},{9,10},{10,1... | collective-permute-start | bytes 393224 | tf_op jit(solution)/shard_map/ppermute | solution.py:223
  39.5 4.8 %attend_last.3 = (bf16[128,1024]{1,0:T(8,128)(2,1)S(1)}, bf16[128,512]{1,0:T(8,128)(2,1)S(1)}) custom-call(s32[6]{0:T(128)S(1)} %stack.63.refs_0_, s32[5]{0:T(128)S(1)} %and_select_fusion.refs_1_.columns, bf16[256,1024]{1,0:T(8,128)(2,1)S(1)} %copy-done, f32[256,1]{1,0:T(8,128)S(1)} %copy.16.refs_2_.refs_3_, ...), custom_call_target="tpu_custom_call" | custom-call | flops 1200000000 | bytes 1048576 | tf_op jit(solution)/shard_map/attend_last/pallas_call | solution.py:177
  44.3 4.9 %collective-permute-start.15 = (bf16[128,1024]{1,0:T(8,128)(2,1)S(1)}, bf16[128,1024]{1,0:T(8,128)(2,1)S(1)}, u32[]{:S(2)}, u32[]{:S(2)}) collective-permute-start(bf16[128,1024]{1,0:T(8,128)(2,1)S(1)} %get-tuple-element.47.own), channel_id=1, source_target_pairs={{0,8},{8,0},{16,24},{24,16},{32,40},{40,32},{48,56},{56,48},{64,72... | collective-permute-start | bytes 786440 | tf_op jit(solution)/shard_map/ppermute | solution.py:211
  49.2 4.5 %project.2 = (bf16[256,512]{1,0:T(8,128)(2,1)S(1)}, bf16[256,512]{1,0:T(8,128)(2,1)S(1)}, bf16[256,512]{1,0:T(8,128)(2,1)S(1)}, bf16[128,512]{1,0:T(8,128)(2,1)S(1)}) custom-call(s32[5]{0:T(128)S(1)} %and_select_fusion.refs_1_.columns, bf16[128,1024]{1,0:T(8,128)(2,1)S(1)} %get-tuple-element.39.own, bf16[128,1024]{1,0:T(8,128)(2,1)S(1)} %collective-permute-done.9.mate, ...), custom_call_target="tpu_custom_call" | custom-call | flops 1000000000 | bytes 1048576 | tf_op jit(solution)/shard_map/project/pallas_call | solution.py:194
  54.0 4.5 %project.3 = (bf16[256,512]{1,0:T(8,128)(2,1)S(1)}, bf16[256,512]{1,0:T(8,128)(2,1)S(1)}, bf16[256,512]{1,0:T(8,128)(2,1)S(1)}, bf16[128,512]{1,0:T(8,128)(2,1)S(1)}) custom-call(s32[5]{0:T(128)S(1)} %and_select_fusion.refs_1_.columns, bf16[128,1024]{1,0:T(8,128)(2,1)S(1)} %get-tuple-element.47.own, bf16[128,1024]{1,0:T(8,128)(2,1)S(1)} %collective-permute-done.15.mate, ...), custom_call_target="tpu_custom_call" | custom-call | flops 1000000000 | bytes 1048576 | tf_op jit(solution)/shard_map/project/pallas_call | solution.py:194
  58.6 1.6 %collective-permute-start.17 = (bf16[256,512]{1,0:T(8,128)(2,1)S(1)}, bf16[256,512]{1,0:T(8,128)(2,1)S(1)}, u32[]{:S(2)}, u32[]{:S(2)}) collective-permute-start(bf16[256,512]{1,0:T(8,128)(2,1)S(1)} %pad_maximum_fusion.1), channel_id=1, source_target_pairs={{0,7},{1,0},{2,1},{3,2},{4,3},{5,4},{6,5},{7,6},{8,9},{9,10},{10,1... | collective-permute-start | bytes 786440 | tf_op jit(solution)/shard_map/ppermute | solution.py:223
  61.1 4.0 %collective-permute-done.17 = bf16[256,512]{1,0:T(8,128)(2,1)S(1)} collective-permute-done((bf16[256,512]{1,0:T(8,128)(2,1)S(1)}, bf16[256,512]{1,0:T(8,128)(2,1)S(1)}, u32[]{:S(2)}, u32[]{:S(2)}) %collective-permute-start.17) | collective-permute-done | bytes 262176 | tf_op jit(solution)/shard_map/ppermute | solution.py:223
  65.8 2.0 %collective-permute-done.12 = bf16[256,512]{1,0:T(8,128)(2,1)S(1)} collective-permute-done((bf16[256,512]{1,0:T(8,128)(2,1)S(1)}, bf16[256,512]{1,0:T(8,128)(2,1)S(1)}, u32[]{:S(2)}, u32[]{:S(2)}) %collective-permute-start.12) | collective-permute-done | bytes 262176 | tf_op jit(solution)/shard_map/ppermute | solution.py:223
  68.7 3.0 %collective-permute-done.18 = bf16[256,512]{1,0:T(8,128)(2,1)S(1)} collective-permute-done((bf16[256,512]{1,0:T(8,128)(2,1)S(1)}, bf16[256,512]{1,0:T(8,128)(2,1)S(1)}, u32[]{:S(2)}, u32[]{:S(2)}) %collective-permute-start.18) | collective-permute-done | bytes 262176 | tf_op jit(solution)/shard_map/ppermute | solution.py:223
  71.8 2.6 %collective-permute-done.13 = bf16[256,512]{1,0:T(8,128)(2,1)S(1)} collective-permute-done((bf16[256,512]{1,0:T(8,128)(2,1)S(1)}, bf16[256,512]{1,0:T(8,128)(2,1)S(1)}, u32[]{:S(2)}, u32[]{:S(2)}) %collective-permute-start.13) | collective-permute-done | bytes 262176 | tf_op jit(solution)/shard_map/ppermute | solution.py:223
  74.5 2.8 %collective-permute-start.14 = (bf16[128,512]{1,0:T(8,128)(2,1)S(1)}, bf16[128,512]{1,0:T(8,128)(2,1)S(1)}, u32[]{:S(2)}, u32[]{:S(2)}) collective-permute-start(bf16[128,512]{1,0:T(8,128)(2,1)S(1)} %slice.33), channel_id=1, source_target_pairs={{0,8},{8,0},{16,24},{24,16},{32,40},{40,32},{48,56},{56,48},{64,72... | collective-permute-start | bytes 393224 | tf_op jit(solution)/shard_map/ppermute | solution.py:211
  77.3 0.9 %collective-permute-done.19 = bf16[256,512]{1,0:T(8,128)(2,1)S(1)} collective-permute-done((bf16[256,512]{1,0:T(8,128)(2,1)S(1)}, bf16[256,512]{1,0:T(8,128)(2,1)S(1)}, u32[]{:S(2)}, u32[]{:S(2)}) %collective-permute-start.19) | collective-permute-done | bytes 262176 | tf_op jit(solution)/shard_map/ppermute | solution.py:223
  78.2 2.9 %collective-permute-start.20 = (bf16[128,512]{1,0:T(8,128)(2,1)S(1)}, bf16[128,512]{1,0:T(8,128)(2,1)S(1)}, u32[]{:S(2)}, u32[]{:S(2)}) collective-permute-start(bf16[128,512]{1,0:T(8,128)(2,1)S(1)} %slice.35), channel_id=1, source_target_pairs={{0,8},{8,0},{16,24},{24,16},{32,40},{40,32},{48,56},{56,48},{64,72... | collective-permute-start | bytes 393224 | tf_op jit(solution)/shard_map/ppermute | solution.py:211
  81.2 0.9 %collective-permute-done.20 = bf16[128,512]{1,0:T(8,128)(2,1)S(1)} collective-permute-done((bf16[128,512]{1,0:T(8,128)(2,1)S(1)}, bf16[128,512]{1,0:T(8,128)(2,1)S(1)}, u32[]{:S(2)}, u32[]{:S(2)}) %collective-permute-start.20) | collective-permute-done | bytes 131104 | tf_op jit(solution)/shard_map/ppermute | solution.py:211
  82.2 0.7 pad_maximum_fusion.2
  (39 shorter events, 3.3 us)
Async XLA Ops:
  1.7 19.5 %collective-permute-start.8 = (bf16[272,256]{1,0:T(8,128)(2,1)S(1)}, bf16[272,256]{1,0:T(8,128)(2,1)S(1)}, u32[]{:S(2)}, u32[]{:S(2)}) collective-permute-start(bf16[272,256]{1,0:T(8,128)(2,1)S(1)} %fusion.1.refs_3_), channel_id=1, source_target_pairs={{0,8},{8,0},{16,24},{24,16},{32,40},{40,32},{48,56},{56,48},{64,72... | collective-permute-start | bytes 417800 | tf_op jit(solution)/shard_map/ppermute | solution.py:211
  2.4 6.4 %collective-permute-start.6 = (bf16[272,256]{1,0:T(8,128)(2,1)S(1)}, bf16[272,256]{1,0:T(8,128)(2,1)S(1)}, u32[]{:S(2)}, u32[]{:S(2)}) collective-permute-start(bf16[272,256]{1,0:T(8,128)(2,1)S(1)} %fusion.1.refs_3_), channel_id=1, source_target_pairs={{0,64},{8,72},{16,80},{24,88},{32,96},{40,104},{48,112},{56,120},{... | collective-permute-start | bytes 417800 | tf_op jit(solution)/shard_map/ppermute | solution.py:215
  3.7 6.6 %collective-permute-start.2 = (bf16[272,256]{1,0:T(8,128)(2,1)S(1)}, bf16[272,256]{1,0:T(8,128)(2,1)S(1)}, u32[]{:S(2)}, u32[]{:S(2)}) collective-permute-start(bf16[272,256]{1,0:T(8,128)(2,1)S(1)} %fusion.1.refs_3_), channel_id=1, source_target_pairs={{0,16},{8,24},{16,32},{24,40},{32,48},{40,56},{48,64},{56,72},{64,... | collective-permute-start | bytes 417800 | tf_op jit(solution)/shard_map/ppermute | solution.py:215
  4.7 8.1 %collective-permute-start.4 = (bf16[272,256]{1,0:T(8,128)(2,1)S(1)}, bf16[272,256]{1,0:T(8,128)(2,1)S(1)}, u32[]{:S(2)}, u32[]{:S(2)}) collective-permute-start(bf16[272,256]{1,0:T(8,128)(2,1)S(1)} %fusion.1.refs_3_), channel_id=1, source_target_pairs={{0,32},{8,40},{16,48},{24,56},{32,64},{40,72},{48,80},{56,88},{64,... | collective-permute-start | bytes 417800 | tf_op jit(solution)/shard_map/ppermute | solution.py:215
  6.0 14.3 %collective-permute-start = (bf16[272,256]{1,0:T(8,128)(2,1)S(1)}, bf16[272,256]{1,0:T(8,128)(2,1)S(1)}, u32[]{:S(2)}, u32[]{:S(2)}) collective-permute-start(bf16[272,256]{1,0:T(8,128)(2,1)S(1)} %fusion.1.refs_3_), channel_id=1, source_target_pairs={{0,48},{8,56},{16,64},{24,72},{32,80},{40,88},{48,96},{56,104},{64... | collective-permute-start | bytes 417800 | tf_op jit(solution)/shard_map/ppermute | solution.py:215
  8.9 15.8 %collective-permute-start.7 = (bf16[272,256]{1,0:T(8,128)(2,1)S(1)}, bf16[272,256]{1,0:T(8,128)(2,1)S(1)}, u32[]{:S(2)}, u32[]{:S(2)}) collective-permute-start(bf16[272,256]{1,0:T(8,128)(2,1)S(1)} %collective-permute-done.6.refs_3_), channel_id=1, source_target_pairs={{0,8},{8,0},{16,24},{24,16},{32,40},{40,32},{48,56},{56,48},{64,72... | collective-permute-start | bytes 417800 | tf_op jit(solution)/shard_map/ppermute | solution.py:211
  10.2 17.6 %collective-permute-start.3 = (bf16[272,256]{1,0:T(8,128)(2,1)S(1)}, bf16[272,256]{1,0:T(8,128)(2,1)S(1)}, u32[]{:S(2)}, u32[]{:S(2)}) collective-permute-start(bf16[272,256]{1,0:T(8,128)(2,1)S(1)} %collective-permute-done.2.refs_3_), channel_id=1, source_target_pairs={{0,8},{8,0},{16,24},{24,16},{32,40},{40,32},{48,56},{56,48},{64,72... | collective-permute-start | bytes 417800 | tf_op jit(solution)/shard_map/ppermute | solution.py:211
  12.7 15.1 %collective-permute-start.5 = (bf16[272,256]{1,0:T(8,128)(2,1)S(1)}, bf16[272,256]{1,0:T(8,128)(2,1)S(1)}, u32[]{:S(2)}, u32[]{:S(2)}) collective-permute-start(bf16[272,256]{1,0:T(8,128)(2,1)S(1)} %collective-permute-done.4.refs_5_), channel_id=1, source_target_pairs={{0,8},{8,0},{16,24},{24,16},{32,40},{40,32},{48,56},{56,48},{64,72... | collective-permute-start | bytes 417800 | tf_op jit(solution)/shard_map/ppermute | solution.py:211
  20.2 12.7 %collective-permute-start.1 = (bf16[272,256]{1,0:T(8,128)(2,1)S(1)}, bf16[272,256]{1,0:T(8,128)(2,1)S(1)}, u32[]{:S(2)}, u32[]{:S(2)}) collective-permute-start(bf16[272,256]{1,0:T(8,128)(2,1)S(1)} %collective-permute-done.refs_4_), channel_id=1, source_target_pairs={{0,8},{8,0},{16,24},{24,16},{32,40},{40,32},{48,56},{56,48},{64,72... | collective-permute-start | bytes 417800 | tf_op jit(solution)/shard_map/ppermute | solution.py:211
  21.1 1.0 %copy-start = (bf16[256,1024]{1,0:T(8,128)(2,1)S(1)}, bf16[256,1024]{1,0:T(8,128)(2,1)}, u32[]{:S(2)}) copy-start(bf16[256,1024]{1,0:T(8,128)(2,1)} %refs_2_.3) | copy-start | bytes 1572868
  37.7 11.6 %collective-permute-start.9 = (bf16[128,1024]{1,0:T(8,128)(2,1)S(1)}, bf16[128,1024]{1,0:T(8,128)(2,1)S(1)}, u32[]{:S(2)}, u32[]{:S(2)}) collective-permute-start(bf16[128,1024]{1,0:T(8,128)(2,1)S(1)} %get-tuple-element.39.own), channel_id=1, source_target_pairs={{0,8},{8,0},{16,24},{24,16},{32,40},{40,32},{48,56},{56,48},{64,72... | collective-permute-start | bytes 786440 | tf_op jit(solution)/shard_map/ppermute | solution.py:211
  37.8 16.0 %collective-permute-start.10 = (bf16[128,512]{1,0:T(8,128)(2,1)S(1)}, bf16[128,512]{1,0:T(8,128)(2,1)S(1)}, u32[]{:S(2)}, u32[]{:S(2)}) collective-permute-start(bf16[128,512]{1,0:T(8,128)(2,1)S(1)} %get-tuple-element.44), channel_id=1, source_target_pairs={{0,7},{1,0},{2,1},{3,2},{4,3},{5,4},{6,5},{7,6},{8,9},{9,10},{10,1... | collective-permute-start | bytes 393224 | tf_op jit(solution)/shard_map/ppermute | solution.py:223
  44.3 9.6 %collective-permute-start.15 = (bf16[128,1024]{1,0:T(8,128)(2,1)S(1)}, bf16[128,1024]{1,0:T(8,128)(2,1)S(1)}, u32[]{:S(2)}, u32[]{:S(2)}) collective-permute-start(bf16[128,1024]{1,0:T(8,128)(2,1)S(1)} %get-tuple-element.47.own), channel_id=1, source_target_pairs={{0,8},{8,0},{16,24},{24,16},{32,40},{40,32},{48,56},{56,48},{64,72... | collective-permute-start | bytes 786440 | tf_op jit(solution)/shard_map/ppermute | solution.py:211
  49.2 9.2 %collective-permute-start.16 = (bf16[128,512]{1,0:T(8,128)(2,1)S(1)}, bf16[128,512]{1,0:T(8,128)(2,1)S(1)}, u32[]{:S(2)}, u32[]{:S(2)}) collective-permute-start(bf16[128,512]{1,0:T(8,128)(2,1)S(1)} %get-tuple-element.52), channel_id=1, source_target_pairs={{0,7},{1,0},{2,1},{3,2},{4,3},{5,4},{6,5},{7,6},{8,9},{9,10},{10,1... | collective-permute-start | bytes 393224 | tf_op jit(solution)/shard_map/ppermute | solution.py:223
  53.9 6.5 %collective-permute-start.11 = (bf16[256,512]{1,0:T(8,128)(2,1)S(1)}, bf16[256,512]{1,0:T(8,128)(2,1)S(1)}, u32[]{:S(2)}, u32[]{:S(2)}) collective-permute-start(bf16[256,512]{1,0:T(8,128)(2,1)S(1)} %pad_maximum_fusion), channel_id=1, source_target_pairs={{0,7},{1,0},{2,1},{3,2},{4,3},{5,4},{6,5},{7,6},{8,9},{9,10},{10,1... | collective-permute-start | bytes 786440 | tf_op jit(solution)/shard_map/ppermute | solution.py:223
  58.6 6.5 %collective-permute-start.17 = (bf16[256,512]{1,0:T(8,128)(2,1)S(1)}, bf16[256,512]{1,0:T(8,128)(2,1)S(1)}, u32[]{:S(2)}, u32[]{:S(2)}) collective-permute-start(bf16[256,512]{1,0:T(8,128)(2,1)S(1)} %pad_maximum_fusion.1), channel_id=1, source_target_pairs={{0,7},{1,0},{2,1},{3,2},{4,3},{5,4},{6,5},{7,6},{8,9},{9,10},{10,1... | collective-permute-start | bytes 786440 | tf_op jit(solution)/shard_map/ppermute | solution.py:223
  60.4 7.4 %collective-permute-start.12 = (bf16[256,512]{1,0:T(8,128)(2,1)S(1)}, bf16[256,512]{1,0:T(8,128)(2,1)S(1)}, u32[]{:S(2)}, u32[]{:S(2)}) collective-permute-start(bf16[256,512]{1,0:T(8,128)(2,1)S(1)} %add.65), channel_id=1, source_target_pairs={{0,7},{1,0},{2,1},{3,2},{4,3},{5,4},{6,5},{7,6},{8,9},{9,10},{10,1... | collective-permute-start | bytes 786440 | tf_op jit(solution)/shard_map/ppermute | solution.py:223
  65.1 6.5 %collective-permute-start.18 = (bf16[256,512]{1,0:T(8,128)(2,1)S(1)}, bf16[256,512]{1,0:T(8,128)(2,1)S(1)}, u32[]{:S(2)}, u32[]{:S(2)}) collective-permute-start(bf16[256,512]{1,0:T(8,128)(2,1)S(1)} %add.70), channel_id=1, source_target_pairs={{0,7},{1,0},{2,1},{3,2},{4,3},{5,4},{6,5},{7,6},{8,9},{9,10},{10,1... | collective-permute-start | bytes 786440 | tf_op jit(solution)/shard_map/ppermute | solution.py:223
  68.0 6.5 %collective-permute-start.13 = (bf16[256,512]{1,0:T(8,128)(2,1)S(1)}, bf16[256,512]{1,0:T(8,128)(2,1)S(1)}, u32[]{:S(2)}, u32[]{:S(2)}) collective-permute-start(bf16[256,512]{1,0:T(8,128)(2,1)S(1)} %add.66), channel_id=1, source_target_pairs={{0,7},{1,0},{2,1},{3,2},{4,3},{5,4},{6,5},{7,6},{8,9},{9,10},{10,1... | collective-permute-start | bytes 786440 | tf_op jit(solution)/shard_map/ppermute | solution.py:223
  71.7 6.5 %collective-permute-start.19 = (bf16[256,512]{1,0:T(8,128)(2,1)S(1)}, bf16[256,512]{1,0:T(8,128)(2,1)S(1)}, u32[]{:S(2)}, u32[]{:S(2)}) collective-permute-start(bf16[256,512]{1,0:T(8,128)(2,1)S(1)} %add.71), channel_id=1, source_target_pairs={{0,7},{1,0},{2,1},{3,2},{4,3},{5,4},{6,5},{7,6},{8,9},{9,10},{10,1... | collective-permute-start | bytes 786440 | tf_op jit(solution)/shard_map/ppermute | solution.py:223
  74.5 6.7 %collective-permute-start.14 = (bf16[128,512]{1,0:T(8,128)(2,1)S(1)}, bf16[128,512]{1,0:T(8,128)(2,1)S(1)}, u32[]{:S(2)}, u32[]{:S(2)}) collective-permute-start(bf16[128,512]{1,0:T(8,128)(2,1)S(1)} %slice.33), channel_id=1, source_target_pairs={{0,8},{8,0},{16,24},{24,16},{32,40},{40,32},{48,56},{56,48},{64,72... | collective-permute-start | bytes 393224 | tf_op jit(solution)/shard_map/ppermute | solution.py:211
  78.2 3.9 %collective-permute-start.20 = (bf16[128,512]{1,0:T(8,128)(2,1)S(1)}, bf16[128,512]{1,0:T(8,128)(2,1)S(1)}, u32[]{:S(2)}, u32[]{:S(2)}) collective-permute-start(bf16[128,512]{1,0:T(8,128)(2,1)S(1)} %slice.35), channel_id=1, source_target_pairs={{0,8},{8,0},{16,24},{24,16},{32,40},{40,32},{48,56},{56,48},{64,72... | collective-permute-start | bytes 393224 | tf_op jit(solution)/shard_map/ppermute | solution.py:211

commit v2 on v1

v2 whole, which is shorter than its diff:
```python
import functools
import math

import jax
import jax.numpy as jnp
from jax import lax
from jax.experimental import pallas as pl
from jax.experimental.pallas import tpu as pltpu
from jax.sharding import PartitionSpec as P

HD = 128
HEADS = 8
TOK = 256
PART = 128
ROWS = HEADS * TOK
PIECE = TOK + 16
CHUNK = 512
SCALE = 1.0 / math.sqrt(HD)
MASKED = -1e30
F32 = jnp.float32
BF16 = jnp.bfloat16


def allowed_keys(valid, own_ids, which, piece, causal):
    key_ids = piece[TOK:PIECE, :][0:1, :].astype(F32)
    key_ids = jnp.where(valid[which] > 0, key_ids, -1.0)
    allowed = own_ids == key_ids
    if causal:
        shape = (own_ids.shape[0], TOK)
        rows = lax.broadcasted_iota(jnp.int32, shape, 0)
        allowed = allowed & (lax.broadcasted_iota(jnp.int32, shape, 1) <= rows)
    return allowed


def attend(valid, query_rows, ids, first, size, pieces, before, keep, scores, peak, causal=False):
    count = len(pieces)
    own_ids = ids[pl.ds(first, size), :]
    masks = [allowed_keys(valid, own_ids, which, piece, causal) for which, piece in pieces]
    for head in range(HEADS):
        rows = pl.ds(head * TOK + first, size)
        best = None
        for at, (_, piece) in enumerate(pieces):
            found = lax.dot_general(
                query_rows[rows, :],
                piece[0:TOK, 0:HD],
                (((1,), (1,)), ((), ())),
                preferred_element_type=F32,
            )
            found = jnp.where(masks[at], found, MASKED)
            scores[rows, at * TOK : (at + 1) * TOK] = found
            here = jnp.maximum(found[:, :HD], found[:, HD:])
            best = here if best is None else jnp.maximum(best, here)
        peak[rows, :] = best
    ones = jnp.ones((TOK, HD), BF16)
    values = jnp.concatenate(
        [jnp.concatenate([piece[0:TOK, HD:], ones], axis=1) for _, piece in pieces], axis=0
    )
    for head in range(HEADS):
        rows = pl.ds(head * TOK + first, size)
        top = jnp.broadcast_to(jnp.max(peak[rows, :], axis=1, keepdims=True), (size, HD))
        if before is not None:
            old = before[0][rows, :]
            top = jnp.maximum(top, old)
        wide = jnp.concatenate([top] * (2 * count), axis=1)
        probs = jnp.exp((scores[rows, 0 : count * TOK] - wide) * SCALE).astype(BF16)
        added = jnp.dot(probs, values, preferred_element_type=F32)
        if before is not None:
            shrink = jnp.exp((old - top) * SCALE)
            added = added + before[1][rows, :] * jnp.concatenate([shrink, shrink], axis=1)
        keep(head, rows, top, added)


def open_kernel(valid, queries, ids, piece, tops, sums, query_rows, scores, peak):
    for head in range(HEADS):
        query_rows[pl.ds(head * TOK, TOK), :] = queries[:, pl.ds(head * HD, HD)]

    def keep(head, rows, top, added):
        tops[rows, :] = top
        sums[rows, :] = added

    attend(valid, query_rows, ids, 0, TOK, [(0, piece)], None, keep, scores, peak, causal=True)


def middle_kernel(which, valid, query_rows, ids, *refs):
    pieces = list(zip(which, refs[: len(which)]))
    old_tops, old_sums, tops, sums, scores, peak = refs[len(which) :]

    def keep(head, rows, top, added):
        tops[rows, :] = top
        sums[rows, :] = added

    attend(valid, query_rows, ids, 0, TOK, pieces, (old_tops, old_sums), keep, scores, peak)


def last_kernel(part, which, valid, columns, query_rows, ids, *refs):
    pieces = list(zip(which, refs[: len(which)]))
    tops, sums, weight, attention, product, scores, peak = refs[len(which) :]

    def finish(head, rows, top, added):
        share = added[:, :HD] / added[:, HD:]
        attention[:, pl.ds(head * HD, HD)] = share.astype(BF16)

    attend(
        valid, query_rows, ids, part * PART, PART, pieces, (tops, sums), finish, scores, peak
    )
    group = pl.ds(pl.multiple_of(columns[0] * CHUNK, CHUNK), CHUNK)
    product[...] = jnp.dot(
        attention[...], weight[:, group], preferred_element_type=F32
    ).astype(BF16)


def project_kernel(columns, own, mate, weight, *outs):
    both = jnp.concatenate([own[...], mate[...]], axis=0)
    for at, out in enumerate(outs):
        rows = both if out.shape[0] == 2 * PART else own[...]
        group = pl.ds(pl.multiple_of(columns[at + 1] * CHUNK, CHUNK), CHUNK)
        out[...] = jnp.dot(rows, weight[:, group], preferred_element_type=F32).astype(BF16)


VMEM = pl.BlockSpec(memory_space=pltpu.VMEM)
SMEM = pl.BlockSpec(memory_space=pltpu.SMEM)
PARAMS = pltpu.CompilerParams(vmem_limit_bytes=24 << 20)
STATE = [jax.ShapeDtypeStruct((ROWS, HD), F32), jax.ShapeDtypeStruct((ROWS, 2 * HD), F32)]


def scratch(count):
    return [pltpu.VMEM((ROWS, count * TOK), F32), pltpu.VMEM((ROWS, HD), F32)]


def costs(flops, size):
    return pl.CostEstimate(flops=int(flops), bytes_accessed=int(size), transcendentals=0)


def opening(valid, queries, ids, piece):
    outs = pl.pallas_call(
        open_kernel,
        out_shape=STATE + [jax.ShapeDtypeStruct((ROWS, HD), BF16)],
        in_specs=[SMEM] + [VMEM] * 3,
        out_specs=[VMEM] * 3,
        scratch_shapes=scratch(1),
        compiler_params=PARAMS,
        cost_estimate=costs(1e6, 1 << 10),
        name="attend_own",
    )(valid, queries, ids, piece)
    return outs[:2], outs[2]


def middle(valid, query_rows, ids, pieces, state):
    which = [item[0] for item in pieces]
    fixed = 3 + len(which)
    return pl.pallas_call(
        functools.partial(middle_kernel, which),
        out_shape=STATE,
        in_specs=[SMEM] + [VMEM] * (4 + len(which)),
        out_specs=[VMEM] * 2,
        scratch_shapes=scratch(len(which)),
        input_output_aliases={fixed: 0, fixed + 1: 1},
        compiler_params=PARAMS,
        cost_estimate=costs(1e6, 1 << 10),
        name="attend_more",
    )(valid, query_rows, ids, *[item[1] for item in pieces], *state)


def last(part, valid, columns, query_rows, ids, pieces, state, weight):
    which = [item[0] for item in pieces]
    return pl.pallas_call(
        functools.partial(last_kernel, part, which),
        out_shape=[
            jax.ShapeDtypeStruct((PART, HEADS * HD), BF16),
            jax.ShapeDtypeStruct((PART, CHUNK), BF16),
        ],
        in_specs=[SMEM, SMEM] + [VMEM] * (5 + len(which)),
        out_specs=[VMEM] * 2,
        scratch_shapes=scratch(len(which)),
        compiler_params=PARAMS,
        cost_estimate=costs(1.5e9, 1 << 20),
        name="attend_last",
    )(valid, columns, query_rows, ids, *[item[1] for item in pieces], *state, weight)


def project(columns, own, mate, weight):
    wide = jax.ShapeDtypeStruct((2 * PART, CHUNK), BF16)
    return pl.pallas_call(
        project_kernel,
        out_shape=[wide, wide, wide, jax.ShapeDtypeStruct((PART, CHUNK), BF16)],
        in_specs=[SMEM] + [VMEM] * 3,
        out_specs=[VMEM] * 4,
        compiler_params=PARAMS,
        cost_estimate=costs(1.5e9, 1 << 20),
        name="project",
    )(columns, own, mate, weight)


def per_device(queries, key_values, prompt_ids, out_weight):
    stretches, ring = lax.axis_size("loop"), lax.axis_size("tp")
    place, tp = lax.axis_index("loop"), lax.axis_index("tp")
    core, chip = place % 2, place // 2
    row = 8

    def to_mate(value):
        return lax.ppermute(value, "loop", [(i, i ^ 1) for i in range(stretches)])

    def from_chip(value, steps):
        pairs = [(i, (i + 2 * steps) % stretches) for i in range(stretches)]
        return lax.ppermute(value, "loop", pairs)

    def along_row(value, steps):
        pairs = [(i, i // row * row + (i + 2 * steps) % row) for i in range(stretches)]
        return lax.ppermute(value, "loop", pairs)

    def along(value):
        pairs = []
        for loop in range(stretches):
            step = 1 if loop % 2 else ring - 1
            for z in range(ring):
                pairs.append((loop * ring + z, loop * ring + (z + step) % ring))
        return lax.ppermute(value, ("loop", "tp"), pairs)

    ids_row = jnp.broadcast_to(prompt_ids.astype(BF16)[None, :], (PIECE - TOK, TOK))
    own = jnp.concatenate([key_values, ids_row], axis=0)
    ids = prompt_ids.astype(F32)[:, None]
    there = [(chip >= s).astype(jnp.int32) for s in (1, 2, 3, 4)]
    valid = jnp.stack([jnp.int32(1)] + there + [jnp.maximum(core, there[3])])
    side = jnp.where(core == 0, 1, -1)
    columns = jnp.stack([tp + 4, tp + 4 + side, tp + 4 + 2 * side, tp + 4 + 3 * side, tp]) % ring

    chip4 = from_chip(own, 4)
    chip1 = from_chip(own, 1)
    chip2 = from_chip(own, 2)
    state, query_rows = opening(valid, queries, ids, own)
    (chip4, state) = lax.optimization_barrier((chip4, state))
    chip3 = along_row(jnp.where(chip % 4 == 0, own, chip4), 3)
    beside = to_mate(jnp.where(core == 0, own, chip4))
    mate1 = to_mate(chip1)
    state = middle(valid, query_rows, ids, [(4, chip4), (5, beside)], state)
    (chip2, chip3, state) = lax.optimization_barrier((chip2, chip3, state))
    mate2 = to_mate(chip2)
    mate3 = to_mate(chip3)
    near = [(1, chip1), (1, mate1), (2, chip2), (2, mate2)]
    state = middle(valid, query_rows, ids, near, state)

    outs = []
    for part in range(TOK // PART):
        attention, product = last(
            part, valid, columns, query_rows, ids, [(3, chip3), (3, mate3)], state, out_weight
        )
        extra = along(product)
        one, two, three, mine = project(columns, attention, to_mate(attention), out_weight)
        moved = along(jnp.concatenate([one[:PART] + extra, one[PART:]], axis=0))
        moved = along(two + moved)
        moved = along(three + moved)
        other = to_mate(moved[PART:])
        total = mine.astype(F32) + moved[:PART].astype(F32) + other.astype(F32)
        outs.append(total.astype(BF16))
    return jnp.concatenate(outs, axis=0)


def solution(mesh):
    in_specs = (P("loop", "tp"), P("loop", "tp"), P("loop"), P("tp", None))
    out_specs = P("loop", "tp")
    return jax.shard_map(
        per_device, mesh=mesh, in_specs=in_specs, out_specs=out_specs, check_vma=False
    )
```

time: 83.2 us -> 70.7 us (0.85)
  the two profiles are of different devices: /device:TPU:17 before, /device:TPU:1 now
where the time goes in v2:
time: 70.7 us; the launch traced here: 70.4 us
  starting transfers between devices  22.5 us (32%)
  waiting for transfers between devices  20.2 us (29%)
  Pallas kernels  17.8 us (25%)
  other arithmetic  5.2 us (7%)
  local copies, waits for them, and re-layouts  4.45 us (6%)
    ppermute x8, waiting for transfers between devices, along(): return lax.ppermute(value, ('loop', 'tp'), pairs)  17.8 us
    ppermute x8, starting transfers between devices, to_mate(): return lax.ppermute(value, 'loop', [(i, i ^ 1) for i in range(stretches)])  13.1 us
    pallas_call x2, Pallas kernels, middle(): pl.pallas_call(functools.partial(middle_kernel, which), out_shape=STATE,...  8.87 us
    ppermute x3, starting transfers between devices, from_chip(): return lax.ppermute(value, 'loop', pairs)  4.87 us
    pallas_call x2, Pallas kernels, last(): pl.pallas_call(functools.partial(last_kernel, part, which), out_shape=[ja...  3.77 us
    unnamed x14, local copies, waits for them, and re-layouts  3.54 us
    pallas_call x2, Pallas kernels, project(): pl.pallas_call(project_kernel, out_shape=[wide, wide, wide, jax.ShapeDtyp...  3.33 us
    ppermute x8, starting transfers between devices, along(): return lax.ppermute(value, ('loop', 'tp'), pairs)  2.68 us
  transfers between devices with their start and end apart: 20, of which 10 were waited for; matrix products, arithmetic and copies ran while one was open for 4% of the time, Pallas kernels for 23%

profile of v2, /device:TPU:1, one launch (start us, length us, event | category | flops | bytes accessed | tf_op | source)
XLA Modules:
  0.0 70.4 jit_solution(688671804776248077)
XLA Ops:
  0.0 0.8 %fusion.1 = (bf16[256]{0:T(256)(128)(2,1)S(1)}, f32[256]{0:T(256)S(1)}) fusion(s32[256]{0:T(256)} %param.6), kind=kLoop, calls=%fused_computation.14 | loop fusion | flops 512 | bytes 2560 | tf_op jit(solution)/shard_map/convert_element_type | solution.py:219
  0.8 1.6 %pad_maximum_fusion.3.piece = bf16[272,256]{1,0:T(8,128)(2,1)} fusion(bf16[16,256]{1,0:T(8,128)(2,1)S(1)} %broadcast_in_dim.10, bf16[256,256]{1,0:T(8,128)(2,1)} %param.5), kind=kLoop, calls=%fused_computation.5 | loop fusion | flops 278528 | bytes 278528 | tf_op jit(solution)/shard_map/concatenate | solution.py:220
  2.3 2.0 %collective-permute-start.1 = (bf16[272,256]{1,0:T(8,128)(2,1)}, bf16[272,256]{1,0:T(8,128)(2,1)S(1)}, u32[]{:S(2)}, u32[]{:S(2)}) collective-permute-start(bf16[272,256]{1,0:T(8,128)(2,1)} %pad_maximum_fusion.3.piece), channel_id=1, source_target_pairs={{0,64},{8,72},{16,80},{24,88},{32,96},{40,104},{48,112},{56,120},{... | collective-permute-start | bytes 417800 | tf_op jit(solution)/shard_map/ppermute | solution.py:205
  4.4 1.3 %collective-permute-start.5 = (bf16[272,256]{1,0:T(8,128)(2,1)}, bf16[272,256]{1,0:T(8,128)(2,1)}, u32[]{:S(2)}, u32[]{:S(2)}) collective-permute-start(bf16[272,256]{1,0:T(8,128)(2,1)} %pad_maximum_fusion.3.piece), channel_id=1, source_target_pairs={{0,16},{8,24},{16,32},{24,40},{32,48},{40,56},{48,64},{56,72},{64,... | collective-permute-start | bytes 417800 | tf_op jit(solution)/shard_map/ppermute | solution.py:205
  5.9 1.0 %copy-done.3 = bf16[256,1024]{1,0:T(8,128)(2,1)S(1)} copy-done((bf16[256,1024]{1,0:T(8,128)(2,1)S(1)}, bf16[256,1024]{1,0:T(8,128)(2,1)}, u32[]{:S(2)}) %copy-start.3) | copy-done | bytes 524312
  7.0 1.9 %attend_own.1 = (f32[2048,128]{1,0:T(8,128)S(1)}, f32[2048,256]{1,0:T(8,128)S(1)}, bf16[2048,128]{1,0:T(8,128)(2,1)S(1)}) custom-call(s32[6]{0:T(128)S(1)} %stack.59.valid, bf16[256,1024]{1,0:T(8,128)(2,1)S(1)} %copy-done.3, f32[256,1]{1,0:T(8,128)S(1)} %copy.9.ids, bf16[272,256]{1,0:T(8,128)(2,1)} %pad_maximum_fusion.3.piece), custom_call_target="tpu_custom_call" | custom-call | flops 1000000 | bytes 1024 | tf_op jit(solution)/shard_map/attend_own/pallas_call | solution.py:135
  8.8 0.8 %copy-done.1 = bf16[2048,128]{1,0:T(8,128)(2,1)} copy-done((bf16[2048,128]{1,0:T(8,128)(2,1)}, bf16[2048,128]{1,0:T(8,128)(2,1)S(1)}, u32[]{:S(2)}) %copy-start.1) | copy-done | bytes 524312
  9.6 1.7 %broadcast_select_fusion = (bf16[272,256]{1,0:T(8,128)(2,1)}, bf16[272,256]{1,0:T(8,128)(2,1)}) fusion(bf16[272,256]{1,0:T(8,128)(2,1)S(1)} %collective-permute-done.1.refs_0_, pred[]{:T(512)S(6)} %eq.12, bf16[16,256]{1,0:T(8,128)(2,1)S(1)} %broadcast_in_dim.10, bf16[256,256]{1,0:T(8,128)(2,1)} %param.5, pred[]{:T(512)S(6)} %eq.13), kind=kLoop, calls=%fused_computation.6 | loop fusion | flops 417792 | bytes 557058 | tf_op jit(solution)/shard_map/jit(_where)/select_n | solution.py:233
  11.3 2.4 %collective-permute-start.3 = (bf16[272,256]{1,0:T(8,128)(2,1)}, bf16[272,256]{1,0:T(8,128)(2,1)}, u32[]{:S(2)}, u32[]{:S(2)}) collective-permute-start(bf16[272,256]{1,0:T(8,128)(2,1)} %get-tuple-element.57), channel_id=1, source_target_pairs={{0,8},{8,0},{16,24},{24,16},{32,40},{40,32},{48,56},{56,48},{64,72... | collective-permute-start | bytes 417800 | tf_op jit(solution)/shard_map/ppermute | solution.py:201
  13.7 1.5 %collective-permute-start = (bf16[272,256]{1,0:T(8,128)(2,1)}, bf16[272,256]{1,0:T(8,128)(2,1)}, u32[]{:S(2)}, u32[]{:S(2)}) collective-permute-start(bf16[272,256]{1,0:T(8,128)(2,1)} %pad_maximum_fusion.3.piece), channel_id=1, source_target_pairs={{0,32},{8,40},{16,48},{24,56},{32,64},{40,72},{48,80},{56,88},{64,... | collective-permute-start | bytes 417800 | tf_op jit(solution)/shard_map/ppermute | solution.py:205
  15.3 1.9 %collective-permute-start.2 = (bf16[272,256]{1,0:T(8,128)(2,1)}, bf16[272,256]{1,0:T(8,128)(2,1)S(1)}, u32[]{:S(2)}, u32[]{:S(2)}) collective-permute-start(bf16[272,256]{1,0:T(8,128)(2,1)} %get-tuple-element.58), channel_id=1, source_target_pairs={{0,48},{8,56},{16,0},{24,8},{32,16},{40,24},{48,32},{56,40},{64,11... | collective-permute-start | bytes 417800 | tf_op jit(solution)/shard_map/ppermute | solution.py:209
  18.4 1.0 %copy-done.2 = bf16[2048,128]{1,0:T(8,128)(2,1)S(1)} copy-done((bf16[2048,128]{1,0:T(8,128)(2,1)S(1)}, bf16[2048,128]{1,0:T(8,128)(2,1)}, u32[]{:S(2)}) %copy-start.2) | copy-done | bytes 524312
  20.1 3.6 %attend_more.2 = (f32[2048,128]{1,0:T(8,128)S(1)}, f32[2048,256]{1,0:T(8,128)S(1)}) custom-call(s32[6]{0:T(128)S(1)} %copy-done.5, bf16[2048,128]{1,0:T(8,128)(2,1)S(1)} %copy-done.2, f32[256,1]{1,0:T(8,128)S(1)} %copy.9.ids, bf16[272,256]{1,0:T(8,128)(2,1)S(1)} %collective-permute-done.1.refs_0_, ...), custom_call_target="tpu_custom_call", output_to_operand_aliasing={{0}: (5, {}), {1}: (6, {})} | custom-call | flops 1000000 | bytes 1024 | tf_op jit(solution)/shard_map/attend_more/pallas_call | solution.py:151
  23.9 0.8 %collective-permute-start.7 = (bf16[272,256]{1,0:T(8,128)(2,1)}, bf16[272,256]{1,0:T(8,128)(2,1)S(1)}, u32[]{:S(2)}, u32[]{:S(2)}) collective-permute-start(bf16[272,256]{1,0:T(8,128)(2,1)} %collective-permute-done.refs_2_), channel_id=1, source_target_pairs={{0,8},{8,0},{16,24},{24,16},{32,40},{40,32},{48,56},{56,48},{64,72... | collective-permute-start | bytes 417800 | tf_op jit(solution)/shard_map/ppermute | solution.py:201
  24.7 1.3 %collective-permute-done.7.refs_3_ = bf16[272,256]{1,0:T(8,128)(2,1)S(1)} collective-permute-done((bf16[272,256]{1,0:T(8,128)(2,1)}, bf16[272,256]{1,0:T(8,128)(2,1)S(1)}, u32[]{:S(2)}, u32[]{:S(2)}) %collective-permute-start.7) | collective-permute-done | bytes 139296 | tf_op jit(solution)/shard_map/ppermute | solution.py:201
  26.0 5.2 %attend_more.3 = (f32[2048,128]{1,0:T(8,128)S(1)}, f32[2048,256]{1,0:T(8,128)S(1)}) custom-call(s32[6]{0:T(128)S(1)} %copy-done.5, bf16[2048,128]{1,0:T(8,128)(2,1)S(1)} %copy-done.2, f32[256,1]{1,0:T(8,128)S(1)} %copy.9.ids, bf16[272,256]{1,0:T(8,128)(2,1)} %collective-permute-done.5.refs_0_, ...), custom_call_target="tpu_custom_call", output_to_operand_aliasing={{0}: (7, {}), {1}: (8, {})} | custom-call | flops 1000000 | bytes 1024 | tf_op jit(solution)/shard_map/attend_more/pallas_call | solution.py:151
  31.3 1.9 %attend_last.2 = (bf16[128,1024]{1,0:T(8,128)(2,1)S(1)}, bf16[128,512]{1,0:T(8,128)(2,1)S(1)}) custom-call(s32[6]{0:T(128)S(1)} %copy-done.5, s32[5]{0:T(128)S(1)} %and_select_fusion.columns, bf16[2048,128]{1,0:T(8,128)(2,1)S(1)} %copy-done.2, f32[256,1]{1,0:T(8,128)S(1)} %copy.9.ids, bf16[272,256]{1,0:T(8,128)(2,1)S(1)} %collective-permute-done.2.refs_0_, ...), custom_call_target="tpu_custom_call" | custom-call | flops 1500000000 | bytes 1048576 | tf_op jit(solution)/shard_map/attend_last/pallas_call | solution.py:166
  33.7 1.6 %collective-permute-start.9 = (bf16[128,512]{1,0:T(8,128)(2,1)S(1)}, bf16[128,512]{1,0:T(8,128)(2,1)S(1)}, u32[]{:S(2)}, u32[]{:S(2)}) collective-permute-start(bf16[128,512]{1,0:T(8,128)(2,1)S(1)} %get-tuple-element.50), channel_id=1, source_target_pairs={{0,7},{1,0},{2,1},{3,2},{4,3},{5,4},{6,5},{7,6},{8,9},{9,10},{10,1... | collective-permute-start | bytes 393224 | tf_op jit(solution)/shard_map/ppermute | solution.py:217
  35.3 1.9 %attend_last.3 = (bf16[128,1024]{1,0:T(8,128)(2,1)S(1)}, bf16[128,512]{1,0:T(8,128)(2,1)S(1)}) custom-call(s32[6]{0:T(128)S(1)} %copy-done.5, s32[5]{0:T(128)S(1)} %and_select_fusion.columns, bf16[2048,128]{1,0:T(8,128)(2,1)S(1)} %copy-done.2, f32[256,1]{1,0:T(8,128)S(1)} %copy.9.ids, bf16[272,256]{1,0:T(8,128)(2,1)S(1)} %collective-permute-done.2.refs_0_, ...), custom_call_target="tpu_custom_call" | custom-call | flops 1500000000 | bytes 1048576 | tf_op jit(solution)/shard_map/attend_last/pallas_call | solution.py:166
  37.2 4.4 %collective-permute-start.14 = (bf16[128,1024]{1,0:T(8,128)(2,1)S(1)}, bf16[128,1024]{1,0:T(8,128)(2,1)S(1)}, u32[]{:S(2)}, u32[]{:S(2)}) collective-permute-start(bf16[128,1024]{1,0:T(8,128)(2,1)S(1)} %get-tuple-element.51.own), channel_id=1, source_target_pairs={{0,8},{8,0},{16,24},{24,16},{32,40},{40,32},{48,56},{56,48},{64,72... | collective-permute-start | bytes 786440 | tf_op jit(solution)/shard_map/ppermute | solution.py:201
  41.6 1.7 %project.2 = (bf16[256,512]{1,0:T(8,128)(2,1)S(1)}, bf16[256,512]{1,0:T(8,128)(2,1)S(1)}, bf16[256,512]{1,0:T(8,128)(2,1)S(1)}, bf16[128,512]{1,0:T(8,128)(2,1)S(1)}) custom-call(s32[5]{0:T(128)S(1)} %and_select_fusion.columns, bf16[128,1024]{1,0:T(8,128)(2,1)S(1)} %get-tuple-element.45.own, bf16[128,1024]{1,0:T(8,128)(2,1)S(1)} %collective-permute-done.8.mate, ...), custom_call_target="tpu_custom_call" | custom-call | flops 1500000000 | bytes 1048576 | tf_op jit(solution)/shard_map/project/pallas_call | solution.py:183
  43.4 1.7 %project.3 = (bf16[256,512]{1,0:T(8,128)(2,1)S(1)}, bf16[256,512]{1,0:T(8,128)(2,1)S(1)}, bf16[256,512]{1,0:T(8,128)(2,1)S(1)}, bf16[128,512]{1,0:T(8,128)(2,1)S(1)}) custom-call(s32[5]{0:T(128)S(1)} %and_select_fusion.columns, bf16[128,1024]{1,0:T(8,128)(2,1)S(1)} %get-tuple-element.51.own, bf16[128,1024]{1,0:T(8,128)(2,1)S(1)} %collective-permute-done.14.mate, ...), custom_call_target="tpu_custom_call" | custom-call | flops 1500000000 | bytes 1048576 | tf_op jit(solution)/shard_map/project/pallas_call | solution.py:183
  45.1 1.5 %collective-permute-done.15 = bf16[128,512]{1,0:T(8,128)(2,1)S(1)} collective-permute-done((bf16[128,512]{1,0:T(8,128)(2,1)S(1)}, bf16[128,512]{1,0:T(8,128)(2,1)S(1)}, u32[]{:S(2)}, u32[]{:S(2)}) %collective-permute-start.15) | collective-permute-done | bytes 131104 | tf_op jit(solution)/shard_map/ppermute | solution.py:217
  47.3 2.5 %collective-permute-done.10 = bf16[256,512]{1,0:T(8,128)(2,1)S(1)} collective-permute-done((bf16[256,512]{1,0:T(8,128)(2,1)S(1)}, bf16[256,512]{1,0:T(8,128)(2,1)S(1)}, u32[]{:S(2)}, u32[]{:S(2)}) %collective-permute-start.10) | collective-permute-done | bytes 262176 | tf_op jit(solution)/shard_map/ppermute | solution.py:217
  50.0 3.4 %collective-permute-done.16 = bf16[256,512]{1,0:T(8,128)(2,1)S(1)} collective-permute-done((bf16[256,512]{1,0:T(8,128)(2,1)S(1)}, bf16[256,512]{1,0:T(8,128)(2,1)S(1)}, u32[]{:S(2)}, u32[]{:S(2)}) %collective-permute-start.16) | collective-permute-done | bytes 262176 | tf_op jit(solution)/shard_map/ppermute | solution.py:217
  53.6 2.9 %collective-permute-done.11 = bf16[256,512]{1,0:T(8,128)(2,1)S(1)} collective-permute-done((bf16[256,512]{1,0:T(8,128)(2,1)S(1)}, bf16[256,512]{1,0:T(8,128)(2,1)S(1)}, u32[]{:S(2)}, u32[]{:S(2)}) %collective-permute-start.11) | collective-permute-done | bytes 262176 | tf_op jit(solution)/shard_map/ppermute | solution.py:217
  56.6 3.4 %collective-permute-done.17 = bf16[256,512]{1,0:T(8,128)(2,1)S(1)} collective-permute-done((bf16[256,512]{1,0:T(8,128)(2,1)S(1)}, bf16[256,512]{1,0:T(8,128)(2,1)S(1)}, u32[]{:S(2)}, u32[]{:S(2)}) %collective-permute-start.17) | collective-permute-done | bytes 262176 | tf_op jit(solution)/shard_map/ppermute | solution.py:217
  60.2 2.9 %collective-permute-done.12 = bf16[256,512]{1,0:T(8,128)(2,1)S(1)} collective-permute-done((bf16[256,512]{1,0:T(8,128)(2,1)S(1)}, bf16[256,512]{1,0:T(8,128)(2,1)S(1)}, u32[]{:S(2)}, u32[]{:S(2)}) %collective-permute-start.12) | collective-permute-done | bytes 262176 | tf_op jit(solution)/shard_map/ppermute | solution.py:217
  63.0 2.3 %collective-permute-start.13 = (bf16[128,512]{1,0:T(8,128)(2,1)S(1)}, bf16[128,512]{1,0:T(8,128)(2,1)S(1)}, u32[]{:S(2)}, u32[]{:S(2)}) collective-permute-start(bf16[128,512]{1,0:T(8,128)(2,1)S(1)} %slice.33), channel_id=1, source_target_pairs={{0,8},{8,0},{16,24},{24,16},{32,40},{40,32},{48,56},{56,48},{64,72... | collective-permute-start | bytes 393224 | tf_op jit(solution)/shard_map/ppermute | solution.py:201
  65.4 1.2 %collective-permute-done.18 = bf16[256,512]{1,0:T(8,128)(2,1)S(1)} collective-permute-done((bf16[256,512]{1,0:T(8,128)(2,1)S(1)}, bf16[256,512]{1,0:T(8,128)(2,1)S(1)}, u32[]{:S(2)}, u32[]{:S(2)}) %collective-permute-start.18) | collective-permute-done | bytes 262176 | tf_op jit(solution)/shard_map/ppermute | solution.py:217
  66.6 2.1 %collective-permute-start.19 = (bf16[128,512]{1,0:T(8,128)(2,1)S(1)}, bf16[128,512]{1,0:T(8,128)(2,1)S(1)}, u32[]{:S(2)}, u32[]{:S(2)}) collective-permute-start(bf16[128,512]{1,0:T(8,128)(2,1)S(1)} %slice.35), channel_id=1, source_target_pairs={{0,8},{8,0},{16,24},{24,16},{32,40},{40,32},{48,56},{56,48},{64,72... | collective-permute-start | bytes 393224 | tf_op jit(solution)/shard_map/ppermute | solution.py:201
  68.7 0.9 %collective-permute-done.19 = bf16[128,512]{1,0:T(8,128)(2,1)S(1)} collective-permute-done((bf16[128,512]{1,0:T(8,128)(2,1)S(1)}, bf16[128,512]{1,0:T(8,128)(2,1)S(1)}, u32[]{:S(2)}, u32[]{:S(2)}) %collective-permute-start.19) | collective-permute-done | bytes 131104 | tf_op jit(solution)/shard_map/ppermute | solution.py:201
  (50 shorter events, 5.0 us)
Async XLA Ops:
  2.3 7.3 %collective-permute-start.1 = (bf16[272,256]{1,0:T(8,128)(2,1)}, bf16[272,256]{1,0:T(8,128)(2,1)S(1)}, u32[]{:S(2)}, u32[]{:S(2)}) collective-permute-start(bf16[272,256]{1,0:T(8,128)(2,1)} %pad_maximum_fusion.3.piece), channel_id=1, source_target_pairs={{0,64},{8,72},{16,80},{24,88},{32,96},{40,104},{48,112},{56,120},{... | collective-permute-start | bytes 417800 | tf_op jit(solution)/shard_map/ppermute | solution.py:205
  4.4 13.5 %collective-permute-start.5 = (bf16[272,256]{1,0:T(8,128)(2,1)}, bf16[272,256]{1,0:T(8,128)(2,1)}, u32[]{:S(2)}, u32[]{:S(2)}) collective-permute-start(bf16[272,256]{1,0:T(8,128)(2,1)} %pad_maximum_fusion.3.piece), channel_id=1, source_target_pairs={{0,16},{8,24},{16,32},{24,40},{32,48},{40,56},{48,64},{56,72},{64,... | collective-permute-start | bytes 417800 | tf_op jit(solution)/shard_map/ppermute | solution.py:205
  5.9 1.0 %copy-start.3 = (bf16[256,1024]{1,0:T(8,128)(2,1)S(1)}, bf16[256,1024]{1,0:T(8,128)(2,1)}, u32[]{:S(2)}) copy-start(bf16[256,1024]{1,0:T(8,128)(2,1)} %queries.1) | copy-start | bytes 1572868
  7.0 8.3 %copy-start.4 = (s32[6]{0:T(128)}, s32[6]{0:T(128)S(1)}, u32[]{:S(2)}) copy-start(s32[6]{0:T(128)S(1)} %stack.59.valid) | copy-start | bytes 76
  8.8 0.8 %copy-start.1 = (bf16[2048,128]{1,0:T(8,128)(2,1)}, bf16[2048,128]{1,0:T(8,128)(2,1)S(1)}, u32[]{:S(2)}) copy-start(bf16[2048,128]{1,0:T(8,128)(2,1)S(1)} %get-tuple-element.31.query_rows) | copy-start | bytes 1572868
  11.3 7.1 %collective-permute-start.3 = (bf16[272,256]{1,0:T(8,128)(2,1)}, bf16[272,256]{1,0:T(8,128)(2,1)}, u32[]{:S(2)}, u32[]{:S(2)}) collective-permute-start(bf16[272,256]{1,0:T(8,128)(2,1)} %get-tuple-element.57), channel_id=1, source_target_pairs={{0,8},{8,0},{16,24},{24,16},{32,40},{40,32},{48,56},{56,48},{64,72... | collective-permute-start | bytes 417800 | tf_op jit(solution)/shard_map/ppermute | solution.py:201
  13.7 10.0 %collective-permute-start = (bf16[272,256]{1,0:T(8,128)(2,1)}, bf16[272,256]{1,0:T(8,128)(2,1)}, u32[]{:S(2)}, u32[]{:S(2)}) collective-permute-start(bf16[272,256]{1,0:T(8,128)(2,1)} %pad_maximum_fusion.3.piece), channel_id=1, source_target_pairs={{0,32},{8,40},{16,48},{24,56},{32,64},{40,72},{48,80},{56,88},{64,... | collective-permute-start | bytes 417800 | tf_op jit(solution)/shard_map/ppermute | solution.py:205
  15.3 8.6 %collective-permute-start.2 = (bf16[272,256]{1,0:T(8,128)(2,1)}, bf16[272,256]{1,0:T(8,128)(2,1)S(1)}, u32[]{:S(2)}, u32[]{:S(2)}) collective-permute-start(bf16[272,256]{1,0:T(8,128)(2,1)} %get-tuple-element.58), channel_id=1, source_target_pairs={{0,48},{8,56},{16,0},{24,8},{32,16},{40,24},{48,32},{56,40},{64,11... | collective-permute-start | bytes 417800 | tf_op jit(solution)/shard_map/ppermute | solution.py:209
  17.8 6.9 %copy-start.6 = (s32[5]{0:T(128)S(1)}, s32[5]{0:T(128)}, u32[]{:S(2)}) copy-start(s32[5]{0:T(128)} %stack.50) | copy-start | bytes 64
  17.8 6.9 %collective-permute-start.6 = (bf16[272,256]{1,0:T(8,128)(2,1)}, bf16[272,256]{1,0:T(8,128)(2,1)S(1)}, u32[]{:S(2)}, u32[]{:S(2)}) collective-permute-start(bf16[272,256]{1,0:T(8,128)(2,1)} %collective-permute-done.5.refs_0_), channel_id=1, source_target_pairs={{0,8},{8,0},{16,24},{24,16},{32,40},{40,32},{48,56},{56,48},{64,72... | collective-permute-start | bytes 417800 | tf_op jit(solution)/shard_map/ppermute | solution.py:201
  18.4 1.0 %copy-start.2 = (bf16[2048,128]{1,0:T(8,128)(2,1)S(1)}, bf16[2048,128]{1,0:T(8,128)(2,1)}, u32[]{:S(2)}) copy-start(bf16[2048,128]{1,0:T(8,128)(2,1)} %copy-done.1) | copy-start | bytes 1572868
  19.4 0.7 copy-start.5
  20.1 11.2 %copy-start = (bf16[1024,4096]{1,0:T(8,128)(2,1)S(1)}, bf16[1024,4096]{1,0:T(8,128)(2,1)}, u32[]{:S(2)}) copy-start(bf16[1024,4096]{1,0:T(8,128)(2,1)} %weight.3) | copy-start | bytes 25165828
  23.9 2.1 %collective-permute-start.7 = (bf16[272,256]{1,0:T(8,128)(2,1)}, bf16[272,256]{1,0:T(8,128)(2,1)S(1)}, u32[]{:S(2)}, u32[]{:S(2)}) collective-permute-start(bf16[272,256]{1,0:T(8,128)(2,1)} %collective-permute-done.refs_2_), channel_id=1, source_target_pairs={{0,8},{8,0},{16,24},{24,16},{32,40},{40,32},{48,56},{56,48},{64,72... | collective-permute-start | bytes 417800 | tf_op jit(solution)/shard_map/ppermute | solution.py:201
  24.7 6.6 %collective-permute-start.4 = (bf16[272,256]{1,0:T(8,128)(2,1)S(1)}, bf16[272,256]{1,0:T(8,128)(2,1)S(1)}, u32[]{:S(2)}, u32[]{:S(2)}) collective-permute-start(bf16[272,256]{1,0:T(8,128)(2,1)S(1)} %collective-permute-done.2.refs_0_), channel_id=1, source_target_pairs={{0,8},{8,0},{16,24},{24,16},{32,40},{40,32},{48,56},{56,48},{64,72... | collective-permute-start | bytes 417800 | tf_op jit(solution)/shard_map/ppermute | solution.py:201
  33.2 8.4 %collective-permute-start.8 = (bf16[128,1024]{1,0:T(8,128)(2,1)S(1)}, bf16[128,1024]{1,0:T(8,128)(2,1)S(1)}, u32[]{:S(2)}, u32[]{:S(2)}) collective-permute-start(bf16[128,1024]{1,0:T(8,128)(2,1)S(1)} %get-tuple-element.45.own), channel_id=1, source_target_pairs={{0,8},{8,0},{16,24},{24,16},{32,40},{40,32},{48,56},{56,48},{64,72... | collective-permute-start | bytes 786440 | tf_op jit(solution)/shard_map/ppermute | solution.py:201
  33.7 9.6 %collective-permute-start.9 = (bf16[128,512]{1,0:T(8,128)(2,1)S(1)}, bf16[128,512]{1,0:T(8,128)(2,1)S(1)}, u32[]{:S(2)}, u32[]{:S(2)}) collective-permute-start(bf16[128,512]{1,0:T(8,128)(2,1)S(1)} %get-tuple-element.50), channel_id=1, source_target_pairs={{0,7},{1,0},{2,1},{3,2},{4,3},{5,4},{6,5},{7,6},{8,9},{9,10},{10,1... | collective-permute-start | bytes 393224 | tf_op jit(solution)/shard_map/ppermute | solution.py:217
  37.2 6.3 %collective-permute-start.14 = (bf16[128,1024]{1,0:T(8,128)(2,1)S(1)}, bf16[128,1024]{1,0:T(8,128)(2,1)S(1)}, u32[]{:S(2)}, u32[]{:S(2)}) collective-permute-start(bf16[128,1024]{1,0:T(8,128)(2,1)S(1)} %get-tuple-element.51.own), channel_id=1, source_target_pairs={{0,8},{8,0},{16,24},{24,16},{32,40},{40,32},{48,56},{56,48},{64,72... | collective-permute-start | bytes 786440 | tf_op jit(solution)/shard_map/ppermute | solution.py:201
  41.6 5.0 %collective-permute-start.15 = (bf16[128,512]{1,0:T(8,128)(2,1)S(1)}, bf16[128,512]{1,0:T(8,128)(2,1)S(1)}, u32[]{:S(2)}, u32[]{:S(2)}) collective-permute-start(bf16[128,512]{1,0:T(8,128)(2,1)S(1)} %get-tuple-element.56), channel_id=1, source_target_pairs={{0,7},{1,0},{2,1},{3,2},{4,3},{5,4},{6,5},{7,6},{8,9},{9,10},{10,1... | collective-permute-start | bytes 393224 | tf_op jit(solution)/shard_map/ppermute | solution.py:217
  43.3 6.5 %collective-permute-start.10 = (bf16[256,512]{1,0:T(8,128)(2,1)S(1)}, bf16[256,512]{1,0:T(8,128)(2,1)S(1)}, u32[]{:S(2)}, u32[]{:S(2)}) collective-permute-start(bf16[256,512]{1,0:T(8,128)(2,1)S(1)} %pad_maximum_fusion), channel_id=1, source_target_pairs={{0,7},{1,0},{2,1},{3,2},{4,3},{5,4},{6,5},{7,6},{8,9},{9,10},{10,1... | collective-permute-start | bytes 786440 | tf_op jit(solution)/shard_map/ppermute | solution.py:217
  46.7 6.7 %collective-permute-start.16 = (bf16[256,512]{1,0:T(8,128)(2,1)S(1)}, bf16[256,512]{1,0:T(8,128)(2,1)S(1)}, u32[]{:S(2)}, u32[]{:S(2)}) collective-permute-start(bf16[256,512]{1,0:T(8,128)(2,1)S(1)} %pad_maximum_fusion.1), channel_id=1, source_target_pairs={{0,7},{1,0},{2,1},{3,2},{4,3},{5,4},{6,5},{7,6},{8,9},{9,10},{10,1... | collective-permute-start | bytes 786440 | tf_op jit(solution)/shard_map/ppermute | solution.py:217
  49.9 6.5 %collective-permute-start.11 = (bf16[256,512]{1,0:T(8,128)(2,1)S(1)}, bf16[256,512]{1,0:T(8,128)(2,1)S(1)}, u32[]{:S(2)}, u32[]{:S(2)}) collective-permute-start(bf16[256,512]{1,0:T(8,128)(2,1)S(1)} %add.67), channel_id=1, source_target_pairs={{0,7},{1,0},{2,1},{3,2},{4,3},{5,4},{6,5},{7,6},{8,9},{9,10},{10,1... | collective-permute-start | bytes 786440 | tf_op jit(solution)/shard_map/ppermute | solution.py:217
  53.5 6.5 %collective-permute-start.17 = (bf16[256,512]{1,0:T(8,128)(2,1)S(1)}, bf16[256,512]{1,0:T(8,128)(2,1)S(1)}, u32[]{:S(2)}, u32[]{:S(2)}) collective-permute-start(bf16[256,512]{1,0:T(8,128)(2,1)S(1)} %add.72), channel_id=1, source_target_pairs={{0,7},{1,0},{2,1},{3,2},{4,3},{5,4},{6,5},{7,6},{8,9},{9,10},{10,1... | collective-permute-start | bytes 786440 | tf_op jit(solution)/shard_map/ppermute | solution.py:217
  56.5 6.5 %collective-permute-start.12 = (bf16[256,512]{1,0:T(8,128)(2,1)S(1)}, bf16[256,512]{1,0:T(8,128)(2,1)S(1)}, u32[]{:S(2)}, u32[]{:S(2)}) collective-permute-start(bf16[256,512]{1,0:T(8,128)(2,1)S(1)} %add.68), channel_id=1, source_target_pairs={{0,7},{1,0},{2,1},{3,2},{4,3},{5,4},{6,5},{7,6},{8,9},{9,10},{10,1... | collective-permute-start | bytes 786440 | tf_op jit(solution)/shard_map/ppermute | solution.py:217
  60.1 6.5 %collective-permute-start.18 = (bf16[256,512]{1,0:T(8,128)(2,1)S(1)}, bf16[256,512]{1,0:T(8,128)(2,1)S(1)}, u32[]{:S(2)}, u32[]{:S(2)}) collective-permute-start(bf16[256,512]{1,0:T(8,128)(2,1)S(1)} %add.73), channel_id=1, source_target_pairs={{0,7},{1,0},{2,1},{3,2},{4,3},{5,4},{6,5},{7,6},{8,9},{9,10},{10,1... | collective-permute-start | bytes 786440 | tf_op jit(solution)/shard_map/ppermute | solution.py:217
  63.0 5.6 %collective-permute-start.13 = (bf16[128,512]{1,0:T(8,128)(2,1)S(1)}, bf16[128,512]{1,0:T(8,128)(2,1)S(1)}, u32[]{:S(2)}, u32[]{:S(2)}) collective-permute-start(bf16[128,512]{1,0:T(8,128)(2,1)S(1)} %slice.33), channel_id=1, source_target_pairs={{0,8},{8,0},{16,24},{24,16},{32,40},{40,32},{48,56},{56,48},{64,72... | collective-permute-start | bytes 393224 | tf_op jit(solution)/shard_map/ppermute | solution.py:201
  66.6 3.1 %collective-permute-start.19 = (bf16[128,512]{1,0:T(8,128)(2,1)S(1)}, bf16[128,512]{1,0:T(8,128)(2,1)S(1)}, u32[]{:S(2)}, u32[]{:S(2)}) collective-permute-start(bf16[128,512]{1,0:T(8,128)(2,1)S(1)} %slice.35), channel_id=1, source_target_pairs={{0,8},{8,0},{16,24},{24,16},{32,40},{40,32},{48,56},{56,48},{64,72... | collective-permute-start | bytes 393224 | tf_op jit(solution)/shard_map/ppermute | solution.py:201

commit v3 on v0

v3 whole, which is shorter than its diff:
```python
import functools
import math

import jax
import jax.numpy as jnp
from jax import lax
from jax.experimental import pallas as pl
from jax.experimental.pallas import tpu as pltpu
from jax.sharding import PartitionSpec as P

HD = 128
HEADS = 8
TOK = 256
PART = 128
ROWS = HEADS * TOK
STEP = 256
PIECE = TOK + 16
CHUNK = 512
ROW = 8
SCALE = 1.0 / math.sqrt(HD)
MASKED = -1e30
F32 = jnp.float32
BF16 = jnp.bfloat16
BESIDE = -1


def place():
    at = lax.axis_index("loop")
    return at // 2, at % 2


def usable(back):
    chip, core = place()
    if back == 0:
        return jnp.bool_(True)
    if back == BESIDE:
        return (chip >= 4) | (core == 1)
    return chip >= back


def pack_kernel(key_values, ids, message):
    message[0:TOK, :] = key_values[...]
    row = jnp.broadcast_to(ids[...].astype(F32), (PIECE - TOK, TOK))
    message[TOK:PIECE, :] = row.astype(BF16)


def column_kernel(message, again, column):
    again[...] = message[...]
    square = (TOK, TOK)
    diagonal = lax.broadcasted_iota(jnp.int32, square, 0) == lax.broadcasted_iota(
        jnp.int32, square, 1
    )
    wide = jnp.broadcast_to(message[TOK:PIECE, :][0:1, :].astype(F32), square)
    column[...] = jnp.sum(jnp.where(diagonal, wide, 0.0), axis=1, keepdims=True)


def pick_kernel(own, far, ids, relayed, beside, ids_again):
    chip, core = place()
    ids_again[...] = ids[...]

    @pl.when(chip % 4 == 0)
    def _():
        relayed[...] = own[...]

    @pl.when(chip % 4 != 0)
    def _():
        relayed[...] = far[...]

    @pl.when(core == 0)
    def _():
        beside[...] = own[...]

    @pl.when(core != 0)
    def _():
        beside[...] = far[...]


def find_scores(query_rows, ids, part, pieces, scores, peak, base):
    own_ids = ids[pl.ds(part * PART, PART), :]
    own_ids = jnp.concatenate([own_ids] * (STEP // PART), axis=0)
    names = []
    for back, piece in pieces:
        key_ids = piece[TOK:PIECE, :][0:1, :].astype(F32)
        names.append(jnp.where(usable(back), key_ids, -1.0))
    for step in range(HEADS * PART // STEP):
        rows = pl.ds(part * HEADS * PART + step * STEP, STEP)
        out = pl.ds(base + step * STEP, STEP)
        best = None
        for at, (back, piece) in enumerate(pieces):
            found = lax.dot_general(
                query_rows[rows, :],
                piece[0:TOK, 0:HD],
                (((1,), (1,)), ((), ())),
                preferred_element_type=F32,
            )
            allowed = own_ids == names[at]
            if back == 0:
                shape = (STEP, TOK)
                token = lax.broadcasted_iota(jnp.int32, shape, 0) % PART + part * PART
                allowed = allowed & (lax.broadcasted_iota(jnp.int32, shape, 1) <= token)
            found = jnp.where(allowed, found, MASKED)
            scores[out, at * TOK : (at + 1) * TOK] = found
            here = jnp.maximum(found[:, :HD], found[:, HD:])
            best = here if best is None else jnp.maximum(best, here)
        peak[out, :] = best


def keep_values(pieces, values):
    for at, (_, piece) in enumerate(pieces):
        values[at * TOK : (at + 1) * TOK, 0:HD] = piece[0:TOK, HD:]
    values[:, HD:] = jnp.ones((values.shape[0], HD), BF16)


def own_kernel(queries, ids, piece, query_rows, scores, peak, values):
    for part in range(TOK // PART):
        for head in range(HEADS):
            rows = pl.ds((part * HEADS + head) * PART, PART)
            query_rows[rows, :] = queries[pl.ds(part * PART, PART), pl.ds(head * HD, HD)]
    keep_values([(0, piece)], values)
    for part in range(TOK // PART):
        find_scores(query_rows, ids, part, [(0, piece)], scores, peak, part * HEADS * PART)


def more_kernel(backs, query_rows, ids, *refs):
    pieces = list(zip(backs, refs[: len(backs)]))
    scores, peak, values = refs[len(backs) :]
    keep_values(pieces, values)
    for part in range(TOK // PART):
        find_scores(query_rows, ids, part, pieces, scores, peak, part * HEADS * PART)


def last_kernel(part, backs, early, query_rows, ids, *refs):
    pieces = list(zip(backs, refs[: len(backs)]))
    refs = refs[len(backs) :]
    kept = [refs[3 * at : 3 * at + 3] for at in range(early)]
    weight, attention, product, scores, peak, values = refs[3 * early :]
    keep_values(pieces, values)
    find_scores(query_rows, ids, part, pieces, scores, peak, 0)
    for step in range(HEADS * PART // STEP):
        rows = pl.ds(step * STEP, STEP)
        given = pl.ds(part * HEADS * PART + step * STEP, STEP)
        top = peak[rows, :]
        for _, other, _ in kept:
            top = jnp.maximum(top, other[given, :])
        top = jnp.broadcast_to(jnp.max(top, axis=1, keepdims=True), (STEP, HD))
        total = None
        for block, keys in [(s[given, :], v) for s, _, v in kept] + [(scores[rows, :], values)]:
            wide = jnp.concatenate([top] * (block.shape[1] // HD), axis=1)
            probs = jnp.exp((block - wide) * SCALE).astype(BF16)
            added = jnp.dot(probs, keys[...], preferred_element_type=F32)
            total = added if total is None else total + added
        share = (total[:, :HD] / total[:, HD:]).astype(BF16)
        for at in range(STEP // PART):
            head = step * (STEP // PART) + at
            attention[:, pl.ds(head * HD, HD)] = share[at * PART : (at + 1) * PART, :]
    group = lax.rem(lax.axis_index("tp") + 4, 8)
    group = pl.ds(pl.multiple_of(group * CHUNK, CHUNK), CHUNK)
    product[...] = jnp.dot(
        attention[...], weight[:, group], preferred_element_type=F32
    ).astype(BF16)


def project_kernel(own, mate, weight, *outs):
    both = jnp.concatenate([own[...], mate[...]], axis=0)
    side = 1 - 2 * place()[1]
    for at, out in enumerate(outs):
        if out.shape[0] == 2 * PART:
            rows, group = both, lax.axis_index("tp") + 4 + (at + 1) * side
        else:
            rows, group = own[...], lax.axis_index("tp")
        group = lax.rem(group, 8)
        group = pl.ds(pl.multiple_of(group * CHUNK, CHUNK), CHUNK)
        out[...] = jnp.dot(rows, weight[:, group], preferred_element_type=F32).astype(BF16)


def finish_kernel(*refs):
    out = refs[-1]
    for part in range(TOK // PART):
        mine, moved, other = refs[3 * part : 3 * part + 3]
        total = mine[...].astype(F32) + moved[0:PART, :].astype(F32) + other[...].astype(F32)
        out[pl.ds(part * PART, PART), :] = total.astype(BF16)


VMEM = pl.BlockSpec(memory_space=pltpu.VMEM)
PARAMS = pltpu.CompilerParams(vmem_limit_bytes=12 << 20)


def shape(rows, columns, kind=BF16):
    return jax.ShapeDtypeStruct((rows, columns), kind)


def call(kernel, name, micros, outs, *args, scratch=()):
    return pl.pallas_call(
        kernel,
        out_shape=outs,
        in_specs=[VMEM] * len(args),
        out_specs=[VMEM] * len(outs) if isinstance(outs, list) else VMEM,
        scratch_shapes=list(scratch),
        compiler_params=PARAMS,
        cost_estimate=pl.CostEstimate(
            flops=int(micros * 1e9), bytes_accessed=1 << 10, transcendentals=0
        ),
        name=name,
    )(*args)


def kept_shapes(count):
    return [shape(ROWS, count * TOK, F32), shape(ROWS, HD, F32), shape(count * TOK, 2 * HD)]


def per_device(queries, key_values, prompt_ids, out_weight):
    stretches, ring = lax.axis_size("loop"), lax.axis_size("tp")

    def to_mate(value):
        return lax.ppermute(value, "loop", [(i, i ^ 1) for i in range(stretches)])

    def from_chip(value, steps):
        pairs = [(i, (i + 2 * steps) % stretches) for i in range(stretches)]
        return lax.ppermute(value, "loop", pairs)

    def along_row(value, steps):
        pairs = [(i, i // ROW * ROW + (i + 2 * steps) % ROW) for i in range(stretches)]
        return lax.ppermute(value, "loop", pairs)

    def along(value):
        pairs = []
        for loop in range(stretches):
            step = 1 if loop % 2 else ring - 1
            for z in range(ring):
                pairs.append((loop * ring + z, loop * ring + (z + step) % ring))
        return lax.ppermute(value, ("loop", "tp"), pairs)

    piece = shape(PIECE, TOK)
    column = shape(TOK, 1, F32)
    own = call(pack_kernel, "pack", 0.5, piece, key_values, prompt_ids[None, :])
    chip4 = from_chip(own, 4)
    again, ids = call(column_kernel, "column", 0.3, [piece, column], own)
    chip1, chip2 = from_chip(again, 1), from_chip(again, 2)
    query_rows, *kept = call(
        own_kernel, "own_scores", 1.5, [shape(ROWS, HD)] + kept_shapes(1), queries, ids, again
    )
    (chip4, kept) = lax.optimization_barrier((chip4, kept))
    relayed, beside, ids = call(
        pick_kernel, "pick", 0.3, [piece, piece, column], again, chip4, ids
    )
    (chip1, ids) = lax.optimization_barrier((chip1, ids))
    chip3 = along_row(relayed, 3)
    beside = to_mate(beside)
    (chip2, beside) = lax.optimization_barrier((chip2, beside))
    mate1, mate2, mate3 = to_mate(chip1), to_mate(chip2), to_mate(chip3)
    (mate2, chip3) = lax.optimization_barrier((mate2, chip3))
    pieces = [(4, chip4), (BESIDE, beside), (1, chip1), (1, mate1), (2, chip2), (2, mate2)]
    more = call(
        functools.partial(more_kernel, [item[0] for item in pieces]),
        "more_scores",
        3,
        kept_shapes(len(pieces)),
        query_rows,
        ids,
        *[item[1] for item in pieces],
    )
    (mate3, more) = lax.optimization_barrier((mate3, more))
    kept = list(kept) + list(more)

    ends = []
    for part in range(TOK // PART):
        attention, product = call(
            functools.partial(last_kernel, part, [3, 3], len(kept) // 3),
            "attend",
            3,
            [shape(PART, HEADS * HD), shape(PART, CHUNK)],
            query_rows,
            ids,
            chip3,
            mate3,
            *kept,
            out_weight,
            scratch=[
                pltpu.VMEM((HEADS * PART, 2 * TOK), F32),
                pltpu.VMEM((HEADS * PART, HD), F32),
                pltpu.VMEM((2 * TOK, 2 * HD), BF16),
            ],
        )
        extra = along(product)
        wide = shape(2 * PART, CHUNK)
        one, two, three, mine = call(
            project_kernel,
            "project",
            1.6,
            [wide, wide, wide, shape(PART, CHUNK)],
            attention,
            to_mate(attention),
            out_weight,
        )
        moved = along(jnp.concatenate([one[:PART] + extra, one[PART:]], axis=0))
        moved = along(two + moved)
        moved = along(three + moved)
        ends += [mine, moved, to_mate(moved[PART:])]
    return call(finish_kernel, "finish", 0.5, shape(TOK, CHUNK), *ends)


def solution(mesh):
    in_specs = (P("loop", "tp"), P("loop", "tp"), P("loop"), P("tp", None))
    out_specs = P("loop", "tp")
    return jax.shard_map(
        per_device, mesh=mesh, in_specs=in_specs, out_specs=out_specs, check_vma=False
    )
```

time: 134 us -> 65.2 us (0.49)
  the two profiles are of different devices: /device:TPU:12 before, /device:TPU:1 now
where the time goes in v3:
time: 65.2 us; the launch traced here: 65 us
  starting transfers between devices  28 us (43%)
  waiting for transfers between devices  23.5 us (36%)
  Pallas kernels  10.1 us (15%)
  local copies, waits for them, and re-layouts  2.82 us (4%)
    ppermute x8, waiting for transfers between devices, along(): return lax.ppermute(value, ('loop', 'tp'), pairs)  18.4 us
    ppermute x8, starting transfers between devices, to_mate(): return lax.ppermute(value, 'loop', [(i, i ^ 1) for i in range(stretches)])  16 us
    pallas_call x10, Pallas kernels, call(): pl.pallas_call(kernel, out_shape=outs, in_specs=[VMEM] * len(args), out_s...  10.1 us
    ppermute x3, starting transfers between devices, from_chip(): return lax.ppermute(value, 'loop', pairs)  5.51 us
    ppermute x8, starting transfers between devices, along(): return lax.ppermute(value, ('loop', 'tp'), pairs)  4.14 us
    ppermute x3, waiting for transfers between devices, from_chip(): return lax.ppermute(value, 'loop', pairs)  3.28 us
    unnamed x10, local copies, waits for them, and re-layouts  2.8 us
    ppermute x1, starting transfers between devices, along_row(): return lax.ppermute(value, 'loop', pairs)  2.31 us
  transfers between devices with their start and end apart: 20, of which 10 were waited for; matrix products, arithmetic and copies ran while one was open for 1% of the time, Pallas kernels for 11%

profile of v3, /device:TPU:1, one launch (start us, length us, event | category | flops | bytes accessed | tf_op | source)
XLA Modules:
  0.0 65.0 jit_solution(7036160582991363759)
XLA Ops:
  0.0 0.9 %copy-done.1 = bf16[256,256]{1,0:T(8,128)(2,1)S(1)} copy-done((bf16[256,256]{1,0:T(8,128)(2,1)S(1)}, bf16[256,256]{1,0:T(8,128)(2,1)}, u32[]{:S(2)}) %copy-start.1) | copy-done | bytes 131096
  0.9 0.7 %copy-done.2 = s32[256]{0:T(256)S(1)} copy-done((s32[256]{0:T(256)S(1)}, s32[256]{0:T(256)}, u32[]{:S(2)}) %copy-start.2) | copy-done | bytes 1048
  1.6 2.1 %collective-permute-start.1 = (bf16[272,256]{1,0:T(8,128)(2,1)S(1)}, bf16[272,256]{1,0:T(8,128)(2,1)S(1)}, u32[]{:S(2)}, u32[]{:S(2)}) collective-permute-start(bf16[272,256]{1,0:T(8,128)(2,1)S(1)} %pack.1.message), channel_id=1, source_target_pairs={{0,64},{8,72},{16,80},{24,88},{32,96},{40,104},{48,112},{56,120},{... | collective-permute-start | bytes 417800 | tf_op jit(solution)/shard_map/ppermute | solution.py:219
  3.8 3.0 %collective-permute-start.2 = (bf16[272,256]{1,0:T(8,128)(2,1)S(1)}, bf16[272,256]{1,0:T(8,128)(2,1)S(1)}, u32[]{:S(2)}, u32[]{:S(2)}) collective-permute-start(bf16[272,256]{1,0:T(8,128)(2,1)S(1)} %get-tuple-element.44.piece.own), channel_id=1, source_target_pairs={{0,32},{8,40},{16,48},{24,56},{32,64},{40,72},{48,80},{56,88},{64,... | collective-permute-start | bytes 417800 | tf_op jit(solution)/shard_map/ppermute | solution.py:219
  6.8 0.4 collective-permute-start
  7.2 1.0 %copy-done = bf16[256,1024]{1,0:T(8,128)(2,1)S(1)} copy-done((bf16[256,1024]{1,0:T(8,128)(2,1)S(1)}, bf16[256,1024]{1,0:T(8,128)(2,1)}, u32[]{:S(2)}) %copy-start) | copy-done | bytes 524312
  8.3 0.5 own_scores.1
  8.8 2.5 %collective-permute-start.3 = (bf16[272,256]{1,0:T(8,128)(2,1)S(1)}, bf16[272,256]{1,0:T(8,128)(2,1)S(1)}, u32[]{:S(2)}, u32[]{:S(2)}) collective-permute-start(bf16[272,256]{1,0:T(8,128)(2,1)S(1)} %get-tuple-element.52), channel_id=1, source_target_pairs={{0,8},{8,0},{16,24},{24,16},{32,40},{40,32},{48,56},{56,48},{64,72... | collective-permute-start | bytes 417800 | tf_op jit(solution)/shard_map/ppermute | solution.py:215
  11.3 2.3 %collective-permute-start.5 = (bf16[272,256]{1,0:T(8,128)(2,1)S(1)}, bf16[272,256]{1,0:T(8,128)(2,1)S(1)}, u32[]{:S(2)}, u32[]{:S(2)}) collective-permute-start(bf16[272,256]{1,0:T(8,128)(2,1)S(1)} %get-tuple-element.54), channel_id=1, source_target_pairs={{0,48},{8,56},{16,0},{24,8},{32,16},{40,24},{48,32},{56,40},{64,11... | collective-permute-start | bytes 417800 | tf_op jit(solution)/shard_map/ppermute | solution.py:223
  13.6 3.3 %collective-permute-done.refs_2_ = bf16[272,256]{1,0:T(8,128)(2,1)S(1)} collective-permute-done((bf16[272,256]{1,0:T(8,128)(2,1)S(1)}, bf16[272,256]{1,0:T(8,128)(2,1)S(1)}, u32[]{:S(2)}, u32[]{:S(2)}) %collective-permute-start) | collective-permute-done | bytes 139296 | tf_op jit(solution)/shard_map/ppermute | solution.py:219
  16.9 1.6 %collective-permute-start.4 = (bf16[272,256]{1,0:T(8,128)(2,1)S(1)}, bf16[272,256]{1,0:T(8,128)(2,1)S(1)}, u32[]{:S(2)}, u32[]{:S(2)}) collective-permute-start(bf16[272,256]{1,0:T(8,128)(2,1)S(1)} %collective-permute-done.2.refs_4_), channel_id=1, source_target_pairs={{0,8},{8,0},{16,24},{24,16},{32,40},{40,32},{48,56},{56,48},{64,72... | collective-permute-start | bytes 417800 | tf_op jit(solution)/shard_map/ppermute | solution.py:215
  18.6 0.4 collective-permute-start.6
  19.0 0.5 collective-permute-done.4.refs_5_
  19.9 2.0 %more_scores.1 = (f32[2048,1536]{1,0:T(8,128)S(1)}, f32[2048,128]{1,0:T(8,128)S(1)}, bf16[1536,256]{1,0:T(8,128)(2,1)S(1)}) custom-call(bf16[2048,128]{1,0:T(8,128)(2,1)S(1)} %get-tuple-element.45.query_rows, f32[256,1]{1,0:T(8,128)S(1)} %get-tuple-element.51.ids, bf16[272,256]{1,0:T(8,128)(2,1)S(1)} %collective-permute-done.1.far.refs_0_, ...), custom_call_target="tpu_custom_call" | custom-call | flops 3000000000 | bytes 1024 | tf_op jit(solution)/shard_map/more_scores/pallas_call | solution.py:193
  22.1 2.2 %attend.2 = (bf16[128,1024]{1,0:T(8,128)(2,1)S(1)}, bf16[128,512]{1,0:T(8,128)(2,1)S(1)}) custom-call(bf16[2048,128]{1,0:T(8,128)(2,1)S(1)} %get-tuple-element.45.query_rows, f32[256,1]{1,0:T(8,128)S(1)} %get-tuple-element.51.ids, bf16[272,256]{1,0:T(8,128)(2,1)S(1)} %collective-permute-done.5.refs_0_, bf16[272,256]{1,0:T(8,128)(2,1)S(1)} %collective-permute-done.6.refs_1_, ...), custom_call_target="tpu_custom_call" | custom-call | flops 3000000000 | bytes 1024 | tf_op jit(solution)/shard_map/attend/pallas_call | solution.py:193
  24.3 0.5 collective-permute-start.8
  24.7 2.2 %attend.3 = (bf16[128,1024]{1,0:T(8,128)(2,1)S(1)}, bf16[128,512]{1,0:T(8,128)(2,1)S(1)}) custom-call(bf16[2048,128]{1,0:T(8,128)(2,1)S(1)} %get-tuple-element.45.query_rows, f32[256,1]{1,0:T(8,128)S(1)} %get-tuple-element.51.ids, bf16[272,256]{1,0:T(8,128)(2,1)S(1)} %collective-permute-done.5.refs_0_, bf16[272,256]{1,0:T(8,128)(2,1)S(1)} %collective-permute-done.6.refs_1_, ...), custom_call_target="tpu_custom_call" | custom-call | flops 3000000000 | bytes 1024 | tf_op jit(solution)/shard_map/attend/pallas_call | solution.py:193
  27.0 1.7 %collective-permute-start.15 = (bf16[128,512]{1,0:T(8,128)(2,1)S(1)}, bf16[128,512]{1,0:T(8,128)(2,1)S(1)}, u32[]{:S(2)}, u32[]{:S(2)}) collective-permute-start(bf16[128,512]{1,0:T(8,128)(2,1)S(1)} %get-tuple-element.80), channel_id=1, source_target_pairs={{0,7},{1,0},{2,1},{3,2},{4,3},{5,4},{6,5},{7,6},{8,9},{9,10},{10,1... | collective-permute-start | bytes 393224 | tf_op jit(solution)/shard_map/ppermute | solution.py:231
  28.7 1.6 %collective-permute-start.9 = (bf16[128,512]{1,0:T(8,128)(2,1)S(1)}, bf16[128,512]{1,0:T(8,128)(2,1)S(1)}, u32[]{:S(2)}, u32[]{:S(2)}) collective-permute-start(bf16[128,512]{1,0:T(8,128)(2,1)S(1)} %get-tuple-element.74), channel_id=1, source_target_pairs={{0,7},{1,0},{2,1},{3,2},{4,3},{5,4},{6,5},{7,6},{8,9},{9,10},{10,1... | collective-permute-start | bytes 393224 | tf_op jit(solution)/shard_map/ppermute | solution.py:231
  30.3 3.9 %collective-permute-start.14 = (bf16[128,1024]{1,0:T(8,128)(2,1)S(1)}, bf16[128,1024]{1,0:T(8,128)(2,1)S(1)}, u32[]{:S(2)}, u32[]{:S(2)}) collective-permute-start(bf16[128,1024]{1,0:T(8,128)(2,1)S(1)} %get-tuple-element.75.own), channel_id=1, source_target_pairs={{0,8},{8,0},{16,24},{24,16},{32,40},{40,32},{48,56},{56,48},{64,72... | collective-permute-start | bytes 786440 | tf_op jit(solution)/shard_map/ppermute | solution.py:215
  34.2 1.1 %project.2 = (bf16[256,512]{1,0:T(8,128)(2,1)S(1)}, bf16[256,512]{1,0:T(8,128)(2,1)S(1)}, bf16[256,512]{1,0:T(8,128)(2,1)S(1)}, bf16[128,512]{1,0:T(8,128)(2,1)S(1)}) custom-call(bf16[128,1024]{1,0:T(8,128)(2,1)S(1)} %get-tuple-element.69.own, bf16[128,1024]{1,0:T(8,128)(2,1)S(1)} %collective-permute-done.8.mate, bf16[1024,4096]{1,0:T(8,128)(2,1)S(1)} %bitcast.2), custom_call_target="tpu_custom_call" | custom-call | flops 1600000000 | bytes 1024 | tf_op jit(solution)/shard_map/project/pallas_call | solution.py:193
  35.4 1.0 %collective-permute-done.9 = bf16[128,512]{1,0:T(8,128)(2,1)S(1)} collective-permute-done((bf16[128,512]{1,0:T(8,128)(2,1)S(1)}, bf16[128,512]{1,0:T(8,128)(2,1)S(1)}, u32[]{:S(2)}, u32[]{:S(2)}) %collective-permute-start.9) | collective-permute-done | bytes 131104 | tf_op jit(solution)/shard_map/ppermute | solution.py:231
  36.6 1.2 %project.3 = (bf16[256,512]{1,0:T(8,128)(2,1)S(1)}, bf16[256,512]{1,0:T(8,128)(2,1)S(1)}, bf16[256,512]{1,0:T(8,128)(2,1)S(1)}, bf16[128,512]{1,0:T(8,128)(2,1)S(1)}) custom-call(bf16[128,1024]{1,0:T(8,128)(2,1)S(1)} %get-tuple-element.75.own, bf16[128,1024]{1,0:T(8,128)(2,1)S(1)} %collective-permute-done.14.mate, bf16[1024,4096]{1,0:T(8,128)(2,1)S(1)} %bitcast.2), custom_call_target="tpu_custom_call" | custom-call | flops 1600000000 | bytes 1024 | tf_op jit(solution)/shard_map/project/pallas_call | solution.py:193
  38.2 4.8 %collective-permute-done.10 = bf16[256,512]{1,0:T(8,128)(2,1)S(1)} collective-permute-done((bf16[256,512]{1,0:T(8,128)(2,1)S(1)}, bf16[256,512]{1,0:T(8,128)(2,1)S(1)}, u32[]{:S(2)}, u32[]{:S(2)}) %collective-permute-start.10) | collective-permute-done | bytes 262176 | tf_op jit(solution)/shard_map/ppermute | solution.py:231
  43.1 2.6 %collective-permute-done.16 = bf16[256,512]{1,0:T(8,128)(2,1)S(1)} collective-permute-done((bf16[256,512]{1,0:T(8,128)(2,1)S(1)}, bf16[256,512]{1,0:T(8,128)(2,1)S(1)}, u32[]{:S(2)}, u32[]{:S(2)}) %collective-permute-start.16) | collective-permute-done | bytes 262176 | tf_op jit(solution)/shard_map/ppermute | solution.py:231
  45.9 3.6 %collective-permute-done.11 = bf16[256,512]{1,0:T(8,128)(2,1)S(1)} collective-permute-done((bf16[256,512]{1,0:T(8,128)(2,1)S(1)}, bf16[256,512]{1,0:T(8,128)(2,1)S(1)}, u32[]{:S(2)}, u32[]{:S(2)}) %collective-permute-start.11) | collective-permute-done | bytes 262176 | tf_op jit(solution)/shard_map/ppermute | solution.py:231
  49.7 2.6 %collective-permute-done.17 = bf16[256,512]{1,0:T(8,128)(2,1)S(1)} collective-permute-done((bf16[256,512]{1,0:T(8,128)(2,1)S(1)}, bf16[256,512]{1,0:T(8,128)(2,1)S(1)}, u32[]{:S(2)}, u32[]{:S(2)}) %collective-permute-start.17) | collective-permute-done | bytes 262176 | tf_op jit(solution)/shard_map/ppermute | solution.py:231
  52.5 3.6 %collective-permute-done.12.refs_1_ = bf16[256,512]{1,0:T(8,128)(2,1)S(1)} collective-permute-done((bf16[256,512]{1,0:T(8,128)(2,1)S(1)}, bf16[256,512]{1,0:T(8,128)(2,1)S(1)}, u32[]{:S(2)}, u32[]{:S(2)}) %collective-permute-start.12) | collective-permute-done | bytes 262176 | tf_op jit(solution)/shard_map/ppermute | solution.py:231
  56.1 4.2 %collective-permute-start.13 = (bf16[128,512]{1,0:T(8,128)(2,1)S(1)}, bf16[128,512]{1,0:T(8,128)(2,1)S(1)}, u32[]{:S(2)}, u32[]{:S(2)}) collective-permute-start(bf16[128,512]{1,0:T(8,128)(2,1)S(1)} %slice.24), channel_id=1, source_target_pairs={{0,8},{8,0},{16,24},{24,16},{32,40},{40,32},{48,56},{56,48},{64,72... | collective-permute-start | bytes 393224 | tf_op jit(solution)/shard_map/ppermute | solution.py:215
  60.4 2.8 %collective-permute-start.19 = (bf16[128,512]{1,0:T(8,128)(2,1)S(1)}, bf16[128,512]{1,0:T(8,128)(2,1)S(1)}, u32[]{:S(2)}, u32[]{:S(2)}) collective-permute-start(bf16[128,512]{1,0:T(8,128)(2,1)S(1)} %slice.25), channel_id=1, source_target_pairs={{0,8},{8,0},{16,24},{24,16},{32,40},{40,32},{48,56},{56,48},{64,72... | collective-permute-start | bytes 393224 | tf_op jit(solution)/shard_map/ppermute | solution.py:215
  63.2 1.0 %collective-permute-done.19.refs_5_ = bf16[128,512]{1,0:T(8,128)(2,1)S(1)} collective-permute-done((bf16[128,512]{1,0:T(8,128)(2,1)S(1)}, bf16[128,512]{1,0:T(8,128)(2,1)S(1)}, u32[]{:S(2)}, u32[]{:S(2)}) %collective-permute-start.19) | collective-permute-done | bytes 131104 | tf_op jit(solution)/shard_map/ppermute | solution.py:215
  64.2 0.8 %finish.1 = bf16[256,512]{1,0:T(8,128)(2,1)} custom-call(bf16[128,512]{1,0:T(8,128)(2,1)S(1)} %get-tuple-element.70.refs_0_, bf16[256,512]{1,0:T(8,128)(2,1)S(1)} %collective-permute-done.12.refs_1_, bf16[128,512]{1,0:T(8,128)(2,1)S(1)} %collective-permute-done.13.refs_2_, bf16[128,512]{1,0:T(8,128)(2,1)S(1)} %get-tuple-element.76.refs_3_, ...), custom_call_target="tpu_custom_call" | custom-call | flops 500000000 | bytes 1024 | tf_op jit(solution)/shard_map/finish/pallas_call | solution.py:193
  (39 shorter events, 2.0 us)
Async XLA Ops:
  0.0 0.9 %copy-start.1 = (bf16[256,256]{1,0:T(8,128)(2,1)S(1)}, bf16[256,256]{1,0:T(8,128)(2,1)}, u32[]{:S(2)}) copy-start(bf16[256,256]{1,0:T(8,128)(2,1)} %key_values.1) | copy-start | bytes 393220
  0.9 0.7 %copy-start.2 = (s32[256]{0:T(256)S(1)}, s32[256]{0:T(256)}, u32[]{:S(2)}) copy-start(s32[256]{0:T(256)} %param.6) | copy-start | bytes 3076
  1.6 7.1 %collective-permute-start.1 = (bf16[272,256]{1,0:T(8,128)(2,1)S(1)}, bf16[272,256]{1,0:T(8,128)(2,1)S(1)}, u32[]{:S(2)}, u32[]{:S(2)}) collective-permute-start(bf16[272,256]{1,0:T(8,128)(2,1)S(1)} %pack.1.message), channel_id=1, source_target_pairs={{0,64},{8,72},{16,80},{24,88},{32,96},{40,104},{48,112},{56,120},{... | collective-permute-start | bytes 417800 | tf_op jit(solution)/shard_map/ppermute | solution.py:219
  3.8 13.1 %collective-permute-start.2 = (bf16[272,256]{1,0:T(8,128)(2,1)S(1)}, bf16[272,256]{1,0:T(8,128)(2,1)S(1)}, u32[]{:S(2)}, u32[]{:S(2)}) collective-permute-start(bf16[272,256]{1,0:T(8,128)(2,1)S(1)} %get-tuple-element.44.piece.own), channel_id=1, source_target_pairs={{0,32},{8,40},{16,48},{24,56},{32,64},{40,72},{48,80},{56,88},{64,... | collective-permute-start | bytes 417800 | tf_op jit(solution)/shard_map/ppermute | solution.py:219
  6.8 10.1 %collective-permute-start = (bf16[272,256]{1,0:T(8,128)(2,1)S(1)}, bf16[272,256]{1,0:T(8,128)(2,1)S(1)}, u32[]{:S(2)}, u32[]{:S(2)}) collective-permute-start(bf16[272,256]{1,0:T(8,128)(2,1)S(1)} %get-tuple-element.44.piece.own), channel_id=1, source_target_pairs={{0,16},{8,24},{16,32},{24,40},{32,48},{40,56},{48,64},{56,72},{64,... | collective-permute-start | bytes 417800 | tf_op jit(solution)/shard_map/ppermute | solution.py:219
  7.2 1.0 %copy-start = (bf16[256,1024]{1,0:T(8,128)(2,1)S(1)}, bf16[256,1024]{1,0:T(8,128)(2,1)}, u32[]{:S(2)}) copy-start(bf16[256,1024]{1,0:T(8,128)(2,1)} %queries.1) | copy-start | bytes 1572868
  8.3 13.6 %slice-start = ((s8[8388608]{0:T(1024)(128)(4,1)}), s8[4194304]{0:T(1024)(128)(4,1)S(1)}, s32[]{:S(2)}) async-start(s8[8388608]{0:T(1024)(128)(4,1)} %bitcast.1), calls=%async_computation | async-start | bytes 8388608
  8.8 8.1 %collective-permute-start.3 = (bf16[272,256]{1,0:T(8,128)(2,1)S(1)}, bf16[272,256]{1,0:T(8,128)(2,1)S(1)}, u32[]{:S(2)}, u32[]{:S(2)}) collective-permute-start(bf16[272,256]{1,0:T(8,128)(2,1)S(1)} %get-tuple-element.52), channel_id=1, source_target_pairs={{0,8},{8,0},{16,24},{24,16},{32,40},{40,32},{48,56},{56,48},{64,72... | collective-permute-start | bytes 417800 | tf_op jit(solution)/shard_map/ppermute | solution.py:215
  11.3 7.3 %collective-permute-start.5 = (bf16[272,256]{1,0:T(8,128)(2,1)S(1)}, bf16[272,256]{1,0:T(8,128)(2,1)S(1)}, u32[]{:S(2)}, u32[]{:S(2)}) collective-permute-start(bf16[272,256]{1,0:T(8,128)(2,1)S(1)} %get-tuple-element.54), channel_id=1, source_target_pairs={{0,48},{8,56},{16,0},{24,8},{32,16},{40,24},{48,32},{56,40},{64,11... | collective-permute-start | bytes 417800 | tf_op jit(solution)/shard_map/ppermute | solution.py:223
  16.9 2.6 %collective-permute-start.4 = (bf16[272,256]{1,0:T(8,128)(2,1)S(1)}, bf16[272,256]{1,0:T(8,128)(2,1)S(1)}, u32[]{:S(2)}, u32[]{:S(2)}) collective-permute-start(bf16[272,256]{1,0:T(8,128)(2,1)S(1)} %collective-permute-done.2.refs_4_), channel_id=1, source_target_pairs={{0,8},{8,0},{16,24},{24,16},{32,40},{40,32},{48,56},{56,48},{64,72... | collective-permute-start | bytes 417800 | tf_op jit(solution)/shard_map/ppermute | solution.py:215
  18.5 1.4 %collective-permute-start.7 = (bf16[272,256]{1,0:T(8,128)(2,1)S(1)}, bf16[272,256]{1,0:T(8,128)(2,1)S(1)}, u32[]{:S(2)}, u32[]{:S(2)}) collective-permute-start(bf16[272,256]{1,0:T(8,128)(2,1)S(1)} %collective-permute-done.refs_2_), channel_id=1, source_target_pairs={{0,8},{8,0},{16,24},{24,16},{32,40},{40,32},{48,56},{56,48},{64,72... | collective-permute-start | bytes 417800 | tf_op jit(solution)/shard_map/ppermute | solution.py:215
  18.6 3.3 %collective-permute-start.6 = (bf16[272,256]{1,0:T(8,128)(2,1)S(1)}, bf16[272,256]{1,0:T(8,128)(2,1)S(1)}, u32[]{:S(2)}, u32[]{:S(2)}) collective-permute-start(bf16[272,256]{1,0:T(8,128)(2,1)S(1)} %collective-permute-done.5.refs_0_), channel_id=1, source_target_pairs={{0,8},{8,0},{16,24},{24,16},{32,40},{40,32},{48,56},{56,48},{64,72... | collective-permute-start | bytes 417800 | tf_op jit(solution)/shard_map/ppermute | solution.py:215
  19.9 2.2 %slice-start.1 = ((s8[8388608]{0:T(1024)(128)(4,1)}), s8[4194304]{0:T(1024)(128)(4,1)S(1)}, s32[]{:S(2)}) async-start(s8[8388608]{0:T(1024)(128)(4,1)} %bitcast.1), calls=%async_computation.1 | async-start | bytes 8388608
  24.3 9.9 %collective-permute-start.8 = (bf16[128,1024]{1,0:T(8,128)(2,1)S(1)}, bf16[128,1024]{1,0:T(8,128)(2,1)S(1)}, u32[]{:S(2)}, u32[]{:S(2)}) collective-permute-start(bf16[128,1024]{1,0:T(8,128)(2,1)S(1)} %get-tuple-element.69.own), channel_id=1, source_target_pairs={{0,8},{8,0},{16,24},{24,16},{32,40},{40,32},{48,56},{56,48},{64,72... | collective-permute-start | bytes 786440 | tf_op jit(solution)/shard_map/ppermute | solution.py:215
  27.0 10.8 %collective-permute-start.15 = (bf16[128,512]{1,0:T(8,128)(2,1)S(1)}, bf16[128,512]{1,0:T(8,128)(2,1)S(1)}, u32[]{:S(2)}, u32[]{:S(2)}) collective-permute-start(bf16[128,512]{1,0:T(8,128)(2,1)S(1)} %get-tuple-element.80), channel_id=1, source_target_pairs={{0,7},{1,0},{2,1},{3,2},{4,3},{5,4},{6,5},{7,6},{8,9},{9,10},{10,1... | collective-permute-start | bytes 393224 | tf_op jit(solution)/shard_map/ppermute | solution.py:231
  28.7 7.7 %collective-permute-start.9 = (bf16[128,512]{1,0:T(8,128)(2,1)S(1)}, bf16[128,512]{1,0:T(8,128)(2,1)S(1)}, u32[]{:S(2)}, u32[]{:S(2)}) collective-permute-start(bf16[128,512]{1,0:T(8,128)(2,1)S(1)} %get-tuple-element.74), channel_id=1, source_target_pairs={{0,7},{1,0},{2,1},{3,2},{4,3},{5,4},{6,5},{7,6},{8,9},{9,10},{10,1... | collective-permute-start | bytes 393224 | tf_op jit(solution)/shard_map/ppermute | solution.py:231
  30.3 6.2 %collective-permute-start.14 = (bf16[128,1024]{1,0:T(8,128)(2,1)S(1)}, bf16[128,1024]{1,0:T(8,128)(2,1)S(1)}, u32[]{:S(2)}, u32[]{:S(2)}) collective-permute-start(bf16[128,1024]{1,0:T(8,128)(2,1)S(1)} %get-tuple-element.75.own), channel_id=1, source_target_pairs={{0,8},{8,0},{16,24},{24,16},{32,40},{40,32},{48,56},{56,48},{64,72... | collective-permute-start | bytes 786440 | tf_op jit(solution)/shard_map/ppermute | solution.py:215
  36.5 6.5 %collective-permute-start.10 = (bf16[256,512]{1,0:T(8,128)(2,1)S(1)}, bf16[256,512]{1,0:T(8,128)(2,1)S(1)}, u32[]{:S(2)}, u32[]{:S(2)}) collective-permute-start(bf16[256,512]{1,0:T(8,128)(2,1)S(1)} %pad_maximum_fusion), channel_id=1, source_target_pairs={{0,7},{1,0},{2,1},{3,2},{4,3},{5,4},{6,5},{7,6},{8,9},{9,10},{10,1... | collective-permute-start | bytes 786440 | tf_op jit(solution)/shard_map/ppermute | solution.py:231
  37.8 8.0 %collective-permute-start.16 = (bf16[256,512]{1,0:T(8,128)(2,1)S(1)}, bf16[256,512]{1,0:T(8,128)(2,1)S(1)}, u32[]{:S(2)}, u32[]{:S(2)}) collective-permute-start(bf16[256,512]{1,0:T(8,128)(2,1)S(1)} %pad_maximum_fusion.1), channel_id=1, source_target_pairs={{0,7},{1,0},{2,1},{3,2},{4,3},{5,4},{6,5},{7,6},{8,9},{9,10},{10,1... | collective-permute-start | bytes 786440 | tf_op jit(solution)/shard_map/ppermute | solution.py:231
  43.0 6.5 %collective-permute-start.11 = (bf16[256,512]{1,0:T(8,128)(2,1)S(1)}, bf16[256,512]{1,0:T(8,128)(2,1)S(1)}, u32[]{:S(2)}, u32[]{:S(2)}) collective-permute-start(bf16[256,512]{1,0:T(8,128)(2,1)S(1)} %add.19), channel_id=1, source_target_pairs={{0,7},{1,0},{2,1},{3,2},{4,3},{5,4},{6,5},{7,6},{8,9},{9,10},{10,1... | collective-permute-start | bytes 786440 | tf_op jit(solution)/shard_map/ppermute | solution.py:231
  45.8 6.5 %collective-permute-start.17 = (bf16[256,512]{1,0:T(8,128)(2,1)S(1)}, bf16[256,512]{1,0:T(8,128)(2,1)S(1)}, u32[]{:S(2)}, u32[]{:S(2)}) collective-permute-start(bf16[256,512]{1,0:T(8,128)(2,1)S(1)} %add.22), channel_id=1, source_target_pairs={{0,7},{1,0},{2,1},{3,2},{4,3},{5,4},{6,5},{7,6},{8,9},{9,10},{10,1... | collective-permute-start | bytes 786440 | tf_op jit(solution)/shard_map/ppermute | solution.py:231
  49.6 6.5 %collective-permute-start.12 = (bf16[256,512]{1,0:T(8,128)(2,1)S(1)}, bf16[256,512]{1,0:T(8,128)(2,1)S(1)}, u32[]{:S(2)}, u32[]{:S(2)}) collective-permute-start(bf16[256,512]{1,0:T(8,128)(2,1)S(1)} %add.20), channel_id=1, source_target_pairs={{0,7},{1,0},{2,1},{3,2},{4,3},{5,4},{6,5},{7,6},{8,9},{9,10},{10,1... | collective-permute-start | bytes 786440 | tf_op jit(solution)/shard_map/ppermute | solution.py:231
  52.4 8.0 %collective-permute-start.18 = (bf16[256,512]{1,0:T(8,128)(2,1)S(1)}, bf16[256,512]{1,0:T(8,128)(2,1)S(1)}, u32[]{:S(2)}, u32[]{:S(2)}) collective-permute-start(bf16[256,512]{1,0:T(8,128)(2,1)S(1)} %add.23), channel_id=1, source_target_pairs={{0,7},{1,0},{2,1},{3,2},{4,3},{5,4},{6,5},{7,6},{8,9},{9,10},{10,1... | collective-permute-start | bytes 786440 | tf_op jit(solution)/shard_map/ppermute | solution.py:231
  56.1 7.1 %collective-permute-start.13 = (bf16[128,512]{1,0:T(8,128)(2,1)S(1)}, bf16[128,512]{1,0:T(8,128)(2,1)S(1)}, u32[]{:S(2)}, u32[]{:S(2)}) collective-permute-start(bf16[128,512]{1,0:T(8,128)(2,1)S(1)} %slice.24), channel_id=1, source_target_pairs={{0,8},{8,0},{16,24},{24,16},{32,40},{40,32},{48,56},{56,48},{64,72... | collective-permute-start | bytes 393224 | tf_op jit(solution)/shard_map/ppermute | solution.py:215
  60.4 3.8 %collective-permute-start.19 = (bf16[128,512]{1,0:T(8,128)(2,1)S(1)}, bf16[128,512]{1,0:T(8,128)(2,1)S(1)}, u32[]{:S(2)}, u32[]{:S(2)}) collective-permute-start(bf16[128,512]{1,0:T(8,128)(2,1)S(1)} %slice.25), channel_id=1, source_target_pairs={{0,8},{8,0},{16,24},{24,16},{32,40},{40,32},{48,56},{56,48},{64,72... | collective-permute-start | bytes 393224 | tf_op jit(solution)/shard_map/ppermute | solution.py:215

commit v4 on v3

--- a/solution.py
+++ b/solution.py
@@ -267,7 +267,7 @@
         attention, product = call(
             functools.partial(last_kernel, part, [3, 3], len(kept) // 3),
             "attend",
-            3,
+            0.01,
             [shape(PART, HEADS * HD), shape(PART, CHUNK)],
             query_rows,
             ids,
@@ -286,7 +286,7 @@
         one, two, three, mine = call(
             project_kernel,
             "project",
-            1.6,
+            0.01,
             [wide, wide, wide, shape(PART, CHUNK)],
             attention,
             to_mate(attention),

time: 65.2 us -> 61.8 us (0.948)
  starting transfers between devices: 28 us -> 24.9 us
    ppermute x8, starting transfers between devices: 16 us -> 12.4 us  [to_mate(): return lax.ppermute(value, 'loop', [(i, i ^ 1) for i in range(stretches)])]
where the time goes in v4:
time: 61.8 us; the launch traced here: 61.6 us
  starting transfers between devices  24.9 us (40%)
  waiting for transfers between devices  23.2 us (38%)
  Pallas kernels  10.1 us (16%)
  local copies, waits for them, and re-layouts  2.82 us (5%)
    ppermute x8, waiting for transfers between devices, along(): return lax.ppermute(value, ('loop', 'tp'), pairs)  18.1 us
    ppermute x8, starting transfers between devices, to_mate(): return lax.ppermute(value, 'loop', [(i, i ^ 1) for i in range(stretches)])  12.4 us
    pallas_call x10, Pallas kernels, call(): pl.pallas_call(kernel, out_shape=outs, in_specs=[VMEM] * len(args), out_s...  10.1 us
    ppermute x3, starting transfers between devices, from_chip(): return lax.ppermute(value, 'loop', pairs)  5.51 us
    ppermute x8, starting transfers between devices, along(): return lax.ppermute(value, ('loop', 'tp'), pairs)  4.69 us
    ppermute x3, waiting for transfers between devices, from_chip(): return lax.ppermute(value, 'loop', pairs)  3.28 us
    unnamed x10, local copies, waits for them, and re-layouts  2.8 us
    ppermute x1, starting transfers between devices, along_row(): return lax.ppermute(value, 'loop', pairs)  2.31 us
  transfers between devices with their start and end apart: 20, of which 10 were waited for; matrix products, arithmetic and copies ran while one was open for 1% of the time, Pallas kernels for 11%

profile of v4, /device:TPU:1, one launch (start us, length us, event | category | flops | bytes accessed | tf_op | source)
XLA Modules:
  0.0 61.6 jit_solution(17773066423675226680)
XLA Ops:
  0.0 0.9 %copy-done.1 = bf16[256,256]{1,0:T(8,128)(2,1)S(1)} copy-done((bf16[256,256]{1,0:T(8,128)(2,1)S(1)}, bf16[256,256]{1,0:T(8,128)(2,1)}, u32[]{:S(2)}) %copy-start.1) | copy-done | bytes 131096
  0.9 0.7 %copy-done.2 = s32[256]{0:T(256)S(1)} copy-done((s32[256]{0:T(256)S(1)}, s32[256]{0:T(256)}, u32[]{:S(2)}) %copy-start.2) | copy-done | bytes 1048
  1.6 2.1 %collective-permute-start.1 = (bf16[272,256]{1,0:T(8,128)(2,1)S(1)}, bf16[272,256]{1,0:T(8,128)(2,1)S(1)}, u32[]{:S(2)}, u32[]{:S(2)}) collective-permute-start(bf16[272,256]{1,0:T(8,128)(2,1)S(1)} %pack.1.message), channel_id=1, source_target_pairs={{0,64},{8,72},{16,80},{24,88},{32,96},{40,104},{48,112},{56,120},{... | collective-permute-start | bytes 417800 | tf_op jit(solution)/shard_map/ppermute | solution.py:219
  3.8 3.0 %collective-permute-start.2 = (bf16[272,256]{1,0:T(8,128)(2,1)S(1)}, bf16[272,256]{1,0:T(8,128)(2,1)S(1)}, u32[]{:S(2)}, u32[]{:S(2)}) collective-permute-start(bf16[272,256]{1,0:T(8,128)(2,1)S(1)} %get-tuple-element.44.piece.own), channel_id=1, source_target_pairs={{0,32},{8,40},{16,48},{24,56},{32,64},{40,72},{48,80},{56,88},{64,... | collective-permute-start | bytes 417800 | tf_op jit(solution)/shard_map/ppermute | solution.py:219
  6.8 0.4 collective-permute-start
  7.2 1.0 %copy-done = bf16[256,1024]{1,0:T(8,128)(2,1)S(1)} copy-done((bf16[256,1024]{1,0:T(8,128)(2,1)S(1)}, bf16[256,1024]{1,0:T(8,128)(2,1)}, u32[]{:S(2)}) %copy-start) | copy-done | bytes 524312
  8.3 0.5 own_scores.1
  8.8 2.5 %collective-permute-start.3 = (bf16[272,256]{1,0:T(8,128)(2,1)S(1)}, bf16[272,256]{1,0:T(8,128)(2,1)S(1)}, u32[]{:S(2)}, u32[]{:S(2)}) collective-permute-start(bf16[272,256]{1,0:T(8,128)(2,1)S(1)} %get-tuple-element.52), channel_id=1, source_target_pairs={{0,8},{8,0},{16,24},{24,16},{32,40},{40,32},{48,56},{56,48},{64,72... | collective-permute-start | bytes 417800 | tf_op jit(solution)/shard_map/ppermute | solution.py:215
  11.3 2.3 %collective-permute-start.5 = (bf16[272,256]{1,0:T(8,128)(2,1)S(1)}, bf16[272,256]{1,0:T(8,128)(2,1)S(1)}, u32[]{:S(2)}, u32[]{:S(2)}) collective-permute-start(bf16[272,256]{1,0:T(8,128)(2,1)S(1)} %get-tuple-element.54), channel_id=1, source_target_pairs={{0,48},{8,56},{16,0},{24,8},{32,16},{40,24},{48,32},{56,40},{64,11... | collective-permute-start | bytes 417800 | tf_op jit(solution)/shard_map/ppermute | solution.py:223
  13.6 3.3 %collective-permute-done.refs_2_ = bf16[272,256]{1,0:T(8,128)(2,1)S(1)} collective-permute-done((bf16[272,256]{1,0:T(8,128)(2,1)S(1)}, bf16[272,256]{1,0:T(8,128)(2,1)S(1)}, u32[]{:S(2)}, u32[]{:S(2)}) %collective-permute-start) | collective-permute-done | bytes 139296 | tf_op jit(solution)/shard_map/ppermute | solution.py:219
  16.9 1.6 %collective-permute-start.4 = (bf16[272,256]{1,0:T(8,128)(2,1)S(1)}, bf16[272,256]{1,0:T(8,128)(2,1)S(1)}, u32[]{:S(2)}, u32[]{:S(2)}) collective-permute-start(bf16[272,256]{1,0:T(8,128)(2,1)S(1)} %collective-permute-done.2.refs_4_), channel_id=1, source_target_pairs={{0,8},{8,0},{16,24},{24,16},{32,40},{40,32},{48,56},{56,48},{64,72... | collective-permute-start | bytes 417800 | tf_op jit(solution)/shard_map/ppermute | solution.py:215
  18.6 0.4 collective-permute-start.6
  19.0 0.5 collective-permute-done.4.refs_5_
  19.9 2.0 %more_scores.1 = (f32[2048,1536]{1,0:T(8,128)S(1)}, f32[2048,128]{1,0:T(8,128)S(1)}, bf16[1536,256]{1,0:T(8,128)(2,1)S(1)}) custom-call(bf16[2048,128]{1,0:T(8,128)(2,1)S(1)} %get-tuple-element.45.query_rows, f32[256,1]{1,0:T(8,128)S(1)} %get-tuple-element.51.ids, bf16[272,256]{1,0:T(8,128)(2,1)S(1)} %collective-permute-done.1.far.refs_0_, ...), custom_call_target="tpu_custom_call" | custom-call | flops 3000000000 | bytes 1024 | tf_op jit(solution)/shard_map/more_scores/pallas_call | solution.py:193
  22.1 2.2 %attend.2 = (bf16[128,1024]{1,0:T(8,128)(2,1)S(1)}, bf16[128,512]{1,0:T(8,128)(2,1)S(1)}) custom-call(bf16[2048,128]{1,0:T(8,128)(2,1)S(1)} %get-tuple-element.45.query_rows, f32[256,1]{1,0:T(8,128)S(1)} %get-tuple-element.51.ids, bf16[272,256]{1,0:T(8,128)(2,1)S(1)} %collective-permute-done.5.refs_0_, bf16[272,256]{1,0:T(8,128)(2,1)S(1)} %collective-permute-done.6.refs_1_, ...), custom_call_target="tpu_custom_call" | custom-call | flops 10000000 | bytes 1024 | tf_op jit(solution)/shard_map/attend/pallas_call | solution.py:193
  24.6 1.7 %collective-permute-start.9 = (bf16[128,512]{1,0:T(8,128)(2,1)S(1)}, bf16[128,512]{1,0:T(8,128)(2,1)S(1)}, u32[]{:S(2)}, u32[]{:S(2)}) collective-permute-start(bf16[128,512]{1,0:T(8,128)(2,1)S(1)} %get-tuple-element.74), channel_id=1, source_target_pairs={{0,7},{1,0},{2,1},{3,2},{4,3},{5,4},{6,5},{7,6},{8,9},{9,10},{10,1... | collective-permute-start | bytes 393224 | tf_op jit(solution)/shard_map/ppermute | solution.py:231
  26.3 2.2 %attend.3 = (bf16[128,1024]{1,0:T(8,128)(2,1)S(1)}, bf16[128,512]{1,0:T(8,128)(2,1)S(1)}) custom-call(bf16[2048,128]{1,0:T(8,128)(2,1)S(1)} %get-tuple-element.45.query_rows, f32[256,1]{1,0:T(8,128)S(1)} %get-tuple-element.51.ids, bf16[272,256]{1,0:T(8,128)(2,1)S(1)} %collective-permute-done.5.refs_0_, bf16[272,256]{1,0:T(8,128)(2,1)S(1)} %collective-permute-done.6.refs_1_, ...), custom_call_target="tpu_custom_call" | custom-call | flops 10000000 | bytes 1024 | tf_op jit(solution)/shard_map/attend/pallas_call | solution.py:193
  28.5 1.7 %collective-permute-start.15 = (bf16[128,512]{1,0:T(8,128)(2,1)S(1)}, bf16[128,512]{1,0:T(8,128)(2,1)S(1)}, u32[]{:S(2)}, u32[]{:S(2)}) collective-permute-start(bf16[128,512]{1,0:T(8,128)(2,1)S(1)} %get-tuple-element.80), channel_id=1, source_target_pairs={{0,7},{1,0},{2,1},{3,2},{4,3},{5,4},{6,5},{7,6},{8,9},{9,10},{10,1... | collective-permute-start | bytes 393224 | tf_op jit(solution)/shard_map/ppermute | solution.py:231
  30.2 3.8 %collective-permute-start.14 = (bf16[128,1024]{1,0:T(8,128)(2,1)S(1)}, bf16[128,1024]{1,0:T(8,128)(2,1)S(1)}, u32[]{:S(2)}, u32[]{:S(2)}) collective-permute-start(bf16[128,1024]{1,0:T(8,128)(2,1)S(1)} %get-tuple-element.75.own), channel_id=1, source_target_pairs={{0,8},{8,0},{16,24},{24,16},{32,40},{40,32},{48,56},{56,48},{64,72... | collective-permute-start | bytes 786440 | tf_op jit(solution)/shard_map/ppermute | solution.py:215
  34.1 1.1 %project.2 = (bf16[256,512]{1,0:T(8,128)(2,1)S(1)}, bf16[256,512]{1,0:T(8,128)(2,1)S(1)}, bf16[256,512]{1,0:T(8,128)(2,1)S(1)}, bf16[128,512]{1,0:T(8,128)(2,1)S(1)}) custom-call(bf16[128,1024]{1,0:T(8,128)(2,1)S(1)} %get-tuple-element.69.own, bf16[128,1024]{1,0:T(8,128)(2,1)S(1)} %collective-permute-done.8.mate, bf16[1024,4096]{1,0:T(8,128)(2,1)S(1)} %bitcast.2), custom_call_target="tpu_custom_call" | custom-call | flops 10000000 | bytes 1024 | tf_op jit(solution)/shard_map/project/pallas_call | solution.py:193
  35.3 0.8 %collective-permute-start.10 = (bf16[256,512]{1,0:T(8,128)(2,1)S(1)}, bf16[256,512]{1,0:T(8,128)(2,1)S(1)}, u32[]{:S(2)}, u32[]{:S(2)}) collective-permute-start(bf16[256,512]{1,0:T(8,128)(2,1)S(1)} %pad_maximum_fusion), channel_id=1, source_target_pairs={{0,7},{1,0},{2,1},{3,2},{4,3},{5,4},{6,5},{7,6},{8,9},{9,10},{10,1... | collective-permute-start | bytes 786440 | tf_op jit(solution)/shard_map/ppermute | solution.py:231
  36.1 1.1 %project.3 = (bf16[256,512]{1,0:T(8,128)(2,1)S(1)}, bf16[256,512]{1,0:T(8,128)(2,1)S(1)}, bf16[256,512]{1,0:T(8,128)(2,1)S(1)}, bf16[128,512]{1,0:T(8,128)(2,1)S(1)}) custom-call(bf16[128,1024]{1,0:T(8,128)(2,1)S(1)} %get-tuple-element.75.own, bf16[128,1024]{1,0:T(8,128)(2,1)S(1)} %collective-permute-done.14.mate, bf16[1024,4096]{1,0:T(8,128)(2,1)S(1)} %bitcast.2), custom_call_target="tpu_custom_call" | custom-call | flops 10000000 | bytes 1024 | tf_op jit(solution)/shard_map/project/pallas_call | solution.py:193
  37.4 4.4 %collective-permute-done.10 = bf16[256,512]{1,0:T(8,128)(2,1)S(1)} collective-permute-done((bf16[256,512]{1,0:T(8,128)(2,1)S(1)}, bf16[256,512]{1,0:T(8,128)(2,1)S(1)}, u32[]{:S(2)}, u32[]{:S(2)}) %collective-permute-start.10) | collective-permute-done | bytes 262176 | tf_op jit(solution)/shard_map/ppermute | solution.py:231
  41.9 2.6 %collective-permute-done.16 = bf16[256,512]{1,0:T(8,128)(2,1)S(1)} collective-permute-done((bf16[256,512]{1,0:T(8,128)(2,1)S(1)}, bf16[256,512]{1,0:T(8,128)(2,1)S(1)}, u32[]{:S(2)}, u32[]{:S(2)}) %collective-permute-start.16) | collective-permute-done | bytes 262176 | tf_op jit(solution)/shard_map/ppermute | solution.py:231
  44.7 3.6 %collective-permute-done.11 = bf16[256,512]{1,0:T(8,128)(2,1)S(1)} collective-permute-done((bf16[256,512]{1,0:T(8,128)(2,1)S(1)}, bf16[256,512]{1,0:T(8,128)(2,1)S(1)}, u32[]{:S(2)}, u32[]{:S(2)}) %collective-permute-start.11) | collective-permute-done | bytes 262176 | tf_op jit(solution)/shard_map/ppermute | solution.py:231
  48.5 2.6 %collective-permute-done.17 = bf16[256,512]{1,0:T(8,128)(2,1)S(1)} collective-permute-done((bf16[256,512]{1,0:T(8,128)(2,1)S(1)}, bf16[256,512]{1,0:T(8,128)(2,1)S(1)}, u32[]{:S(2)}, u32[]{:S(2)}) %collective-permute-start.17) | collective-permute-done | bytes 262176 | tf_op jit(solution)/shard_map/ppermute | solution.py:231
  51.3 3.6 %collective-permute-done.12.refs_1_ = bf16[256,512]{1,0:T(8,128)(2,1)S(1)} collective-permute-done((bf16[256,512]{1,0:T(8,128)(2,1)S(1)}, bf16[256,512]{1,0:T(8,128)(2,1)S(1)}, u32[]{:S(2)}, u32[]{:S(2)}) %collective-permute-start.12) | collective-permute-done | bytes 262176 | tf_op jit(solution)/shard_map/ppermute | solution.py:231
  54.9 1.6 %collective-permute-start.13 = (bf16[128,512]{1,0:T(8,128)(2,1)S(1)}, bf16[128,512]{1,0:T(8,128)(2,1)S(1)}, u32[]{:S(2)}, u32[]{:S(2)}) collective-permute-start(bf16[128,512]{1,0:T(8,128)(2,1)S(1)} %slice.24), channel_id=1, source_target_pairs={{0,8},{8,0},{16,24},{24,16},{32,40},{40,32},{48,56},{56,48},{64,72... | collective-permute-start | bytes 393224 | tf_op jit(solution)/shard_map/ppermute | solution.py:215
  56.5 1.2 %collective-permute-done.18.refs_4_ = bf16[256,512]{1,0:T(8,128)(2,1)S(1)} collective-permute-done((bf16[256,512]{1,0:T(8,128)(2,1)S(1)}, bf16[256,512]{1,0:T(8,128)(2,1)S(1)}, u32[]{:S(2)}, u32[]{:S(2)}) %collective-permute-start.18) | collective-permute-done | bytes 262176 | tf_op jit(solution)/shard_map/ppermute | solution.py:231
  57.7 2.1 %collective-permute-start.19 = (bf16[128,512]{1,0:T(8,128)(2,1)S(1)}, bf16[128,512]{1,0:T(8,128)(2,1)S(1)}, u32[]{:S(2)}, u32[]{:S(2)}) collective-permute-start(bf16[128,512]{1,0:T(8,128)(2,1)S(1)} %slice.25), channel_id=1, source_target_pairs={{0,8},{8,0},{16,24},{24,16},{32,40},{40,32},{48,56},{56,48},{64,72... | collective-permute-start | bytes 393224 | tf_op jit(solution)/shard_map/ppermute | solution.py:215
  59.8 1.0 %collective-permute-done.19.refs_5_ = bf16[128,512]{1,0:T(8,128)(2,1)S(1)} collective-permute-done((bf16[128,512]{1,0:T(8,128)(2,1)S(1)}, bf16[128,512]{1,0:T(8,128)(2,1)S(1)}, u32[]{:S(2)}, u32[]{:S(2)}) %collective-permute-start.19) | collective-permute-done | bytes 131104 | tf_op jit(solution)/shard_map/ppermute | solution.py:215
  60.8 0.8 %finish.1 = bf16[256,512]{1,0:T(8,128)(2,1)} custom-call(bf16[128,512]{1,0:T(8,128)(2,1)S(1)} %get-tuple-element.70.refs_0_, bf16[256,512]{1,0:T(8,128)(2,1)S(1)} %collective-permute-done.12.refs_1_, bf16[128,512]{1,0:T(8,128)(2,1)S(1)} %collective-permute-done.13.refs_2_, bf16[128,512]{1,0:T(8,128)(2,1)S(1)} %get-tuple-element.76.refs_3_, ...), custom_call_target="tpu_custom_call" | custom-call | flops 500000000 | bytes 1024 | tf_op jit(solution)/shard_map/finish/pallas_call | solution.py:193
  (39 shorter events, 1.9 us)
Async XLA Ops:
  0.0 0.9 %copy-start.1 = (bf16[256,256]{1,0:T(8,128)(2,1)S(1)}, bf16[256,256]{1,0:T(8,128)(2,1)}, u32[]{:S(2)}) copy-start(bf16[256,256]{1,0:T(8,128)(2,1)} %key_values.1) | copy-start | bytes 393220
  0.9 0.7 %copy-start.2 = (s32[256]{0:T(256)S(1)}, s32[256]{0:T(256)}, u32[]{:S(2)}) copy-start(s32[256]{0:T(256)} %param.6) | copy-start | bytes 3076
  1.6 7.1 %collective-permute-start.1 = (bf16[272,256]{1,0:T(8,128)(2,1)S(1)}, bf16[272,256]{1,0:T(8,128)(2,1)S(1)}, u32[]{:S(2)}, u32[]{:S(2)}) collective-permute-start(bf16[272,256]{1,0:T(8,128)(2,1)S(1)} %pack.1.message), channel_id=1, source_target_pairs={{0,64},{8,72},{16,80},{24,88},{32,96},{40,104},{48,112},{56,120},{... | collective-permute-start | bytes 417800 | tf_op jit(solution)/shard_map/ppermute | solution.py:219
  3.8 13.1 %collective-permute-start.2 = (bf16[272,256]{1,0:T(8,128)(2,1)S(1)}, bf16[272,256]{1,0:T(8,128)(2,1)S(1)}, u32[]{:S(2)}, u32[]{:S(2)}) collective-permute-start(bf16[272,256]{1,0:T(8,128)(2,1)S(1)} %get-tuple-element.44.piece.own), channel_id=1, source_target_pairs={{0,32},{8,40},{16,48},{24,56},{32,64},{40,72},{48,80},{56,88},{64,... | collective-permute-start | bytes 417800 | tf_op jit(solution)/shard_map/ppermute | solution.py:219
  6.8 10.1 %collective-permute-start = (bf16[272,256]{1,0:T(8,128)(2,1)S(1)}, bf16[272,256]{1,0:T(8,128)(2,1)S(1)}, u32[]{:S(2)}, u32[]{:S(2)}) collective-permute-start(bf16[272,256]{1,0:T(8,128)(2,1)S(1)} %get-tuple-element.44.piece.own), channel_id=1, source_target_pairs={{0,16},{8,24},{16,32},{24,40},{32,48},{40,56},{48,64},{56,72},{64,... | collective-permute-start | bytes 417800 | tf_op jit(solution)/shard_map/ppermute | solution.py:219
  7.2 1.0 %copy-start = (bf16[256,1024]{1,0:T(8,128)(2,1)S(1)}, bf16[256,1024]{1,0:T(8,128)(2,1)}, u32[]{:S(2)}) copy-start(bf16[256,1024]{1,0:T(8,128)(2,1)} %queries.1) | copy-start | bytes 1572868
  8.3 13.6 %slice-start = ((s8[8388608]{0:T(1024)(128)(4,1)}), s8[4194304]{0:T(1024)(128)(4,1)S(1)}, s32[]{:S(2)}) async-start(s8[8388608]{0:T(1024)(128)(4,1)} %bitcast.1), calls=%async_computation | async-start | bytes 8388608
  8.8 8.1 %collective-permute-start.3 = (bf16[272,256]{1,0:T(8,128)(2,1)S(1)}, bf16[272,256]{1,0:T(8,128)(2,1)S(1)}, u32[]{:S(2)}, u32[]{:S(2)}) collective-permute-start(bf16[272,256]{1,0:T(8,128)(2,1)S(1)} %get-tuple-element.52), channel_id=1, source_target_pairs={{0,8},{8,0},{16,24},{24,16},{32,40},{40,32},{48,56},{56,48},{64,72... | collective-permute-start | bytes 417800 | tf_op jit(solution)/shard_map/ppermute | solution.py:215
  11.3 7.3 %collective-permute-start.5 = (bf16[272,256]{1,0:T(8,128)(2,1)S(1)}, bf16[272,256]{1,0:T(8,128)(2,1)S(1)}, u32[]{:S(2)}, u32[]{:S(2)}) collective-permute-start(bf16[272,256]{1,0:T(8,128)(2,1)S(1)} %get-tuple-element.54), channel_id=1, source_target_pairs={{0,48},{8,56},{16,0},{24,8},{32,16},{40,24},{48,32},{56,40},{64,11... | collective-permute-start | bytes 417800 | tf_op jit(solution)/shard_map/ppermute | solution.py:223
  16.9 2.6 %collective-permute-start.4 = (bf16[272,256]{1,0:T(8,128)(2,1)S(1)}, bf16[272,256]{1,0:T(8,128)(2,1)S(1)}, u32[]{:S(2)}, u32[]{:S(2)}) collective-permute-start(bf16[272,256]{1,0:T(8,128)(2,1)S(1)} %collective-permute-done.2.refs_4_), channel_id=1, source_target_pairs={{0,8},{8,0},{16,24},{24,16},{32,40},{40,32},{48,56},{56,48},{64,72... | collective-permute-start | bytes 417800 | tf_op jit(solution)/shard_map/ppermute | solution.py:215
  18.5 1.4 %collective-permute-start.7 = (bf16[272,256]{1,0:T(8,128)(2,1)S(1)}, bf16[272,256]{1,0:T(8,128)(2,1)S(1)}, u32[]{:S(2)}, u32[]{:S(2)}) collective-permute-start(bf16[272,256]{1,0:T(8,128)(2,1)S(1)} %collective-permute-done.refs_2_), channel_id=1, source_target_pairs={{0,8},{8,0},{16,24},{24,16},{32,40},{40,32},{48,56},{56,48},{64,72... | collective-permute-start | bytes 417800 | tf_op jit(solution)/shard_map/ppermute | solution.py:215
  18.6 3.3 %collective-permute-start.6 = (bf16[272,256]{1,0:T(8,128)(2,1)S(1)}, bf16[272,256]{1,0:T(8,128)(2,1)S(1)}, u32[]{:S(2)}, u32[]{:S(2)}) collective-permute-start(bf16[272,256]{1,0:T(8,128)(2,1)S(1)} %collective-permute-done.5.refs_0_), channel_id=1, source_target_pairs={{0,8},{8,0},{16,24},{24,16},{32,40},{40,32},{48,56},{56,48},{64,72... | collective-permute-start | bytes 417800 | tf_op jit(solution)/shard_map/ppermute | solution.py:215
  19.9 2.2 %slice-start.1 = ((s8[8388608]{0:T(1024)(128)(4,1)}), s8[4194304]{0:T(1024)(128)(4,1)S(1)}, s32[]{:S(2)}) async-start(s8[8388608]{0:T(1024)(128)(4,1)} %bitcast.1), calls=%async_computation.1 | async-start | bytes 8388608
  24.3 9.8 %collective-permute-start.8 = (bf16[128,1024]{1,0:T(8,128)(2,1)S(1)}, bf16[128,1024]{1,0:T(8,128)(2,1)S(1)}, u32[]{:S(2)}, u32[]{:S(2)}) collective-permute-start(bf16[128,1024]{1,0:T(8,128)(2,1)S(1)} %get-tuple-element.69.own), channel_id=1, source_target_pairs={{0,8},{8,0},{16,24},{24,16},{32,40},{40,32},{48,56},{56,48},{64,72... | collective-permute-start | bytes 786440 | tf_op jit(solution)/shard_map/ppermute | solution.py:215
  24.6 10.6 %collective-permute-start.9 = (bf16[128,512]{1,0:T(8,128)(2,1)S(1)}, bf16[128,512]{1,0:T(8,128)(2,1)S(1)}, u32[]{:S(2)}, u32[]{:S(2)}) collective-permute-start(bf16[128,512]{1,0:T(8,128)(2,1)S(1)} %get-tuple-element.74), channel_id=1, source_target_pairs={{0,7},{1,0},{2,1},{3,2},{4,3},{5,4},{6,5},{7,6},{8,9},{9,10},{10,1... | collective-permute-start | bytes 393224 | tf_op jit(solution)/shard_map/ppermute | solution.py:231
  28.5 8.7 %collective-permute-start.15 = (bf16[128,512]{1,0:T(8,128)(2,1)S(1)}, bf16[128,512]{1,0:T(8,128)(2,1)S(1)}, u32[]{:S(2)}, u32[]{:S(2)}) collective-permute-start(bf16[128,512]{1,0:T(8,128)(2,1)S(1)} %get-tuple-element.80), channel_id=1, source_target_pairs={{0,7},{1,0},{2,1},{3,2},{4,3},{5,4},{6,5},{7,6},{8,9},{9,10},{10,1... | collective-permute-start | bytes 393224 | tf_op jit(solution)/shard_map/ppermute | solution.py:231
  30.2 5.9 %collective-permute-start.14 = (bf16[128,1024]{1,0:T(8,128)(2,1)S(1)}, bf16[128,1024]{1,0:T(8,128)(2,1)S(1)}, u32[]{:S(2)}, u32[]{:S(2)}) collective-permute-start(bf16[128,1024]{1,0:T(8,128)(2,1)S(1)} %get-tuple-element.75.own), channel_id=1, source_target_pairs={{0,8},{8,0},{16,24},{24,16},{32,40},{40,32},{48,56},{56,48},{64,72... | collective-permute-start | bytes 786440 | tf_op jit(solution)/shard_map/ppermute | solution.py:215
  35.3 6.5 %collective-permute-start.10 = (bf16[256,512]{1,0:T(8,128)(2,1)S(1)}, bf16[256,512]{1,0:T(8,128)(2,1)S(1)}, u32[]{:S(2)}, u32[]{:S(2)}) collective-permute-start(bf16[256,512]{1,0:T(8,128)(2,1)S(1)} %pad_maximum_fusion), channel_id=1, source_target_pairs={{0,7},{1,0},{2,1},{3,2},{4,3},{5,4},{6,5},{7,6},{8,9},{9,10},{10,1... | collective-permute-start | bytes 786440 | tf_op jit(solution)/shard_map/ppermute | solution.py:231
  37.3 7.3 %collective-permute-start.16 = (bf16[256,512]{1,0:T(8,128)(2,1)S(1)}, bf16[256,512]{1,0:T(8,128)(2,1)S(1)}, u32[]{:S(2)}, u32[]{:S(2)}) collective-permute-start(bf16[256,512]{1,0:T(8,128)(2,1)S(1)} %pad_maximum_fusion.1), channel_id=1, source_target_pairs={{0,7},{1,0},{2,1},{3,2},{4,3},{5,4},{6,5},{7,6},{8,9},{9,10},{10,1... | collective-permute-start | bytes 786440 | tf_op jit(solution)/shard_map/ppermute | solution.py:231
  41.8 6.5 %collective-permute-start.11 = (bf16[256,512]{1,0:T(8,128)(2,1)S(1)}, bf16[256,512]{1,0:T(8,128)(2,1)S(1)}, u32[]{:S(2)}, u32[]{:S(2)}) collective-permute-start(bf16[256,512]{1,0:T(8,128)(2,1)S(1)} %add.19), channel_id=1, source_target_pairs={{0,7},{1,0},{2,1},{3,2},{4,3},{5,4},{6,5},{7,6},{8,9},{9,10},{10,1... | collective-permute-start | bytes 786440 | tf_op jit(solution)/shard_map/ppermute | solution.py:231
  44.6 6.5 %collective-permute-start.17 = (bf16[256,512]{1,0:T(8,128)(2,1)S(1)}, bf16[256,512]{1,0:T(8,128)(2,1)S(1)}, u32[]{:S(2)}, u32[]{:S(2)}) collective-permute-start(bf16[256,512]{1,0:T(8,128)(2,1)S(1)} %add.22), channel_id=1, source_target_pairs={{0,7},{1,0},{2,1},{3,2},{4,3},{5,4},{6,5},{7,6},{8,9},{9,10},{10,1... | collective-permute-start | bytes 786440 | tf_op jit(solution)/shard_map/ppermute | solution.py:231
  48.4 6.5 %collective-permute-start.12 = (bf16[256,512]{1,0:T(8,128)(2,1)S(1)}, bf16[256,512]{1,0:T(8,128)(2,1)S(1)}, u32[]{:S(2)}, u32[]{:S(2)}) collective-permute-start(bf16[256,512]{1,0:T(8,128)(2,1)S(1)} %add.20), channel_id=1, source_target_pairs={{0,7},{1,0},{2,1},{3,2},{4,3},{5,4},{6,5},{7,6},{8,9},{9,10},{10,1... | collective-permute-start | bytes 786440 | tf_op jit(solution)/shard_map/ppermute | solution.py:231
  51.2 6.5 %collective-permute-start.18 = (bf16[256,512]{1,0:T(8,128)(2,1)S(1)}, bf16[256,512]{1,0:T(8,128)(2,1)S(1)}, u32[]{:S(2)}, u32[]{:S(2)}) collective-permute-start(bf16[256,512]{1,0:T(8,128)(2,1)S(1)} %add.23), channel_id=1, source_target_pairs={{0,7},{1,0},{2,1},{3,2},{4,3},{5,4},{6,5},{7,6},{8,9},{9,10},{10,1... | collective-permute-start | bytes 786440 | tf_op jit(solution)/shard_map/ppermute | solution.py:231
  54.9 4.9 %collective-permute-start.13 = (bf16[128,512]{1,0:T(8,128)(2,1)S(1)}, bf16[128,512]{1,0:T(8,128)(2,1)S(1)}, u32[]{:S(2)}, u32[]{:S(2)}) collective-permute-start(bf16[128,512]{1,0:T(8,128)(2,1)S(1)} %slice.24), channel_id=1, source_target_pairs={{0,8},{8,0},{16,24},{24,16},{32,40},{40,32},{48,56},{56,48},{64,72... | collective-permute-start | bytes 393224 | tf_op jit(solution)/shard_map/ppermute | solution.py:215
  57.7 3.0 %collective-permute-start.19 = (bf16[128,512]{1,0:T(8,128)(2,1)S(1)}, bf16[128,512]{1,0:T(8,128)(2,1)S(1)}, u32[]{:S(2)}, u32[]{:S(2)}) collective-permute-start(bf16[128,512]{1,0:T(8,128)(2,1)S(1)} %slice.25), channel_id=1, source_target_pairs={{0,8},{8,0},{16,24},{24,16},{32,40},{40,32},{48,56},{56,48},{64,72... | collective-permute-start | bytes 393224 | tf_op jit(solution)/shard_map/ppermute | solution.py:215

commit v5 on v4

--- a/solution.py
+++ b/solution.py
@@ -40,8 +40,7 @@
 
 def pack_kernel(key_values, ids, message):
     message[0:TOK, :] = key_values[...]
-    row = jnp.broadcast_to(ids[...].astype(F32), (PIECE - TOK, TOK))
-    message[TOK:PIECE, :] = row.astype(BF16)
+    message[TOK:PIECE, :] = jnp.broadcast_to(ids[...], (PIECE - TOK, TOK)).astype(BF16)
 
 
 def column_kernel(message, again, column):
@@ -121,6 +120,45 @@
         find_scores(query_rows, ids, part, [(0, piece)], scores, peak, part * HEADS * PART)
 
 
+def weigh(part, step, scored, folded):
+    given = pl.ds(part * HEADS * PART + step * STEP, STEP)
+    within = pl.ds(step * STEP, STEP)
+    top, blocks = None, []
+    for scores, peak, values in scored:
+        rows = given if scores.shape[0] == ROWS else within
+        best = peak[rows, :]
+        top = best if top is None else jnp.maximum(top, best)
+        blocks.append((scores, rows, values))
+    top = jnp.broadcast_to(jnp.max(top, axis=1, keepdims=True), (STEP, HD))
+    total = None
+    if folded is not None:
+        old = folded[0][given, :]
+        top = jnp.maximum(top, old)
+        shrink = jnp.exp((old - top) * SCALE)
+        total = folded[1][given, :] * jnp.concatenate([shrink, shrink], axis=1)
+    for scores, rows, values in blocks:
+        wide = jnp.concatenate([top] * (scores.shape[1] // HD), axis=1)
+        probs = jnp.exp((scores[rows, :] - wide) * SCALE).astype(BF16)
+        added = jnp.dot(probs, values[...], preferred_element_type=F32)
+        total = added if total is None else total + added
+    return top, total
+
+
+def fold_kernel(backs, early, query_rows, ids, *refs):
+    pieces = list(zip(backs, refs[: len(backs)]))
+    refs = refs[len(backs) :]
+    kept = [refs[3 * at : 3 * at + 3] for at in range(early)]
+    tops, sums, scores, peak, values = refs[3 * early :]
+    keep_values(pieces, values)
+    for part in range(TOK // PART):
+        find_scores(query_rows, ids, part, pieces, scores, peak, 0)
+        for step in range(HEADS * PART // STEP):
+            rows = pl.ds(part * HEADS * PART + step * STEP, STEP)
+            top, total = weigh(part, step, kept + [(scores, peak, values)], None)
+            tops[rows, :] = top
+            sums[rows, :] = total
+
+
 def more_kernel(backs, query_rows, ids, *refs):
     pieces = list(zip(backs, refs[: len(backs)]))
     scores, peak, values = refs[len(backs) :]
@@ -133,22 +171,11 @@
     pieces = list(zip(backs, refs[: len(backs)]))
     refs = refs[len(backs) :]
     kept = [refs[3 * at : 3 * at + 3] for at in range(early)]
-    weight, attention, product, scores, peak, values = refs[3 * early :]
+    tops, sums, weight, attention, product, scores, peak, values = refs[3 * early :]
     keep_values(pieces, values)
     find_scores(query_rows, ids, part, pieces, scores, peak, 0)
     for step in range(HEADS * PART // STEP):
-        rows = pl.ds(step * STEP, STEP)
-        given = pl.ds(part * HEADS * PART + step * STEP, STEP)
-        top = peak[rows, :]
-        for _, other, _ in kept:
-            top = jnp.maximum(top, other[given, :])
-        top = jnp.broadcast_to(jnp.max(top, axis=1, keepdims=True), (STEP, HD))
-        total = None
-        for block, keys in [(s[given, :], v) for s, _, v in kept] + [(scores[rows, :], values)]:
-            wide = jnp.concatenate([top] * (block.shape[1] // HD), axis=1)
-            probs = jnp.exp((block - wide) * SCALE).astype(BF16)
-            added = jnp.dot(probs, keys[...], preferred_element_type=F32)
-            total = added if total is None else total + added
+        _, total = weigh(part, step, kept + [(scores, peak, values)], (tops, sums))
         share = (total[:, :HD] / total[:, HD:]).astype(BF16)
         for at in range(STEP // PART):
             head = step * (STEP // PART) + at
@@ -177,7 +204,7 @@
     out = refs[-1]
     for part in range(TOK // PART):
         mine, moved, other = refs[3 * part : 3 * part + 3]
-        total = mine[...].astype(F32) + moved[0:PART, :].astype(F32) + other[...].astype(F32)
+        total = mine[...].astype(F32) + moved[...].astype(F32) + other[...].astype(F32)
         out[pl.ds(part * PART, PART), :] = total.astype(BF16)
 
 
@@ -222,64 +249,71 @@
         pairs = [(i, i // ROW * ROW + (i + 2 * steps) % ROW) for i in range(stretches)]
         return lax.ppermute(value, "loop", pairs)
 
-    def along(value):
+    def along(value, swap=0):
         pairs = []
         for loop in range(stretches):
             step = 1 if loop % 2 else ring - 1
             for z in range(ring):
-                pairs.append((loop * ring + z, loop * ring + (z + step) % ring))
+                pairs.append((loop * ring + z, (loop ^ swap) * ring + (z + step) % ring))
         return lax.ppermute(value, ("loop", "tp"), pairs)
 
     piece = shape(PIECE, TOK)
     column = shape(TOK, 1, F32)
-    own = call(pack_kernel, "pack", 0.5, piece, key_values, prompt_ids[None, :])
+    own = call(pack_kernel, "pack", 0.05, piece, key_values, prompt_ids.astype(F32)[None, :])
     chip4 = from_chip(own, 4)
-    again, ids = call(column_kernel, "column", 0.3, [piece, column], own)
+    again, ids = call(column_kernel, "column", 0.05, [piece, column], own)
     chip1, chip2 = from_chip(again, 1), from_chip(again, 2)
     query_rows, *kept = call(
-        own_kernel, "own_scores", 1.5, [shape(ROWS, HD)] + kept_shapes(1), queries, ids, again
+        own_kernel, "own_scores", 0.1, [shape(ROWS, HD)] + kept_shapes(1), queries, ids, again
     )
     (chip4, kept) = lax.optimization_barrier((chip4, kept))
     relayed, beside, ids = call(
-        pick_kernel, "pick", 0.3, [piece, piece, column], again, chip4, ids
-    )
-    (chip1, ids) = lax.optimization_barrier((chip1, ids))
+        pick_kernel, "pick", 0.05, [piece, piece, column], again, chip4, ids
+    )
     chip3 = along_row(relayed, 3)
     beside = to_mate(beside)
+    mate1 = to_mate(chip1)
     (chip2, beside) = lax.optimization_barrier((chip2, beside))
-    mate1, mate2, mate3 = to_mate(chip1), to_mate(chip2), to_mate(chip3)
-    (mate2, chip3) = lax.optimization_barrier((mate2, chip3))
-    pieces = [(4, chip4), (BESIDE, beside), (1, chip1), (1, mate1), (2, chip2), (2, mate2)]
-    more = call(
-        functools.partial(more_kernel, [item[0] for item in pieces]),
-        "more_scores",
-        3,
-        kept_shapes(len(pieces)),
+    mate2 = to_mate(chip2)
+    pieces = [(4, chip4), (BESIDE, beside), (1, chip1), (1, mate1)]
+    state = call(
+        functools.partial(fold_kernel, [item[0] for item in pieces], 1),
+        "fold",
+        0.01,
+        [shape(ROWS, HD, F32), shape(ROWS, 2 * HD, F32)],
         query_rows,
         ids,
         *[item[1] for item in pieces],
-    )
-    (mate3, more) = lax.optimization_barrier((mate3, more))
-    kept = list(kept) + list(more)
+        *kept,
+        scratch=later(4),
+    )
+    (chip3, state) = lax.optimization_barrier((chip3, state))
+    mate3 = to_mate(chip3)
+    pieces = [(2, chip2), (2, mate2), (3, chip3)]
+    kept = call(
+        functools.partial(more_kernel, [item[0] for item in pieces]),
+        "more_scores",
+        0.7,
+        kept_shapes(3),
+        query_rows,
+        ids,
+        *[item[1] for item in pieces],
+    )
 
     ends = []
     for part in range(TOK // PART):
         attention, product = call(
-            functools.partial(last_kernel, part, [3, 3], len(kept) // 3),
+            functools.partial(last_kernel, part, [3], 1),
             "attend",
             0.01,
             [shape(PART, HEADS * HD), shape(PART, CHUNK)],
             query_rows,
             ids,
-            chip3,
             mate3,
             *kept,
+            *state,
             out_weight,
-            scratch=[
-                pltpu.VMEM((HEADS * PART, 2 * TOK), F32),
-                pltpu.VMEM((HEADS * PART, HD), F32),
-                pltpu.VMEM((2 * TOK, 2 * HD), BF16),
-            ],
+            scratch=later(1),
         )
         extra = along(product)
         wide = shape(2 * PART, CHUNK)
@@ -294,9 +328,17 @@
         )
         moved = along(jnp.concatenate([one[:PART] + extra, one[PART:]], axis=0))
         moved = along(two + moved)
-        moved = along(three + moved)
-        ends += [mine, moved, to_mate(moved[PART:])]
+        ends += [mine, along(three[:PART] + moved[:PART])]
+        ends += [along(three[PART:] + moved[PART:], swap=1)]
     return call(finish_kernel, "finish", 0.5, shape(TOK, CHUNK), *ends)
+
+
+def later(count):
+    return [
+        pltpu.VMEM((HEADS * PART, count * TOK), F32),
+        pltpu.VMEM((HEADS * PART, HD), F32),
+        pltpu.VMEM((count * TOK, 2 * HD), BF16),
+    ]
 
 
 def solution(mesh):

time: 61.8 us -> 62.3 us (level)
  Pallas kernels: 10.1 us -> 11.6 us
  starting transfers between devices: 24.9 us -> 23.7 us
  other arithmetic: 0.36 us -> 1.11 us
  local copies, waits for them, and re-layouts: 2.82 us -> 2.07 us
    ppermute x8 -> x10, starting transfers between devices: 4.69 us -> 7.27 us  [along(): return lax.ppermute(value, ('loop', 'tp'), pairs)]
    ppermute x1, starting transfers between devices: 2.31 us -> 0.01 us  [along_row(): return lax.ppermute(value, 'loop', pairs)]
    ppermute x8 -> x6, starting transfers between devices: 12.4 us -> 10.3 us  [to_mate(): return lax.ppermute(value, 'loop', [(i, i ^ 1) for i in range(stretches)])]
    pallas_call x10 -> x11, Pallas kernels: 10.1 us -> 11.6 us  [call(): pl.pallas_call(kernel, out_shape=outs, in_specs=[VMEM] * len(args), out_s...]
    ppermute x8 -> x10, waiting for transfers between devices: 18.1 us -> 19.1 us  [along(): return lax.ppermute(value, ('loop', 'tp'), pairs)]
    ppermute x8 -> x6, waiting for transfers between devices: 1.84 us -> 0.9 us  [to_mate(): return lax.ppermute(value, 'loop', [(i, i ^ 1) for i in range(stretches)])]
    convert_element_type x0 -> x1, other arithmetic: none -> 0.83 us  [per_device(): prompt_ids.astype(F32)[None, :]]
    unnamed x10 -> x6, local copies, waits for them, and re-layouts: 2.8 us -> 2.07 us
  transfers between devices with their start and end apart: 20 -> 20, of which waited for: 10 -> 10; matrix products, arithmetic and copies ran while one was open for 1% -> 0% of each run, Pallas kernels for 11% -> 15%
where the time goes in v5:
time: 62.3 us; the launch traced here: 62.2 us
  starting transfers between devices  23.7 us (38%)
  waiting for transfers between devices  23.5 us (38%)
  Pallas kernels  11.6 us (19%)
  local copies, waits for them, and re-layouts  2.07 us (3%)
  other arithmetic  1.11 us (2%)
    ppermute x10, waiting for transfers between devices, along(): return lax.ppermute(value, ('loop', 'tp'), pairs)  19.1 us
    pallas_call x11, Pallas kernels, call(): pl.pallas_call(kernel, out_shape=outs, in_specs=[VMEM] * len(args), out_s...  11.6 us
    ppermute x6, starting transfers between devices, to_mate(): return lax.ppermute(value, 'loop', [(i, i ^ 1) for i in range(stretches)])  10.3 us
    ppermute x10, starting transfers between devices, along(): return lax.ppermute(value, ('loop', 'tp'), pairs)  7.27 us
    ppermute x3, starting transfers between devices, from_chip(): return lax.ppermute(value, 'loop', pairs)  6.11 us
    ppermute x3, waiting for transfers between devices, from_chip(): return lax.ppermute(value, 'loop', pairs)  2.99 us
    unnamed x6, local copies, waits for them, and re-layouts  2.07 us
  transfers between devices with their start and end apart: 20, of which 10 were waited for; matrix products, arithmetic and copies ran while one was open for 0% of the time, Pallas kernels for 15%

profile of v5, /device:TPU:1, one launch (start us, length us, event | category | flops | bytes accessed | tf_op | source)
XLA Modules:
  0.0 62.2 jit_solution(9582189528780396528)
XLA Ops:
  0.0 0.8 %convert_element_type.3 = f32[256]{0:T(256)S(1)} convert(s32[256]{0:T(256)} %param.6) | non-fusion elementwise | flops 256 | bytes 2048 | tf_op jit(solution)/shard_map/convert_element_type | solution.py:262
  0.8 1.0 %copy-done.2 = bf16[256,256]{1,0:T(8,128)(2,1)S(1)} copy-done((bf16[256,256]{1,0:T(8,128)(2,1)S(1)}, bf16[256,256]{1,0:T(8,128)(2,1)}, u32[]{:S(2)}) %copy-start.2) | copy-done | bytes 131096
  1.9 2.1 %collective-permute-start = (bf16[272,256]{1,0:T(8,128)(2,1)S(1)}, bf16[272,256]{1,0:T(8,128)(2,1)S(1)}, u32[]{:S(2)}, u32[]{:S(2)}) collective-permute-start(bf16[272,256]{1,0:T(8,128)(2,1)S(1)} %pack.1.message), channel_id=1, source_target_pairs={{0,64},{8,72},{16,80},{24,88},{32,96},{40,104},{48,112},{56,120},{... | collective-permute-start | bytes 417800 | tf_op jit(solution)/shard_map/ppermute | solution.py:246
  4.1 1.4 %collective-permute-start.4 = (bf16[272,256]{1,0:T(8,128)(2,1)S(1)}, bf16[272,256]{1,0:T(8,128)(2,1)S(1)}, u32[]{:S(2)}, u32[]{:S(2)}) collective-permute-start(bf16[272,256]{1,0:T(8,128)(2,1)S(1)} %get-tuple-element.41.piece.own), channel_id=1, source_target_pairs={{0,16},{8,24},{16,32},{24,40},{32,48},{40,56},{48,64},{56,72},{64,... | collective-permute-start | bytes 417800 | tf_op jit(solution)/shard_map/ppermute | solution.py:246
  5.5 2.6 %collective-permute-start.2 = (bf16[272,256]{1,0:T(8,128)(2,1)S(1)}, bf16[272,256]{1,0:T(8,128)(2,1)S(1)}, u32[]{:S(2)}, u32[]{:S(2)}) collective-permute-start(bf16[272,256]{1,0:T(8,128)(2,1)S(1)} %get-tuple-element.41.piece.own), channel_id=1, source_target_pairs={{0,32},{8,40},{16,48},{24,56},{32,64},{40,72},{48,80},{56,88},{64,... | collective-permute-start | bytes 417800 | tf_op jit(solution)/shard_map/ppermute | solution.py:246
  8.1 1.0 %copy-done.1 = bf16[256,1024]{1,0:T(8,128)(2,1)S(1)} copy-done((bf16[256,1024]{1,0:T(8,128)(2,1)S(1)}, bf16[256,1024]{1,0:T(8,128)(2,1)}, u32[]{:S(2)}) %copy-start.1) | copy-done | bytes 524312
  9.7 1.9 %collective-permute-start.3 = (bf16[272,256]{1,0:T(8,128)(2,1)S(1)}, bf16[272,256]{1,0:T(8,128)(2,1)S(1)}, u32[]{:S(2)}, u32[]{:S(2)}) collective-permute-start(bf16[272,256]{1,0:T(8,128)(2,1)S(1)} %get-tuple-element.49), channel_id=1, source_target_pairs={{0,8},{8,0},{16,24},{24,16},{32,40},{40,32},{48,56},{56,48},{64,72... | collective-permute-start | bytes 417800 | tf_op jit(solution)/shard_map/ppermute | solution.py:242
  11.6 3.0 %collective-permute-done.4.refs_2_ = bf16[272,256]{1,0:T(8,128)(2,1)S(1)} collective-permute-done((bf16[272,256]{1,0:T(8,128)(2,1)S(1)}, bf16[272,256]{1,0:T(8,128)(2,1)S(1)}, u32[]{:S(2)}, u32[]{:S(2)}) %collective-permute-start.4) | collective-permute-done | bytes 139296 | tf_op jit(solution)/shard_map/ppermute | solution.py:246
  14.6 3.2 %collective-permute-start.5 = (bf16[272,256]{1,0:T(8,128)(2,1)S(1)}, bf16[272,256]{1,0:T(8,128)(2,1)S(1)}, u32[]{:S(2)}, u32[]{:S(2)}) collective-permute-start(bf16[272,256]{1,0:T(8,128)(2,1)S(1)} %collective-permute-done.4.refs_2_), channel_id=1, source_target_pairs={{0,8},{8,0},{16,24},{24,16},{32,40},{40,32},{48,56},{56,48},{64,72... | collective-permute-start | bytes 417800 | tf_op jit(solution)/shard_map/ppermute | solution.py:242
  17.9 0.9 %collective-permute-done.5.refs_3_ = bf16[272,256]{1,0:T(8,128)(2,1)S(1)} collective-permute-done((bf16[272,256]{1,0:T(8,128)(2,1)S(1)}, bf16[272,256]{1,0:T(8,128)(2,1)S(1)}, u32[]{:S(2)}, u32[]{:S(2)}) %collective-permute-start.5) | collective-permute-done | bytes 139296 | tf_op jit(solution)/shard_map/ppermute | solution.py:242
  18.8 3.8 %fold.1 = (f32[2048,128]{1,0:T(8,128)S(1)}, f32[2048,256]{1,0:T(8,128)S(1)}) custom-call(bf16[2048,128]{1,0:T(8,128)(2,1)S(1)} %get-tuple-element.42.query_rows, f32[256,1]{1,0:T(8,128)S(1)} %get-tuple-element.47.ids, bf16[272,256]{1,0:T(8,128)(2,1)S(1)} %collective-permute-done.far.refs_0_, bf16[272,256]{1,0:T(8,128)(2,1)S(1)} %collective-permute-done.3.refs_1_, ...), custom_call_target="tpu_custom_call" | custom-call | flops 10000000 | bytes 1024 | tf_op jit(solution)/shard_map/fold/pallas_call | solution.py:220
  23.1 0.8 %collective-permute-start.6 = (bf16[272,256]{1,0:T(8,128)(2,1)S(1)}, bf16[272,256]{1,0:T(8,128)(2,1)S(1)}, u32[]{:S(2)}, u32[]{:S(2)}) collective-permute-start(bf16[272,256]{1,0:T(8,128)(2,1)S(1)} %collective-permute-done.1.refs_2_), channel_id=1, source_target_pairs={{0,8},{8,0},{16,24},{24,16},{32,40},{40,32},{48,56},{56,48},{64,72... | collective-permute-start | bytes 417800 | tf_op jit(solution)/shard_map/ppermute | solution.py:242
  23.9 1.0 %more_scores.1 = (f32[2048,768]{1,0:T(8,128)S(1)}, f32[2048,128]{1,0:T(8,128)S(1)}, bf16[768,256]{1,0:T(8,128)(2,1)S(1)}) custom-call(bf16[2048,128]{1,0:T(8,128)(2,1)S(1)} %get-tuple-element.42.query_rows, f32[256,1]{1,0:T(8,128)S(1)} %get-tuple-element.47.ids, bf16[272,256]{1,0:T(8,128)(2,1)S(1)} %collective-permute-done.2.refs_0_, ...), custom_call_target="tpu_custom_call" | custom-call | flops 700000000 | bytes 1024 | tf_op jit(solution)/shard_map/more_scores/pallas_call | solution.py:220
  25.0 1.5 %attend.2 = (bf16[128,1024]{1,0:T(8,128)(2,1)S(1)}, bf16[128,512]{1,0:T(8,128)(2,1)S(1)}) custom-call(bf16[2048,128]{1,0:T(8,128)(2,1)S(1)} %get-tuple-element.42.query_rows, f32[256,1]{1,0:T(8,128)S(1)} %get-tuple-element.47.ids, bf16[272,256]{1,0:T(8,128)(2,1)S(1)} %collective-permute-done.6.refs_0_, f32[2048,768]{1,0:T(8,128)S(1)} %get-tuple-element.58.refs_1_, ...), custom_call_target="tpu_custom_call" | custom-call | flops 10000000 | bytes 1024 | tf_op jit(solution)/shard_map/attend/pallas_call | solution.py:220
  27.0 1.6 %collective-permute-start.9 = (bf16[128,512]{1,0:T(8,128)(2,1)S(1)}, bf16[128,512]{1,0:T(8,128)(2,1)S(1)}, u32[]{:S(2)}, u32[]{:S(2)}) collective-permute-start(bf16[128,512]{1,0:T(8,128)(2,1)S(1)} %get-tuple-element.68), channel_id=1, source_target_pairs={{0,7},{1,0},{2,1},{3,2},{4,3},{5,4},{6,5},{7,6},{8,9},{9,10},{10,1... | collective-permute-start | bytes 393224 | tf_op jit(solution)/shard_map/ppermute | solution.py:258
  28.6 1.5 %attend.3 = (bf16[128,1024]{1,0:T(8,128)(2,1)S(1)}, bf16[128,512]{1,0:T(8,128)(2,1)S(1)}) custom-call(bf16[2048,128]{1,0:T(8,128)(2,1)S(1)} %get-tuple-element.42.query_rows, f32[256,1]{1,0:T(8,128)S(1)} %get-tuple-element.47.ids, bf16[272,256]{1,0:T(8,128)(2,1)S(1)} %collective-permute-done.6.refs_0_, f32[2048,768]{1,0:T(8,128)S(1)} %get-tuple-element.58.refs_1_, ...), custom_call_target="tpu_custom_call" | custom-call | flops 10000000 | bytes 1024 | tf_op jit(solution)/shard_map/attend/pallas_call | solution.py:220
  30.2 1.7 %collective-permute-start.15 = (bf16[128,512]{1,0:T(8,128)(2,1)S(1)}, bf16[128,512]{1,0:T(8,128)(2,1)S(1)}, u32[]{:S(2)}, u32[]{:S(2)}) collective-permute-start(bf16[128,512]{1,0:T(8,128)(2,1)S(1)} %get-tuple-element.74), channel_id=1, source_target_pairs={{0,7},{1,0},{2,1},{3,2},{4,3},{5,4},{6,5},{7,6},{8,9},{9,10},{10,1... | collective-permute-start | bytes 393224 | tf_op jit(solution)/shard_map/ppermute | solution.py:258
  31.9 3.8 %collective-permute-start.14 = (bf16[128,1024]{1,0:T(8,128)(2,1)S(1)}, bf16[128,1024]{1,0:T(8,128)(2,1)S(1)}, u32[]{:S(2)}, u32[]{:S(2)}) collective-permute-start(bf16[128,1024]{1,0:T(8,128)(2,1)S(1)} %get-tuple-element.69.own), channel_id=1, source_target_pairs={{0,8},{8,0},{16,24},{24,16},{32,40},{40,32},{48,56},{56,48},{64,72... | collective-permute-start | bytes 786440 | tf_op jit(solution)/shard_map/ppermute | solution.py:242
  35.7 1.1 %project.2 = (bf16[256,512]{1,0:T(8,128)(2,1)S(1)}, bf16[256,512]{1,0:T(8,128)(2,1)S(1)}, bf16[256,512]{1,0:T(8,128)(2,1)S(1)}, bf16[128,512]{1,0:T(8,128)(2,1)S(1)}) custom-call(bf16[128,1024]{1,0:T(8,128)(2,1)S(1)} %get-tuple-element.63.own, bf16[128,1024]{1,0:T(8,128)(2,1)S(1)} %collective-permute-done.8.mate, bf16[1024,4096]{1,0:T(8,128)(2,1)S(1)} %copy-done), custom_call_target="tpu_custom_call" | custom-call | flops 10000000 | bytes 1024 | tf_op jit(solution)/shard_map/project/pallas_call | solution.py:220
  36.9 0.8 %collective-permute-start.10 = (bf16[256,512]{1,0:T(8,128)(2,1)S(1)}, bf16[256,512]{1,0:T(8,128)(2,1)S(1)}, u32[]{:S(2)}, u32[]{:S(2)}) collective-permute-start(bf16[256,512]{1,0:T(8,128)(2,1)S(1)} %pad_maximum_fusion), channel_id=1, source_target_pairs={{0,7},{1,0},{2,1},{3,2},{4,3},{5,4},{6,5},{7,6},{8,9},{9,10},{10,1... | collective-permute-start | bytes 786440 | tf_op jit(solution)/shard_map/ppermute | solution.py:258
  37.7 1.1 %project.3 = (bf16[256,512]{1,0:T(8,128)(2,1)S(1)}, bf16[256,512]{1,0:T(8,128)(2,1)S(1)}, bf16[256,512]{1,0:T(8,128)(2,1)S(1)}, bf16[128,512]{1,0:T(8,128)(2,1)S(1)}) custom-call(bf16[128,1024]{1,0:T(8,128)(2,1)S(1)} %get-tuple-element.69.own, bf16[128,1024]{1,0:T(8,128)(2,1)S(1)} %collective-permute-done.14.mate, bf16[1024,4096]{1,0:T(8,128)(2,1)S(1)} %copy-done), custom_call_target="tpu_custom_call" | custom-call | flops 10000000 | bytes 1024 | tf_op jit(solution)/shard_map/project/pallas_call | solution.py:220
  39.0 4.4 %collective-permute-done.10 = bf16[256,512]{1,0:T(8,128)(2,1)S(1)} collective-permute-done((bf16[256,512]{1,0:T(8,128)(2,1)S(1)}, bf16[256,512]{1,0:T(8,128)(2,1)S(1)}, u32[]{:S(2)}, u32[]{:S(2)}) %collective-permute-start.10) | collective-permute-done | bytes 262176 | tf_op jit(solution)/shard_map/ppermute | solution.py:258
  43.6 2.6 %collective-permute-done.16 = bf16[256,512]{1,0:T(8,128)(2,1)S(1)} collective-permute-done((bf16[256,512]{1,0:T(8,128)(2,1)S(1)}, bf16[256,512]{1,0:T(8,128)(2,1)S(1)}, u32[]{:S(2)}, u32[]{:S(2)}) %collective-permute-start.16) | collective-permute-done | bytes 262176 | tf_op jit(solution)/shard_map/ppermute | solution.py:258
  46.4 3.6 %collective-permute-done.11 = bf16[256,512]{1,0:T(8,128)(2,1)S(1)} collective-permute-done((bf16[256,512]{1,0:T(8,128)(2,1)S(1)}, bf16[256,512]{1,0:T(8,128)(2,1)S(1)}, u32[]{:S(2)}, u32[]{:S(2)}) %collective-permute-start.11) | collective-permute-done | bytes 262176 | tf_op jit(solution)/shard_map/ppermute | solution.py:258
  50.0 0.6 collective-permute-start.13
  50.6 0.6 %collective-permute-start.12 = (bf16[128,512]{1,0:T(8,128)(2,1)S(1)}, bf16[128,512]{1,0:T(8,128)(2,1)S(1)}, u32[]{:S(2)}, u32[]{:S(2)}) collective-permute-start(bf16[128,512]{1,0:T(8,128)(2,1)S(1)} %get-tuple-element.78), channel_id=1, source_target_pairs={{0,7},{1,0},{2,1},{3,2},{4,3},{5,4},{6,5},{7,6},{8,9},{9,10},{10,1... | collective-permute-start | bytes 393224 | tf_op jit(solution)/shard_map/ppermute | solution.py:258
  51.3 1.5 %collective-permute-done.17 = bf16[256,512]{1,0:T(8,128)(2,1)S(1)} collective-permute-done((bf16[256,512]{1,0:T(8,128)(2,1)S(1)}, bf16[256,512]{1,0:T(8,128)(2,1)S(1)}, u32[]{:S(2)}, u32[]{:S(2)}) %collective-permute-start.17) | collective-permute-done | bytes 262176 | tf_op jit(solution)/shard_map/ppermute | solution.py:258
  52.8 0.6 collective-permute-start.19
  53.4 1.0 %collective-permute-start.18 = (bf16[128,512]{1,0:T(8,128)(2,1)S(1)}, bf16[128,512]{1,0:T(8,128)(2,1)S(1)}, u32[]{:S(2)}, u32[]{:S(2)}) collective-permute-start(bf16[128,512]{1,0:T(8,128)(2,1)S(1)} %get-tuple-element.76), channel_id=1, source_target_pairs={{0,7},{1,0},{2,1},{3,2},{4,3},{5,4},{6,5},{7,6},{8,9},{9,10},{10,1... | collective-permute-start | bytes 393224 | tf_op jit(solution)/shard_map/ppermute | solution.py:258
  54.5 3.0 %collective-permute-done.12.refs_1_ = bf16[128,512]{1,0:T(8,128)(2,1)S(1)} collective-permute-done((bf16[128,512]{1,0:T(8,128)(2,1)S(1)}, bf16[128,512]{1,0:T(8,128)(2,1)S(1)}, u32[]{:S(2)}, u32[]{:S(2)}) %collective-permute-start.12) | collective-permute-done | bytes 131104 | tf_op jit(solution)/shard_map/ppermute | solution.py:258
  57.5 3.9 %collective-permute-done.18.refs_4_ = bf16[128,512]{1,0:T(8,128)(2,1)S(1)} collective-permute-done((bf16[128,512]{1,0:T(8,128)(2,1)S(1)}, bf16[128,512]{1,0:T(8,128)(2,1)S(1)}, u32[]{:S(2)}, u32[]{:S(2)}) %collective-permute-start.18) | collective-permute-done | bytes 131104 | tf_op jit(solution)/shard_map/ppermute | solution.py:258
  61.4 0.8 %finish.1 = bf16[256,512]{1,0:T(8,128)(2,1)} custom-call(bf16[128,512]{1,0:T(8,128)(2,1)S(1)} %get-tuple-element.64.refs_0_, bf16[128,512]{1,0:T(8,128)(2,1)S(1)} %collective-permute-done.12.refs_1_, bf16[128,512]{1,0:T(8,128)(2,1)S(1)} %collective-permute-done.13.refs_2_, bf16[128,512]{1,0:T(8,128)(2,1)S(1)} %get-tuple-element.70.refs_3_, ...), custom_call_target="tpu_custom_call" | custom-call | flops 500000000 | bytes 1024 | tf_op jit(solution)/shard_map/finish/pallas_call | solution.py:220
  (34 shorter events, 2.5 us)
Async XLA Ops:
  0.0 24.9 %copy-start = (bf16[1024,4096]{1,0:T(8,128)(2,1)S(1)}, bf16[1024,4096]{1,0:T(8,128)(2,1)}, u32[]{:S(2)}) copy-start(bf16[1024,4096]{1,0:T(8,128)(2,1)} %weight.3) | copy-start | bytes 25165828
  0.8 1.0 %copy-start.2 = (bf16[256,256]{1,0:T(8,128)(2,1)S(1)}, bf16[256,256]{1,0:T(8,128)(2,1)}, u32[]{:S(2)}) copy-start(bf16[256,256]{1,0:T(8,128)(2,1)} %key_values.1) | copy-start | bytes 393220
  1.9 7.8 %collective-permute-start = (bf16[272,256]{1,0:T(8,128)(2,1)S(1)}, bf16[272,256]{1,0:T(8,128)(2,1)S(1)}, u32[]{:S(2)}, u32[]{:S(2)}) collective-permute-start(bf16[272,256]{1,0:T(8,128)(2,1)S(1)} %pack.1.message), channel_id=1, source_target_pairs={{0,64},{8,72},{16,80},{24,88},{32,96},{40,104},{48,112},{56,120},{... | collective-permute-start | bytes 417800 | tf_op jit(solution)/shard_map/ppermute | solution.py:246
  4.1 10.5 %collective-permute-start.4 = (bf16[272,256]{1,0:T(8,128)(2,1)S(1)}, bf16[272,256]{1,0:T(8,128)(2,1)S(1)}, u32[]{:S(2)}, u32[]{:S(2)}) collective-permute-start(bf16[272,256]{1,0:T(8,128)(2,1)S(1)} %get-tuple-element.41.piece.own), channel_id=1, source_target_pairs={{0,16},{8,24},{16,32},{24,40},{32,48},{40,56},{48,64},{56,72},{64,... | collective-permute-start | bytes 417800 | tf_op jit(solution)/shard_map/ppermute | solution.py:246
  5.5 12.3 %collective-permute-start.2 = (bf16[272,256]{1,0:T(8,128)(2,1)S(1)}, bf16[272,256]{1,0:T(8,128)(2,1)S(1)}, u32[]{:S(2)}, u32[]{:S(2)}) collective-permute-start(bf16[272,256]{1,0:T(8,128)(2,1)S(1)} %get-tuple-element.41.piece.own), channel_id=1, source_target_pairs={{0,32},{8,40},{16,48},{24,56},{32,64},{40,72},{48,80},{56,88},{64,... | collective-permute-start | bytes 417800 | tf_op jit(solution)/shard_map/ppermute | solution.py:246
  8.1 1.0 %copy-start.1 = (bf16[256,1024]{1,0:T(8,128)(2,1)S(1)}, bf16[256,1024]{1,0:T(8,128)(2,1)}, u32[]{:S(2)}) copy-start(bf16[256,1024]{1,0:T(8,128)(2,1)} %queries.1) | copy-start | bytes 1572868
  9.7 8.1 %collective-permute-start.3 = (bf16[272,256]{1,0:T(8,128)(2,1)S(1)}, bf16[272,256]{1,0:T(8,128)(2,1)S(1)}, u32[]{:S(2)}, u32[]{:S(2)}) collective-permute-start(bf16[272,256]{1,0:T(8,128)(2,1)S(1)} %get-tuple-element.49), channel_id=1, source_target_pairs={{0,8},{8,0},{16,24},{24,16},{32,40},{40,32},{48,56},{56,48},{64,72... | collective-permute-start | bytes 417800 | tf_op jit(solution)/shard_map/ppermute | solution.py:242
  14.6 4.2 %collective-permute-start.5 = (bf16[272,256]{1,0:T(8,128)(2,1)S(1)}, bf16[272,256]{1,0:T(8,128)(2,1)S(1)}, u32[]{:S(2)}, u32[]{:S(2)}) collective-permute-start(bf16[272,256]{1,0:T(8,128)(2,1)S(1)} %collective-permute-done.4.refs_2_), channel_id=1, source_target_pairs={{0,8},{8,0},{16,24},{24,16},{32,40},{40,32},{48,56},{56,48},{64,72... | collective-permute-start | bytes 417800 | tf_op jit(solution)/shard_map/ppermute | solution.py:242
  17.8 5.3 %collective-permute-start.1 = (bf16[272,256]{1,0:T(8,128)(2,1)S(1)}, bf16[272,256]{1,0:T(8,128)(2,1)S(1)}, u32[]{:S(2)}, u32[]{:S(2)}) collective-permute-start(bf16[272,256]{1,0:T(8,128)(2,1)S(1)} %get-tuple-element.48), channel_id=1, source_target_pairs={{0,48},{8,56},{16,0},{24,8},{32,16},{40,24},{48,32},{56,40},{64,11... | collective-permute-start | bytes 417800 | tf_op jit(solution)/shard_map/ppermute | solution.py:250
  17.8 6.1 %collective-permute-start.7 = (bf16[272,256]{1,0:T(8,128)(2,1)S(1)}, bf16[272,256]{1,0:T(8,128)(2,1)S(1)}, u32[]{:S(2)}, u32[]{:S(2)}) collective-permute-start(bf16[272,256]{1,0:T(8,128)(2,1)S(1)} %collective-permute-done.2.refs_0_), channel_id=1, source_target_pairs={{0,8},{8,0},{16,24},{24,16},{32,40},{40,32},{48,56},{56,48},{64,72... | collective-permute-start | bytes 417800 | tf_op jit(solution)/shard_map/ppermute | solution.py:242
  23.1 1.8 %collective-permute-start.6 = (bf16[272,256]{1,0:T(8,128)(2,1)S(1)}, bf16[272,256]{1,0:T(8,128)(2,1)S(1)}, u32[]{:S(2)}, u32[]{:S(2)}) collective-permute-start(bf16[272,256]{1,0:T(8,128)(2,1)S(1)} %collective-permute-done.1.refs_2_), channel_id=1, source_target_pairs={{0,8},{8,0},{16,24},{24,16},{32,40},{40,32},{48,56},{56,48},{64,72... | collective-permute-start | bytes 417800 | tf_op jit(solution)/shard_map/ppermute | solution.py:242
  26.5 9.2 %collective-permute-start.8 = (bf16[128,1024]{1,0:T(8,128)(2,1)S(1)}, bf16[128,1024]{1,0:T(8,128)(2,1)S(1)}, u32[]{:S(2)}, u32[]{:S(2)}) collective-permute-start(bf16[128,1024]{1,0:T(8,128)(2,1)S(1)} %get-tuple-element.63.own), channel_id=1, source_target_pairs={{0,8},{8,0},{16,24},{24,16},{32,40},{40,32},{48,56},{56,48},{64,72... | collective-permute-start | bytes 786440 | tf_op jit(solution)/shard_map/ppermute | solution.py:242
  27.0 9.8 %collective-permute-start.9 = (bf16[128,512]{1,0:T(8,128)(2,1)S(1)}, bf16[128,512]{1,0:T(8,128)(2,1)S(1)}, u32[]{:S(2)}, u32[]{:S(2)}) collective-permute-start(bf16[128,512]{1,0:T(8,128)(2,1)S(1)} %get-tuple-element.68), channel_id=1, source_target_pairs={{0,7},{1,0},{2,1},{3,2},{4,3},{5,4},{6,5},{7,6},{8,9},{9,10},{10,1... | collective-permute-start | bytes 393224 | tf_op jit(solution)/shard_map/ppermute | solution.py:258
  30.2 8.7 %collective-permute-start.15 = (bf16[128,512]{1,0:T(8,128)(2,1)S(1)}, bf16[128,512]{1,0:T(8,128)(2,1)S(1)}, u32[]{:S(2)}, u32[]{:S(2)}) collective-permute-start(bf16[128,512]{1,0:T(8,128)(2,1)S(1)} %get-tuple-element.74), channel_id=1, source_target_pairs={{0,7},{1,0},{2,1},{3,2},{4,3},{5,4},{6,5},{7,6},{8,9},{9,10},{10,1... | collective-permute-start | bytes 393224 | tf_op jit(solution)/shard_map/ppermute | solution.py:258
  31.9 5.8 %collective-permute-start.14 = (bf16[128,1024]{1,0:T(8,128)(2,1)S(1)}, bf16[128,1024]{1,0:T(8,128)(2,1)S(1)}, u32[]{:S(2)}, u32[]{:S(2)}) collective-permute-start(bf16[128,1024]{1,0:T(8,128)(2,1)S(1)} %get-tuple-element.69.own), channel_id=1, source_target_pairs={{0,8},{8,0},{16,24},{24,16},{32,40},{40,32},{48,56},{56,48},{64,72... | collective-permute-start | bytes 786440 | tf_op jit(solution)/shard_map/ppermute | solution.py:242
  36.9 6.5 %collective-permute-start.10 = (bf16[256,512]{1,0:T(8,128)(2,1)S(1)}, bf16[256,512]{1,0:T(8,128)(2,1)S(1)}, u32[]{:S(2)}, u32[]{:S(2)}) collective-permute-start(bf16[256,512]{1,0:T(8,128)(2,1)S(1)} %pad_maximum_fusion), channel_id=1, source_target_pairs={{0,7},{1,0},{2,1},{3,2},{4,3},{5,4},{6,5},{7,6},{8,9},{9,10},{10,1... | collective-permute-start | bytes 786440 | tf_op jit(solution)/shard_map/ppermute | solution.py:258
  38.9 7.3 %collective-permute-start.16 = (bf16[256,512]{1,0:T(8,128)(2,1)S(1)}, bf16[256,512]{1,0:T(8,128)(2,1)S(1)}, u32[]{:S(2)}, u32[]{:S(2)}) collective-permute-start(bf16[256,512]{1,0:T(8,128)(2,1)S(1)} %pad_maximum_fusion.1), channel_id=1, source_target_pairs={{0,7},{1,0},{2,1},{3,2},{4,3},{5,4},{6,5},{7,6},{8,9},{9,10},{10,1... | collective-permute-start | bytes 786440 | tf_op jit(solution)/shard_map/ppermute | solution.py:258
  43.5 6.5 %collective-permute-start.11 = (bf16[256,512]{1,0:T(8,128)(2,1)S(1)}, bf16[256,512]{1,0:T(8,128)(2,1)S(1)}, u32[]{:S(2)}, u32[]{:S(2)}) collective-permute-start(bf16[256,512]{1,0:T(8,128)(2,1)S(1)} %add.25), channel_id=1, source_target_pairs={{0,7},{1,0},{2,1},{3,2},{4,3},{5,4},{6,5},{7,6},{8,9},{9,10},{10,1... | collective-permute-start | bytes 786440 | tf_op jit(solution)/shard_map/ppermute | solution.py:258
  46.3 6.5 %collective-permute-start.17 = (bf16[256,512]{1,0:T(8,128)(2,1)S(1)}, bf16[256,512]{1,0:T(8,128)(2,1)S(1)}, u32[]{:S(2)}, u32[]{:S(2)}) collective-permute-start(bf16[256,512]{1,0:T(8,128)(2,1)S(1)} %add.29), channel_id=1, source_target_pairs={{0,7},{1,0},{2,1},{3,2},{4,3},{5,4},{6,5},{7,6},{8,9},{9,10},{10,1... | collective-permute-start | bytes 786440 | tf_op jit(solution)/shard_map/ppermute | solution.py:258
  50.0 4.5 %collective-permute-start.13 = (bf16[128,512]{1,0:T(8,128)(2,1)S(1)}, bf16[128,512]{1,0:T(8,128)(2,1)S(1)}, u32[]{:S(2)}, u32[]{:S(2)}) collective-permute-start(bf16[128,512]{1,0:T(8,128)(2,1)S(1)} %get-tuple-element.77), channel_id=1, source_target_pairs={{0,15},{1,8},{2,9},{3,10},{4,11},{5,12},{6,13},{7,14},{8,1},{9,2},... | collective-permute-start | bytes 393224 | tf_op jit(solution)/shard_map/ppermute | solution.py:258
  50.6 6.8 %collective-permute-start.12 = (bf16[128,512]{1,0:T(8,128)(2,1)S(1)}, bf16[128,512]{1,0:T(8,128)(2,1)S(1)}, u32[]{:S(2)}, u32[]{:S(2)}) collective-permute-start(bf16[128,512]{1,0:T(8,128)(2,1)S(1)} %get-tuple-element.78), channel_id=1, source_target_pairs={{0,7},{1,0},{2,1},{3,2},{4,3},{5,4},{6,5},{7,6},{8,9},{9,10},{10,1... | collective-permute-start | bytes 393224 | tf_op jit(solution)/shard_map/ppermute | solution.py:258
  52.8 4.6 %collective-permute-start.19 = (bf16[128,512]{1,0:T(8,128)(2,1)S(1)}, bf16[128,512]{1,0:T(8,128)(2,1)S(1)}, u32[]{:S(2)}, u32[]{:S(2)}) collective-permute-start(bf16[128,512]{1,0:T(8,128)(2,1)S(1)} %get-tuple-element.75), channel_id=1, source_target_pairs={{0,15},{1,8},{2,9},{3,10},{4,11},{5,12},{6,13},{7,14},{8,1},{9,2},... | collective-permute-start | bytes 393224 | tf_op jit(solution)/shard_map/ppermute | solution.py:258
  53.4 7.9 %collective-permute-start.18 = (bf16[128,512]{1,0:T(8,128)(2,1)S(1)}, bf16[128,512]{1,0:T(8,128)(2,1)S(1)}, u32[]{:S(2)}, u32[]{:S(2)}) collective-permute-start(bf16[128,512]{1,0:T(8,128)(2,1)S(1)} %get-tuple-element.76), channel_id=1, source_target_pairs={{0,7},{1,0},{2,1},{3,2},{4,3},{5,4},{6,5},{7,6},{8,9},{9,10},{10,1... | collective-permute-start | bytes 393224 | tf_op jit(solution)/shard_map/ppermute | solution.py:258

commit v6 on v5

--- a/solution.py
+++ b/solution.py
@@ -16,7 +16,6 @@
 STEP = 256
 PIECE = TOK + 16
 CHUNK = 512
-ROW = 8
 SCALE = 1.0 / math.sqrt(HD)
 MASKED = -1e30
 F32 = jnp.float32
@@ -53,17 +52,9 @@
     column[...] = jnp.sum(jnp.where(diagonal, wide, 0.0), axis=1, keepdims=True)
 
 
-def pick_kernel(own, far, ids, relayed, beside, ids_again):
-    chip, core = place()
+def pick_kernel(own, far, ids, beside, ids_again):
+    _, core = place()
     ids_again[...] = ids[...]
-
-    @pl.when(chip % 4 == 0)
-    def _():
-        relayed[...] = own[...]
-
-    @pl.when(chip % 4 != 0)
-    def _():
-        relayed[...] = far[...]
 
     @pl.when(core == 0)
     def _():
@@ -245,10 +236,6 @@
         pairs = [(i, (i + 2 * steps) % stretches) for i in range(stretches)]
         return lax.ppermute(value, "loop", pairs)
 
-    def along_row(value, steps):
-        pairs = [(i, i // ROW * ROW + (i + 2 * steps) % ROW) for i in range(stretches)]
-        return lax.ppermute(value, "loop", pairs)
-
     def along(value, swap=0):
         pairs = []
         for loop in range(stretches):
@@ -262,20 +249,16 @@
     own = call(pack_kernel, "pack", 0.05, piece, key_values, prompt_ids.astype(F32)[None, :])
     chip4 = from_chip(own, 4)
     again, ids = call(column_kernel, "column", 0.05, [piece, column], own)
-    chip1, chip2 = from_chip(again, 1), from_chip(again, 2)
+    chip1, chip2, chip3 = [from_chip(again, s) for s in (1, 2, 3)]
     query_rows, *kept = call(
         own_kernel, "own_scores", 0.1, [shape(ROWS, HD)] + kept_shapes(1), queries, ids, again
     )
     (chip4, kept) = lax.optimization_barrier((chip4, kept))
-    relayed, beside, ids = call(
-        pick_kernel, "pick", 0.05, [piece, piece, column], again, chip4, ids
-    )
-    chip3 = along_row(relayed, 3)
+    beside, ids = call(pick_kernel, "pick", 0.05, [piece, column], again, chip4, ids)
     beside = to_mate(beside)
     mate1 = to_mate(chip1)
-    (chip2, beside) = lax.optimization_barrier((chip2, beside))
     mate2 = to_mate(chip2)
-    pieces = [(4, chip4), (BESIDE, beside), (1, chip1), (1, mate1)]
+    pieces = [(4, chip4), (1, chip1)]
     state = call(
         functools.partial(fold_kernel, [item[0] for item in pieces], 1),
         "fold",
@@ -285,16 +268,16 @@
         ids,
         *[item[1] for item in pieces],
         *kept,
-        scratch=later(4),
+        scratch=later(2),
     )
     (chip3, state) = lax.optimization_barrier((chip3, state))
     mate3 = to_mate(chip3)
-    pieces = [(2, chip2), (2, mate2), (3, chip3)]
+    pieces = [(BESIDE, beside), (1, mate1), (2, chip2), (2, mate2), (3, chip3)]
     kept = call(
         functools.partial(more_kernel, [item[0] for item in pieces]),
         "more_scores",
         0.7,
-        kept_shapes(3),
+        kept_shapes(5),
         query_rows,
         ids,
         *[item[1] for item in pieces],

time: 62.3 us -> 61.6 us (0.989)
  waiting for transfers between devices: 23.5 us -> 20.8 us
  starting transfers between devices: 23.7 us -> 25.9 us
    ppermute x3 -> x4, starting transfers between devices: 6.11 us -> 8.71 us  [from_chip(): return lax.ppermute(value, 'loop', pairs)]
    ppermute x3 -> x4, waiting for transfers between devices: 2.99 us -> 1.94 us  [from_chip(): return lax.ppermute(value, 'loop', pairs)]
    ppermute x6, waiting for transfers between devices: 0.9 us -> 0.02 us  [to_mate(): return lax.ppermute(value, 'loop', [(i, i ^ 1) for i in range(stretches)])]
  transfers between devices with their start and end apart: 20 -> 20, of which waited for: 10 -> 9; matrix products, arithmetic and copies ran while one was open for 0% -> 0% of each run, Pallas kernels for 15% -> 14%
where the time goes in v6:
time: 61.6 us; the launch traced here: 61.5 us
  starting transfers between devices  25.9 us (42%)
  waiting for transfers between devices  20.8 us (34%)
  Pallas kernels  11.4 us (19%)
  local copies, waits for them, and re-layouts  2.07 us (3%)
  other arithmetic  1.11 us (2%)
    ppermute x10, waiting for transfers between devices, along(): return lax.ppermute(value, ('loop', 'tp'), pairs)  18.8 us
    pallas_call x11, Pallas kernels, call(): pl.pallas_call(kernel, out_shape=outs, in_specs=[VMEM] * len(args), out_s...  11.4 us
    ppermute x6, starting transfers between devices, to_mate(): return lax.ppermute(value, 'loop', [(i, i ^ 1) for i in range(stretches)])  9.77 us
    ppermute x4, starting transfers between devices, from_chip(): return lax.ppermute(value, 'loop', pairs)  8.71 us
    ppermute x10, starting transfers between devices, along(): return lax.ppermute(value, ('loop', 'tp'), pairs)  7.41 us
    unnamed x6, local copies, waits for them, and re-layouts  2.07 us
    ppermute x4, waiting for transfers between devices, from_chip(): return lax.ppermute(value, 'loop', pairs)  1.94 us
  transfers between devices with their start and end apart: 20, of which 9 were waited for; matrix products, arithmetic and copies ran while one was open for 0% of the time, Pallas kernels for 14%

profile of v6, /device:TPU:1, one launch (start us, length us, event | category | flops | bytes accessed | tf_op | source)
XLA Modules:
  0.0 61.5 jit_solution(12212847183461519211)
XLA Ops:
  0.0 0.8 %convert_element_type.3 = f32[256]{0:T(256)S(1)} convert(s32[256]{0:T(256)} %param.6) | non-fusion elementwise | flops 256 | bytes 2048 | tf_op jit(solution)/shard_map/convert_element_type | solution.py:249
  0.8 1.0 %copy-done.2 = bf16[256,256]{1,0:T(8,128)(2,1)S(1)} copy-done((bf16[256,256]{1,0:T(8,128)(2,1)S(1)}, bf16[256,256]{1,0:T(8,128)(2,1)}, u32[]{:S(2)}) %copy-start.2) | copy-done | bytes 131096
  1.9 2.1 %collective-permute-start = (bf16[272,256]{1,0:T(8,128)(2,1)S(1)}, bf16[272,256]{1,0:T(8,128)(2,1)S(1)}, u32[]{:S(2)}, u32[]{:S(2)}) collective-permute-start(bf16[272,256]{1,0:T(8,128)(2,1)S(1)} %pack.1.message), channel_id=1, source_target_pairs={{0,64},{8,72},{16,80},{24,88},{32,96},{40,104},{48,112},{56,120},{... | collective-permute-start | bytes 417800 | tf_op jit(solution)/shard_map/ppermute | solution.py:237
  4.1 3.0 %collective-permute-start.6 = (bf16[272,256]{1,0:T(8,128)(2,1)S(1)}, bf16[272,256]{1,0:T(8,128)(2,1)S(1)}, u32[]{:S(2)}, u32[]{:S(2)}) collective-permute-start(bf16[272,256]{1,0:T(8,128)(2,1)S(1)} %get-tuple-element.38.piece.own), channel_id=1, source_target_pairs={{0,32},{8,40},{16,48},{24,56},{32,64},{40,72},{48,80},{56,88},{64,... | collective-permute-start | bytes 417800 | tf_op jit(solution)/shard_map/ppermute | solution.py:237
  7.5 3.2 %collective-permute-start.1 = (bf16[272,256]{1,0:T(8,128)(2,1)S(1)}, bf16[272,256]{1,0:T(8,128)(2,1)S(1)}, u32[]{:S(2)}, u32[]{:S(2)}) collective-permute-start(bf16[272,256]{1,0:T(8,128)(2,1)S(1)} %get-tuple-element.38.piece.own), channel_id=1, source_target_pairs={{0,48},{8,56},{16,64},{24,72},{32,80},{40,88},{48,96},{56,104},{64... | collective-permute-start | bytes 417800 | tf_op jit(solution)/shard_map/ppermute | solution.py:237
  10.7 1.0 %copy-done.1 = bf16[256,1024]{1,0:T(8,128)(2,1)S(1)} copy-done((bf16[256,1024]{1,0:T(8,128)(2,1)S(1)}, bf16[256,1024]{1,0:T(8,128)(2,1)}, u32[]{:S(2)}) %copy-start.1) | copy-done | bytes 524312
  11.7 0.5 own_scores.1
  12.2 1.9 %collective-permute-done.6.refs_2_ = bf16[272,256]{1,0:T(8,128)(2,1)S(1)} collective-permute-done((bf16[272,256]{1,0:T(8,128)(2,1)S(1)}, bf16[272,256]{1,0:T(8,128)(2,1)S(1)}, u32[]{:S(2)}, u32[]{:S(2)}) %collective-permute-start.6) | collective-permute-done | bytes 139296 | tf_op jit(solution)/shard_map/ppermute | solution.py:237
  14.1 3.0 %collective-permute-start.7 = (bf16[272,256]{1,0:T(8,128)(2,1)S(1)}, bf16[272,256]{1,0:T(8,128)(2,1)S(1)}, u32[]{:S(2)}, u32[]{:S(2)}) collective-permute-start(bf16[272,256]{1,0:T(8,128)(2,1)S(1)} %collective-permute-done.6.refs_2_), channel_id=1, source_target_pairs={{0,8},{8,0},{16,24},{24,16},{32,40},{40,32},{48,56},{56,48},{64,72... | collective-permute-start | bytes 417800 | tf_op jit(solution)/shard_map/ppermute | solution.py:233
  17.2 2.2 %collective-permute-start.5 = (bf16[272,256]{1,0:T(8,128)(2,1)S(1)}, bf16[272,256]{1,0:T(8,128)(2,1)S(1)}, u32[]{:S(2)}, u32[]{:S(2)}) collective-permute-start(bf16[272,256]{1,0:T(8,128)(2,1)S(1)} %collective-permute-done.2.refs_1_), channel_id=1, source_target_pairs={{0,8},{8,0},{16,24},{24,16},{32,40},{40,32},{48,56},{56,48},{64,72... | collective-permute-start | bytes 417800 | tf_op jit(solution)/shard_map/ppermute | solution.py:233
  19.4 2.3 %fold.1 = (f32[2048,128]{1,0:T(8,128)S(1)}, f32[2048,256]{1,0:T(8,128)S(1)}) custom-call(bf16[2048,128]{1,0:T(8,128)(2,1)S(1)} %get-tuple-element.39.query_rows, f32[256,1]{1,0:T(8,128)S(1)} %get-tuple-element.44.ids, bf16[272,256]{1,0:T(8,128)(2,1)S(1)} %collective-permute-done.far.refs_0_, bf16[272,256]{1,0:T(8,128)(2,1)S(1)} %collective-permute-done.2.refs_1_, ...), custom_call_target="tpu_custom_call" | custom-call | flops 10000000 | bytes 1024 | tf_op jit(solution)/shard_map/fold/pallas_call | solution.py:211
  21.7 0.6 collective-permute-start.3
  22.4 1.7 %more_scores.1 = (f32[2048,1280]{1,0:T(8,128)S(1)}, f32[2048,128]{1,0:T(8,128)S(1)}, bf16[1280,256]{1,0:T(8,128)(2,1)S(1)}) custom-call(bf16[2048,128]{1,0:T(8,128)(2,1)S(1)} %get-tuple-element.39.query_rows, f32[256,1]{1,0:T(8,128)S(1)} %get-tuple-element.44.ids, bf16[272,256]{1,0:T(8,128)(2,1)S(1)} %collective-permute-done.4.refs_0_, ...), custom_call_target="tpu_custom_call" | custom-call | flops 700000000 | bytes 1024 | tf_op jit(solution)/shard_map/more_scores/pallas_call | solution.py:211
  24.1 1.8 %attend.2 = (bf16[128,1024]{1,0:T(8,128)(2,1)S(1)}, bf16[128,512]{1,0:T(8,128)(2,1)S(1)}) custom-call(bf16[2048,128]{1,0:T(8,128)(2,1)S(1)} %get-tuple-element.39.query_rows, f32[256,1]{1,0:T(8,128)S(1)} %get-tuple-element.44.ids, bf16[272,256]{1,0:T(8,128)(2,1)S(1)} %collective-permute-done.3.refs_0_, f32[2048,1280]{1,0:T(8,128)S(1)} %get-tuple-element.52.refs_1_, ...), custom_call_target="tpu_custom_call" | custom-call | flops 10000000 | bytes 1024 | tf_op jit(solution)/shard_map/attend/pallas_call | solution.py:211
  26.1 1.8 %collective-permute-start.9 = (bf16[128,512]{1,0:T(8,128)(2,1)S(1)}, bf16[128,512]{1,0:T(8,128)(2,1)S(1)}, u32[]{:S(2)}, u32[]{:S(2)}) collective-permute-start(bf16[128,512]{1,0:T(8,128)(2,1)S(1)} %get-tuple-element.62), channel_id=1, source_target_pairs={{0,7},{1,0},{2,1},{3,2},{4,3},{5,4},{6,5},{7,6},{8,9},{9,10},{10,1... | collective-permute-start | bytes 393224 | tf_op jit(solution)/shard_map/ppermute | solution.py:245
  27.9 1.9 %attend.3 = (bf16[128,1024]{1,0:T(8,128)(2,1)S(1)}, bf16[128,512]{1,0:T(8,128)(2,1)S(1)}) custom-call(bf16[2048,128]{1,0:T(8,128)(2,1)S(1)} %get-tuple-element.39.query_rows, f32[256,1]{1,0:T(8,128)S(1)} %get-tuple-element.44.ids, bf16[272,256]{1,0:T(8,128)(2,1)S(1)} %collective-permute-done.3.refs_0_, f32[2048,1280]{1,0:T(8,128)S(1)} %get-tuple-element.52.refs_1_, ...), custom_call_target="tpu_custom_call" | custom-call | flops 10000000 | bytes 1024 | tf_op jit(solution)/shard_map/attend/pallas_call | solution.py:211
  29.8 1.7 %collective-permute-start.15 = (bf16[128,512]{1,0:T(8,128)(2,1)S(1)}, bf16[128,512]{1,0:T(8,128)(2,1)S(1)}, u32[]{:S(2)}, u32[]{:S(2)}) collective-permute-start(bf16[128,512]{1,0:T(8,128)(2,1)S(1)} %get-tuple-element.68), channel_id=1, source_target_pairs={{0,7},{1,0},{2,1},{3,2},{4,3},{5,4},{6,5},{7,6},{8,9},{9,10},{10,1... | collective-permute-start | bytes 393224 | tf_op jit(solution)/shard_map/ppermute | solution.py:245
  31.5 3.8 %collective-permute-start.14 = (bf16[128,1024]{1,0:T(8,128)(2,1)S(1)}, bf16[128,1024]{1,0:T(8,128)(2,1)S(1)}, u32[]{:S(2)}, u32[]{:S(2)}) collective-permute-start(bf16[128,1024]{1,0:T(8,128)(2,1)S(1)} %get-tuple-element.63.own), channel_id=1, source_target_pairs={{0,8},{8,0},{16,24},{24,16},{32,40},{40,32},{48,56},{56,48},{64,72... | collective-permute-start | bytes 786440 | tf_op jit(solution)/shard_map/ppermute | solution.py:233
  35.3 1.1 %project.2 = (bf16[256,512]{1,0:T(8,128)(2,1)S(1)}, bf16[256,512]{1,0:T(8,128)(2,1)S(1)}, bf16[256,512]{1,0:T(8,128)(2,1)S(1)}, bf16[128,512]{1,0:T(8,128)(2,1)S(1)}) custom-call(bf16[128,1024]{1,0:T(8,128)(2,1)S(1)} %get-tuple-element.57.own, bf16[128,1024]{1,0:T(8,128)(2,1)S(1)} %collective-permute-done.8.mate, bf16[1024,4096]{1,0:T(8,128)(2,1)S(1)} %copy-done), custom_call_target="tpu_custom_call" | custom-call | flops 10000000 | bytes 1024 | tf_op jit(solution)/shard_map/project/pallas_call | solution.py:211
  36.5 0.8 %collective-permute-start.10 = (bf16[256,512]{1,0:T(8,128)(2,1)S(1)}, bf16[256,512]{1,0:T(8,128)(2,1)S(1)}, u32[]{:S(2)}, u32[]{:S(2)}) collective-permute-start(bf16[256,512]{1,0:T(8,128)(2,1)S(1)} %pad_maximum_fusion), channel_id=1, source_target_pairs={{0,7},{1,0},{2,1},{3,2},{4,3},{5,4},{6,5},{7,6},{8,9},{9,10},{10,1... | collective-permute-start | bytes 786440 | tf_op jit(solution)/shard_map/ppermute | solution.py:245
  37.3 1.1 %project.3 = (bf16[256,512]{1,0:T(8,128)(2,1)S(1)}, bf16[256,512]{1,0:T(8,128)(2,1)S(1)}, bf16[256,512]{1,0:T(8,128)(2,1)S(1)}, bf16[128,512]{1,0:T(8,128)(2,1)S(1)}) custom-call(bf16[128,1024]{1,0:T(8,128)(2,1)S(1)} %get-tuple-element.63.own, bf16[128,1024]{1,0:T(8,128)(2,1)S(1)} %collective-permute-done.14.mate, bf16[1024,4096]{1,0:T(8,128)(2,1)S(1)} %copy-done), custom_call_target="tpu_custom_call" | custom-call | flops 10000000 | bytes 1024 | tf_op jit(solution)/shard_map/project/pallas_call | solution.py:211
  38.7 4.4 %collective-permute-done.10 = bf16[256,512]{1,0:T(8,128)(2,1)S(1)} collective-permute-done((bf16[256,512]{1,0:T(8,128)(2,1)S(1)}, bf16[256,512]{1,0:T(8,128)(2,1)S(1)}, u32[]{:S(2)}, u32[]{:S(2)}) %collective-permute-start.10) | collective-permute-done | bytes 262176 | tf_op jit(solution)/shard_map/ppermute | solution.py:245
  43.2 2.6 %collective-permute-done.16 = bf16[256,512]{1,0:T(8,128)(2,1)S(1)} collective-permute-done((bf16[256,512]{1,0:T(8,128)(2,1)S(1)}, bf16[256,512]{1,0:T(8,128)(2,1)S(1)}, u32[]{:S(2)}, u32[]{:S(2)}) %collective-permute-start.16) | collective-permute-done | bytes 262176 | tf_op jit(solution)/shard_map/ppermute | solution.py:245
  46.0 3.6 %collective-permute-done.11 = bf16[256,512]{1,0:T(8,128)(2,1)S(1)} collective-permute-done((bf16[256,512]{1,0:T(8,128)(2,1)S(1)}, bf16[256,512]{1,0:T(8,128)(2,1)S(1)}, u32[]{:S(2)}, u32[]{:S(2)}) %collective-permute-start.11) | collective-permute-done | bytes 262176 | tf_op jit(solution)/shard_map/ppermute | solution.py:245
  49.7 0.6 collective-permute-start.13
  50.2 0.6 %collective-permute-start.12 = (bf16[128,512]{1,0:T(8,128)(2,1)S(1)}, bf16[128,512]{1,0:T(8,128)(2,1)S(1)}, u32[]{:S(2)}, u32[]{:S(2)}) collective-permute-start(bf16[128,512]{1,0:T(8,128)(2,1)S(1)} %get-tuple-element.72), channel_id=1, source_target_pairs={{0,7},{1,0},{2,1},{3,2},{4,3},{5,4},{6,5},{7,6},{8,9},{9,10},{10,1... | collective-permute-start | bytes 393224 | tf_op jit(solution)/shard_map/ppermute | solution.py:245
  50.9 1.6 %collective-permute-done.17 = bf16[256,512]{1,0:T(8,128)(2,1)S(1)} collective-permute-done((bf16[256,512]{1,0:T(8,128)(2,1)S(1)}, bf16[256,512]{1,0:T(8,128)(2,1)S(1)}, u32[]{:S(2)}, u32[]{:S(2)}) %collective-permute-start.17) | collective-permute-done | bytes 262176 | tf_op jit(solution)/shard_map/ppermute | solution.py:245
  52.5 0.6 collective-permute-start.19
  53.1 1.0 %collective-permute-start.18 = (bf16[128,512]{1,0:T(8,128)(2,1)S(1)}, bf16[128,512]{1,0:T(8,128)(2,1)S(1)}, u32[]{:S(2)}, u32[]{:S(2)}) collective-permute-start(bf16[128,512]{1,0:T(8,128)(2,1)S(1)} %get-tuple-element.70), channel_id=1, source_target_pairs={{0,7},{1,0},{2,1},{3,2},{4,3},{5,4},{6,5},{7,6},{8,9},{9,10},{10,1... | collective-permute-start | bytes 393224 | tf_op jit(solution)/shard_map/ppermute | solution.py:245
  54.4 2.3 %collective-permute-done.12.refs_1_ = bf16[128,512]{1,0:T(8,128)(2,1)S(1)} collective-permute-done((bf16[128,512]{1,0:T(8,128)(2,1)S(1)}, bf16[128,512]{1,0:T(8,128)(2,1)S(1)}, u32[]{:S(2)}, u32[]{:S(2)}) %collective-permute-start.12) | collective-permute-done | bytes 131104 | tf_op jit(solution)/shard_map/ppermute | solution.py:245
  57.0 3.7 %collective-permute-done.18.refs_4_ = bf16[128,512]{1,0:T(8,128)(2,1)S(1)} collective-permute-done((bf16[128,512]{1,0:T(8,128)(2,1)S(1)}, bf16[128,512]{1,0:T(8,128)(2,1)S(1)}, u32[]{:S(2)}, u32[]{:S(2)}) %collective-permute-start.18) | collective-permute-done | bytes 131104 | tf_op jit(solution)/shard_map/ppermute | solution.py:245
  60.7 0.8 %finish.1 = bf16[256,512]{1,0:T(8,128)(2,1)} custom-call(bf16[128,512]{1,0:T(8,128)(2,1)S(1)} %get-tuple-element.58.refs_0_, bf16[128,512]{1,0:T(8,128)(2,1)S(1)} %collective-permute-done.12.refs_1_, bf16[128,512]{1,0:T(8,128)(2,1)S(1)} %collective-permute-done.13.refs_2_, bf16[128,512]{1,0:T(8,128)(2,1)S(1)} %get-tuple-element.64.refs_3_, ...), custom_call_target="tpu_custom_call" | custom-call | flops 500000000 | bytes 1024 | tf_op jit(solution)/shard_map/finish/pallas_call | solution.py:211
  (34 shorter events, 1.9 us)
Async XLA Ops:
  0.0 24.1 %copy-start = (bf16[1024,4096]{1,0:T(8,128)(2,1)S(1)}, bf16[1024,4096]{1,0:T(8,128)(2,1)}, u32[]{:S(2)}) copy-start(bf16[1024,4096]{1,0:T(8,128)(2,1)} %weight.3) | copy-start | bytes 25165828
  0.8 1.0 %copy-start.2 = (bf16[256,256]{1,0:T(8,128)(2,1)S(1)}, bf16[256,256]{1,0:T(8,128)(2,1)}, u32[]{:S(2)}) copy-start(bf16[256,256]{1,0:T(8,128)(2,1)} %key_values.1) | copy-start | bytes 393220
  1.9 10.4 %collective-permute-start = (bf16[272,256]{1,0:T(8,128)(2,1)S(1)}, bf16[272,256]{1,0:T(8,128)(2,1)S(1)}, u32[]{:S(2)}, u32[]{:S(2)}) collective-permute-start(bf16[272,256]{1,0:T(8,128)(2,1)S(1)} %pack.1.message), channel_id=1, source_target_pairs={{0,64},{8,72},{16,80},{24,88},{32,96},{40,104},{48,112},{56,120},{... | collective-permute-start | bytes 417800 | tf_op jit(solution)/shard_map/ppermute | solution.py:237
  4.1 10.0 %collective-permute-start.6 = (bf16[272,256]{1,0:T(8,128)(2,1)S(1)}, bf16[272,256]{1,0:T(8,128)(2,1)S(1)}, u32[]{:S(2)}, u32[]{:S(2)}) collective-permute-start(bf16[272,256]{1,0:T(8,128)(2,1)S(1)} %get-tuple-element.38.piece.own), channel_id=1, source_target_pairs={{0,32},{8,40},{16,48},{24,56},{32,64},{40,72},{48,80},{56,88},{64,... | collective-permute-start | bytes 417800 | tf_op jit(solution)/shard_map/ppermute | solution.py:237
  7.1 10.1 %collective-permute-start.2 = (bf16[272,256]{1,0:T(8,128)(2,1)S(1)}, bf16[272,256]{1,0:T(8,128)(2,1)S(1)}, u32[]{:S(2)}, u32[]{:S(2)}) collective-permute-start(bf16[272,256]{1,0:T(8,128)(2,1)S(1)} %get-tuple-element.38.piece.own), channel_id=1, source_target_pairs={{0,16},{8,24},{16,32},{24,40},{32,48},{40,56},{48,64},{56,72},{64,... | collective-permute-start | bytes 417800 | tf_op jit(solution)/shard_map/ppermute | solution.py:237
  7.5 14.2 %collective-permute-start.1 = (bf16[272,256]{1,0:T(8,128)(2,1)S(1)}, bf16[272,256]{1,0:T(8,128)(2,1)S(1)}, u32[]{:S(2)}, u32[]{:S(2)}) collective-permute-start(bf16[272,256]{1,0:T(8,128)(2,1)S(1)} %get-tuple-element.38.piece.own), channel_id=1, source_target_pairs={{0,48},{8,56},{16,64},{24,72},{32,80},{40,88},{48,96},{56,104},{64... | collective-permute-start | bytes 417800 | tf_op jit(solution)/shard_map/ppermute | solution.py:237
  10.7 1.0 %copy-start.1 = (bf16[256,1024]{1,0:T(8,128)(2,1)S(1)}, bf16[256,1024]{1,0:T(8,128)(2,1)}, u32[]{:S(2)}) copy-start(bf16[256,1024]{1,0:T(8,128)(2,1)} %queries.1) | copy-start | bytes 1572868
  14.1 8.2 %collective-permute-start.7 = (bf16[272,256]{1,0:T(8,128)(2,1)S(1)}, bf16[272,256]{1,0:T(8,128)(2,1)S(1)}, u32[]{:S(2)}, u32[]{:S(2)}) collective-permute-start(bf16[272,256]{1,0:T(8,128)(2,1)S(1)} %collective-permute-done.6.refs_2_), channel_id=1, source_target_pairs={{0,8},{8,0},{16,24},{24,16},{32,40},{40,32},{48,56},{56,48},{64,72... | collective-permute-start | bytes 417800 | tf_op jit(solution)/shard_map/ppermute | solution.py:233
  17.2 5.2 %collective-permute-start.5 = (bf16[272,256]{1,0:T(8,128)(2,1)S(1)}, bf16[272,256]{1,0:T(8,128)(2,1)S(1)}, u32[]{:S(2)}, u32[]{:S(2)}) collective-permute-start(bf16[272,256]{1,0:T(8,128)(2,1)S(1)} %collective-permute-done.2.refs_1_), channel_id=1, source_target_pairs={{0,8},{8,0},{16,24},{24,16},{32,40},{40,32},{48,56},{56,48},{64,72... | collective-permute-start | bytes 417800 | tf_op jit(solution)/shard_map/ppermute | solution.py:233
  19.4 2.9 %collective-permute-start.4 = (bf16[272,256]{1,0:T(8,128)(2,1)S(1)}, bf16[272,256]{1,0:T(8,128)(2,1)S(1)}, u32[]{:S(2)}, u32[]{:S(2)}) collective-permute-start(bf16[272,256]{1,0:T(8,128)(2,1)S(1)} %get-tuple-element.51), channel_id=1, source_target_pairs={{0,8},{8,0},{16,24},{24,16},{32,40},{40,32},{48,56},{56,48},{64,72... | collective-permute-start | bytes 417800 | tf_op jit(solution)/shard_map/ppermute | solution.py:233
  21.7 2.3 %collective-permute-start.3 = (bf16[272,256]{1,0:T(8,128)(2,1)S(1)}, bf16[272,256]{1,0:T(8,128)(2,1)S(1)}, u32[]{:S(2)}, u32[]{:S(2)}) collective-permute-start(bf16[272,256]{1,0:T(8,128)(2,1)S(1)} %collective-permute-done.1.refs_4_), channel_id=1, source_target_pairs={{0,8},{8,0},{16,24},{24,16},{32,40},{40,32},{48,56},{56,48},{64,72... | collective-permute-start | bytes 417800 | tf_op jit(solution)/shard_map/ppermute | solution.py:233
  26.0 9.4 %collective-permute-start.8 = (bf16[128,1024]{1,0:T(8,128)(2,1)S(1)}, bf16[128,1024]{1,0:T(8,128)(2,1)S(1)}, u32[]{:S(2)}, u32[]{:S(2)}) collective-permute-start(bf16[128,1024]{1,0:T(8,128)(2,1)S(1)} %get-tuple-element.57.own), channel_id=1, source_target_pairs={{0,8},{8,0},{16,24},{24,16},{32,40},{40,32},{48,56},{56,48},{64,72... | collective-permute-start | bytes 786440 | tf_op jit(solution)/shard_map/ppermute | solution.py:233
  26.1 10.4 %collective-permute-start.9 = (bf16[128,512]{1,0:T(8,128)(2,1)S(1)}, bf16[128,512]{1,0:T(8,128)(2,1)S(1)}, u32[]{:S(2)}, u32[]{:S(2)}) collective-permute-start(bf16[128,512]{1,0:T(8,128)(2,1)S(1)} %get-tuple-element.62), channel_id=1, source_target_pairs={{0,7},{1,0},{2,1},{3,2},{4,3},{5,4},{6,5},{7,6},{8,9},{9,10},{10,1... | collective-permute-start | bytes 393224 | tf_op jit(solution)/shard_map/ppermute | solution.py:245
  29.8 8.7 %collective-permute-start.15 = (bf16[128,512]{1,0:T(8,128)(2,1)S(1)}, bf16[128,512]{1,0:T(8,128)(2,1)S(1)}, u32[]{:S(2)}, u32[]{:S(2)}) collective-permute-start(bf16[128,512]{1,0:T(8,128)(2,1)S(1)} %get-tuple-element.68), channel_id=1, source_target_pairs={{0,7},{1,0},{2,1},{3,2},{4,3},{5,4},{6,5},{7,6},{8,9},{9,10},{10,1... | collective-permute-start | bytes 393224 | tf_op jit(solution)/shard_map/ppermute | solution.py:245
  31.5 5.8 %collective-permute-start.14 = (bf16[128,1024]{1,0:T(8,128)(2,1)S(1)}, bf16[128,1024]{1,0:T(8,128)(2,1)S(1)}, u32[]{:S(2)}, u32[]{:S(2)}) collective-permute-start(bf16[128,1024]{1,0:T(8,128)(2,1)S(1)} %get-tuple-element.63.own), channel_id=1, source_target_pairs={{0,8},{8,0},{16,24},{24,16},{32,40},{40,32},{48,56},{56,48},{64,72... | collective-permute-start | bytes 786440 | tf_op jit(solution)/shard_map/ppermute | solution.py:233
  36.5 6.5 %collective-permute-start.10 = (bf16[256,512]{1,0:T(8,128)(2,1)S(1)}, bf16[256,512]{1,0:T(8,128)(2,1)S(1)}, u32[]{:S(2)}, u32[]{:S(2)}) collective-permute-start(bf16[256,512]{1,0:T(8,128)(2,1)S(1)} %pad_maximum_fusion), channel_id=1, source_target_pairs={{0,7},{1,0},{2,1},{3,2},{4,3},{5,4},{6,5},{7,6},{8,9},{9,10},{10,1... | collective-permute-start | bytes 786440 | tf_op jit(solution)/shard_map/ppermute | solution.py:245
  38.5 7.3 %collective-permute-start.16 = (bf16[256,512]{1,0:T(8,128)(2,1)S(1)}, bf16[256,512]{1,0:T(8,128)(2,1)S(1)}, u32[]{:S(2)}, u32[]{:S(2)}) collective-permute-start(bf16[256,512]{1,0:T(8,128)(2,1)S(1)} %pad_maximum_fusion.1), channel_id=1, source_target_pairs={{0,7},{1,0},{2,1},{3,2},{4,3},{5,4},{6,5},{7,6},{8,9},{9,10},{10,1... | collective-permute-start | bytes 786440 | tf_op jit(solution)/shard_map/ppermute | solution.py:245
  43.1 6.5 %collective-permute-start.11 = (bf16[256,512]{1,0:T(8,128)(2,1)S(1)}, bf16[256,512]{1,0:T(8,128)(2,1)S(1)}, u32[]{:S(2)}, u32[]{:S(2)}) collective-permute-start(bf16[256,512]{1,0:T(8,128)(2,1)S(1)} %add.25), channel_id=1, source_target_pairs={{0,7},{1,0},{2,1},{3,2},{4,3},{5,4},{6,5},{7,6},{8,9},{9,10},{10,1... | collective-permute-start | bytes 786440 | tf_op jit(solution)/shard_map/ppermute | solution.py:245
  45.9 6.5 %collective-permute-start.17 = (bf16[256,512]{1,0:T(8,128)(2,1)S(1)}, bf16[256,512]{1,0:T(8,128)(2,1)S(1)}, u32[]{:S(2)}, u32[]{:S(2)}) collective-permute-start(bf16[256,512]{1,0:T(8,128)(2,1)S(1)} %add.29), channel_id=1, source_target_pairs={{0,7},{1,0},{2,1},{3,2},{4,3},{5,4},{6,5},{7,6},{8,9},{9,10},{10,1... | collective-permute-start | bytes 786440 | tf_op jit(solution)/shard_map/ppermute | solution.py:245
  49.7 4.8 %collective-permute-start.13 = (bf16[128,512]{1,0:T(8,128)(2,1)S(1)}, bf16[128,512]{1,0:T(8,128)(2,1)S(1)}, u32[]{:S(2)}, u32[]{:S(2)}) collective-permute-start(bf16[128,512]{1,0:T(8,128)(2,1)S(1)} %get-tuple-element.71), channel_id=1, source_target_pairs={{0,15},{1,8},{2,9},{3,10},{4,11},{5,12},{6,13},{7,14},{8,1},{9,2},... | collective-permute-start | bytes 393224 | tf_op jit(solution)/shard_map/ppermute | solution.py:245
  50.2 6.5 %collective-permute-start.12 = (bf16[128,512]{1,0:T(8,128)(2,1)S(1)}, bf16[128,512]{1,0:T(8,128)(2,1)S(1)}, u32[]{:S(2)}, u32[]{:S(2)}) collective-permute-start(bf16[128,512]{1,0:T(8,128)(2,1)S(1)} %get-tuple-element.72), channel_id=1, source_target_pairs={{0,7},{1,0},{2,1},{3,2},{4,3},{5,4},{6,5},{7,6},{8,9},{9,10},{10,1... | collective-permute-start | bytes 393224 | tf_op jit(solution)/shard_map/ppermute | solution.py:245
  52.5 4.5 %collective-permute-start.19 = (bf16[128,512]{1,0:T(8,128)(2,1)S(1)}, bf16[128,512]{1,0:T(8,128)(2,1)S(1)}, u32[]{:S(2)}, u32[]{:S(2)}) collective-permute-start(bf16[128,512]{1,0:T(8,128)(2,1)S(1)} %get-tuple-element.69), channel_id=1, source_target_pairs={{0,15},{1,8},{2,9},{3,10},{4,11},{5,12},{6,13},{7,14},{8,1},{9,2},... | collective-permute-start | bytes 393224 | tf_op jit(solution)/shard_map/ppermute | solution.py:245
  53.1 7.6 %collective-permute-start.18 = (bf16[128,512]{1,0:T(8,128)(2,1)S(1)}, bf16[128,512]{1,0:T(8,128)(2,1)S(1)}, u32[]{:S(2)}, u32[]{:S(2)}) collective-permute-start(bf16[128,512]{1,0:T(8,128)(2,1)S(1)} %get-tuple-element.70), channel_id=1, source_target_pairs={{0,7},{1,0},{2,1},{3,2},{4,3},{5,4},{6,5},{7,6},{8,9},{9,10},{10,1... | collective-permute-start | bytes 393224 | tf_op jit(solution)/shard_map/ppermute | solution.py:245

commit v7 on v6

--- a/solution.py
+++ b/solution.py
@@ -52,9 +52,19 @@
     column[...] = jnp.sum(jnp.where(diagonal, wide, 0.0), axis=1, keepdims=True)
 
 
-def pick_kernel(own, far, ids, beside, ids_again):
-    _, core = place()
+def pick_kernel(own, far, ids, beside, ids_again, *relayed):
+    chip, core = place()
     ids_again[...] = ids[...]
+    for at, piece in enumerate(relayed):
+        inside = chip % 4 + at + 1 < 4
+
+        @pl.when(inside)
+        def _(piece=piece):
+            piece[...] = own[...]
+
+        @pl.when(jnp.logical_not(inside))
+        def _(piece=piece):
+            piece[...] = far[...]
 
     @pl.when(core == 0)
     def _():
@@ -236,6 +246,10 @@
         pairs = [(i, (i + 2 * steps) % stretches) for i in range(stretches)]
         return lax.ppermute(value, "loop", pairs)
 
+    def along_row(value, steps):
+        pairs = [(i, i // 8 * 8 + (i + 2 * steps) % 8) for i in range(stretches)]
+        return lax.ppermute(value, "loop", pairs)
+
     def along(value, swap=0):
         pairs = []
         for loop in range(stretches):
@@ -249,35 +263,35 @@
     own = call(pack_kernel, "pack", 0.05, piece, key_values, prompt_ids.astype(F32)[None, :])
     chip4 = from_chip(own, 4)
     again, ids = call(column_kernel, "column", 0.05, [piece, column], own)
-    chip1, chip2, chip3 = [from_chip(again, s) for s in (1, 2, 3)]
     query_rows, *kept = call(
         own_kernel, "own_scores", 0.1, [shape(ROWS, HD)] + kept_shapes(1), queries, ids, again
     )
     (chip4, kept) = lax.optimization_barrier((chip4, kept))
-    beside, ids = call(pick_kernel, "pick", 0.05, [piece, column], again, chip4, ids)
+    beside, ids, *relayed = call(
+        pick_kernel, "pick", 0.05, [piece, column, piece, piece, piece], again, chip4, ids
+    )
+    chip1, chip2, chip3 = [along_row(relayed[s - 1], s) for s in (1, 2, 3)]
     beside = to_mate(beside)
-    mate1 = to_mate(chip1)
-    mate2 = to_mate(chip2)
-    pieces = [(4, chip4), (1, chip1)]
+    pieces = [(4, chip4)]
     state = call(
         functools.partial(fold_kernel, [item[0] for item in pieces], 1),
         "fold",
-        0.01,
+        3.0,
         [shape(ROWS, HD, F32), shape(ROWS, 2 * HD, F32)],
         query_rows,
         ids,
         *[item[1] for item in pieces],
         *kept,
-        scratch=later(2),
-    )
-    (chip3, state) = lax.optimization_barrier((chip3, state))
-    mate3 = to_mate(chip3)
-    pieces = [(BESIDE, beside), (1, mate1), (2, chip2), (2, mate2), (3, chip3)]
+        scratch=later(1),
+    )
+    (chip1, chip2, chip3, state) = lax.optimization_barrier((chip1, chip2, chip3, state))
+    mate1, mate2, mate3 = [to_mate(chip) for chip in (chip1, chip2, chip3)]
+    pieces = [(BESIDE, beside), (1, chip1), (2, chip2), (3, chip3)]
     kept = call(
         functools.partial(more_kernel, [item[0] for item in pieces]),
         "more_scores",
-        0.7,
-        kept_shapes(5),
+        3.0,
+        kept_shapes(4),
         query_rows,
         ids,
         *[item[1] for item in pieces],
@@ -286,17 +300,19 @@
     ends = []
     for part in range(TOK // PART):
         attention, product = call(
-            functools.partial(last_kernel, part, [3], 1),
+            functools.partial(last_kernel, part, [1, 2, 3], 1),
             "attend",
             0.01,
             [shape(PART, HEADS * HD), shape(PART, CHUNK)],
             query_rows,
             ids,
+            mate1,
+            mate2,
             mate3,
             *kept,
             *state,
             out_weight,
-            scratch=later(1),
+            scratch=later(3),
         )
         extra = along(product)
         wide = shape(2 * PART, CHUNK)

time: 61.6 us -> 60.1 us (0.976)
  starting transfers between devices: 25.9 us -> 25 us
    ppermute x4 -> x1, starting transfers between devices: 8.71 us -> 2.12 us  [from_chip(): return lax.ppermute(value, 'loop', pairs)]
    ppermute x0 -> x3, starting transfers between devices: none -> 5.89 us  [along_row(): return lax.ppermute(value, 'loop', pairs)]
    ppermute x10, waiting for transfers between devices: 18.8 us -> 18.2 us  [along(): return lax.ppermute(value, ('loop', 'tp'), pairs)]
    ppermute x4 -> x1, waiting for transfers between devices: 1.94 us -> 2.08 us  [from_chip(): return lax.ppermute(value, 'loop', pairs)]
    unnamed x6 -> x8, local copies, waits for them, and re-layouts: 2.07 us -> 1.95 us
where the time goes in v7:
time: 60.1 us; the launch traced here: 59.9 us
  starting transfers between devices  25 us (42%)
  waiting for transfers between devices  20.3 us (34%)
  Pallas kernels  11.5 us (19%)
  local copies, waits for them, and re-layouts  1.95 us (3%)
  other arithmetic  0.96 us (2%)
    ppermute x10, waiting for transfers between devices, along(): return lax.ppermute(value, ('loop', 'tp'), pairs)  18.2 us
    pallas_call x11, Pallas kernels, call(): pl.pallas_call(kernel, out_shape=outs, in_specs=[VMEM] * len(args), out_s...  11.5 us
    ppermute x6, starting transfers between devices, to_mate(): return lax.ppermute(value, 'loop', [(i, i ^ 1) for i in range(stretches)])  9.67 us
    ppermute x10, starting transfers between devices, along(): return lax.ppermute(value, ('loop', 'tp'), pairs)  7.32 us
    ppermute x3, starting transfers between devices, along_row(): return lax.ppermute(value, 'loop', pairs)  5.89 us
    ppermute x1, starting transfers between devices, from_chip(): return lax.ppermute(value, 'loop', pairs)  2.12 us
    ppermute x1, waiting for transfers between devices, from_chip(): return lax.ppermute(value, 'loop', pairs)  2.08 us
    unnamed x8, local copies, waits for them, and re-layouts  1.95 us
  transfers between devices with their start and end apart: 20, of which 9 were waited for; matrix products, arithmetic and copies ran while one was open for 0% of the time, Pallas kernels for 14%

profile of v7, /device:TPU:1, one launch (start us, length us, event | category | flops | bytes accessed | tf_op | source)
XLA Modules:
  0.0 59.9 jit_solution(7285300436339066165)
XLA Ops:
  0.0 0.7 %convert_element_type.3 = f32[256]{0:T(256)S(1)} convert(s32[256]{0:T(256)} %param.6) | non-fusion elementwise | flops 256 | bytes 2048 | tf_op jit(solution)/shard_map/convert_element_type | solution.py:263
  0.7 0.9 %copy-done.1 = bf16[256,256]{1,0:T(8,128)(2,1)S(1)} copy-done((bf16[256,256]{1,0:T(8,128)(2,1)S(1)}, bf16[256,256]{1,0:T(8,128)(2,1)}, u32[]{:S(2)}) %copy-start.1) | copy-done | bytes 131096
  1.6 2.1 %collective-permute-start = (bf16[272,256]{1,0:T(8,128)(2,1)S(1)}, bf16[272,256]{1,0:T(8,128)(2,1)S(1)}, u32[]{:S(2)}, u32[]{:S(2)}) collective-permute-start(bf16[272,256]{1,0:T(8,128)(2,1)S(1)} %pack.1.message), channel_id=1, source_target_pairs={{0,64},{8,72},{16,80},{24,88},{32,96},{40,104},{48,112},{56,120},{... | collective-permute-start | bytes 417800 | tf_op jit(solution)/shard_map/ppermute | solution.py:247
  3.8 1.0 %copy-done = bf16[256,1024]{1,0:T(8,128)(2,1)S(1)} copy-done((bf16[256,1024]{1,0:T(8,128)(2,1)S(1)}, bf16[256,1024]{1,0:T(8,128)(2,1)}, u32[]{:S(2)}) %copy-start) | copy-done | bytes 524312
  5.4 2.1 %collective-permute-done.far.refs_0_ = bf16[272,256]{1,0:T(8,128)(2,1)S(1)} collective-permute-done((bf16[272,256]{1,0:T(8,128)(2,1)S(1)}, bf16[272,256]{1,0:T(8,128)(2,1)S(1)}, u32[]{:S(2)}, u32[]{:S(2)}) %collective-permute-start) | collective-permute-done | bytes 139296 | tf_op jit(solution)/shard_map/ppermute | solution.py:247
  7.5 2.2 %collective-permute-start.1 = (bf16[272,256]{1,0:T(8,128)(2,1)S(1)}, bf16[272,256]{1,0:T(8,128)(2,1)S(1)}, u32[]{:S(2)}, u32[]{:S(2)}) collective-permute-start(bf16[272,256]{1,0:T(8,128)(2,1)S(1)} %get-tuple-element.50), channel_id=1, source_target_pairs={{0,16},{8,24},{16,32},{24,40},{32,48},{40,56},{48,0},{56,8},{64,80... | collective-permute-start | bytes 417800 | tf_op jit(solution)/shard_map/ppermute | solution.py:251
  9.7 2.6 %collective-permute-start.2 = (bf16[272,256]{1,0:T(8,128)(2,1)S(1)}, bf16[272,256]{1,0:T(8,128)(2,1)S(1)}, u32[]{:S(2)}, u32[]{:S(2)}) collective-permute-start(bf16[272,256]{1,0:T(8,128)(2,1)S(1)} %get-tuple-element.51), channel_id=1, source_target_pairs={{0,32},{8,40},{16,48},{24,56},{32,0},{40,8},{48,16},{56,24},{64,96... | collective-permute-start | bytes 417800 | tf_op jit(solution)/shard_map/ppermute | solution.py:251
  12.3 1.1 %collective-permute-start.3 = (bf16[272,256]{1,0:T(8,128)(2,1)S(1)}, bf16[272,256]{1,0:T(8,128)(2,1)S(1)}, u32[]{:S(2)}, u32[]{:S(2)}) collective-permute-start(bf16[272,256]{1,0:T(8,128)(2,1)S(1)} %get-tuple-element.52), channel_id=1, source_target_pairs={{0,48},{8,56},{16,0},{24,8},{32,16},{40,24},{48,32},{56,40},{64,11... | collective-permute-start | bytes 417800 | tf_op jit(solution)/shard_map/ppermute | solution.py:251
  13.4 2.4 %collective-permute-start.7 = (bf16[272,256]{1,0:T(8,128)(2,1)S(1)}, bf16[272,256]{1,0:T(8,128)(2,1)S(1)}, u32[]{:S(2)}, u32[]{:S(2)}) collective-permute-start(bf16[272,256]{1,0:T(8,128)(2,1)S(1)} %get-tuple-element.61), channel_id=1, source_target_pairs={{0,8},{8,0},{16,24},{24,16},{32,40},{40,32},{48,56},{56,48},{64,72... | collective-permute-start | bytes 417800 | tf_op jit(solution)/shard_map/ppermute | solution.py:243
  15.8 1.5 %fold.1 = (f32[2048,128]{1,0:T(8,128)S(1)}, f32[2048,256]{1,0:T(8,128)S(1)}) custom-call(bf16[2048,128]{1,0:T(8,128)(2,1)S(1)} %get-tuple-element.44.query_rows, f32[256,1]{1,0:T(8,128)S(1)} %get-tuple-element.49.ids, bf16[272,256]{1,0:T(8,128)(2,1)S(1)} %collective-permute-done.far.refs_0_, f32[2048,256]{1,0:T(8,128)S(1)} %get-tuple-element.53.refs_1_, ...), custom_call_target="tpu_custom_call" | custom-call | flops 3000000000 | bytes 1024 | tf_op jit(solution)/shard_map/fold/pallas_call | solution.py:221
  17.3 2.7 %collective-permute-start.4 = (bf16[272,256]{1,0:T(8,128)(2,1)S(1)}, bf16[272,256]{1,0:T(8,128)(2,1)S(1)}, u32[]{:S(2)}, u32[]{:S(2)}) collective-permute-start(bf16[272,256]{1,0:T(8,128)(2,1)S(1)} %collective-permute-done.1.refs_1_), channel_id=1, source_target_pairs={{0,8},{8,0},{16,24},{24,16},{32,40},{40,32},{48,56},{56,48},{64,72... | collective-permute-start | bytes 417800 | tf_op jit(solution)/shard_map/ppermute | solution.py:243
  20.5 1.4 %more_scores.1 = (f32[2048,1024]{1,0:T(8,128)S(1)}, f32[2048,128]{1,0:T(8,128)S(1)}, bf16[1024,256]{1,0:T(8,128)(2,1)S(1)}) custom-call(bf16[2048,128]{1,0:T(8,128)(2,1)S(1)} %get-tuple-element.44.query_rows, f32[256,1]{1,0:T(8,128)S(1)} %get-tuple-element.49.ids, bf16[272,256]{1,0:T(8,128)(2,1)S(1)} %collective-permute-done.7.refs_0_, ...), custom_call_target="tpu_custom_call" | custom-call | flops 3000000000 | bytes 1024 | tf_op jit(solution)/shard_map/more_scores/pallas_call | solution.py:221
  22.0 2.5 %attend.2 = (bf16[128,1024]{1,0:T(8,128)(2,1)S(1)}, bf16[128,512]{1,0:T(8,128)(2,1)S(1)}) custom-call(bf16[2048,128]{1,0:T(8,128)(2,1)S(1)} %get-tuple-element.44.query_rows, f32[256,1]{1,0:T(8,128)S(1)} %get-tuple-element.49.ids, bf16[272,256]{1,0:T(8,128)(2,1)S(1)} %collective-permute-done.4.refs_0_, bf16[272,256]{1,0:T(8,128)(2,1)S(1)} %collective-permute-done.5.refs_1_, ...), custom_call_target="tpu_custom_call" | custom-call | flops 10000000 | bytes 1024 | tf_op jit(solution)/shard_map/attend/pallas_call | solution.py:221
  24.7 1.7 %collective-permute-start.9 = (bf16[128,512]{1,0:T(8,128)(2,1)S(1)}, bf16[128,512]{1,0:T(8,128)(2,1)S(1)}, u32[]{:S(2)}, u32[]{:S(2)}) collective-permute-start(bf16[128,512]{1,0:T(8,128)(2,1)S(1)} %get-tuple-element.72), channel_id=1, source_target_pairs={{0,7},{1,0},{2,1},{3,2},{4,3},{5,4},{6,5},{7,6},{8,9},{9,10},{10,1... | collective-permute-start | bytes 393224 | tf_op jit(solution)/shard_map/ppermute | solution.py:259
  26.4 2.5 %attend.3 = (bf16[128,1024]{1,0:T(8,128)(2,1)S(1)}, bf16[128,512]{1,0:T(8,128)(2,1)S(1)}) custom-call(bf16[2048,128]{1,0:T(8,128)(2,1)S(1)} %get-tuple-element.44.query_rows, f32[256,1]{1,0:T(8,128)S(1)} %get-tuple-element.49.ids, bf16[272,256]{1,0:T(8,128)(2,1)S(1)} %collective-permute-done.4.refs_0_, bf16[272,256]{1,0:T(8,128)(2,1)S(1)} %collective-permute-done.5.refs_1_, ...), custom_call_target="tpu_custom_call" | custom-call | flops 10000000 | bytes 1024 | tf_op jit(solution)/shard_map/attend/pallas_call | solution.py:221
  28.9 1.7 %collective-permute-start.15 = (bf16[128,512]{1,0:T(8,128)(2,1)S(1)}, bf16[128,512]{1,0:T(8,128)(2,1)S(1)}, u32[]{:S(2)}, u32[]{:S(2)}) collective-permute-start(bf16[128,512]{1,0:T(8,128)(2,1)S(1)} %get-tuple-element.78), channel_id=1, source_target_pairs={{0,7},{1,0},{2,1},{3,2},{4,3},{5,4},{6,5},{7,6},{8,9},{9,10},{10,1... | collective-permute-start | bytes 393224 | tf_op jit(solution)/shard_map/ppermute | solution.py:259
  30.6 3.8 %collective-permute-start.14 = (bf16[128,1024]{1,0:T(8,128)(2,1)S(1)}, bf16[128,1024]{1,0:T(8,128)(2,1)S(1)}, u32[]{:S(2)}, u32[]{:S(2)}) collective-permute-start(bf16[128,1024]{1,0:T(8,128)(2,1)S(1)} %get-tuple-element.73.own), channel_id=1, source_target_pairs={{0,8},{8,0},{16,24},{24,16},{32,40},{40,32},{48,56},{56,48},{64,72... | collective-permute-start | bytes 786440 | tf_op jit(solution)/shard_map/ppermute | solution.py:243
  34.4 1.1 %project.2 = (bf16[256,512]{1,0:T(8,128)(2,1)S(1)}, bf16[256,512]{1,0:T(8,128)(2,1)S(1)}, bf16[256,512]{1,0:T(8,128)(2,1)S(1)}, bf16[128,512]{1,0:T(8,128)(2,1)S(1)}) custom-call(bf16[128,1024]{1,0:T(8,128)(2,1)S(1)} %get-tuple-element.67.own, bf16[128,1024]{1,0:T(8,128)(2,1)S(1)} %collective-permute-done.8.mate, bf16[1024,4096]{1,0:T(8,128)(2,1)S(1)} %bitcast.2), custom_call_target="tpu_custom_call" | custom-call | flops 10000000 | bytes 1024 | tf_op jit(solution)/shard_map/project/pallas_call | solution.py:221
  35.6 0.8 %collective-permute-start.10 = (bf16[256,512]{1,0:T(8,128)(2,1)S(1)}, bf16[256,512]{1,0:T(8,128)(2,1)S(1)}, u32[]{:S(2)}, u32[]{:S(2)}) collective-permute-start(bf16[256,512]{1,0:T(8,128)(2,1)S(1)} %pad_maximum_fusion), channel_id=1, source_target_pairs={{0,7},{1,0},{2,1},{3,2},{4,3},{5,4},{6,5},{7,6},{8,9},{9,10},{10,1... | collective-permute-start | bytes 786440 | tf_op jit(solution)/shard_map/ppermute | solution.py:259
  36.5 1.1 %project.3 = (bf16[256,512]{1,0:T(8,128)(2,1)S(1)}, bf16[256,512]{1,0:T(8,128)(2,1)S(1)}, bf16[256,512]{1,0:T(8,128)(2,1)S(1)}, bf16[128,512]{1,0:T(8,128)(2,1)S(1)}) custom-call(bf16[128,1024]{1,0:T(8,128)(2,1)S(1)} %get-tuple-element.73.own, bf16[128,1024]{1,0:T(8,128)(2,1)S(1)} %collective-permute-done.14.mate, bf16[1024,4096]{1,0:T(8,128)(2,1)S(1)} %bitcast.2), custom_call_target="tpu_custom_call" | custom-call | flops 10000000 | bytes 1024 | tf_op jit(solution)/shard_map/project/pallas_call | solution.py:221
  37.8 4.4 %collective-permute-done.10 = bf16[256,512]{1,0:T(8,128)(2,1)S(1)} collective-permute-done((bf16[256,512]{1,0:T(8,128)(2,1)S(1)}, bf16[256,512]{1,0:T(8,128)(2,1)S(1)}, u32[]{:S(2)}, u32[]{:S(2)}) %collective-permute-start.10) | collective-permute-done | bytes 262176 | tf_op jit(solution)/shard_map/ppermute | solution.py:259
  42.3 2.6 %collective-permute-done.16 = bf16[256,512]{1,0:T(8,128)(2,1)S(1)} collective-permute-done((bf16[256,512]{1,0:T(8,128)(2,1)S(1)}, bf16[256,512]{1,0:T(8,128)(2,1)S(1)}, u32[]{:S(2)}, u32[]{:S(2)}) %collective-permute-start.16) | collective-permute-done | bytes 262176 | tf_op jit(solution)/shard_map/ppermute | solution.py:259
  45.1 3.6 %collective-permute-done.11 = bf16[256,512]{1,0:T(8,128)(2,1)S(1)} collective-permute-done((bf16[256,512]{1,0:T(8,128)(2,1)S(1)}, bf16[256,512]{1,0:T(8,128)(2,1)S(1)}, u32[]{:S(2)}, u32[]{:S(2)}) %collective-permute-start.11) | collective-permute-done | bytes 262176 | tf_op jit(solution)/shard_map/ppermute | solution.py:259
  48.8 0.6 %collective-permute-start.13 = (bf16[128,512]{1,0:T(8,128)(2,1)S(1)}, bf16[128,512]{1,0:T(8,128)(2,1)S(1)}, u32[]{:S(2)}, u32[]{:S(2)}) collective-permute-start(bf16[128,512]{1,0:T(8,128)(2,1)S(1)} %get-tuple-element.81), channel_id=1, source_target_pairs={{0,15},{1,8},{2,9},{3,10},{4,11},{5,12},{6,13},{7,14},{8,1},{9,2},... | collective-permute-start | bytes 393224 | tf_op jit(solution)/shard_map/ppermute | solution.py:259
  49.4 0.6 %collective-permute-start.12 = (bf16[128,512]{1,0:T(8,128)(2,1)S(1)}, bf16[128,512]{1,0:T(8,128)(2,1)S(1)}, u32[]{:S(2)}, u32[]{:S(2)}) collective-permute-start(bf16[128,512]{1,0:T(8,128)(2,1)S(1)} %get-tuple-element.82), channel_id=1, source_target_pairs={{0,7},{1,0},{2,1},{3,2},{4,3},{5,4},{6,5},{7,6},{8,9},{9,10},{10,1... | collective-permute-start | bytes 393224 | tf_op jit(solution)/shard_map/ppermute | solution.py:259
  50.0 1.5 %collective-permute-done.17 = bf16[256,512]{1,0:T(8,128)(2,1)S(1)} collective-permute-done((bf16[256,512]{1,0:T(8,128)(2,1)S(1)}, bf16[256,512]{1,0:T(8,128)(2,1)S(1)}, u32[]{:S(2)}, u32[]{:S(2)}) %collective-permute-start.17) | collective-permute-done | bytes 262176 | tf_op jit(solution)/shard_map/ppermute | solution.py:259
  51.6 0.6 %collective-permute-start.19 = (bf16[128,512]{1,0:T(8,128)(2,1)S(1)}, bf16[128,512]{1,0:T(8,128)(2,1)S(1)}, u32[]{:S(2)}, u32[]{:S(2)}) collective-permute-start(bf16[128,512]{1,0:T(8,128)(2,1)S(1)} %get-tuple-element.79), channel_id=1, source_target_pairs={{0,15},{1,8},{2,9},{3,10},{4,11},{5,12},{6,13},{7,14},{8,1},{9,2},... | collective-permute-start | bytes 393224 | tf_op jit(solution)/shard_map/ppermute | solution.py:259
  52.2 1.0 %collective-permute-start.18 = (bf16[128,512]{1,0:T(8,128)(2,1)S(1)}, bf16[128,512]{1,0:T(8,128)(2,1)S(1)}, u32[]{:S(2)}, u32[]{:S(2)}) collective-permute-start(bf16[128,512]{1,0:T(8,128)(2,1)S(1)} %get-tuple-element.80), channel_id=1, source_target_pairs={{0,7},{1,0},{2,1},{3,2},{4,3},{5,4},{6,5},{7,6},{8,9},{9,10},{10,1... | collective-permute-start | bytes 393224 | tf_op jit(solution)/shard_map/ppermute | solution.py:259
  53.5 1.7 %collective-permute-done.12.refs_1_ = bf16[128,512]{1,0:T(8,128)(2,1)S(1)} collective-permute-done((bf16[128,512]{1,0:T(8,128)(2,1)S(1)}, bf16[128,512]{1,0:T(8,128)(2,1)S(1)}, u32[]{:S(2)}, u32[]{:S(2)}) %collective-permute-start.12) | collective-permute-done | bytes 131104 | tf_op jit(solution)/shard_map/ppermute | solution.py:259
  55.2 0.8 %collective-permute-done.19.refs_5_ = bf16[128,512]{1,0:T(8,128)(2,1)S(1)} collective-permute-done((bf16[128,512]{1,0:T(8,128)(2,1)S(1)}, bf16[128,512]{1,0:T(8,128)(2,1)S(1)}, u32[]{:S(2)}, u32[]{:S(2)}) %collective-permute-start.19) | collective-permute-done | bytes 131104 | tf_op jit(solution)/shard_map/ppermute | solution.py:259
  56.0 3.1 %collective-permute-done.18.refs_4_ = bf16[128,512]{1,0:T(8,128)(2,1)S(1)} collective-permute-done((bf16[128,512]{1,0:T(8,128)(2,1)S(1)}, bf16[128,512]{1,0:T(8,128)(2,1)S(1)}, u32[]{:S(2)}, u32[]{:S(2)}) %collective-permute-start.18) | collective-permute-done | bytes 131104 | tf_op jit(solution)/shard_map/ppermute | solution.py:259
  59.1 0.8 %finish.1 = bf16[256,512]{1,0:T(8,128)(2,1)} custom-call(bf16[128,512]{1,0:T(8,128)(2,1)S(1)} %get-tuple-element.68.refs_0_, bf16[128,512]{1,0:T(8,128)(2,1)S(1)} %collective-permute-done.12.refs_1_, bf16[128,512]{1,0:T(8,128)(2,1)S(1)} %collective-permute-done.13.refs_2_, bf16[128,512]{1,0:T(8,128)(2,1)S(1)} %get-tuple-element.74.refs_3_, ...), custom_call_target="tpu_custom_call" | custom-call | flops 500000000 | bytes 1024 | tf_op jit(solution)/shard_map/finish/pallas_call | solution.py:221
  (37 shorter events, 2.5 us)
Async XLA Ops:
  0.7 0.9 %copy-start.1 = (bf16[256,256]{1,0:T(8,128)(2,1)S(1)}, bf16[256,256]{1,0:T(8,128)(2,1)}, u32[]{:S(2)}) copy-start(bf16[256,256]{1,0:T(8,128)(2,1)} %key_values.1) | copy-start | bytes 393220
  1.6 5.8 %collective-permute-start = (bf16[272,256]{1,0:T(8,128)(2,1)S(1)}, bf16[272,256]{1,0:T(8,128)(2,1)S(1)}, u32[]{:S(2)}, u32[]{:S(2)}) collective-permute-start(bf16[272,256]{1,0:T(8,128)(2,1)S(1)} %pack.1.message), channel_id=1, source_target_pairs={{0,64},{8,72},{16,80},{24,88},{32,96},{40,104},{48,112},{56,120},{... | collective-permute-start | bytes 417800 | tf_op jit(solution)/shard_map/ppermute | solution.py:247
  3.8 1.0 %copy-start = (bf16[256,1024]{1,0:T(8,128)(2,1)S(1)}, bf16[256,1024]{1,0:T(8,128)(2,1)}, u32[]{:S(2)}) copy-start(bf16[256,1024]{1,0:T(8,128)(2,1)} %queries.1) | copy-start | bytes 1572868
  7.5 9.8 %collective-permute-start.1 = (bf16[272,256]{1,0:T(8,128)(2,1)S(1)}, bf16[272,256]{1,0:T(8,128)(2,1)S(1)}, u32[]{:S(2)}, u32[]{:S(2)}) collective-permute-start(bf16[272,256]{1,0:T(8,128)(2,1)S(1)} %get-tuple-element.50), channel_id=1, source_target_pairs={{0,16},{8,24},{16,32},{24,40},{32,48},{40,56},{48,0},{56,8},{64,80... | collective-permute-start | bytes 417800 | tf_op jit(solution)/shard_map/ppermute | solution.py:251
  9.7 7.6 %collective-permute-start.2 = (bf16[272,256]{1,0:T(8,128)(2,1)S(1)}, bf16[272,256]{1,0:T(8,128)(2,1)S(1)}, u32[]{:S(2)}, u32[]{:S(2)}) collective-permute-start(bf16[272,256]{1,0:T(8,128)(2,1)S(1)} %get-tuple-element.51), channel_id=1, source_target_pairs={{0,32},{8,40},{16,48},{24,56},{32,0},{40,8},{48,16},{56,24},{64,96... | collective-permute-start | bytes 417800 | tf_op jit(solution)/shard_map/ppermute | solution.py:251
  12.3 5.0 %collective-permute-start.3 = (bf16[272,256]{1,0:T(8,128)(2,1)S(1)}, bf16[272,256]{1,0:T(8,128)(2,1)S(1)}, u32[]{:S(2)}, u32[]{:S(2)}) collective-permute-start(bf16[272,256]{1,0:T(8,128)(2,1)S(1)} %get-tuple-element.52), channel_id=1, source_target_pairs={{0,48},{8,56},{16,0},{24,8},{32,16},{40,24},{48,32},{56,40},{64,11... | collective-permute-start | bytes 417800 | tf_op jit(solution)/shard_map/ppermute | solution.py:251
  13.4 7.1 %collective-permute-start.7 = (bf16[272,256]{1,0:T(8,128)(2,1)S(1)}, bf16[272,256]{1,0:T(8,128)(2,1)S(1)}, u32[]{:S(2)}, u32[]{:S(2)}) collective-permute-start(bf16[272,256]{1,0:T(8,128)(2,1)S(1)} %get-tuple-element.61), channel_id=1, source_target_pairs={{0,8},{8,0},{16,24},{24,16},{32,40},{40,32},{48,56},{56,48},{64,72... | collective-permute-start | bytes 417800 | tf_op jit(solution)/shard_map/ppermute | solution.py:243
  15.8 6.1 %slice-start = ((s8[8388608]{0:T(1024)(128)(4,1)}), s8[4194304]{0:T(1024)(128)(4,1)S(1)}, s32[]{:S(2)}) async-start(s8[8388608]{0:T(1024)(128)(4,1)} %bitcast.1), calls=%async_computation | async-start | bytes 8388608
  17.3 4.6 %slice-start.1 = ((s8[8388608]{0:T(1024)(128)(4,1)}), s8[4194304]{0:T(1024)(128)(4,1)S(1)}, s32[]{:S(2)}) async-start(s8[8388608]{0:T(1024)(128)(4,1)} %bitcast.1), calls=%async_computation.1 | async-start | bytes 8388608
  17.3 4.6 %collective-permute-start.4 = (bf16[272,256]{1,0:T(8,128)(2,1)S(1)}, bf16[272,256]{1,0:T(8,128)(2,1)S(1)}, u32[]{:S(2)}, u32[]{:S(2)}) collective-permute-start(bf16[272,256]{1,0:T(8,128)(2,1)S(1)} %collective-permute-done.1.refs_1_), channel_id=1, source_target_pairs={{0,8},{8,0},{16,24},{24,16},{32,40},{40,32},{48,56},{56,48},{64,72... | collective-permute-start | bytes 417800 | tf_op jit(solution)/shard_map/ppermute | solution.py:243
  20.0 1.9 %collective-permute-start.5 = (bf16[272,256]{1,0:T(8,128)(2,1)S(1)}, bf16[272,256]{1,0:T(8,128)(2,1)S(1)}, u32[]{:S(2)}, u32[]{:S(2)}) collective-permute-start(bf16[272,256]{1,0:T(8,128)(2,1)S(1)} %collective-permute-done.2.refs_2_), channel_id=1, source_target_pairs={{0,8},{8,0},{16,24},{24,16},{32,40},{40,32},{48,56},{56,48},{64,72... | collective-permute-start | bytes 417800 | tf_op jit(solution)/shard_map/ppermute | solution.py:243
  20.1 1.8 %collective-permute-start.6 = (bf16[272,256]{1,0:T(8,128)(2,1)S(1)}, bf16[272,256]{1,0:T(8,128)(2,1)S(1)}, u32[]{:S(2)}, u32[]{:S(2)}) collective-permute-start(bf16[272,256]{1,0:T(8,128)(2,1)S(1)} %collective-permute-done.3.refs_3_), channel_id=1, source_target_pairs={{0,8},{8,0},{16,24},{24,16},{32,40},{40,32},{48,56},{56,48},{64,72... | collective-permute-start | bytes 417800 | tf_op jit(solution)/shard_map/ppermute | solution.py:243
  24.5 10.0 %collective-permute-start.8 = (bf16[128,1024]{1,0:T(8,128)(2,1)S(1)}, bf16[128,1024]{1,0:T(8,128)(2,1)S(1)}, u32[]{:S(2)}, u32[]{:S(2)}) collective-permute-start(bf16[128,1024]{1,0:T(8,128)(2,1)S(1)} %get-tuple-element.67.own), channel_id=1, source_target_pairs={{0,8},{8,0},{16,24},{24,16},{32,40},{40,32},{48,56},{56,48},{64,72... | collective-permute-start | bytes 786440 | tf_op jit(solution)/shard_map/ppermute | solution.py:243
  24.7 10.8 %collective-permute-start.9 = (bf16[128,512]{1,0:T(8,128)(2,1)S(1)}, bf16[128,512]{1,0:T(8,128)(2,1)S(1)}, u32[]{:S(2)}, u32[]{:S(2)}) collective-permute-start(bf16[128,512]{1,0:T(8,128)(2,1)S(1)} %get-tuple-element.72), channel_id=1, source_target_pairs={{0,7},{1,0},{2,1},{3,2},{4,3},{5,4},{6,5},{7,6},{8,9},{9,10},{10,1... | collective-permute-start | bytes 393224 | tf_op jit(solution)/shard_map/ppermute | solution.py:259
  28.9 8.7 %collective-permute-start.15 = (bf16[128,512]{1,0:T(8,128)(2,1)S(1)}, bf16[128,512]{1,0:T(8,128)(2,1)S(1)}, u32[]{:S(2)}, u32[]{:S(2)}) collective-permute-start(bf16[128,512]{1,0:T(8,128)(2,1)S(1)} %get-tuple-element.78), channel_id=1, source_target_pairs={{0,7},{1,0},{2,1},{3,2},{4,3},{5,4},{6,5},{7,6},{8,9},{9,10},{10,1... | collective-permute-start | bytes 393224 | tf_op jit(solution)/shard_map/ppermute | solution.py:259
  30.6 5.9 %collective-permute-start.14 = (bf16[128,1024]{1,0:T(8,128)(2,1)S(1)}, bf16[128,1024]{1,0:T(8,128)(2,1)S(1)}, u32[]{:S(2)}, u32[]{:S(2)}) collective-permute-start(bf16[128,1024]{1,0:T(8,128)(2,1)S(1)} %get-tuple-element.73.own), channel_id=1, source_target_pairs={{0,8},{8,0},{16,24},{24,16},{32,40},{40,32},{48,56},{56,48},{64,72... | collective-permute-start | bytes 786440 | tf_op jit(solution)/shard_map/ppermute | solution.py:243
  35.6 6.5 %collective-permute-start.10 = (bf16[256,512]{1,0:T(8,128)(2,1)S(1)}, bf16[256,512]{1,0:T(8,128)(2,1)S(1)}, u32[]{:S(2)}, u32[]{:S(2)}) collective-permute-start(bf16[256,512]{1,0:T(8,128)(2,1)S(1)} %pad_maximum_fusion), channel_id=1, source_target_pairs={{0,7},{1,0},{2,1},{3,2},{4,3},{5,4},{6,5},{7,6},{8,9},{9,10},{10,1... | collective-permute-start | bytes 786440 | tf_op jit(solution)/shard_map/ppermute | solution.py:259
  37.6 7.3 %collective-permute-start.16 = (bf16[256,512]{1,0:T(8,128)(2,1)S(1)}, bf16[256,512]{1,0:T(8,128)(2,1)S(1)}, u32[]{:S(2)}, u32[]{:S(2)}) collective-permute-start(bf16[256,512]{1,0:T(8,128)(2,1)S(1)} %pad_maximum_fusion.1), channel_id=1, source_target_pairs={{0,7},{1,0},{2,1},{3,2},{4,3},{5,4},{6,5},{7,6},{8,9},{9,10},{10,1... | collective-permute-start | bytes 786440 | tf_op jit(solution)/shard_map/ppermute | solution.py:259
  42.2 6.5 %collective-permute-start.11 = (bf16[256,512]{1,0:T(8,128)(2,1)S(1)}, bf16[256,512]{1,0:T(8,128)(2,1)S(1)}, u32[]{:S(2)}, u32[]{:S(2)}) collective-permute-start(bf16[256,512]{1,0:T(8,128)(2,1)S(1)} %add.25), channel_id=1, source_target_pairs={{0,7},{1,0},{2,1},{3,2},{4,3},{5,4},{6,5},{7,6},{8,9},{9,10},{10,1... | collective-permute-start | bytes 786440 | tf_op jit(solution)/shard_map/ppermute | solution.py:259
  45.0 6.5 %collective-permute-start.17 = (bf16[256,512]{1,0:T(8,128)(2,1)S(1)}, bf16[256,512]{1,0:T(8,128)(2,1)S(1)}, u32[]{:S(2)}, u32[]{:S(2)}) collective-permute-start(bf16[256,512]{1,0:T(8,128)(2,1)S(1)} %add.29), channel_id=1, source_target_pairs={{0,7},{1,0},{2,1},{3,2},{4,3},{5,4},{6,5},{7,6},{8,9},{9,10},{10,1... | collective-permute-start | bytes 786440 | tf_op jit(solution)/shard_map/ppermute | solution.py:259
  48.8 4.8 %collective-permute-start.13 = (bf16[128,512]{1,0:T(8,128)(2,1)S(1)}, bf16[128,512]{1,0:T(8,128)(2,1)S(1)}, u32[]{:S(2)}, u32[]{:S(2)}) collective-permute-start(bf16[128,512]{1,0:T(8,128)(2,1)S(1)} %get-tuple-element.81), channel_id=1, source_target_pairs={{0,15},{1,8},{2,9},{3,10},{4,11},{5,12},{6,13},{7,14},{8,1},{9,2},... | collective-permute-start | bytes 393224 | tf_op jit(solution)/shard_map/ppermute | solution.py:259
  49.4 5.9 %collective-permute-start.12 = (bf16[128,512]{1,0:T(8,128)(2,1)S(1)}, bf16[128,512]{1,0:T(8,128)(2,1)S(1)}, u32[]{:S(2)}, u32[]{:S(2)}) collective-permute-start(bf16[128,512]{1,0:T(8,128)(2,1)S(1)} %get-tuple-element.82), channel_id=1, source_target_pairs={{0,7},{1,0},{2,1},{3,2},{4,3},{5,4},{6,5},{7,6},{8,9},{9,10},{10,1... | collective-permute-start | bytes 393224 | tf_op jit(solution)/shard_map/ppermute | solution.py:259
  51.6 4.5 %collective-permute-start.19 = (bf16[128,512]{1,0:T(8,128)(2,1)S(1)}, bf16[128,512]{1,0:T(8,128)(2,1)S(1)}, u32[]{:S(2)}, u32[]{:S(2)}) collective-permute-start(bf16[128,512]{1,0:T(8,128)(2,1)S(1)} %get-tuple-element.79), channel_id=1, source_target_pairs={{0,15},{1,8},{2,9},{3,10},{4,11},{5,12},{6,13},{7,14},{8,1},{9,2},... | collective-permute-start | bytes 393224 | tf_op jit(solution)/shard_map/ppermute | solution.py:259
  52.2 7.0 %collective-permute-start.18 = (bf16[128,512]{1,0:T(8,128)(2,1)S(1)}, bf16[128,512]{1,0:T(8,128)(2,1)S(1)}, u32[]{:S(2)}, u32[]{:S(2)}) collective-permute-start(bf16[128,512]{1,0:T(8,128)(2,1)S(1)} %get-tuple-element.80), channel_id=1, source_target_pairs={{0,7},{1,0},{2,1},{3,2},{4,3},{5,4},{6,5},{7,6},{8,9},{9,10},{10,1... | collective-permute-start | bytes 393224 | tf_op jit(solution)/shard_map/ppermute | solution.py:259

commit v8 on v7

--- a/solution.py
+++ b/solution.py
@@ -37,24 +37,26 @@
     return chip >= back
 
 
-def pack_kernel(key_values, ids, message):
-    message[0:TOK, :] = key_values[...]
-    message[TOK:PIECE, :] = jnp.broadcast_to(ids[...], (PIECE - TOK, TOK)).astype(BF16)
-
-
-def column_kernel(message, again, column):
-    again[...] = message[...]
+def write_piece(out, rows, ids):
+    out[0:TOK, :] = rows
+    out[TOK:PIECE, :] = jnp.broadcast_to(ids, (PIECE - TOK, TOK)).astype(BF16)
+
+
+def pack_kernel(key_values, ids, message, column):
+    write_piece(message, key_values[...], ids[...])
     square = (TOK, TOK)
     diagonal = lax.broadcasted_iota(jnp.int32, square, 0) == lax.broadcasted_iota(
         jnp.int32, square, 1
     )
-    wide = jnp.broadcast_to(message[TOK:PIECE, :][0:1, :].astype(F32), square)
+    wide = jnp.broadcast_to(ids[...], square)
     column[...] = jnp.sum(jnp.where(diagonal, wide, 0.0), axis=1, keepdims=True)
 
 
-def pick_kernel(own, far, ids, beside, ids_again, *relayed):
+def pick_kernel(own, far, far_ids, ids, beside, ids_again, packed, *relayed):
     chip, core = place()
     ids_again[...] = ids[...]
+    write_piece(packed, far[...], far_ids[...])
+
     for at, piece in enumerate(relayed):
         inside = chip % 4 + at + 1 < 4
 
@@ -64,7 +66,7 @@
 
         @pl.when(jnp.logical_not(inside))
         def _(piece=piece):
-            piece[...] = far[...]
+            piece[...] = packed[...]
 
     @pl.when(core == 0)
     def _():
@@ -72,7 +74,7 @@
 
     @pl.when(core != 0)
     def _():
-        beside[...] = far[...]
+        beside[...] = packed[...]
 
 
 def find_scores(query_rows, ids, part, pieces, scores, peak, base):
@@ -145,17 +147,19 @@
     return top, total
 
 
-def fold_kernel(backs, early, query_rows, ids, *refs):
+def fold_kernel(backs, early, has_state, query_rows, ids, *refs):
     pieces = list(zip(backs, refs[: len(backs)]))
     refs = refs[len(backs) :]
     kept = [refs[3 * at : 3 * at + 3] for at in range(early)]
-    tops, sums, scores, peak, values = refs[3 * early :]
+    refs = refs[3 * early :]
+    folded = refs[:2] if has_state else None
+    tops, sums, scores, peak, values = refs[2 * has_state :]
     keep_values(pieces, values)
     for part in range(TOK // PART):
         find_scores(query_rows, ids, part, pieces, scores, peak, 0)
         for step in range(HEADS * PART // STEP):
             rows = pl.ds(part * HEADS * PART + step * STEP, STEP)
-            top, total = weigh(part, step, kept + [(scores, peak, values)], None)
+            top, total = weigh(part, step, kept + [(scores, peak, values)], folded)
             tops[rows, :] = top
             sums[rows, :] = total
 
@@ -217,13 +221,14 @@
     return jax.ShapeDtypeStruct((rows, columns), kind)
 
 
-def call(kernel, name, micros, outs, *args, scratch=()):
+def call(kernel, name, micros, outs, *args, scratch=(), aliases={}):
     return pl.pallas_call(
         kernel,
         out_shape=outs,
         in_specs=[VMEM] * len(args),
         out_specs=[VMEM] * len(outs) if isinstance(outs, list) else VMEM,
         scratch_shapes=list(scratch),
+        input_output_aliases=aliases,
         compiler_params=PARAMS,
         cost_estimate=pl.CostEstimate(
             flops=int(micros * 1e9), bytes_accessed=1 << 10, transcendentals=0
@@ -260,59 +265,70 @@
 
     piece = shape(PIECE, TOK)
     column = shape(TOK, 1, F32)
-    own = call(pack_kernel, "pack", 0.05, piece, key_values, prompt_ids.astype(F32)[None, :])
-    chip4 = from_chip(own, 4)
-    again, ids = call(column_kernel, "column", 0.05, [piece, column], own)
+    far = from_chip(key_values, 4)
+    row = prompt_ids.astype(F32)[None, :]
+    far_ids = from_chip(row, 4)
+    own, ids = call(pack_kernel, "pack", 0.1, [piece, column], key_values, row)
     query_rows, *kept = call(
-        own_kernel, "own_scores", 0.1, [shape(ROWS, HD)] + kept_shapes(1), queries, ids, again
-    )
-    (chip4, kept) = lax.optimization_barrier((chip4, kept))
-    beside, ids, *relayed = call(
-        pick_kernel, "pick", 0.05, [piece, column, piece, piece, piece], again, chip4, ids
+        own_kernel, "own_scores", 0.1, [shape(ROWS, HD)] + kept_shapes(1), queries, ids, own
+    )
+    (far, kept) = lax.optimization_barrier((far, kept))
+    beside, ids, chip4, *relayed = call(
+        pick_kernel, "pick", 0.05, [piece, column] + [piece] * 4, own, far, far_ids, ids
     )
     chip1, chip2, chip3 = [along_row(relayed[s - 1], s) for s in (1, 2, 3)]
     beside = to_mate(beside)
-    pieces = [(4, chip4)]
-    state = call(
-        functools.partial(fold_kernel, [item[0] for item in pieces], 1),
-        "fold",
-        3.0,
-        [shape(ROWS, HD, F32), shape(ROWS, 2 * HD, F32)],
+
+    def fold(pieces, kept, state):
+        fixed = 2 + len(pieces) + len(kept)
+        return call(
+            functools.partial(
+                fold_kernel, [item[0] for item in pieces], len(kept) // 3, bool(state)
+            ),
+            "fold",
+            0.01,
+            [shape(ROWS, HD, F32), shape(ROWS, 2 * HD, F32)],
+            query_rows,
+            ids,
+            *[item[1] for item in pieces],
+            *kept,
+            *state,
+            scratch=later(len(pieces)),
+            aliases={fixed: 0, fixed + 1: 1} if state else {},
+        )
+
+    state = fold([(4, chip4)], kept, [])
+    (chip1, beside, state) = lax.optimization_barrier((chip1, beside, state))
+    state = fold([(BESIDE, beside), (1, chip1)], [], state)
+    (chip2, state) = lax.optimization_barrier((chip2, state))
+    state = fold([(2, chip2)], [], state)
+    (chip3, state) = lax.optimization_barrier((chip3, state))
+    mate1, mate2, mate3 = [to_mate(chip) for chip in (chip1, chip2, chip3)]
+    pieces = [(3, chip3), (1, mate1), (2, mate2)]
+    kept = call(
+        functools.partial(more_kernel, [item[0] for item in pieces]),
+        "more_scores",
+        1.5,
+        kept_shapes(len(pieces)),
         query_rows,
         ids,
         *[item[1] for item in pieces],
-        *kept,
-        scratch=later(1),
-    )
-    (chip1, chip2, chip3, state) = lax.optimization_barrier((chip1, chip2, chip3, state))
-    mate1, mate2, mate3 = [to_mate(chip) for chip in (chip1, chip2, chip3)]
-    pieces = [(BESIDE, beside), (1, chip1), (2, chip2), (3, chip3)]
-    kept = call(
-        functools.partial(more_kernel, [item[0] for item in pieces]),
-        "more_scores",
-        3.0,
-        kept_shapes(4),
-        query_rows,
-        ids,
-        *[item[1] for item in pieces],
     )
 
     ends = []
     for part in range(TOK // PART):
         attention, product = call(
-            functools.partial(last_kernel, part, [1, 2, 3], 1),
+            functools.partial(last_kernel, part, [3], 1),
             "attend",
             0.01,
             [shape(PART, HEADS * HD), shape(PART, CHUNK)],
             query_rows,
             ids,
-            mate1,
-            mate2,
             mate3,
             *kept,
             *state,
             out_weight,
-            scratch=later(3),
+            scratch=later(1),
         )
         extra = along(product)
         wide = shape(2 * PART, CHUNK)

time: 60.1 us -> 59.9 us (level)
  Pallas kernels: 11.5 us -> 13.6 us
  starting transfers between devices: 25 us -> 23.8 us
  waiting for transfers between devices: 20.3 us -> 19.2 us
    pallas_call x11 -> x12, Pallas kernels: 11.5 us -> 13.6 us  [call(): pl.pallas_call(kernel, out_shape=outs, in_specs=[VMEM] * len(args), out_s...]
    ppermute x1 -> x2, waiting for transfers between devices: 2.08 us -> 0.01 us  [from_chip(): return lax.ppermute(value, 'loop', pairs)]
    ppermute x10, starting transfers between devices: 7.32 us -> 6.13 us  [along(): return lax.ppermute(value, ('loop', 'tp'), pairs)]
    ppermute x1 -> x2, starting transfers between devices: 2.12 us -> 3.25 us  [from_chip(): return lax.ppermute(value, 'loop', pairs)]
    ppermute x10, waiting for transfers between devices: 18.2 us -> 19.2 us  [along(): return lax.ppermute(value, ('loop', 'tp'), pairs)]
    ppermute x3, starting transfers between devices: 5.89 us -> 5.21 us  [along_row(): return lax.ppermute(value, 'loop', pairs)]
  transfers between devices with their start and end apart: 20 -> 21, of which waited for: 9 -> 7; matrix products, arithmetic and copies ran while one was open for 0% -> 2% of each run, Pallas kernels for 14% -> 19%
where the time goes in v8:
time: 59.9 us; the launch traced here: 59.8 us
  starting transfers between devices  23.8 us (40%)
  waiting for transfers between devices  19.2 us (32%)
  Pallas kernels  13.6 us (23%)
  local copies, waits for them, and re-layouts  1.95 us (3%)
  other arithmetic  0.96 us (2%)
    ppermute x10, waiting for transfers between devices, along(): return lax.ppermute(value, ('loop', 'tp'), pairs)  19.2 us
    pallas_call x12, Pallas kernels, call(): pl.pallas_call(kernel, out_shape=outs, in_specs=[VMEM] * len(args), out_s...  13.6 us
    ppermute x6, starting transfers between devices, to_mate(): return lax.ppermute(value, 'loop', [(i, i ^ 1) for i in range(stretches)])  9.17 us
    ppermute x10, starting transfers between devices, along(): return lax.ppermute(value, ('loop', 'tp'), pairs)  6.13 us
    ppermute x3, starting transfers between devices, along_row(): return lax.ppermute(value, 'loop', pairs)  5.21 us
    ppermute x2, starting transfers between devices, from_chip(): return lax.ppermute(value, 'loop', pairs)  3.25 us
    unnamed x8, local copies, waits for them, and re-layouts  1.95 us
  transfers between devices with their start and end apart: 21, of which 7 were waited for; matrix products, arithmetic and copies ran while one was open for 2% of the time, Pallas kernels for 19%

profile of v8, /device:TPU:1, one launch (start us, length us, event | category | flops | bytes accessed | tf_op | source)
XLA Modules:
  0.0 59.8 jit_solution(10081574259365034849)
XLA Ops:
  0.0 2.0 %collective-permute-start = (bf16[256,256]{1,0:T(8,128)(2,1)}, bf16[256,256]{1,0:T(8,128)(2,1)S(1)}, u32[]{:S(2)}, u32[]{:S(2)}) collective-permute-start(bf16[256,256]{1,0:T(8,128)(2,1)} %key_values.1), channel_id=1, source_target_pairs={{0,64},{8,72},{16,80},{24,88},{32,96},{40,104},{48,112},{56,120},{... | collective-permute-start | bytes 393224 | tf_op jit(solution)/shard_map/ppermute | solution.py:252
  2.0 0.7 %convert_element_type.3 = f32[256]{0:T(256)S(1)} convert(s32[256]{0:T(256)} %param.6) | non-fusion elementwise | flops 256 | bytes 2048 | tf_op jit(solution)/shard_map/convert_element_type | solution.py:269
  2.7 1.2 %collective-permute-start.1 = (f32[1,256]{1,0:T(1,128)S(1)}, f32[1,256]{1,0:T(1,128)S(1)}, u32[]{:S(2)}, u32[]{:S(2)}) collective-permute-start(f32[1,256]{1,0:T(1,128)S(1)} %bitcast.3), channel_id=1, source_target_pairs={{0,64},{8,72},{16,80},{24,88},{32,96},{40,104},{48,112},{56,120},{... | collective-permute-start | bytes 3080 | tf_op jit(solution)/shard_map/ppermute | solution.py:252
  3.9 0.9 %copy-done.1 = bf16[256,256]{1,0:T(8,128)(2,1)S(1)} copy-done((bf16[256,256]{1,0:T(8,128)(2,1)S(1)}, bf16[256,256]{1,0:T(8,128)(2,1)}, u32[]{:S(2)}) %copy-start.1) | copy-done | bytes 131096
  5.0 1.0 %copy-done = bf16[256,1024]{1,0:T(8,128)(2,1)S(1)} copy-done((bf16[256,1024]{1,0:T(8,128)(2,1)S(1)}, bf16[256,1024]{1,0:T(8,128)(2,1)}, u32[]{:S(2)}) %copy-start) | copy-done | bytes 524312
  6.6 1.5 %collective-permute-start.4 = (bf16[272,256]{1,0:T(8,128)(2,1)S(1)}, bf16[272,256]{1,0:T(8,128)(2,1)S(1)}, u32[]{:S(2)}, u32[]{:S(2)}) collective-permute-start(bf16[272,256]{1,0:T(8,128)(2,1)S(1)} %get-tuple-element.62), channel_id=1, source_target_pairs={{0,16},{8,24},{16,32},{24,40},{32,48},{40,56},{48,0},{56,8},{64,80... | collective-permute-start | bytes 417800 | tf_op jit(solution)/shard_map/ppermute | solution.py:256
  8.1 2.1 %collective-permute-start.5 = (bf16[272,256]{1,0:T(8,128)(2,1)S(1)}, bf16[272,256]{1,0:T(8,128)(2,1)S(1)}, u32[]{:S(2)}, u32[]{:S(2)}) collective-permute-start(bf16[272,256]{1,0:T(8,128)(2,1)S(1)} %get-tuple-element.63), channel_id=1, source_target_pairs={{0,8},{8,0},{16,24},{24,16},{32,40},{40,32},{48,56},{56,48},{64,72... | collective-permute-start | bytes 417800 | tf_op jit(solution)/shard_map/ppermute | solution.py:248
  10.2 2.6 %collective-permute-start.3 = (bf16[272,256]{1,0:T(8,128)(2,1)S(1)}, bf16[272,256]{1,0:T(8,128)(2,1)S(1)}, u32[]{:S(2)}, u32[]{:S(2)}) collective-permute-start(bf16[272,256]{1,0:T(8,128)(2,1)S(1)} %get-tuple-element.61), channel_id=1, source_target_pairs={{0,32},{8,40},{16,48},{24,56},{32,0},{40,8},{48,16},{56,24},{64,96... | collective-permute-start | bytes 417800 | tf_op jit(solution)/shard_map/ppermute | solution.py:256
  12.8 1.1 %collective-permute-start.2 = (bf16[272,256]{1,0:T(8,128)(2,1)S(1)}, bf16[272,256]{1,0:T(8,128)(2,1)S(1)}, u32[]{:S(2)}, u32[]{:S(2)}) collective-permute-start(bf16[272,256]{1,0:T(8,128)(2,1)S(1)} %get-tuple-element.60), channel_id=1, source_target_pairs={{0,48},{8,56},{16,0},{24,8},{32,16},{40,24},{48,32},{56,40},{64,11... | collective-permute-start | bytes 417800 | tf_op jit(solution)/shard_map/ppermute | solution.py:256
  13.9 1.5 %fold.3 = (f32[2048,128]{1,0:T(8,128)S(1)}, f32[2048,256]{1,0:T(8,128)S(1)}) custom-call(bf16[2048,128]{1,0:T(8,128)(2,1)S(1)} %get-tuple-element.54.query_rows, f32[256,1]{1,0:T(8,128)S(1)} %get-tuple-element.59.ids, bf16[272,256]{1,0:T(8,128)(2,1)S(1)} %get-tuple-element.64.refs_0_, f32[2048,256]{1,0:T(8,128)S(1)} %get-tuple-element.65.refs_1_, ...), custom_call_target="tpu_custom_call" | custom-call | flops 10000000 | bytes 1024 | tf_op jit(solution)/shard_map/fold/pallas_call | solution.py:225
  15.4 2.7 %fold.4 = (f32[2048,128]{1,0:T(8,128)S(1)}, f32[2048,256]{1,0:T(8,128)S(1)}) custom-call(bf16[2048,128]{1,0:T(8,128)(2,1)S(1)} %get-tuple-element.54.query_rows, f32[256,1]{1,0:T(8,128)S(1)} %get-tuple-element.59.ids, bf16[272,256]{1,0:T(8,128)(2,1)S(1)} %collective-permute-done.5.refs_0_, ...), custom_call_target="tpu_custom_call", output_to_operand_aliasing={{0}: (4, {}), {1}: (5, {})} | custom-call | flops 10000000 | bytes 1024 | tf_op jit(solution)/shard_map/fold/pallas_call | solution.py:225
  18.1 2.1 %collective-permute-start.8 = (bf16[272,256]{1,0:T(8,128)(2,1)S(1)}, bf16[272,256]{1,0:T(8,128)(2,1)S(1)}, u32[]{:S(2)}, u32[]{:S(2)}) collective-permute-start(bf16[272,256]{1,0:T(8,128)(2,1)S(1)} %collective-permute-done.3.refs_0_), channel_id=1, source_target_pairs={{0,8},{8,0},{16,24},{24,16},{32,40},{40,32},{48,56},{56,48},{64,72... | collective-permute-start | bytes 417800 | tf_op jit(solution)/shard_map/ppermute | solution.py:248
  20.3 1.7 %fold.5 = (f32[2048,128]{1,0:T(8,128)S(1)}, f32[2048,256]{1,0:T(8,128)S(1)}) custom-call(bf16[2048,128]{1,0:T(8,128)(2,1)S(1)} %get-tuple-element.54.query_rows, f32[256,1]{1,0:T(8,128)S(1)} %get-tuple-element.59.ids, bf16[272,256]{1,0:T(8,128)(2,1)S(1)} %collective-permute-done.3.refs_0_, ...), custom_call_target="tpu_custom_call", output_to_operand_aliasing={{0}: (3, {}), {1}: (4, {})} | custom-call | flops 10000000 | bytes 1024 | tf_op jit(solution)/shard_map/fold/pallas_call | solution.py:225
  22.0 0.7 %collective-permute-start.6 = (bf16[272,256]{1,0:T(8,128)(2,1)S(1)}, bf16[272,256]{1,0:T(8,128)(2,1)S(1)}, u32[]{:S(2)}, u32[]{:S(2)}) collective-permute-start(bf16[272,256]{1,0:T(8,128)(2,1)S(1)} %collective-permute-done.2.refs_0_), channel_id=1, source_target_pairs={{0,8},{8,0},{16,24},{24,16},{32,40},{40,32},{48,56},{56,48},{64,72... | collective-permute-start | bytes 417800 | tf_op jit(solution)/shard_map/ppermute | solution.py:248
  22.7 1.1 %more_scores.1 = (f32[2048,768]{1,0:T(8,128)S(1)}, f32[2048,128]{1,0:T(8,128)S(1)}, bf16[768,256]{1,0:T(8,128)(2,1)S(1)}) custom-call(bf16[2048,128]{1,0:T(8,128)(2,1)S(1)} %get-tuple-element.54.query_rows, f32[256,1]{1,0:T(8,128)S(1)} %get-tuple-element.59.ids, bf16[272,256]{1,0:T(8,128)(2,1)S(1)} %collective-permute-done.2.refs_0_, ...), custom_call_target="tpu_custom_call" | custom-call | flops 1500000000 | bytes 1024 | tf_op jit(solution)/shard_map/more_scores/pallas_call | solution.py:225
  23.8 1.5 %attend.2 = (bf16[128,1024]{1,0:T(8,128)(2,1)S(1)}, bf16[128,512]{1,0:T(8,128)(2,1)S(1)}) custom-call(bf16[2048,128]{1,0:T(8,128)(2,1)S(1)} %get-tuple-element.54.query_rows, f32[256,1]{1,0:T(8,128)S(1)} %get-tuple-element.59.ids, bf16[272,256]{1,0:T(8,128)(2,1)S(1)} %collective-permute-done.6.refs_0_, f32[2048,768]{1,0:T(8,128)S(1)} %get-tuple-element.82.refs_1_, ...), custom_call_target="tpu_custom_call" | custom-call | flops 10000000 | bytes 1024 | tf_op jit(solution)/shard_map/attend/pallas_call | solution.py:225
  26.2 1.5 %attend.3 = (bf16[128,1024]{1,0:T(8,128)(2,1)S(1)}, bf16[128,512]{1,0:T(8,128)(2,1)S(1)}) custom-call(bf16[2048,128]{1,0:T(8,128)(2,1)S(1)} %get-tuple-element.54.query_rows, f32[256,1]{1,0:T(8,128)S(1)} %get-tuple-element.59.ids, bf16[272,256]{1,0:T(8,128)(2,1)S(1)} %collective-permute-done.6.refs_0_, f32[2048,768]{1,0:T(8,128)S(1)} %get-tuple-element.82.refs_1_, ...), custom_call_target="tpu_custom_call" | custom-call | flops 10000000 | bytes 1024 | tf_op jit(solution)/shard_map/attend/pallas_call | solution.py:225
  27.7 1.7 %collective-permute-start.16 = (bf16[128,512]{1,0:T(8,128)(2,1)S(1)}, bf16[128,512]{1,0:T(8,128)(2,1)S(1)}, u32[]{:S(2)}, u32[]{:S(2)}) collective-permute-start(bf16[128,512]{1,0:T(8,128)(2,1)S(1)} %get-tuple-element.98), channel_id=1, source_target_pairs={{0,7},{1,0},{2,1},{3,2},{4,3},{5,4},{6,5},{7,6},{8,9},{9,10},{10,1... | collective-permute-start | bytes 393224 | tf_op jit(solution)/shard_map/ppermute | solution.py:264
  29.4 3.9 %collective-permute-start.15 = (bf16[128,1024]{1,0:T(8,128)(2,1)S(1)}, bf16[128,1024]{1,0:T(8,128)(2,1)S(1)}, u32[]{:S(2)}, u32[]{:S(2)}) collective-permute-start(bf16[128,1024]{1,0:T(8,128)(2,1)S(1)} %get-tuple-element.93.own), channel_id=1, source_target_pairs={{0,8},{8,0},{16,24},{24,16},{32,40},{40,32},{48,56},{56,48},{64,72... | collective-permute-start | bytes 786440 | tf_op jit(solution)/shard_map/ppermute | solution.py:248
  33.3 1.1 %project.2 = (bf16[256,512]{1,0:T(8,128)(2,1)S(1)}, bf16[256,512]{1,0:T(8,128)(2,1)S(1)}, bf16[256,512]{1,0:T(8,128)(2,1)S(1)}, bf16[128,512]{1,0:T(8,128)(2,1)S(1)}) custom-call(bf16[128,1024]{1,0:T(8,128)(2,1)S(1)} %get-tuple-element.87.own, bf16[128,1024]{1,0:T(8,128)(2,1)S(1)} %collective-permute-done.9.mate, bf16[1024,4096]{1,0:T(8,128)(2,1)S(1)} %bitcast.2), custom_call_target="tpu_custom_call" | custom-call | flops 10000000 | bytes 1024 | tf_op jit(solution)/shard_map/project/pallas_call | solution.py:225
  34.5 0.8 %collective-permute-start.11 = (bf16[256,512]{1,0:T(8,128)(2,1)S(1)}, bf16[256,512]{1,0:T(8,128)(2,1)S(1)}, u32[]{:S(2)}, u32[]{:S(2)}) collective-permute-start(bf16[256,512]{1,0:T(8,128)(2,1)S(1)} %pad_maximum_fusion), channel_id=1, source_target_pairs={{0,7},{1,0},{2,1},{3,2},{4,3},{5,4},{6,5},{7,6},{8,9},{9,10},{10,1... | collective-permute-start | bytes 786440 | tf_op jit(solution)/shard_map/ppermute | solution.py:264
  35.3 1.1 %project.3 = (bf16[256,512]{1,0:T(8,128)(2,1)S(1)}, bf16[256,512]{1,0:T(8,128)(2,1)S(1)}, bf16[256,512]{1,0:T(8,128)(2,1)S(1)}, bf16[128,512]{1,0:T(8,128)(2,1)S(1)}) custom-call(bf16[128,1024]{1,0:T(8,128)(2,1)S(1)} %get-tuple-element.93.own, bf16[128,1024]{1,0:T(8,128)(2,1)S(1)} %collective-permute-done.15.mate, bf16[1024,4096]{1,0:T(8,128)(2,1)S(1)} %bitcast.2), custom_call_target="tpu_custom_call" | custom-call | flops 10000000 | bytes 1024 | tf_op jit(solution)/shard_map/project/pallas_call | solution.py:225
  36.7 4.4 %collective-permute-done.11 = bf16[256,512]{1,0:T(8,128)(2,1)S(1)} collective-permute-done((bf16[256,512]{1,0:T(8,128)(2,1)S(1)}, bf16[256,512]{1,0:T(8,128)(2,1)S(1)}, u32[]{:S(2)}, u32[]{:S(2)}) %collective-permute-start.11) | collective-permute-done | bytes 262176 | tf_op jit(solution)/shard_map/ppermute | solution.py:264
  41.2 2.6 %collective-permute-done.17 = bf16[256,512]{1,0:T(8,128)(2,1)S(1)} collective-permute-done((bf16[256,512]{1,0:T(8,128)(2,1)S(1)}, bf16[256,512]{1,0:T(8,128)(2,1)S(1)}, u32[]{:S(2)}, u32[]{:S(2)}) %collective-permute-start.17) | collective-permute-done | bytes 262176 | tf_op jit(solution)/shard_map/ppermute | solution.py:264
  44.0 3.6 %collective-permute-done.12 = bf16[256,512]{1,0:T(8,128)(2,1)S(1)} collective-permute-done((bf16[256,512]{1,0:T(8,128)(2,1)S(1)}, bf16[256,512]{1,0:T(8,128)(2,1)S(1)}, u32[]{:S(2)}, u32[]{:S(2)}) %collective-permute-start.12) | collective-permute-done | bytes 262176 | tf_op jit(solution)/shard_map/ppermute | solution.py:264
  47.6 0.6 %collective-permute-start.14 = (bf16[128,512]{1,0:T(8,128)(2,1)S(1)}, bf16[128,512]{1,0:T(8,128)(2,1)S(1)}, u32[]{:S(2)}, u32[]{:S(2)}) collective-permute-start(bf16[128,512]{1,0:T(8,128)(2,1)S(1)} %get-tuple-element.101), channel_id=1, source_target_pairs={{0,15},{1,8},{2,9},{3,10},{4,11},{5,12},{6,13},{7,14},{8,1},{9,2},... | collective-permute-start | bytes 393224 | tf_op jit(solution)/shard_map/ppermute | solution.py:264
  48.8 1.6 %collective-permute-done.18 = bf16[256,512]{1,0:T(8,128)(2,1)S(1)} collective-permute-done((bf16[256,512]{1,0:T(8,128)(2,1)S(1)}, bf16[256,512]{1,0:T(8,128)(2,1)S(1)}, u32[]{:S(2)}, u32[]{:S(2)}) %collective-permute-start.18) | collective-permute-done | bytes 262176 | tf_op jit(solution)/shard_map/ppermute | solution.py:264
  50.5 0.6 %collective-permute-start.20 = (bf16[128,512]{1,0:T(8,128)(2,1)S(1)}, bf16[128,512]{1,0:T(8,128)(2,1)S(1)}, u32[]{:S(2)}, u32[]{:S(2)}) collective-permute-start(bf16[128,512]{1,0:T(8,128)(2,1)S(1)} %get-tuple-element.99), channel_id=1, source_target_pairs={{0,15},{1,8},{2,9},{3,10},{4,11},{5,12},{6,13},{7,14},{8,1},{9,2},... | collective-permute-start | bytes 393224 | tf_op jit(solution)/shard_map/ppermute | solution.py:264
  51.1 0.9 %collective-permute-start.19 = (bf16[128,512]{1,0:T(8,128)(2,1)S(1)}, bf16[128,512]{1,0:T(8,128)(2,1)S(1)}, u32[]{:S(2)}, u32[]{:S(2)}) collective-permute-start(bf16[128,512]{1,0:T(8,128)(2,1)S(1)} %get-tuple-element.100), channel_id=1, source_target_pairs={{0,7},{1,0},{2,1},{3,2},{4,3},{5,4},{6,5},{7,6},{8,9},{9,10},{10,1... | collective-permute-start | bytes 393224 | tf_op jit(solution)/shard_map/ppermute | solution.py:264
  52.1 3.0 %collective-permute-done.13.refs_1_ = bf16[128,512]{1,0:T(8,128)(2,1)S(1)} collective-permute-done((bf16[128,512]{1,0:T(8,128)(2,1)S(1)}, bf16[128,512]{1,0:T(8,128)(2,1)S(1)}, u32[]{:S(2)}, u32[]{:S(2)}) %collective-permute-start.13) | collective-permute-done | bytes 131104 | tf_op jit(solution)/shard_map/ppermute | solution.py:264
  55.1 3.9 %collective-permute-done.19.refs_4_ = bf16[128,512]{1,0:T(8,128)(2,1)S(1)} collective-permute-done((bf16[128,512]{1,0:T(8,128)(2,1)S(1)}, bf16[128,512]{1,0:T(8,128)(2,1)S(1)}, u32[]{:S(2)}, u32[]{:S(2)}) %collective-permute-start.19) | collective-permute-done | bytes 131104 | tf_op jit(solution)/shard_map/ppermute | solution.py:264
  59.0 0.8 %finish.1 = bf16[256,512]{1,0:T(8,128)(2,1)} custom-call(bf16[128,512]{1,0:T(8,128)(2,1)S(1)} %get-tuple-element.88.refs_0_, bf16[128,512]{1,0:T(8,128)(2,1)S(1)} %collective-permute-done.13.refs_1_, bf16[128,512]{1,0:T(8,128)(2,1)S(1)} %collective-permute-done.14.refs_2_, bf16[128,512]{1,0:T(8,128)(2,1)S(1)} %get-tuple-element.94.refs_3_, ...), custom_call_target="tpu_custom_call" | custom-call | flops 500000000 | bytes 1024 | tf_op jit(solution)/shard_map/finish/pallas_call | solution.py:225
  (40 shorter events, 3.0 us)
Async XLA Ops:
  0.0 6.5 %collective-permute-start = (bf16[256,256]{1,0:T(8,128)(2,1)}, bf16[256,256]{1,0:T(8,128)(2,1)S(1)}, u32[]{:S(2)}, u32[]{:S(2)}) collective-permute-start(bf16[256,256]{1,0:T(8,128)(2,1)} %key_values.1), channel_id=1, source_target_pairs={{0,64},{8,72},{16,80},{24,88},{32,96},{40,104},{48,112},{56,120},{... | collective-permute-start | bytes 393224 | tf_op jit(solution)/shard_map/ppermute | solution.py:252
  2.7 3.8 %collective-permute-start.1 = (f32[1,256]{1,0:T(1,128)S(1)}, f32[1,256]{1,0:T(1,128)S(1)}, u32[]{:S(2)}, u32[]{:S(2)}) collective-permute-start(f32[1,256]{1,0:T(1,128)S(1)} %bitcast.3), channel_id=1, source_target_pairs={{0,64},{8,72},{16,80},{24,88},{32,96},{40,104},{48,112},{56,120},{... | collective-permute-start | bytes 3080 | tf_op jit(solution)/shard_map/ppermute | solution.py:252
  3.9 0.9 %copy-start.1 = (bf16[256,256]{1,0:T(8,128)(2,1)S(1)}, bf16[256,256]{1,0:T(8,128)(2,1)}, u32[]{:S(2)}) copy-start(bf16[256,256]{1,0:T(8,128)(2,1)} %key_values.1) | copy-start | bytes 393220
  5.0 1.0 %copy-start = (bf16[256,1024]{1,0:T(8,128)(2,1)S(1)}, bf16[256,1024]{1,0:T(8,128)(2,1)}, u32[]{:S(2)}) copy-start(bf16[256,1024]{1,0:T(8,128)(2,1)} %queries.1) | copy-start | bytes 1572868
  6.6 8.8 %collective-permute-start.4 = (bf16[272,256]{1,0:T(8,128)(2,1)S(1)}, bf16[272,256]{1,0:T(8,128)(2,1)S(1)}, u32[]{:S(2)}, u32[]{:S(2)}) collective-permute-start(bf16[272,256]{1,0:T(8,128)(2,1)S(1)} %get-tuple-element.62), channel_id=1, source_target_pairs={{0,16},{8,24},{16,32},{24,40},{32,48},{40,56},{48,0},{56,8},{64,80... | collective-permute-start | bytes 417800 | tf_op jit(solution)/shard_map/ppermute | solution.py:256
  8.1 7.3 %collective-permute-start.5 = (bf16[272,256]{1,0:T(8,128)(2,1)S(1)}, bf16[272,256]{1,0:T(8,128)(2,1)S(1)}, u32[]{:S(2)}, u32[]{:S(2)}) collective-permute-start(bf16[272,256]{1,0:T(8,128)(2,1)S(1)} %get-tuple-element.63), channel_id=1, source_target_pairs={{0,8},{8,0},{16,24},{24,16},{32,40},{40,32},{48,56},{56,48},{64,72... | collective-permute-start | bytes 417800 | tf_op jit(solution)/shard_map/ppermute | solution.py:248
  10.2 7.8 %collective-permute-start.3 = (bf16[272,256]{1,0:T(8,128)(2,1)S(1)}, bf16[272,256]{1,0:T(8,128)(2,1)S(1)}, u32[]{:S(2)}, u32[]{:S(2)}) collective-permute-start(bf16[272,256]{1,0:T(8,128)(2,1)S(1)} %get-tuple-element.61), channel_id=1, source_target_pairs={{0,32},{8,40},{16,48},{24,56},{32,0},{40,8},{48,16},{56,24},{64,96... | collective-permute-start | bytes 417800 | tf_op jit(solution)/shard_map/ppermute | solution.py:256
  12.8 9.2 %collective-permute-start.2 = (bf16[272,256]{1,0:T(8,128)(2,1)S(1)}, bf16[272,256]{1,0:T(8,128)(2,1)S(1)}, u32[]{:S(2)}, u32[]{:S(2)}) collective-permute-start(bf16[272,256]{1,0:T(8,128)(2,1)S(1)} %get-tuple-element.60), channel_id=1, source_target_pairs={{0,48},{8,56},{16,0},{24,8},{32,16},{40,24},{48,32},{56,40},{64,11... | collective-permute-start | bytes 417800 | tf_op jit(solution)/shard_map/ppermute | solution.py:256
  13.9 9.9 %slice-start = ((s8[8388608]{0:T(1024)(128)(4,1)}), s8[4194304]{0:T(1024)(128)(4,1)S(1)}, s32[]{:S(2)}) async-start(s8[8388608]{0:T(1024)(128)(4,1)} %bitcast.1), calls=%async_computation | async-start | bytes 8388608
  18.1 5.8 %slice-start.1 = ((s8[8388608]{0:T(1024)(128)(4,1)}), s8[4194304]{0:T(1024)(128)(4,1)S(1)}, s32[]{:S(2)}) async-start(s8[8388608]{0:T(1024)(128)(4,1)} %bitcast.1), calls=%async_computation.1 | async-start | bytes 8388608
  18.1 4.6 %collective-permute-start.8 = (bf16[272,256]{1,0:T(8,128)(2,1)S(1)}, bf16[272,256]{1,0:T(8,128)(2,1)S(1)}, u32[]{:S(2)}, u32[]{:S(2)}) collective-permute-start(bf16[272,256]{1,0:T(8,128)(2,1)S(1)} %collective-permute-done.3.refs_0_), channel_id=1, source_target_pairs={{0,8},{8,0},{16,24},{24,16},{32,40},{40,32},{48,56},{56,48},{64,72... | collective-permute-start | bytes 417800 | tf_op jit(solution)/shard_map/ppermute | solution.py:248
  20.2 2.5 %collective-permute-start.7 = (bf16[272,256]{1,0:T(8,128)(2,1)S(1)}, bf16[272,256]{1,0:T(8,128)(2,1)S(1)}, u32[]{:S(2)}, u32[]{:S(2)}) collective-permute-start(bf16[272,256]{1,0:T(8,128)(2,1)S(1)} %collective-permute-done.4.refs_1_), channel_id=1, source_target_pairs={{0,8},{8,0},{16,24},{24,16},{32,40},{40,32},{48,56},{56,48},{64,72... | collective-permute-start | bytes 417800 | tf_op jit(solution)/shard_map/ppermute | solution.py:248
  22.0 1.8 %collective-permute-start.6 = (bf16[272,256]{1,0:T(8,128)(2,1)S(1)}, bf16[272,256]{1,0:T(8,128)(2,1)S(1)}, u32[]{:S(2)}, u32[]{:S(2)}) collective-permute-start(bf16[272,256]{1,0:T(8,128)(2,1)S(1)} %collective-permute-done.2.refs_0_), channel_id=1, source_target_pairs={{0,8},{8,0},{16,24},{24,16},{32,40},{40,32},{48,56},{56,48},{64,72... | collective-permute-start | bytes 417800 | tf_op jit(solution)/shard_map/ppermute | solution.py:248
  25.3 8.0 %collective-permute-start.9 = (bf16[128,1024]{1,0:T(8,128)(2,1)S(1)}, bf16[128,1024]{1,0:T(8,128)(2,1)S(1)}, u32[]{:S(2)}, u32[]{:S(2)}) collective-permute-start(bf16[128,1024]{1,0:T(8,128)(2,1)S(1)} %get-tuple-element.87.own), channel_id=1, source_target_pairs={{0,8},{8,0},{16,24},{24,16},{32,40},{40,32},{48,56},{56,48},{64,72... | collective-permute-start | bytes 786440 | tf_op jit(solution)/shard_map/ppermute | solution.py:248
  25.7 8.8 %collective-permute-start.10 = (bf16[128,512]{1,0:T(8,128)(2,1)S(1)}, bf16[128,512]{1,0:T(8,128)(2,1)S(1)}, u32[]{:S(2)}, u32[]{:S(2)}) collective-permute-start(bf16[128,512]{1,0:T(8,128)(2,1)S(1)} %get-tuple-element.92), channel_id=1, source_target_pairs={{0,7},{1,0},{2,1},{3,2},{4,3},{5,4},{6,5},{7,6},{8,9},{9,10},{10,1... | collective-permute-start | bytes 393224 | tf_op jit(solution)/shard_map/ppermute | solution.py:264
  27.7 8.7 %collective-permute-start.16 = (bf16[128,512]{1,0:T(8,128)(2,1)S(1)}, bf16[128,512]{1,0:T(8,128)(2,1)S(1)}, u32[]{:S(2)}, u32[]{:S(2)}) collective-permute-start(bf16[128,512]{1,0:T(8,128)(2,1)S(1)} %get-tuple-element.98), channel_id=1, source_target_pairs={{0,7},{1,0},{2,1},{3,2},{4,3},{5,4},{6,5},{7,6},{8,9},{9,10},{10,1... | collective-permute-start | bytes 393224 | tf_op jit(solution)/shard_map/ppermute | solution.py:264
  29.4 5.9 %collective-permute-start.15 = (bf16[128,1024]{1,0:T(8,128)(2,1)S(1)}, bf16[128,1024]{1,0:T(8,128)(2,1)S(1)}, u32[]{:S(2)}, u32[]{:S(2)}) collective-permute-start(bf16[128,1024]{1,0:T(8,128)(2,1)S(1)} %get-tuple-element.93.own), channel_id=1, source_target_pairs={{0,8},{8,0},{16,24},{24,16},{32,40},{40,32},{48,56},{56,48},{64,72... | collective-permute-start | bytes 786440 | tf_op jit(solution)/shard_map/ppermute | solution.py:248
  34.5 6.5 %collective-permute-start.11 = (bf16[256,512]{1,0:T(8,128)(2,1)S(1)}, bf16[256,512]{1,0:T(8,128)(2,1)S(1)}, u32[]{:S(2)}, u32[]{:S(2)}) collective-permute-start(bf16[256,512]{1,0:T(8,128)(2,1)S(1)} %pad_maximum_fusion), channel_id=1, source_target_pairs={{0,7},{1,0},{2,1},{3,2},{4,3},{5,4},{6,5},{7,6},{8,9},{9,10},{10,1... | collective-permute-start | bytes 786440 | tf_op jit(solution)/shard_map/ppermute | solution.py:264
  36.5 7.3 %collective-permute-start.17 = (bf16[256,512]{1,0:T(8,128)(2,1)S(1)}, bf16[256,512]{1,0:T(8,128)(2,1)S(1)}, u32[]{:S(2)}, u32[]{:S(2)}) collective-permute-start(bf16[256,512]{1,0:T(8,128)(2,1)S(1)} %pad_maximum_fusion.1), channel_id=1, source_target_pairs={{0,7},{1,0},{2,1},{3,2},{4,3},{5,4},{6,5},{7,6},{8,9},{9,10},{10,1... | collective-permute-start | bytes 786440 | tf_op jit(solution)/shard_map/ppermute | solution.py:264
  41.1 6.5 %collective-permute-start.12 = (bf16[256,512]{1,0:T(8,128)(2,1)S(1)}, bf16[256,512]{1,0:T(8,128)(2,1)S(1)}, u32[]{:S(2)}, u32[]{:S(2)}) collective-permute-start(bf16[256,512]{1,0:T(8,128)(2,1)S(1)} %add.25), channel_id=1, source_target_pairs={{0,7},{1,0},{2,1},{3,2},{4,3},{5,4},{6,5},{7,6},{8,9},{9,10},{10,1... | collective-permute-start | bytes 786440 | tf_op jit(solution)/shard_map/ppermute | solution.py:264
  43.9 6.5 %collective-permute-start.18 = (bf16[256,512]{1,0:T(8,128)(2,1)S(1)}, bf16[256,512]{1,0:T(8,128)(2,1)S(1)}, u32[]{:S(2)}, u32[]{:S(2)}) collective-permute-start(bf16[256,512]{1,0:T(8,128)(2,1)S(1)} %add.29), channel_id=1, source_target_pairs={{0,7},{1,0},{2,1},{3,2},{4,3},{5,4},{6,5},{7,6},{8,9},{9,10},{10,1... | collective-permute-start | bytes 786440 | tf_op jit(solution)/shard_map/ppermute | solution.py:264
  47.6 4.5 %collective-permute-start.14 = (bf16[128,512]{1,0:T(8,128)(2,1)S(1)}, bf16[128,512]{1,0:T(8,128)(2,1)S(1)}, u32[]{:S(2)}, u32[]{:S(2)}) collective-permute-start(bf16[128,512]{1,0:T(8,128)(2,1)S(1)} %get-tuple-element.101), channel_id=1, source_target_pairs={{0,15},{1,8},{2,9},{3,10},{4,11},{5,12},{6,13},{7,14},{8,1},{9,2},... | collective-permute-start | bytes 393224 | tf_op jit(solution)/shard_map/ppermute | solution.py:264
  48.2 6.8 %collective-permute-start.13 = (bf16[128,512]{1,0:T(8,128)(2,1)S(1)}, bf16[128,512]{1,0:T(8,128)(2,1)S(1)}, u32[]{:S(2)}, u32[]{:S(2)}) collective-permute-start(bf16[128,512]{1,0:T(8,128)(2,1)S(1)} %get-tuple-element.102), channel_id=1, source_target_pairs={{0,7},{1,0},{2,1},{3,2},{4,3},{5,4},{6,5},{7,6},{8,9},{9,10},{10,1... | collective-permute-start | bytes 393224 | tf_op jit(solution)/shard_map/ppermute | solution.py:264
  50.5 4.6 %collective-permute-start.20 = (bf16[128,512]{1,0:T(8,128)(2,1)S(1)}, bf16[128,512]{1,0:T(8,128)(2,1)S(1)}, u32[]{:S(2)}, u32[]{:S(2)}) collective-permute-start(bf16[128,512]{1,0:T(8,128)(2,1)S(1)} %get-tuple-element.99), channel_id=1, source_target_pairs={{0,15},{1,8},{2,9},{3,10},{4,11},{5,12},{6,13},{7,14},{8,1},{9,2},... | collective-permute-start | bytes 393224 | tf_op jit(solution)/shard_map/ppermute | solution.py:264
  51.1 7.9 %collective-permute-start.19 = (bf16[128,512]{1,0:T(8,128)(2,1)S(1)}, bf16[128,512]{1,0:T(8,128)(2,1)S(1)}, u32[]{:S(2)}, u32[]{:S(2)}) collective-permute-start(bf16[128,512]{1,0:T(8,128)(2,1)S(1)} %get-tuple-element.100), channel_id=1, source_target_pairs={{0,7},{1,0},{2,1},{3,2},{4,3},{5,4},{6,5},{7,6},{8,9},{9,10},{10,1... | collective-permute-start | bytes 393224 | tf_op jit(solution)/shard_map/ppermute | solution.py:264

commit v9 on v8

--- a/solution.py
+++ b/solution.py
@@ -16,7 +16,7 @@
 STEP = 256
 PIECE = TOK + 16
 CHUNK = 512
-SCALE = 1.0 / math.sqrt(HD)
+SCALE = math.log2(math.e) / math.sqrt(HD)
 MASKED = -1e30
 F32 = jnp.float32
 BF16 = jnp.bfloat16
@@ -57,8 +57,8 @@
     ids_again[...] = ids[...]
     write_piece(packed, far[...], far_ids[...])
 
-    for at, piece in enumerate(relayed):
-        inside = chip % 4 + at + 1 < 4
+    for steps, piece in zip((1, 3), relayed):
+        inside = chip % 4 + steps < 4
 
         @pl.when(inside)
         def _(piece=piece):
@@ -137,11 +137,11 @@
     if folded is not None:
         old = folded[0][given, :]
         top = jnp.maximum(top, old)
-        shrink = jnp.exp((old - top) * SCALE)
+        shrink = jnp.exp2((old - top) * SCALE)
         total = folded[1][given, :] * jnp.concatenate([shrink, shrink], axis=1)
     for scores, rows, values in blocks:
         wide = jnp.concatenate([top] * (scores.shape[1] // HD), axis=1)
-        probs = jnp.exp((scores[rows, :] - wide) * SCALE).astype(BF16)
+        probs = jnp.exp2((scores[rows, :] - wide) * SCALE).astype(BF16)
         added = jnp.dot(probs, values[...], preferred_element_type=F32)
         total = added if total is None else total + added
     return top, total
@@ -269,14 +269,15 @@
     row = prompt_ids.astype(F32)[None, :]
     far_ids = from_chip(row, 4)
     own, ids = call(pack_kernel, "pack", 0.1, [piece, column], key_values, row)
+    chip2 = from_chip(own, 2)
     query_rows, *kept = call(
         own_kernel, "own_scores", 0.1, [shape(ROWS, HD)] + kept_shapes(1), queries, ids, own
     )
     (far, kept) = lax.optimization_barrier((far, kept))
     beside, ids, chip4, *relayed = call(
-        pick_kernel, "pick", 0.05, [piece, column] + [piece] * 4, own, far, far_ids, ids
-    )
-    chip1, chip2, chip3 = [along_row(relayed[s - 1], s) for s in (1, 2, 3)]
+        pick_kernel, "pick", 0.05, [piece, column] + [piece] * 3, own, far, far_ids, ids
+    )
+    chip1, chip3 = along_row(relayed[0], 1), along_row(relayed[1], 3)
     beside = to_mate(beside)
 
     def fold(pieces, kept, state):
@@ -286,7 +287,7 @@
                 fold_kernel, [item[0] for item in pieces], len(kept) // 3, bool(state)
             ),
             "fold",
-            0.01,
+            2.0,
             [shape(ROWS, HD, F32), shape(ROWS, 2 * HD, F32)],
             query_rows,
             ids,
@@ -298,13 +299,12 @@
         )
 
     state = fold([(4, chip4)], kept, [])
-    (chip1, beside, state) = lax.optimization_barrier((chip1, beside, state))
-    state = fold([(BESIDE, beside), (1, chip1)], [], state)
     (chip2, state) = lax.optimization_barrier((chip2, state))
-    state = fold([(2, chip2)], [], state)
-    (chip3, state) = lax.optimization_barrier((chip3, state))
-    mate1, mate2, mate3 = [to_mate(chip) for chip in (chip1, chip2, chip3)]
-    pieces = [(3, chip3), (1, mate1), (2, mate2)]
+    mate2 = to_mate(chip2)
+    state = fold([(BESIDE, beside), (2, chip2)], [], state)
+    (chip1, chip3, state) = lax.optimization_barrier((chip1, chip3, state))
+    mate1, mate3 = to_mate(chip1), to_mate(chip3)
+    pieces = [(2, mate2), (1, chip1), (3, chip3)]
     kept = call(
         functools.partial(more_kernel, [item[0] for item in pieces]),
         "more_scores",
@@ -318,17 +318,18 @@
     ends = []
     for part in range(TOK // PART):
         attention, product = call(
-            functools.partial(last_kernel, part, [3], 1),
+            functools.partial(last_kernel, part, [1, 3], 1),
             "attend",
             0.01,
             [shape(PART, HEADS * HD), shape(PART, CHUNK)],
             query_rows,
             ids,
+            mate1,
             mate3,
             *kept,
             *state,
             out_weight,
-            scratch=later(1),
+            scratch=later(2),
         )
         extra = along(product)
         wide = shape(2 * PART, CHUNK)

time: 59.9 us -> 57.8 us (0.965)
  Pallas kernels: 13.6 us -> 11.9 us
    ppermute x2 -> x3, starting transfers between devices: 3.25 us -> 6.24 us  [from_chip(): return lax.ppermute(value, 'loop', pairs)]
    ppermute x3 -> x2, starting transfers between devices: 5.21 us -> 2.75 us  [along_row(): return lax.ppermute(value, 'loop', pairs)]
    ppermute x6, starting transfers between devices: 9.17 us -> 7.21 us  [to_mate(): return lax.ppermute(value, 'loop', [(i, i ^ 1) for i in range(stretches)])]
    pallas_call x12 -> x11, Pallas kernels: 13.6 us -> 11.9 us  [call(): pl.pallas_call(kernel, out_shape=outs, in_specs=[VMEM] * len(args), out_s...]
    ppermute x10, starting transfers between devices: 6.13 us -> 7.12 us  [along(): return lax.ppermute(value, ('loop', 'tp'), pairs)]
  transfers between devices with their start and end apart: 21 -> 21, of which waited for: 7 -> 7; matrix products, arithmetic and copies ran while one was open for 2% -> 2% of each run, Pallas kernels for 19% -> 16%
where the time goes in v9:
time: 57.8 us; the launch traced here: 57.6 us
  starting transfers between devices  23.3 us (40%)
  waiting for transfers between devices  19.2 us (33%)
  Pallas kernels  11.9 us (21%)
  local copies, waits for them, and re-layouts  1.96 us (3%)
  other arithmetic  0.96 us (2%)
    ppermute x10, waiting for transfers between devices, along(): return lax.ppermute(value, ('loop', 'tp'), pairs)  19.2 us
    pallas_call x11, Pallas kernels, call(): pl.pallas_call(kernel, out_shape=outs, in_specs=[VMEM] * len(args), out_s...  11.9 us
    ppermute x6, starting transfers between devices, to_mate(): return lax.ppermute(value, 'loop', [(i, i ^ 1) for i in range(stretches)])  7.21 us
    ppermute x10, starting transfers between devices, along(): return lax.ppermute(value, ('loop', 'tp'), pairs)  7.12 us
    ppermute x3, starting transfers between devices, from_chip(): return lax.ppermute(value, 'loop', pairs)  6.24 us
    ppermute x2, starting transfers between devices, along_row(): return lax.ppermute(value, 'loop', pairs)  2.75 us
    unnamed x8, local copies, waits for them, and re-layouts  1.96 us
  transfers between devices with their start and end apart: 21, of which 7 were waited for; matrix products, arithmetic and copies ran while one was open for 2% of the time, Pallas kernels for 16%

profile of v9, /device:TPU:1, one launch (start us, length us, event | category | flops | bytes accessed | tf_op | source)
XLA Modules:
  0.0 57.6 jit_solution(11110714518438571909)
XLA Ops:
  0.0 2.0 %collective-permute-start = (bf16[256,256]{1,0:T(8,128)(2,1)}, bf16[256,256]{1,0:T(8,128)(2,1)S(1)}, u32[]{:S(2)}, u32[]{:S(2)}) collective-permute-start(bf16[256,256]{1,0:T(8,128)(2,1)} %key_values.1), channel_id=1, source_target_pairs={{0,64},{8,72},{16,80},{24,88},{32,96},{40,104},{48,112},{56,120},{... | collective-permute-start | bytes 393224 | tf_op jit(solution)/shard_map/ppermute | solution.py:252
  2.0 0.7 %convert_element_type.3 = f32[256]{0:T(256)S(1)} convert(s32[256]{0:T(256)} %param.6) | non-fusion elementwise | flops 256 | bytes 2048 | tf_op jit(solution)/shard_map/convert_element_type | solution.py:269
  2.7 1.2 %collective-permute-start.1 = (f32[1,256]{1,0:T(1,128)S(1)}, f32[1,256]{1,0:T(1,128)S(1)}, u32[]{:S(2)}, u32[]{:S(2)}) collective-permute-start(f32[1,256]{1,0:T(1,128)S(1)} %bitcast.3), channel_id=1, source_target_pairs={{0,64},{8,72},{16,80},{24,88},{32,96},{40,104},{48,112},{56,120},{... | collective-permute-start | bytes 3080 | tf_op jit(solution)/shard_map/ppermute | solution.py:252
  3.9 0.9 %copy-done.1 = bf16[256,256]{1,0:T(8,128)(2,1)S(1)} copy-done((bf16[256,256]{1,0:T(8,128)(2,1)S(1)}, bf16[256,256]{1,0:T(8,128)(2,1)}, u32[]{:S(2)}) %copy-start.1) | copy-done | bytes 131096
  5.0 3.0 %collective-permute-start.5 = (bf16[272,256]{1,0:T(8,128)(2,1)S(1)}, bf16[272,256]{1,0:T(8,128)(2,1)S(1)}, u32[]{:S(2)}, u32[]{:S(2)}) collective-permute-start(bf16[272,256]{1,0:T(8,128)(2,1)S(1)} %get-tuple-element.47.piece.own), channel_id=1, source_target_pairs={{0,32},{8,40},{16,48},{24,56},{32,64},{40,72},{48,80},{56,88},{64,... | collective-permute-start | bytes 417800 | tf_op jit(solution)/shard_map/ppermute | solution.py:252
  7.9 1.0 %copy-done = bf16[256,1024]{1,0:T(8,128)(2,1)S(1)} copy-done((bf16[256,1024]{1,0:T(8,128)(2,1)S(1)}, bf16[256,1024]{1,0:T(8,128)(2,1)}, u32[]{:S(2)}) %copy-start) | copy-done | bytes 524312
  9.0 0.5 own_scores.1
  10.0 2.3 %collective-permute-start.3 = (bf16[272,256]{1,0:T(8,128)(2,1)S(1)}, bf16[272,256]{1,0:T(8,128)(2,1)S(1)}, u32[]{:S(2)}, u32[]{:S(2)}) collective-permute-start(bf16[272,256]{1,0:T(8,128)(2,1)S(1)} %get-tuple-element.55), channel_id=1, source_target_pairs={{0,48},{8,56},{16,0},{24,8},{32,16},{40,24},{48,32},{56,40},{64,11... | collective-permute-start | bytes 417800 | tf_op jit(solution)/shard_map/ppermute | solution.py:256
  12.3 2.1 %collective-permute-start.4 = (bf16[272,256]{1,0:T(8,128)(2,1)S(1)}, bf16[272,256]{1,0:T(8,128)(2,1)S(1)}, u32[]{:S(2)}, u32[]{:S(2)}) collective-permute-start(bf16[272,256]{1,0:T(8,128)(2,1)S(1)} %get-tuple-element.56), channel_id=1, source_target_pairs={{0,8},{8,0},{16,24},{24,16},{32,40},{40,32},{48,56},{56,48},{64,72... | collective-permute-start | bytes 417800 | tf_op jit(solution)/shard_map/ppermute | solution.py:248
  14.4 1.4 %fold.2 = (f32[2048,128]{1,0:T(8,128)S(1)}, f32[2048,256]{1,0:T(8,128)S(1)}) custom-call(bf16[2048,128]{1,0:T(8,128)(2,1)S(1)} %get-tuple-element.48.query_rows, f32[256,1]{1,0:T(8,128)S(1)} %get-tuple-element.53.ids, bf16[272,256]{1,0:T(8,128)(2,1)S(1)} %get-tuple-element.57.refs_0_, f32[2048,256]{1,0:T(8,128)S(1)} %get-tuple-element.58.refs_1_, ...), custom_call_target="tpu_custom_call" | custom-call | flops 2000000000 | bytes 1024 | tf_op jit(solution)/shard_map/fold/pallas_call | solution.py:225
  15.9 2.5 %fold.3 = (f32[2048,128]{1,0:T(8,128)S(1)}, f32[2048,256]{1,0:T(8,128)S(1)}) custom-call(bf16[2048,128]{1,0:T(8,128)(2,1)S(1)} %get-tuple-element.48.query_rows, f32[256,1]{1,0:T(8,128)S(1)} %get-tuple-element.53.ids, bf16[272,256]{1,0:T(8,128)(2,1)S(1)} %collective-permute-done.4.refs_0_, ...), custom_call_target="tpu_custom_call", output_to_operand_aliasing={{0}: (4, {}), {1}: (5, {})} | custom-call | flops 2000000000 | bytes 1024 | tf_op jit(solution)/shard_map/fold/pallas_call | solution.py:225
  18.5 0.6 collective-permute-start.6
  19.4 1.1 %more_scores.1 = (f32[2048,768]{1,0:T(8,128)S(1)}, f32[2048,128]{1,0:T(8,128)S(1)}, bf16[768,256]{1,0:T(8,128)(2,1)S(1)}) custom-call(bf16[2048,128]{1,0:T(8,128)(2,1)S(1)} %get-tuple-element.48.query_rows, f32[256,1]{1,0:T(8,128)S(1)} %get-tuple-element.53.ids, bf16[272,256]{1,0:T(8,128)(2,1)S(1)} %collective-permute-done.8.refs_0_, ...), custom_call_target="tpu_custom_call" | custom-call | flops 1500000000 | bytes 1024 | tf_op jit(solution)/shard_map/more_scores/pallas_call | solution.py:225
  20.5 1.6 %attend.2 = (bf16[128,1024]{1,0:T(8,128)(2,1)S(1)}, bf16[128,512]{1,0:T(8,128)(2,1)S(1)}) custom-call(bf16[2048,128]{1,0:T(8,128)(2,1)S(1)} %get-tuple-element.48.query_rows, f32[256,1]{1,0:T(8,128)S(1)} %get-tuple-element.53.ids, bf16[272,256]{1,0:T(8,128)(2,1)S(1)} %collective-permute-done.6.refs_0_, bf16[272,256]{1,0:T(8,128)(2,1)S(1)} %collective-permute-done.7.refs_1_, ...), custom_call_target="tpu_custom_call" | custom-call | flops 10000000 | bytes 1024 | tf_op jit(solution)/shard_map/attend/pallas_call | solution.py:225
  22.4 1.7 %collective-permute-start.10 = (bf16[128,512]{1,0:T(8,128)(2,1)S(1)}, bf16[128,512]{1,0:T(8,128)(2,1)S(1)}, u32[]{:S(2)}, u32[]{:S(2)}) collective-permute-start(bf16[128,512]{1,0:T(8,128)(2,1)S(1)} %get-tuple-element.80), channel_id=1, source_target_pairs={{0,7},{1,0},{2,1},{3,2},{4,3},{5,4},{6,5},{7,6},{8,9},{9,10},{10,1... | collective-permute-start | bytes 393224 | tf_op jit(solution)/shard_map/ppermute | solution.py:264
  24.1 1.6 %attend.3 = (bf16[128,1024]{1,0:T(8,128)(2,1)S(1)}, bf16[128,512]{1,0:T(8,128)(2,1)S(1)}) custom-call(bf16[2048,128]{1,0:T(8,128)(2,1)S(1)} %get-tuple-element.48.query_rows, f32[256,1]{1,0:T(8,128)S(1)} %get-tuple-element.53.ids, bf16[272,256]{1,0:T(8,128)(2,1)S(1)} %collective-permute-done.6.refs_0_, bf16[272,256]{1,0:T(8,128)(2,1)S(1)} %collective-permute-done.7.refs_1_, ...), custom_call_target="tpu_custom_call" | custom-call | flops 10000000 | bytes 1024 | tf_op jit(solution)/shard_map/attend/pallas_call | solution.py:225
  25.6 1.7 %collective-permute-start.16 = (bf16[128,512]{1,0:T(8,128)(2,1)S(1)}, bf16[128,512]{1,0:T(8,128)(2,1)S(1)}, u32[]{:S(2)}, u32[]{:S(2)}) collective-permute-start(bf16[128,512]{1,0:T(8,128)(2,1)S(1)} %get-tuple-element.86), channel_id=1, source_target_pairs={{0,7},{1,0},{2,1},{3,2},{4,3},{5,4},{6,5},{7,6},{8,9},{9,10},{10,1... | collective-permute-start | bytes 393224 | tf_op jit(solution)/shard_map/ppermute | solution.py:264
  27.4 3.9 %collective-permute-start.15 = (bf16[128,1024]{1,0:T(8,128)(2,1)S(1)}, bf16[128,1024]{1,0:T(8,128)(2,1)S(1)}, u32[]{:S(2)}, u32[]{:S(2)}) collective-permute-start(bf16[128,1024]{1,0:T(8,128)(2,1)S(1)} %get-tuple-element.81.own), channel_id=1, source_target_pairs={{0,8},{8,0},{16,24},{24,16},{32,40},{40,32},{48,56},{56,48},{64,72... | collective-permute-start | bytes 786440 | tf_op jit(solution)/shard_map/ppermute | solution.py:248
  31.2 1.1 %project.2 = (bf16[256,512]{1,0:T(8,128)(2,1)S(1)}, bf16[256,512]{1,0:T(8,128)(2,1)S(1)}, bf16[256,512]{1,0:T(8,128)(2,1)S(1)}, bf16[128,512]{1,0:T(8,128)(2,1)S(1)}) custom-call(bf16[128,1024]{1,0:T(8,128)(2,1)S(1)} %get-tuple-element.75.own, bf16[128,1024]{1,0:T(8,128)(2,1)S(1)} %collective-permute-done.9.mate, bf16[1024,4096]{1,0:T(8,128)(2,1)S(1)} %bitcast.2), custom_call_target="tpu_custom_call" | custom-call | flops 10000000 | bytes 1024 | tf_op jit(solution)/shard_map/project/pallas_call | solution.py:225
  32.5 0.8 %collective-permute-start.11 = (bf16[256,512]{1,0:T(8,128)(2,1)S(1)}, bf16[256,512]{1,0:T(8,128)(2,1)S(1)}, u32[]{:S(2)}, u32[]{:S(2)}) collective-permute-start(bf16[256,512]{1,0:T(8,128)(2,1)S(1)} %pad_maximum_fusion), channel_id=1, source_target_pairs={{0,7},{1,0},{2,1},{3,2},{4,3},{5,4},{6,5},{7,6},{8,9},{9,10},{10,1... | collective-permute-start | bytes 786440 | tf_op jit(solution)/shard_map/ppermute | solution.py:264
  33.2 1.1 %project.3 = (bf16[256,512]{1,0:T(8,128)(2,1)S(1)}, bf16[256,512]{1,0:T(8,128)(2,1)S(1)}, bf16[256,512]{1,0:T(8,128)(2,1)S(1)}, bf16[128,512]{1,0:T(8,128)(2,1)S(1)}) custom-call(bf16[128,1024]{1,0:T(8,128)(2,1)S(1)} %get-tuple-element.81.own, bf16[128,1024]{1,0:T(8,128)(2,1)S(1)} %collective-permute-done.15.mate, bf16[1024,4096]{1,0:T(8,128)(2,1)S(1)} %bitcast.2), custom_call_target="tpu_custom_call" | custom-call | flops 10000000 | bytes 1024 | tf_op jit(solution)/shard_map/project/pallas_call | solution.py:225
  34.6 4.4 %collective-permute-done.11 = bf16[256,512]{1,0:T(8,128)(2,1)S(1)} collective-permute-done((bf16[256,512]{1,0:T(8,128)(2,1)S(1)}, bf16[256,512]{1,0:T(8,128)(2,1)S(1)}, u32[]{:S(2)}, u32[]{:S(2)}) %collective-permute-start.11) | collective-permute-done | bytes 262176 | tf_op jit(solution)/shard_map/ppermute | solution.py:264
  39.1 2.6 %collective-permute-done.17 = bf16[256,512]{1,0:T(8,128)(2,1)S(1)} collective-permute-done((bf16[256,512]{1,0:T(8,128)(2,1)S(1)}, bf16[256,512]{1,0:T(8,128)(2,1)S(1)}, u32[]{:S(2)}, u32[]{:S(2)}) %collective-permute-start.17) | collective-permute-done | bytes 262176 | tf_op jit(solution)/shard_map/ppermute | solution.py:264
  41.9 3.6 %collective-permute-done.12 = bf16[256,512]{1,0:T(8,128)(2,1)S(1)} collective-permute-done((bf16[256,512]{1,0:T(8,128)(2,1)S(1)}, bf16[256,512]{1,0:T(8,128)(2,1)S(1)}, u32[]{:S(2)}, u32[]{:S(2)}) %collective-permute-start.12) | collective-permute-done | bytes 262176 | tf_op jit(solution)/shard_map/ppermute | solution.py:264
  45.6 0.6 collective-permute-start.14
  46.2 0.6 %collective-permute-start.13 = (bf16[128,512]{1,0:T(8,128)(2,1)S(1)}, bf16[128,512]{1,0:T(8,128)(2,1)S(1)}, u32[]{:S(2)}, u32[]{:S(2)}) collective-permute-start(bf16[128,512]{1,0:T(8,128)(2,1)S(1)} %get-tuple-element.90), channel_id=1, source_target_pairs={{0,7},{1,0},{2,1},{3,2},{4,3},{5,4},{6,5},{7,6},{8,9},{9,10},{10,1... | collective-permute-start | bytes 393224 | tf_op jit(solution)/shard_map/ppermute | solution.py:264
  46.7 1.6 %collective-permute-done.18 = bf16[256,512]{1,0:T(8,128)(2,1)S(1)} collective-permute-done((bf16[256,512]{1,0:T(8,128)(2,1)S(1)}, bf16[256,512]{1,0:T(8,128)(2,1)S(1)}, u32[]{:S(2)}, u32[]{:S(2)}) %collective-permute-start.18) | collective-permute-done | bytes 262176 | tf_op jit(solution)/shard_map/ppermute | solution.py:264
  48.4 0.6 collective-permute-start.20
  49.0 0.9 %collective-permute-start.19 = (bf16[128,512]{1,0:T(8,128)(2,1)S(1)}, bf16[128,512]{1,0:T(8,128)(2,1)S(1)}, u32[]{:S(2)}, u32[]{:S(2)}) collective-permute-start(bf16[128,512]{1,0:T(8,128)(2,1)S(1)} %get-tuple-element.88), channel_id=1, source_target_pairs={{0,7},{1,0},{2,1},{3,2},{4,3},{5,4},{6,5},{7,6},{8,9},{9,10},{10,1... | collective-permute-start | bytes 393224 | tf_op jit(solution)/shard_map/ppermute | solution.py:264
  50.1 2.9 %collective-permute-done.13.refs_1_ = bf16[128,512]{1,0:T(8,128)(2,1)S(1)} collective-permute-done((bf16[128,512]{1,0:T(8,128)(2,1)S(1)}, bf16[128,512]{1,0:T(8,128)(2,1)S(1)}, u32[]{:S(2)}, u32[]{:S(2)}) %collective-permute-start.13) | collective-permute-done | bytes 131104 | tf_op jit(solution)/shard_map/ppermute | solution.py:264
  52.9 3.9 %collective-permute-done.19.refs_4_ = bf16[128,512]{1,0:T(8,128)(2,1)S(1)} collective-permute-done((bf16[128,512]{1,0:T(8,128)(2,1)S(1)}, bf16[128,512]{1,0:T(8,128)(2,1)S(1)}, u32[]{:S(2)}, u32[]{:S(2)}) %collective-permute-start.19) | collective-permute-done | bytes 131104 | tf_op jit(solution)/shard_map/ppermute | solution.py:264
  56.8 0.8 %finish.1 = bf16[256,512]{1,0:T(8,128)(2,1)} custom-call(bf16[128,512]{1,0:T(8,128)(2,1)S(1)} %get-tuple-element.76.refs_0_, bf16[128,512]{1,0:T(8,128)(2,1)S(1)} %collective-permute-done.13.refs_1_, bf16[128,512]{1,0:T(8,128)(2,1)S(1)} %collective-permute-done.14.refs_2_, bf16[128,512]{1,0:T(8,128)(2,1)S(1)} %get-tuple-element.82.refs_3_, ...), custom_call_target="tpu_custom_call" | custom-call | flops 500000000 | bytes 1024 | tf_op jit(solution)/shard_map/finish/pallas_call | solution.py:225
  (39 shorter events, 2.1 us)
Async XLA Ops:
  0.0 9.5 %collective-permute-start = (bf16[256,256]{1,0:T(8,128)(2,1)}, bf16[256,256]{1,0:T(8,128)(2,1)S(1)}, u32[]{:S(2)}, u32[]{:S(2)}) collective-permute-start(bf16[256,256]{1,0:T(8,128)(2,1)} %key_values.1), channel_id=1, source_target_pairs={{0,64},{8,72},{16,80},{24,88},{32,96},{40,104},{48,112},{56,120},{... | collective-permute-start | bytes 393224 | tf_op jit(solution)/shard_map/ppermute | solution.py:252
  2.7 6.8 %collective-permute-start.1 = (f32[1,256]{1,0:T(1,128)S(1)}, f32[1,256]{1,0:T(1,128)S(1)}, u32[]{:S(2)}, u32[]{:S(2)}) collective-permute-start(f32[1,256]{1,0:T(1,128)S(1)} %bitcast.3), channel_id=1, source_target_pairs={{0,64},{8,72},{16,80},{24,88},{32,96},{40,104},{48,112},{56,120},{... | collective-permute-start | bytes 3080 | tf_op jit(solution)/shard_map/ppermute | solution.py:252
  3.9 0.9 %copy-start.1 = (bf16[256,256]{1,0:T(8,128)(2,1)S(1)}, bf16[256,256]{1,0:T(8,128)(2,1)}, u32[]{:S(2)}) copy-start(bf16[256,256]{1,0:T(8,128)(2,1)} %key_values.1) | copy-start | bytes 393220
  5.0 10.9 %collective-permute-start.5 = (bf16[272,256]{1,0:T(8,128)(2,1)S(1)}, bf16[272,256]{1,0:T(8,128)(2,1)S(1)}, u32[]{:S(2)}, u32[]{:S(2)}) collective-permute-start(bf16[272,256]{1,0:T(8,128)(2,1)S(1)} %get-tuple-element.47.piece.own), channel_id=1, source_target_pairs={{0,32},{8,40},{16,48},{24,56},{32,64},{40,72},{48,80},{56,88},{64,... | collective-permute-start | bytes 417800 | tf_op jit(solution)/shard_map/ppermute | solution.py:252
  7.9 1.0 %copy-start = (bf16[256,1024]{1,0:T(8,128)(2,1)S(1)}, bf16[256,1024]{1,0:T(8,128)(2,1)}, u32[]{:S(2)}) copy-start(bf16[256,1024]{1,0:T(8,128)(2,1)} %queries.1) | copy-start | bytes 1572868
  9.6 8.9 %collective-permute-start.2 = (bf16[272,256]{1,0:T(8,128)(2,1)S(1)}, bf16[272,256]{1,0:T(8,128)(2,1)S(1)}, u32[]{:S(2)}, u32[]{:S(2)}) collective-permute-start(bf16[272,256]{1,0:T(8,128)(2,1)S(1)} %get-tuple-element.54), channel_id=1, source_target_pairs={{0,16},{8,24},{16,32},{24,40},{32,48},{40,56},{48,0},{56,8},{64,80... | collective-permute-start | bytes 417800 | tf_op jit(solution)/shard_map/ppermute | solution.py:256
  10.0 8.4 %collective-permute-start.3 = (bf16[272,256]{1,0:T(8,128)(2,1)S(1)}, bf16[272,256]{1,0:T(8,128)(2,1)S(1)}, u32[]{:S(2)}, u32[]{:S(2)}) collective-permute-start(bf16[272,256]{1,0:T(8,128)(2,1)S(1)} %get-tuple-element.55), channel_id=1, source_target_pairs={{0,48},{8,56},{16,0},{24,8},{32,16},{40,24},{48,32},{56,40},{64,11... | collective-permute-start | bytes 417800 | tf_op jit(solution)/shard_map/ppermute | solution.py:256
  12.3 3.6 %collective-permute-start.4 = (bf16[272,256]{1,0:T(8,128)(2,1)S(1)}, bf16[272,256]{1,0:T(8,128)(2,1)S(1)}, u32[]{:S(2)}, u32[]{:S(2)}) collective-permute-start(bf16[272,256]{1,0:T(8,128)(2,1)S(1)} %get-tuple-element.56), channel_id=1, source_target_pairs={{0,8},{8,0},{16,24},{24,16},{32,40},{40,32},{48,56},{56,48},{64,72... | collective-permute-start | bytes 417800 | tf_op jit(solution)/shard_map/ppermute | solution.py:248
  14.4 6.1 %slice-start = ((s8[8388608]{0:T(1024)(128)(4,1)}), s8[4194304]{0:T(1024)(128)(4,1)S(1)}, s32[]{:S(2)}) async-start(s8[8388608]{0:T(1024)(128)(4,1)} %bitcast.1), calls=%async_computation | async-start | bytes 8388608
  15.8 4.7 %slice-start.1 = ((s8[8388608]{0:T(1024)(128)(4,1)}), s8[4194304]{0:T(1024)(128)(4,1)S(1)}, s32[]{:S(2)}) async-start(s8[8388608]{0:T(1024)(128)(4,1)} %bitcast.1), calls=%async_computation.1 | async-start | bytes 8388608
  15.8 3.5 %collective-permute-start.8 = (bf16[272,256]{1,0:T(8,128)(2,1)S(1)}, bf16[272,256]{1,0:T(8,128)(2,1)S(1)}, u32[]{:S(2)}, u32[]{:S(2)}) collective-permute-start(bf16[272,256]{1,0:T(8,128)(2,1)S(1)} %collective-permute-done.5.refs_1_), channel_id=1, source_target_pairs={{0,8},{8,0},{16,24},{24,16},{32,40},{40,32},{48,56},{56,48},{64,72... | collective-permute-start | bytes 417800 | tf_op jit(solution)/shard_map/ppermute | solution.py:248
  18.5 2.0 %collective-permute-start.6 = (bf16[272,256]{1,0:T(8,128)(2,1)S(1)}, bf16[272,256]{1,0:T(8,128)(2,1)S(1)}, u32[]{:S(2)}, u32[]{:S(2)}) collective-permute-start(bf16[272,256]{1,0:T(8,128)(2,1)S(1)} %collective-permute-done.2.refs_1_), channel_id=1, source_target_pairs={{0,8},{8,0},{16,24},{24,16},{32,40},{40,32},{48,56},{56,48},{64,72... | collective-permute-start | bytes 417800 | tf_op jit(solution)/shard_map/ppermute | solution.py:248
  19.1 1.4 %collective-permute-start.7 = (bf16[272,256]{1,0:T(8,128)(2,1)S(1)}, bf16[272,256]{1,0:T(8,128)(2,1)S(1)}, u32[]{:S(2)}, u32[]{:S(2)}) collective-permute-start(bf16[272,256]{1,0:T(8,128)(2,1)S(1)} %collective-permute-done.3.refs_2_), channel_id=1, source_target_pairs={{0,8},{8,0},{16,24},{24,16},{32,40},{40,32},{48,56},{56,48},{64,72... | collective-permute-start | bytes 417800 | tf_op jit(solution)/shard_map/ppermute | solution.py:248
  22.1 9.1 %collective-permute-start.9 = (bf16[128,1024]{1,0:T(8,128)(2,1)S(1)}, bf16[128,1024]{1,0:T(8,128)(2,1)S(1)}, u32[]{:S(2)}, u32[]{:S(2)}) collective-permute-start(bf16[128,1024]{1,0:T(8,128)(2,1)S(1)} %get-tuple-element.75.own), channel_id=1, source_target_pairs={{0,8},{8,0},{16,24},{24,16},{32,40},{40,32},{48,56},{56,48},{64,72... | collective-permute-start | bytes 786440 | tf_op jit(solution)/shard_map/ppermute | solution.py:248
  22.4 10.0 %collective-permute-start.10 = (bf16[128,512]{1,0:T(8,128)(2,1)S(1)}, bf16[128,512]{1,0:T(8,128)(2,1)S(1)}, u32[]{:S(2)}, u32[]{:S(2)}) collective-permute-start(bf16[128,512]{1,0:T(8,128)(2,1)S(1)} %get-tuple-element.80), channel_id=1, source_target_pairs={{0,7},{1,0},{2,1},{3,2},{4,3},{5,4},{6,5},{7,6},{8,9},{9,10},{10,1... | collective-permute-start | bytes 393224 | tf_op jit(solution)/shard_map/ppermute | solution.py:264
  25.6 8.7 %collective-permute-start.16 = (bf16[128,512]{1,0:T(8,128)(2,1)S(1)}, bf16[128,512]{1,0:T(8,128)(2,1)S(1)}, u32[]{:S(2)}, u32[]{:S(2)}) collective-permute-start(bf16[128,512]{1,0:T(8,128)(2,1)S(1)} %get-tuple-element.86), channel_id=1, source_target_pairs={{0,7},{1,0},{2,1},{3,2},{4,3},{5,4},{6,5},{7,6},{8,9},{9,10},{10,1... | collective-permute-start | bytes 393224 | tf_op jit(solution)/shard_map/ppermute | solution.py:264
  27.4 5.9 %collective-permute-start.15 = (bf16[128,1024]{1,0:T(8,128)(2,1)S(1)}, bf16[128,1024]{1,0:T(8,128)(2,1)S(1)}, u32[]{:S(2)}, u32[]{:S(2)}) collective-permute-start(bf16[128,1024]{1,0:T(8,128)(2,1)S(1)} %get-tuple-element.81.own), channel_id=1, source_target_pairs={{0,8},{8,0},{16,24},{24,16},{32,40},{40,32},{48,56},{56,48},{64,72... | collective-permute-start | bytes 786440 | tf_op jit(solution)/shard_map/ppermute | solution.py:248
  32.5 6.5 %collective-permute-start.11 = (bf16[256,512]{1,0:T(8,128)(2,1)S(1)}, bf16[256,512]{1,0:T(8,128)(2,1)S(1)}, u32[]{:S(2)}, u32[]{:S(2)}) collective-permute-start(bf16[256,512]{1,0:T(8,128)(2,1)S(1)} %pad_maximum_fusion), channel_id=1, source_target_pairs={{0,7},{1,0},{2,1},{3,2},{4,3},{5,4},{6,5},{7,6},{8,9},{9,10},{10,1... | collective-permute-start | bytes 786440 | tf_op jit(solution)/shard_map/ppermute | solution.py:264
  34.5 7.3 %collective-permute-start.17 = (bf16[256,512]{1,0:T(8,128)(2,1)S(1)}, bf16[256,512]{1,0:T(8,128)(2,1)S(1)}, u32[]{:S(2)}, u32[]{:S(2)}) collective-permute-start(bf16[256,512]{1,0:T(8,128)(2,1)S(1)} %pad_maximum_fusion.1), channel_id=1, source_target_pairs={{0,7},{1,0},{2,1},{3,2},{4,3},{5,4},{6,5},{7,6},{8,9},{9,10},{10,1... | collective-permute-start | bytes 786440 | tf_op jit(solution)/shard_map/ppermute | solution.py:264
  39.0 6.5 %collective-permute-start.12 = (bf16[256,512]{1,0:T(8,128)(2,1)S(1)}, bf16[256,512]{1,0:T(8,128)(2,1)S(1)}, u32[]{:S(2)}, u32[]{:S(2)}) collective-permute-start(bf16[256,512]{1,0:T(8,128)(2,1)S(1)} %add.25), channel_id=1, source_target_pairs={{0,7},{1,0},{2,1},{3,2},{4,3},{5,4},{6,5},{7,6},{8,9},{9,10},{10,1... | collective-permute-start | bytes 786440 | tf_op jit(solution)/shard_map/ppermute | solution.py:264
  41.8 6.5 %collective-permute-start.18 = (bf16[256,512]{1,0:T(8,128)(2,1)S(1)}, bf16[256,512]{1,0:T(8,128)(2,1)S(1)}, u32[]{:S(2)}, u32[]{:S(2)}) collective-permute-start(bf16[256,512]{1,0:T(8,128)(2,1)S(1)} %add.29), channel_id=1, source_target_pairs={{0,7},{1,0},{2,1},{3,2},{4,3},{5,4},{6,5},{7,6},{8,9},{9,10},{10,1... | collective-permute-start | bytes 786440 | tf_op jit(solution)/shard_map/ppermute | solution.py:264
  45.6 4.5 %collective-permute-start.14 = (bf16[128,512]{1,0:T(8,128)(2,1)S(1)}, bf16[128,512]{1,0:T(8,128)(2,1)S(1)}, u32[]{:S(2)}, u32[]{:S(2)}) collective-permute-start(bf16[128,512]{1,0:T(8,128)(2,1)S(1)} %get-tuple-element.89), channel_id=1, source_target_pairs={{0,15},{1,8},{2,9},{3,10},{4,11},{5,12},{6,13},{7,14},{8,1},{9,2},... | collective-permute-start | bytes 393224 | tf_op jit(solution)/shard_map/ppermute | solution.py:264
  46.2 6.8 %collective-permute-start.13 = (bf16[128,512]{1,0:T(8,128)(2,1)S(1)}, bf16[128,512]{1,0:T(8,128)(2,1)S(1)}, u32[]{:S(2)}, u32[]{:S(2)}) collective-permute-start(bf16[128,512]{1,0:T(8,128)(2,1)S(1)} %get-tuple-element.90), channel_id=1, source_target_pairs={{0,7},{1,0},{2,1},{3,2},{4,3},{5,4},{6,5},{7,6},{8,9},{9,10},{10,1... | collective-permute-start | bytes 393224 | tf_op jit(solution)/shard_map/ppermute | solution.py:264
  48.4 4.5 %collective-permute-start.20 = (bf16[128,512]{1,0:T(8,128)(2,1)S(1)}, bf16[128,512]{1,0:T(8,128)(2,1)S(1)}, u32[]{:S(2)}, u32[]{:S(2)}) collective-permute-start(bf16[128,512]{1,0:T(8,128)(2,1)S(1)} %get-tuple-element.87), channel_id=1, source_target_pairs={{0,15},{1,8},{2,9},{3,10},{4,11},{5,12},{6,13},{7,14},{8,1},{9,2},... | collective-permute-start | bytes 393224 | tf_op jit(solution)/shard_map/ppermute | solution.py:264
  49.0 7.9 %collective-permute-start.19 = (bf16[128,512]{1,0:T(8,128)(2,1)S(1)}, bf16[128,512]{1,0:T(8,128)(2,1)S(1)}, u32[]{:S(2)}, u32[]{:S(2)}) collective-permute-start(bf16[128,512]{1,0:T(8,128)(2,1)S(1)} %get-tuple-element.88), channel_id=1, source_target_pairs={{0,7},{1,0},{2,1},{3,2},{4,3},{5,4},{6,5},{7,6},{8,9},{9,10},{10,1... | collective-permute-start | bytes 393224 | tf_op jit(solution)/shard_map/ppermute | solution.py:264

commit v10 on v9

--- a/solution.py
+++ b/solution.py
@@ -55,7 +55,7 @@
 def pick_kernel(own, far, far_ids, ids, beside, ids_again, packed, *relayed):
     chip, core = place()
     ids_again[...] = ids[...]
-    write_piece(packed, far[...], far_ids[...])
+    write_piece(packed, far[...], far_ids[...].astype(F32))
 
     for steps, piece in zip((1, 3), relayed):
         inside = chip % 4 + steps < 4
@@ -267,8 +267,8 @@
     column = shape(TOK, 1, F32)
     far = from_chip(key_values, 4)
     row = prompt_ids.astype(F32)[None, :]
-    far_ids = from_chip(row, 4)
-    own, ids = call(pack_kernel, "pack", 0.1, [piece, column], key_values, row)
+    far_ids = from_chip(prompt_ids[None, :], 4)
+    own, ids = call(pack_kernel, "pack", 2.0, [piece, column], key_values, row)
     chip2 = from_chip(own, 2)
     query_rows, *kept = call(
         own_kernel, "own_scores", 0.1, [shape(ROWS, HD)] + kept_shapes(1), queries, ids, own
@@ -344,8 +344,12 @@
         )
         moved = along(jnp.concatenate([one[:PART] + extra, one[PART:]], axis=0))
         moved = along(two + moved)
-        ends += [mine, along(three[:PART] + moved[:PART])]
-        ends += [along(three[PART:] + moved[PART:], swap=1)]
+        if part == 0:
+            moved = along(three + moved)
+            ends += [mine, moved[:PART], to_mate(moved[PART:])]
+        else:
+            ends += [mine, along(three[:PART] + moved[:PART])]
+            ends += [along(three[PART:] + moved[PART:], swap=1)]
     return call(finish_kernel, "finish", 0.5, shape(TOK, CHUNK), *ends)
 
 

time: 57.8 us -> 56.7 us (0.981)
  local copies, waits for them, and re-layouts: 1.96 us -> 0.94 us
  starting transfers between devices: 23.3 us -> 24.2 us
  waiting for transfers between devices: 19.2 us -> 18.3 us
    ppermute x6 -> x7, starting transfers between devices: 7.21 us -> 9.41 us  [to_mate(): return lax.ppermute(value, 'loop', [(i, i ^ 1) for i in range(stretches)])]
    ppermute x10 -> x9, starting transfers between devices: 7.12 us -> 5.76 us  [along(): return lax.ppermute(value, ('loop', 'tp'), pairs)]
    unnamed x8, local copies, waits for them, and re-layouts: 1.96 us -> 0.92 us
    ppermute x10 -> x9, waiting for transfers between devices: 19.2 us -> 18.3 us  [along(): return lax.ppermute(value, ('loop', 'tp'), pairs)]
  transfers between devices with their start and end apart: 21 -> 21, of which waited for: 7 -> 6; matrix products, arithmetic and copies ran while one was open for 2% -> 2% of each run, Pallas kernels for 16% -> 17%
where the time goes in v10:
time: 56.7 us; the launch traced here: 56.6 us
  starting transfers between devices  24.2 us (43%)
  waiting for transfers between devices  18.3 us (32%)
  Pallas kernels  11.9 us (21%)
  other arithmetic  1.01 us (2%)
  local copies, waits for them, and re-layouts  0.94 us (2%)
    ppermute x9, waiting for transfers between devices, along(): return lax.ppermute(value, ('loop', 'tp'), pairs)  18.3 us
    pallas_call x11, Pallas kernels, call(): pl.pallas_call(kernel, out_shape=outs, in_specs=[VMEM] * len(args), out_s...  11.9 us
    ppermute x7, starting transfers between devices, to_mate(): return lax.ppermute(value, 'loop', [(i, i ^ 1) for i in range(stretches)])  9.41 us
    ppermute x3, starting transfers between devices, from_chip(): return lax.ppermute(value, 'loop', pairs)  6.24 us
    ppermute x9, starting transfers between devices, along(): return lax.ppermute(value, ('loop', 'tp'), pairs)  5.76 us
    ppermute x2, starting transfers between devices, along_row(): return lax.ppermute(value, 'loop', pairs)  2.75 us
  transfers between devices with their start and end apart: 21, of which 6 were waited for; matrix products, arithmetic and copies ran while one was open for 2% of the time, Pallas kernels for 17%

profile of v10, /device:TPU:1, one launch (start us, length us, event | category | flops | bytes accessed | tf_op | source)
XLA Modules:
  0.0 56.6 jit_solution(7627770378678300700)
XLA Ops:
  0.0 2.0 %collective-permute-start.1 = (s32[1,256]{1,0:T(1,128)}, s32[1,256]{1,0:T(1,128)S(1)}, u32[]{:S(2)}, u32[]{:S(2)}) collective-permute-start(s32[1,256]{1,0:T(1,128)} %bitcast.5), channel_id=1, source_target_pairs={{0,64},{8,72},{16,80},{24,88},{32,96},{40,104},{48,112},{56,120},{... | collective-permute-start | bytes 3080 | tf_op jit(solution)/shard_map/ppermute | solution.py:252
  2.0 1.2 %collective-permute-start = (bf16[256,256]{1,0:T(8,128)(2,1)}, bf16[256,256]{1,0:T(8,128)(2,1)S(1)}, u32[]{:S(2)}, u32[]{:S(2)}) collective-permute-start(bf16[256,256]{1,0:T(8,128)(2,1)} %key_values.1), channel_id=1, source_target_pairs={{0,64},{8,72},{16,80},{24,88},{32,96},{40,104},{48,112},{56,120},{... | collective-permute-start | bytes 393224 | tf_op jit(solution)/shard_map/ppermute | solution.py:252
  3.3 0.7 %convert_element_type.3 = f32[256]{0:T(256)S(1)} convert(s32[256]{0:T(256)} %param.6) | non-fusion elementwise | flops 256 | bytes 2048 | tf_op jit(solution)/shard_map/convert_element_type | solution.py:269
  3.9 0.9 %copy-done.1 = bf16[256,256]{1,0:T(8,128)(2,1)S(1)} copy-done((bf16[256,256]{1,0:T(8,128)(2,1)S(1)}, bf16[256,256]{1,0:T(8,128)(2,1)}, u32[]{:S(2)}) %copy-start.1) | copy-done | bytes 131096
  5.0 3.0 %collective-permute-start.5 = (bf16[272,256]{1,0:T(8,128)(2,1)S(1)}, bf16[272,256]{1,0:T(8,128)(2,1)S(1)}, u32[]{:S(2)}, u32[]{:S(2)}) collective-permute-start(bf16[272,256]{1,0:T(8,128)(2,1)S(1)} %get-tuple-element.47.piece.own), channel_id=1, source_target_pairs={{0,32},{8,40},{16,48},{24,56},{32,64},{40,72},{48,80},{56,88},{64,... | collective-permute-start | bytes 417800 | tf_op jit(solution)/shard_map/ppermute | solution.py:252
  8.0 0.5 own_scores.1
  8.5 0.5 collective-permute-start.2
  9.0 2.3 %collective-permute-start.3 = (bf16[272,256]{1,0:T(8,128)(2,1)S(1)}, bf16[272,256]{1,0:T(8,128)(2,1)S(1)}, u32[]{:S(2)}, u32[]{:S(2)}) collective-permute-start(bf16[272,256]{1,0:T(8,128)(2,1)S(1)} %get-tuple-element.55), channel_id=1, source_target_pairs={{0,48},{8,56},{16,0},{24,8},{32,16},{40,24},{48,32},{56,40},{64,11... | collective-permute-start | bytes 417800 | tf_op jit(solution)/shard_map/ppermute | solution.py:256
  11.3 2.1 %collective-permute-start.4 = (bf16[272,256]{1,0:T(8,128)(2,1)S(1)}, bf16[272,256]{1,0:T(8,128)(2,1)S(1)}, u32[]{:S(2)}, u32[]{:S(2)}) collective-permute-start(bf16[272,256]{1,0:T(8,128)(2,1)S(1)} %get-tuple-element.56), channel_id=1, source_target_pairs={{0,8},{8,0},{16,24},{24,16},{32,40},{40,32},{48,56},{56,48},{64,72... | collective-permute-start | bytes 417800 | tf_op jit(solution)/shard_map/ppermute | solution.py:248
  13.4 1.4 %fold.2 = (f32[2048,128]{1,0:T(8,128)S(1)}, f32[2048,256]{1,0:T(8,128)S(1)}) custom-call(bf16[2048,128]{1,0:T(8,128)(2,1)S(1)} %get-tuple-element.48.query_rows, f32[256,1]{1,0:T(8,128)S(1)} %get-tuple-element.53.ids, bf16[272,256]{1,0:T(8,128)(2,1)S(1)} %get-tuple-element.57.refs_0_, f32[2048,256]{1,0:T(8,128)S(1)} %get-tuple-element.58.refs_1_, ...), custom_call_target="tpu_custom_call" | custom-call | flops 2000000000 | bytes 1024 | tf_op jit(solution)/shard_map/fold/pallas_call | solution.py:225
  14.8 0.4 collective-permute-start.8
  15.2 2.5 %fold.3 = (f32[2048,128]{1,0:T(8,128)S(1)}, f32[2048,256]{1,0:T(8,128)S(1)}) custom-call(bf16[2048,128]{1,0:T(8,128)(2,1)S(1)} %get-tuple-element.48.query_rows, f32[256,1]{1,0:T(8,128)S(1)} %get-tuple-element.53.ids, bf16[272,256]{1,0:T(8,128)(2,1)S(1)} %collective-permute-done.4.refs_0_, ...), custom_call_target="tpu_custom_call", output_to_operand_aliasing={{0}: (4, {}), {1}: (5, {})} | custom-call | flops 2000000000 | bytes 1024 | tf_op jit(solution)/shard_map/fold/pallas_call | solution.py:225
  18.3 1.1 %more_scores.1 = (f32[2048,768]{1,0:T(8,128)S(1)}, f32[2048,128]{1,0:T(8,128)S(1)}, bf16[768,256]{1,0:T(8,128)(2,1)S(1)}) custom-call(bf16[2048,128]{1,0:T(8,128)(2,1)S(1)} %get-tuple-element.48.query_rows, f32[256,1]{1,0:T(8,128)S(1)} %get-tuple-element.53.ids, bf16[272,256]{1,0:T(8,128)(2,1)S(1)} %collective-permute-done.8.refs_0_, ...), custom_call_target="tpu_custom_call" | custom-call | flops 1500000000 | bytes 1024 | tf_op jit(solution)/shard_map/more_scores/pallas_call | solution.py:225
  19.5 1.6 %attend.2 = (bf16[128,1024]{1,0:T(8,128)(2,1)S(1)}, bf16[128,512]{1,0:T(8,128)(2,1)S(1)}) custom-call(bf16[2048,128]{1,0:T(8,128)(2,1)S(1)} %get-tuple-element.48.query_rows, f32[256,1]{1,0:T(8,128)S(1)} %get-tuple-element.53.ids, bf16[272,256]{1,0:T(8,128)(2,1)S(1)} %collective-permute-done.6.refs_0_, bf16[272,256]{1,0:T(8,128)(2,1)S(1)} %collective-permute-done.7.refs_1_, ...), custom_call_target="tpu_custom_call" | custom-call | flops 10000000 | bytes 1024 | tf_op jit(solution)/shard_map/attend/pallas_call | solution.py:225
  21.1 0.4 collective-permute-start.9
  21.4 1.7 %collective-permute-start.10 = (bf16[128,512]{1,0:T(8,128)(2,1)S(1)}, bf16[128,512]{1,0:T(8,128)(2,1)S(1)}, u32[]{:S(2)}, u32[]{:S(2)}) collective-permute-start(bf16[128,512]{1,0:T(8,128)(2,1)S(1)} %get-tuple-element.80), channel_id=1, source_target_pairs={{0,7},{1,0},{2,1},{3,2},{4,3},{5,4},{6,5},{7,6},{8,9},{9,10},{10,1... | collective-permute-start | bytes 393224 | tf_op jit(solution)/shard_map/ppermute | solution.py:264
  23.1 1.6 %attend.3 = (bf16[128,1024]{1,0:T(8,128)(2,1)S(1)}, bf16[128,512]{1,0:T(8,128)(2,1)S(1)}) custom-call(bf16[2048,128]{1,0:T(8,128)(2,1)S(1)} %get-tuple-element.48.query_rows, f32[256,1]{1,0:T(8,128)S(1)} %get-tuple-element.53.ids, bf16[272,256]{1,0:T(8,128)(2,1)S(1)} %collective-permute-done.6.refs_0_, bf16[272,256]{1,0:T(8,128)(2,1)S(1)} %collective-permute-done.7.refs_1_, ...), custom_call_target="tpu_custom_call" | custom-call | flops 10000000 | bytes 1024 | tf_op jit(solution)/shard_map/attend/pallas_call | solution.py:225
  24.7 1.7 %collective-permute-start.16 = (bf16[128,512]{1,0:T(8,128)(2,1)S(1)}, bf16[128,512]{1,0:T(8,128)(2,1)S(1)}, u32[]{:S(2)}, u32[]{:S(2)}) collective-permute-start(bf16[128,512]{1,0:T(8,128)(2,1)S(1)} %get-tuple-element.86), channel_id=1, source_target_pairs={{0,7},{1,0},{2,1},{3,2},{4,3},{5,4},{6,5},{7,6},{8,9},{9,10},{10,1... | collective-permute-start | bytes 393224 | tf_op jit(solution)/shard_map/ppermute | solution.py:264
  26.4 3.8 %collective-permute-start.15 = (bf16[128,1024]{1,0:T(8,128)(2,1)S(1)}, bf16[128,1024]{1,0:T(8,128)(2,1)S(1)}, u32[]{:S(2)}, u32[]{:S(2)}) collective-permute-start(bf16[128,1024]{1,0:T(8,128)(2,1)S(1)} %get-tuple-element.81.own), channel_id=1, source_target_pairs={{0,8},{8,0},{16,24},{24,16},{32,40},{40,32},{48,56},{56,48},{64,72... | collective-permute-start | bytes 786440 | tf_op jit(solution)/shard_map/ppermute | solution.py:248
  30.2 1.1 %project.2 = (bf16[256,512]{1,0:T(8,128)(2,1)S(1)}, bf16[256,512]{1,0:T(8,128)(2,1)S(1)}, bf16[256,512]{1,0:T(8,128)(2,1)S(1)}, bf16[128,512]{1,0:T(8,128)(2,1)S(1)}) custom-call(bf16[128,1024]{1,0:T(8,128)(2,1)S(1)} %get-tuple-element.75.own, bf16[128,1024]{1,0:T(8,128)(2,1)S(1)} %collective-permute-done.9.mate, bf16[1024,4096]{1,0:T(8,128)(2,1)S(1)} %bitcast.3), custom_call_target="tpu_custom_call" | custom-call | flops 10000000 | bytes 1024 | tf_op jit(solution)/shard_map/project/pallas_call | solution.py:225
  31.4 0.8 %collective-permute-start.11 = (bf16[256,512]{1,0:T(8,128)(2,1)S(1)}, bf16[256,512]{1,0:T(8,128)(2,1)S(1)}, u32[]{:S(2)}, u32[]{:S(2)}) collective-permute-start(bf16[256,512]{1,0:T(8,128)(2,1)S(1)} %pad_maximum_fusion), channel_id=1, source_target_pairs={{0,7},{1,0},{2,1},{3,2},{4,3},{5,4},{6,5},{7,6},{8,9},{9,10},{10,1... | collective-permute-start | bytes 786440 | tf_op jit(solution)/shard_map/ppermute | solution.py:264
  32.2 1.1 %project.3 = (bf16[256,512]{1,0:T(8,128)(2,1)S(1)}, bf16[256,512]{1,0:T(8,128)(2,1)S(1)}, bf16[256,512]{1,0:T(8,128)(2,1)S(1)}, bf16[128,512]{1,0:T(8,128)(2,1)S(1)}) custom-call(bf16[128,1024]{1,0:T(8,128)(2,1)S(1)} %get-tuple-element.81.own, bf16[128,1024]{1,0:T(8,128)(2,1)S(1)} %collective-permute-done.15.mate, bf16[1024,4096]{1,0:T(8,128)(2,1)S(1)} %bitcast.3), custom_call_target="tpu_custom_call" | custom-call | flops 10000000 | bytes 1024 | tf_op jit(solution)/shard_map/project/pallas_call | solution.py:225
  33.5 4.4 %collective-permute-done.11 = bf16[256,512]{1,0:T(8,128)(2,1)S(1)} collective-permute-done((bf16[256,512]{1,0:T(8,128)(2,1)S(1)}, bf16[256,512]{1,0:T(8,128)(2,1)S(1)}, u32[]{:S(2)}, u32[]{:S(2)}) %collective-permute-start.11) | collective-permute-done | bytes 262176 | tf_op jit(solution)/shard_map/ppermute | solution.py:264
  38.1 2.6 %collective-permute-done.17 = bf16[256,512]{1,0:T(8,128)(2,1)S(1)} collective-permute-done((bf16[256,512]{1,0:T(8,128)(2,1)S(1)}, bf16[256,512]{1,0:T(8,128)(2,1)S(1)}, u32[]{:S(2)}, u32[]{:S(2)}) %collective-permute-start.17) | collective-permute-done | bytes 262176 | tf_op jit(solution)/shard_map/ppermute | solution.py:264
  40.9 3.6 %collective-permute-done.12 = bf16[256,512]{1,0:T(8,128)(2,1)S(1)} collective-permute-done((bf16[256,512]{1,0:T(8,128)(2,1)S(1)}, bf16[256,512]{1,0:T(8,128)(2,1)S(1)}, u32[]{:S(2)}, u32[]{:S(2)}) %collective-permute-start.12) | collective-permute-done | bytes 262176 | tf_op jit(solution)/shard_map/ppermute | solution.py:264
  44.7 2.6 %collective-permute-done.18 = bf16[256,512]{1,0:T(8,128)(2,1)S(1)} collective-permute-done((bf16[256,512]{1,0:T(8,128)(2,1)S(1)}, bf16[256,512]{1,0:T(8,128)(2,1)S(1)}, u32[]{:S(2)}, u32[]{:S(2)}) %collective-permute-start.18) | collective-permute-done | bytes 262176 | tf_op jit(solution)/shard_map/ppermute | solution.py:264
  47.4 0.6 %collective-permute-start.20 = (bf16[128,512]{1,0:T(8,128)(2,1)S(1)}, bf16[128,512]{1,0:T(8,128)(2,1)S(1)}, u32[]{:S(2)}, u32[]{:S(2)}) collective-permute-start(bf16[128,512]{1,0:T(8,128)(2,1)S(1)} %get-tuple-element.87), channel_id=1, source_target_pairs={{0,15},{1,8},{2,9},{3,10},{4,11},{5,12},{6,13},{7,14},{8,1},{9,2},... | collective-permute-start | bytes 393224 | tf_op jit(solution)/shard_map/ppermute | solution.py:264
  47.9 0.6 %collective-permute-start.19 = (bf16[128,512]{1,0:T(8,128)(2,1)S(1)}, bf16[128,512]{1,0:T(8,128)(2,1)S(1)}, u32[]{:S(2)}, u32[]{:S(2)}) collective-permute-start(bf16[128,512]{1,0:T(8,128)(2,1)S(1)} %get-tuple-element.88), channel_id=1, source_target_pairs={{0,7},{1,0},{2,1},{3,2},{4,3},{5,4},{6,5},{7,6},{8,9},{9,10},{10,1... | collective-permute-start | bytes 393224 | tf_op jit(solution)/shard_map/ppermute | solution.py:264
  48.6 2.5 %collective-permute-done.13 = bf16[256,512]{1,0:T(8,128)(2,1)S(1)} collective-permute-done((bf16[256,512]{1,0:T(8,128)(2,1)S(1)}, bf16[256,512]{1,0:T(8,128)(2,1)S(1)}, u32[]{:S(2)}, u32[]{:S(2)}) %collective-permute-start.13) | collective-permute-done | bytes 262176 | tf_op jit(solution)/shard_map/ppermute | solution.py:264
  51.1 2.2 %collective-permute-start.14 = (bf16[128,512]{1,0:T(8,128)(2,1)S(1)}, bf16[128,512]{1,0:T(8,128)(2,1)S(1)}, u32[]{:S(2)}, u32[]{:S(2)}) collective-permute-start(bf16[128,512]{1,0:T(8,128)(2,1)S(1)} %get-tuple-element.91), channel_id=1, source_target_pairs={{0,8},{8,0},{16,24},{24,16},{32,40},{40,32},{48,56},{56,48},{64,72... | collective-permute-start | bytes 393224 | tf_op jit(solution)/shard_map/ppermute | solution.py:248
  53.3 2.4 %collective-permute-done.19.refs_4_ = bf16[128,512]{1,0:T(8,128)(2,1)S(1)} collective-permute-done((bf16[128,512]{1,0:T(8,128)(2,1)S(1)}, bf16[128,512]{1,0:T(8,128)(2,1)S(1)}, u32[]{:S(2)}, u32[]{:S(2)}) %collective-permute-start.19) | collective-permute-done | bytes 131104 | tf_op jit(solution)/shard_map/ppermute | solution.py:264
  55.8 0.8 %finish.1 = bf16[256,512]{1,0:T(8,128)(2,1)} custom-call(bf16[128,512]{1,0:T(8,128)(2,1)S(1)} %get-tuple-element.76.refs_0_, bf16[128,512]{1,0:T(8,128)(2,1)S(1)} %get-tuple-element.92.refs_1_, bf16[128,512]{1,0:T(8,128)(2,1)S(1)} %collective-permute-done.14.refs_2_, bf16[128,512]{1,0:T(8,128)(2,1)S(1)} %get-tuple-element.82.refs_3_, ...), custom_call_target="tpu_custom_call" | custom-call | flops 500000000 | bytes 1024 | tf_op jit(solution)/shard_map/finish/pallas_call | solution.py:225
  (40 shorter events, 1.6 us)
Async XLA Ops:
  0.0 8.5 %collective-permute-start.1 = (s32[1,256]{1,0:T(1,128)}, s32[1,256]{1,0:T(1,128)S(1)}, u32[]{:S(2)}, u32[]{:S(2)}) collective-permute-start(s32[1,256]{1,0:T(1,128)} %bitcast.5), channel_id=1, source_target_pairs={{0,64},{8,72},{16,80},{24,88},{32,96},{40,104},{48,112},{56,120},{... | collective-permute-start | bytes 3080 | tf_op jit(solution)/shard_map/ppermute | solution.py:252
  2.0 6.4 %collective-permute-start = (bf16[256,256]{1,0:T(8,128)(2,1)}, bf16[256,256]{1,0:T(8,128)(2,1)S(1)}, u32[]{:S(2)}, u32[]{:S(2)}) collective-permute-start(bf16[256,256]{1,0:T(8,128)(2,1)} %key_values.1), channel_id=1, source_target_pairs={{0,64},{8,72},{16,80},{24,88},{32,96},{40,104},{48,112},{56,120},{... | collective-permute-start | bytes 393224 | tf_op jit(solution)/shard_map/ppermute | solution.py:252
  3.9 0.9 %copy-start.1 = (bf16[256,256]{1,0:T(8,128)(2,1)S(1)}, bf16[256,256]{1,0:T(8,128)(2,1)}, u32[]{:S(2)}) copy-start(bf16[256,256]{1,0:T(8,128)(2,1)} %key_values.1) | copy-start | bytes 393220
  4.8 3.1 %copy-start = (bf16[256,1024]{1,0:T(8,128)(2,1)S(1)}, bf16[256,1024]{1,0:T(8,128)(2,1)}, u32[]{:S(2)}) copy-start(bf16[256,1024]{1,0:T(8,128)(2,1)} %queries.1) | copy-start | bytes 1572868
  5.0 9.8 %collective-permute-start.5 = (bf16[272,256]{1,0:T(8,128)(2,1)S(1)}, bf16[272,256]{1,0:T(8,128)(2,1)S(1)}, u32[]{:S(2)}, u32[]{:S(2)}) collective-permute-start(bf16[272,256]{1,0:T(8,128)(2,1)S(1)} %get-tuple-element.47.piece.own), channel_id=1, source_target_pairs={{0,32},{8,40},{16,48},{24,56},{32,64},{40,72},{48,80},{56,88},{64,... | collective-permute-start | bytes 417800 | tf_op jit(solution)/shard_map/ppermute | solution.py:252
  8.5 9.2 %collective-permute-start.2 = (bf16[272,256]{1,0:T(8,128)(2,1)S(1)}, bf16[272,256]{1,0:T(8,128)(2,1)S(1)}, u32[]{:S(2)}, u32[]{:S(2)}) collective-permute-start(bf16[272,256]{1,0:T(8,128)(2,1)S(1)} %get-tuple-element.54), channel_id=1, source_target_pairs={{0,16},{8,24},{16,32},{24,40},{32,48},{40,56},{48,0},{56,8},{64,80... | collective-permute-start | bytes 417800 | tf_op jit(solution)/shard_map/ppermute | solution.py:256
  9.0 8.7 %collective-permute-start.3 = (bf16[272,256]{1,0:T(8,128)(2,1)S(1)}, bf16[272,256]{1,0:T(8,128)(2,1)S(1)}, u32[]{:S(2)}, u32[]{:S(2)}) collective-permute-start(bf16[272,256]{1,0:T(8,128)(2,1)S(1)} %get-tuple-element.55), channel_id=1, source_target_pairs={{0,48},{8,56},{16,0},{24,8},{32,16},{40,24},{48,32},{56,40},{64,11... | collective-permute-start | bytes 417800 | tf_op jit(solution)/shard_map/ppermute | solution.py:256
  11.3 3.9 %collective-permute-start.4 = (bf16[272,256]{1,0:T(8,128)(2,1)S(1)}, bf16[272,256]{1,0:T(8,128)(2,1)S(1)}, u32[]{:S(2)}, u32[]{:S(2)}) collective-permute-start(bf16[272,256]{1,0:T(8,128)(2,1)S(1)} %get-tuple-element.56), channel_id=1, source_target_pairs={{0,8},{8,0},{16,24},{24,16},{32,40},{40,32},{48,56},{56,48},{64,72... | collective-permute-start | bytes 417800 | tf_op jit(solution)/shard_map/ppermute | solution.py:248
  13.4 6.1 %slice-start = ((s8[8388608]{0:T(1024)(128)(4,1)}), s8[4194304]{0:T(1024)(128)(4,1)S(1)}, s32[]{:S(2)}) async-start(s8[8388608]{0:T(1024)(128)(4,1)} %bitcast.2), calls=%async_computation | async-start | bytes 8388608
  14.8 4.7 %slice-start.1 = ((s8[8388608]{0:T(1024)(128)(4,1)}), s8[4194304]{0:T(1024)(128)(4,1)S(1)}, s32[]{:S(2)}) async-start(s8[8388608]{0:T(1024)(128)(4,1)} %bitcast.2), calls=%async_computation.1 | async-start | bytes 8388608
  14.8 3.5 %collective-permute-start.8 = (bf16[272,256]{1,0:T(8,128)(2,1)S(1)}, bf16[272,256]{1,0:T(8,128)(2,1)S(1)}, u32[]{:S(2)}, u32[]{:S(2)}) collective-permute-start(bf16[272,256]{1,0:T(8,128)(2,1)S(1)} %collective-permute-done.5.refs_1_), channel_id=1, source_target_pairs={{0,8},{8,0},{16,24},{24,16},{32,40},{40,32},{48,56},{56,48},{64,72... | collective-permute-start | bytes 417800 | tf_op jit(solution)/shard_map/ppermute | solution.py:248
  17.7 1.7 %collective-permute-start.6 = (bf16[272,256]{1,0:T(8,128)(2,1)S(1)}, bf16[272,256]{1,0:T(8,128)(2,1)S(1)}, u32[]{:S(2)}, u32[]{:S(2)}) collective-permute-start(bf16[272,256]{1,0:T(8,128)(2,1)S(1)} %collective-permute-done.2.refs_1_), channel_id=1, source_target_pairs={{0,8},{8,0},{16,24},{24,16},{32,40},{40,32},{48,56},{56,48},{64,72... | collective-permute-start | bytes 417800 | tf_op jit(solution)/shard_map/ppermute | solution.py:248
  18.0 1.4 %collective-permute-start.7 = (bf16[272,256]{1,0:T(8,128)(2,1)S(1)}, bf16[272,256]{1,0:T(8,128)(2,1)S(1)}, u32[]{:S(2)}, u32[]{:S(2)}) collective-permute-start(bf16[272,256]{1,0:T(8,128)(2,1)S(1)} %collective-permute-done.3.refs_2_), channel_id=1, source_target_pairs={{0,8},{8,0},{16,24},{24,16},{32,40},{40,32},{48,56},{56,48},{64,72... | collective-permute-start | bytes 417800 | tf_op jit(solution)/shard_map/ppermute | solution.py:248
  21.1 9.1 %collective-permute-start.9 = (bf16[128,1024]{1,0:T(8,128)(2,1)S(1)}, bf16[128,1024]{1,0:T(8,128)(2,1)S(1)}, u32[]{:S(2)}, u32[]{:S(2)}) collective-permute-start(bf16[128,1024]{1,0:T(8,128)(2,1)S(1)} %get-tuple-element.75.own), channel_id=1, source_target_pairs={{0,8},{8,0},{16,24},{24,16},{32,40},{40,32},{48,56},{56,48},{64,72... | collective-permute-start | bytes 786440 | tf_op jit(solution)/shard_map/ppermute | solution.py:248
  21.4 9.9 %collective-permute-start.10 = (bf16[128,512]{1,0:T(8,128)(2,1)S(1)}, bf16[128,512]{1,0:T(8,128)(2,1)S(1)}, u32[]{:S(2)}, u32[]{:S(2)}) collective-permute-start(bf16[128,512]{1,0:T(8,128)(2,1)S(1)} %get-tuple-element.80), channel_id=1, source_target_pairs={{0,7},{1,0},{2,1},{3,2},{4,3},{5,4},{6,5},{7,6},{8,9},{9,10},{10,1... | collective-permute-start | bytes 393224 | tf_op jit(solution)/shard_map/ppermute | solution.py:264
  24.7 8.7 %collective-permute-start.16 = (bf16[128,512]{1,0:T(8,128)(2,1)S(1)}, bf16[128,512]{1,0:T(8,128)(2,1)S(1)}, u32[]{:S(2)}, u32[]{:S(2)}) collective-permute-start(bf16[128,512]{1,0:T(8,128)(2,1)S(1)} %get-tuple-element.86), channel_id=1, source_target_pairs={{0,7},{1,0},{2,1},{3,2},{4,3},{5,4},{6,5},{7,6},{8,9},{9,10},{10,1... | collective-permute-start | bytes 393224 | tf_op jit(solution)/shard_map/ppermute | solution.py:264
  26.4 5.8 %collective-permute-start.15 = (bf16[128,1024]{1,0:T(8,128)(2,1)S(1)}, bf16[128,1024]{1,0:T(8,128)(2,1)S(1)}, u32[]{:S(2)}, u32[]{:S(2)}) collective-permute-start(bf16[128,1024]{1,0:T(8,128)(2,1)S(1)} %get-tuple-element.81.own), channel_id=1, source_target_pairs={{0,8},{8,0},{16,24},{24,16},{32,40},{40,32},{48,56},{56,48},{64,72... | collective-permute-start | bytes 786440 | tf_op jit(solution)/shard_map/ppermute | solution.py:248
  31.4 6.5 %collective-permute-start.11 = (bf16[256,512]{1,0:T(8,128)(2,1)S(1)}, bf16[256,512]{1,0:T(8,128)(2,1)S(1)}, u32[]{:S(2)}, u32[]{:S(2)}) collective-permute-start(bf16[256,512]{1,0:T(8,128)(2,1)S(1)} %pad_maximum_fusion), channel_id=1, source_target_pairs={{0,7},{1,0},{2,1},{3,2},{4,3},{5,4},{6,5},{7,6},{8,9},{9,10},{10,1... | collective-permute-start | bytes 786440 | tf_op jit(solution)/shard_map/ppermute | solution.py:264
  33.4 7.3 %collective-permute-start.17 = (bf16[256,512]{1,0:T(8,128)(2,1)S(1)}, bf16[256,512]{1,0:T(8,128)(2,1)S(1)}, u32[]{:S(2)}, u32[]{:S(2)}) collective-permute-start(bf16[256,512]{1,0:T(8,128)(2,1)S(1)} %pad_maximum_fusion.1), channel_id=1, source_target_pairs={{0,7},{1,0},{2,1},{3,2},{4,3},{5,4},{6,5},{7,6},{8,9},{9,10},{10,1... | collective-permute-start | bytes 786440 | tf_op jit(solution)/shard_map/ppermute | solution.py:264
  38.0 6.5 %collective-permute-start.12 = (bf16[256,512]{1,0:T(8,128)(2,1)S(1)}, bf16[256,512]{1,0:T(8,128)(2,1)S(1)}, u32[]{:S(2)}, u32[]{:S(2)}) collective-permute-start(bf16[256,512]{1,0:T(8,128)(2,1)S(1)} %add.22), channel_id=1, source_target_pairs={{0,7},{1,0},{2,1},{3,2},{4,3},{5,4},{6,5},{7,6},{8,9},{9,10},{10,1... | collective-permute-start | bytes 786440 | tf_op jit(solution)/shard_map/ppermute | solution.py:264
  40.8 6.5 %collective-permute-start.18 = (bf16[256,512]{1,0:T(8,128)(2,1)S(1)}, bf16[256,512]{1,0:T(8,128)(2,1)S(1)}, u32[]{:S(2)}, u32[]{:S(2)}) collective-permute-start(bf16[256,512]{1,0:T(8,128)(2,1)S(1)} %add.25), channel_id=1, source_target_pairs={{0,7},{1,0},{2,1},{3,2},{4,3},{5,4},{6,5},{7,6},{8,9},{9,10},{10,1... | collective-permute-start | bytes 786440 | tf_op jit(solution)/shard_map/ppermute | solution.py:264
  44.6 6.5 %collective-permute-start.13 = (bf16[256,512]{1,0:T(8,128)(2,1)S(1)}, bf16[256,512]{1,0:T(8,128)(2,1)S(1)}, u32[]{:S(2)}, u32[]{:S(2)}) collective-permute-start(bf16[256,512]{1,0:T(8,128)(2,1)S(1)} %add.23), channel_id=1, source_target_pairs={{0,7},{1,0},{2,1},{3,2},{4,3},{5,4},{6,5},{7,6},{8,9},{9,10},{10,1... | collective-permute-start | bytes 786440 | tf_op jit(solution)/shard_map/ppermute | solution.py:264
  47.4 5.9 %collective-permute-start.20 = (bf16[128,512]{1,0:T(8,128)(2,1)S(1)}, bf16[128,512]{1,0:T(8,128)(2,1)S(1)}, u32[]{:S(2)}, u32[]{:S(2)}) collective-permute-start(bf16[128,512]{1,0:T(8,128)(2,1)S(1)} %get-tuple-element.87), channel_id=1, source_target_pairs={{0,15},{1,8},{2,9},{3,10},{4,11},{5,12},{6,13},{7,14},{8,1},{9,2},... | collective-permute-start | bytes 393224 | tf_op jit(solution)/shard_map/ppermute | solution.py:264
  47.9 7.8 %collective-permute-start.19 = (bf16[128,512]{1,0:T(8,128)(2,1)S(1)}, bf16[128,512]{1,0:T(8,128)(2,1)S(1)}, u32[]{:S(2)}, u32[]{:S(2)}) collective-permute-start(bf16[128,512]{1,0:T(8,128)(2,1)S(1)} %get-tuple-element.88), channel_id=1, source_target_pairs={{0,7},{1,0},{2,1},{3,2},{4,3},{5,4},{6,5},{7,6},{8,9},{9,10},{10,1... | collective-permute-start | bytes 393224 | tf_op jit(solution)/shard_map/ppermute | solution.py:264
  51.1 4.6 %collective-permute-start.14 = (bf16[128,512]{1,0:T(8,128)(2,1)S(1)}, bf16[128,512]{1,0:T(8,128)(2,1)S(1)}, u32[]{:S(2)}, u32[]{:S(2)}) collective-permute-start(bf16[128,512]{1,0:T(8,128)(2,1)S(1)} %get-tuple-element.91), channel_id=1, source_target_pairs={{0,8},{8,0},{16,24},{24,16},{32,40},{40,32},{48,56},{56,48},{64,72... | collective-permute-start | bytes 393224 | tf_op jit(solution)/shard_map/ppermute | solution.py:248

commit v11 on v10

--- a/solution.py
+++ b/solution.py
@@ -268,7 +268,7 @@
     far = from_chip(key_values, 4)
     row = prompt_ids.astype(F32)[None, :]
     far_ids = from_chip(prompt_ids[None, :], 4)
-    own, ids = call(pack_kernel, "pack", 2.0, [piece, column], key_values, row)
+    own, ids = call(pack_kernel, "pack", 1.0, [piece, column], key_values, row)
     chip2 = from_chip(own, 2)
     query_rows, *kept = call(
         own_kernel, "own_scores", 0.1, [shape(ROWS, HD)] + kept_shapes(1), queries, ids, own

time: 56.7 us -> 56.7 us (level)
  no operation moved by 1% of the time
where the time goes in v11:
time: 56.7 us; the launch traced here: 56.6 us
  starting transfers between devices  24.1 us (43%)
  waiting for transfers between devices  18.4 us (32%)
  Pallas kernels  11.9 us (21%)
  other arithmetic  1.04 us (2%)
  local copies, waits for them, and re-layouts  0.94 us (2%)
    ppermute x9, waiting for transfers between devices, along(): return lax.ppermute(value, ('loop', 'tp'), pairs)  18.3 us
    pallas_call x11, Pallas kernels, call(): pl.pallas_call(kernel, out_shape=outs, in_specs=[VMEM] * len(args), out_s...  11.9 us
    ppermute x7, starting transfers between devices, to_mate(): return lax.ppermute(value, 'loop', [(i, i ^ 1) for i in range(stretches)])  9.4 us
    ppermute x3, starting transfers between devices, from_chip(): return lax.ppermute(value, 'loop', pairs)  6.24 us
    ppermute x9, starting transfers between devices, along(): return lax.ppermute(value, ('loop', 'tp'), pairs)  5.69 us
    ppermute x2, starting transfers between devices, along_row(): return lax.ppermute(value, 'loop', pairs)  2.75 us
  transfers between devices with their start and end apart: 21, of which 6 were waited for; matrix products, arithmetic and copies ran while one was open for 2% of the time, Pallas kernels for 17%

profile of v11, /device:TPU:1, one launch (start us, length us, event | category | flops | bytes accessed | tf_op | source)
XLA Modules:
  0.0 56.6 jit_solution(16306114657948981956)
XLA Ops:
  0.0 2.0 %collective-permute-start = (bf16[256,256]{1,0:T(8,128)(2,1)}, bf16[256,256]{1,0:T(8,128)(2,1)S(1)}, u32[]{:S(2)}, u32[]{:S(2)}) collective-permute-start(bf16[256,256]{1,0:T(8,128)(2,1)} %key_values.1), channel_id=1, source_target_pairs={{0,64},{8,72},{16,80},{24,88},{32,96},{40,104},{48,112},{56,120},{... | collective-permute-start | bytes 393224 | tf_op jit(solution)/shard_map/ppermute | solution.py:252
  2.0 1.2 %collective-permute-start.1 = (s32[1,256]{1,0:T(1,128)}, s32[1,256]{1,0:T(1,128)S(1)}, u32[]{:S(2)}, u32[]{:S(2)}) collective-permute-start(s32[1,256]{1,0:T(1,128)} %bitcast.5), channel_id=1, source_target_pairs={{0,64},{8,72},{16,80},{24,88},{32,96},{40,104},{48,112},{56,120},{... | collective-permute-start | bytes 3080 | tf_op jit(solution)/shard_map/ppermute | solution.py:252
  3.3 0.7 %convert_element_type.3 = f32[256]{0:T(256)S(1)} convert(s32[256]{0:T(256)} %param.6) | non-fusion elementwise | flops 256 | bytes 2048 | tf_op jit(solution)/shard_map/convert_element_type | solution.py:269
  4.0 0.9 %copy-done.1 = bf16[256,256]{1,0:T(8,128)(2,1)S(1)} copy-done((bf16[256,256]{1,0:T(8,128)(2,1)S(1)}, bf16[256,256]{1,0:T(8,128)(2,1)}, u32[]{:S(2)}) %copy-start.1) | copy-done | bytes 131096
  5.0 3.0 %collective-permute-start.5 = (bf16[272,256]{1,0:T(8,128)(2,1)S(1)}, bf16[272,256]{1,0:T(8,128)(2,1)S(1)}, u32[]{:S(2)}, u32[]{:S(2)}) collective-permute-start(bf16[272,256]{1,0:T(8,128)(2,1)S(1)} %get-tuple-element.47.piece.own), channel_id=1, source_target_pairs={{0,32},{8,40},{16,48},{24,56},{32,64},{40,72},{48,80},{56,88},{64,... | collective-permute-start | bytes 417800 | tf_op jit(solution)/shard_map/ppermute | solution.py:252
  8.0 0.5 own_scores.1
  8.6 0.5 collective-permute-start.2
  9.1 2.3 %collective-permute-start.3 = (bf16[272,256]{1,0:T(8,128)(2,1)S(1)}, bf16[272,256]{1,0:T(8,128)(2,1)S(1)}, u32[]{:S(2)}, u32[]{:S(2)}) collective-permute-start(bf16[272,256]{1,0:T(8,128)(2,1)S(1)} %get-tuple-element.55), channel_id=1, source_target_pairs={{0,48},{8,56},{16,0},{24,8},{32,16},{40,24},{48,32},{56,40},{64,11... | collective-permute-start | bytes 417800 | tf_op jit(solution)/shard_map/ppermute | solution.py:256
  11.3 2.1 %collective-permute-start.4 = (bf16[272,256]{1,0:T(8,128)(2,1)S(1)}, bf16[272,256]{1,0:T(8,128)(2,1)S(1)}, u32[]{:S(2)}, u32[]{:S(2)}) collective-permute-start(bf16[272,256]{1,0:T(8,128)(2,1)S(1)} %get-tuple-element.56), channel_id=1, source_target_pairs={{0,8},{8,0},{16,24},{24,16},{32,40},{40,32},{48,56},{56,48},{64,72... | collective-permute-start | bytes 417800 | tf_op jit(solution)/shard_map/ppermute | solution.py:248
  13.4 1.4 %fold.2 = (f32[2048,128]{1,0:T(8,128)S(1)}, f32[2048,256]{1,0:T(8,128)S(1)}) custom-call(bf16[2048,128]{1,0:T(8,128)(2,1)S(1)} %get-tuple-element.48.query_rows, f32[256,1]{1,0:T(8,128)S(1)} %get-tuple-element.53.ids, bf16[272,256]{1,0:T(8,128)(2,1)S(1)} %get-tuple-element.57.refs_0_, f32[2048,256]{1,0:T(8,128)S(1)} %get-tuple-element.58.refs_1_, ...), custom_call_target="tpu_custom_call" | custom-call | flops 2000000000 | bytes 1024 | tf_op jit(solution)/shard_map/fold/pallas_call | solution.py:225
  15.1 2.5 %fold.3 = (f32[2048,128]{1,0:T(8,128)S(1)}, f32[2048,256]{1,0:T(8,128)S(1)}) custom-call(bf16[2048,128]{1,0:T(8,128)(2,1)S(1)} %get-tuple-element.48.query_rows, f32[256,1]{1,0:T(8,128)S(1)} %get-tuple-element.53.ids, bf16[272,256]{1,0:T(8,128)(2,1)S(1)} %collective-permute-done.4.refs_0_, ...), custom_call_target="tpu_custom_call", output_to_operand_aliasing={{0}: (4, {}), {1}: (5, {})} | custom-call | flops 2000000000 | bytes 1024 | tf_op jit(solution)/shard_map/fold/pallas_call | solution.py:225
  17.6 0.4 collective-permute-start.6
  18.4 1.1 %more_scores.1 = (f32[2048,768]{1,0:T(8,128)S(1)}, f32[2048,128]{1,0:T(8,128)S(1)}, bf16[768,256]{1,0:T(8,128)(2,1)S(1)}) custom-call(bf16[2048,128]{1,0:T(8,128)(2,1)S(1)} %get-tuple-element.48.query_rows, f32[256,1]{1,0:T(8,128)S(1)} %get-tuple-element.53.ids, bf16[272,256]{1,0:T(8,128)(2,1)S(1)} %collective-permute-done.8.refs_0_, ...), custom_call_target="tpu_custom_call" | custom-call | flops 1500000000 | bytes 1024 | tf_op jit(solution)/shard_map/more_scores/pallas_call | solution.py:225
  19.5 1.6 %attend.2 = (bf16[128,1024]{1,0:T(8,128)(2,1)S(1)}, bf16[128,512]{1,0:T(8,128)(2,1)S(1)}) custom-call(bf16[2048,128]{1,0:T(8,128)(2,1)S(1)} %get-tuple-element.48.query_rows, f32[256,1]{1,0:T(8,128)S(1)} %get-tuple-element.53.ids, bf16[272,256]{1,0:T(8,128)(2,1)S(1)} %collective-permute-done.6.refs_0_, bf16[272,256]{1,0:T(8,128)(2,1)S(1)} %collective-permute-done.7.refs_1_, ...), custom_call_target="tpu_custom_call" | custom-call | flops 10000000 | bytes 1024 | tf_op jit(solution)/shard_map/attend/pallas_call | solution.py:225
  21.1 0.3 collective-permute-start.9
  21.4 1.7 %collective-permute-start.10 = (bf16[128,512]{1,0:T(8,128)(2,1)S(1)}, bf16[128,512]{1,0:T(8,128)(2,1)S(1)}, u32[]{:S(2)}, u32[]{:S(2)}) collective-permute-start(bf16[128,512]{1,0:T(8,128)(2,1)S(1)} %get-tuple-element.80), channel_id=1, source_target_pairs={{0,7},{1,0},{2,1},{3,2},{4,3},{5,4},{6,5},{7,6},{8,9},{9,10},{10,1... | collective-permute-start | bytes 393224 | tf_op jit(solution)/shard_map/ppermute | solution.py:264
  23.1 1.6 %attend.3 = (bf16[128,1024]{1,0:T(8,128)(2,1)S(1)}, bf16[128,512]{1,0:T(8,128)(2,1)S(1)}) custom-call(bf16[2048,128]{1,0:T(8,128)(2,1)S(1)} %get-tuple-element.48.query_rows, f32[256,1]{1,0:T(8,128)S(1)} %get-tuple-element.53.ids, bf16[272,256]{1,0:T(8,128)(2,1)S(1)} %collective-permute-done.6.refs_0_, bf16[272,256]{1,0:T(8,128)(2,1)S(1)} %collective-permute-done.7.refs_1_, ...), custom_call_target="tpu_custom_call" | custom-call | flops 10000000 | bytes 1024 | tf_op jit(solution)/shard_map/attend/pallas_call | solution.py:225
  24.6 1.7 %collective-permute-start.16 = (bf16[128,512]{1,0:T(8,128)(2,1)S(1)}, bf16[128,512]{1,0:T(8,128)(2,1)S(1)}, u32[]{:S(2)}, u32[]{:S(2)}) collective-permute-start(bf16[128,512]{1,0:T(8,128)(2,1)S(1)} %get-tuple-element.86), channel_id=1, source_target_pairs={{0,7},{1,0},{2,1},{3,2},{4,3},{5,4},{6,5},{7,6},{8,9},{9,10},{10,1... | collective-permute-start | bytes 393224 | tf_op jit(solution)/shard_map/ppermute | solution.py:264
  26.4 3.9 %collective-permute-start.15 = (bf16[128,1024]{1,0:T(8,128)(2,1)S(1)}, bf16[128,1024]{1,0:T(8,128)(2,1)S(1)}, u32[]{:S(2)}, u32[]{:S(2)}) collective-permute-start(bf16[128,1024]{1,0:T(8,128)(2,1)S(1)} %get-tuple-element.81.own), channel_id=1, source_target_pairs={{0,8},{8,0},{16,24},{24,16},{32,40},{40,32},{48,56},{56,48},{64,72... | collective-permute-start | bytes 786440 | tf_op jit(solution)/shard_map/ppermute | solution.py:248
  30.2 1.1 %project.2 = (bf16[256,512]{1,0:T(8,128)(2,1)S(1)}, bf16[256,512]{1,0:T(8,128)(2,1)S(1)}, bf16[256,512]{1,0:T(8,128)(2,1)S(1)}, bf16[128,512]{1,0:T(8,128)(2,1)S(1)}) custom-call(bf16[128,1024]{1,0:T(8,128)(2,1)S(1)} %get-tuple-element.75.own, bf16[128,1024]{1,0:T(8,128)(2,1)S(1)} %collective-permute-done.9.mate, bf16[1024,4096]{1,0:T(8,128)(2,1)S(1)} %bitcast.3), custom_call_target="tpu_custom_call" | custom-call | flops 10000000 | bytes 1024 | tf_op jit(solution)/shard_map/project/pallas_call | solution.py:225
  31.5 0.8 %collective-permute-start.11 = (bf16[256,512]{1,0:T(8,128)(2,1)S(1)}, bf16[256,512]{1,0:T(8,128)(2,1)S(1)}, u32[]{:S(2)}, u32[]{:S(2)}) collective-permute-start(bf16[256,512]{1,0:T(8,128)(2,1)S(1)} %pad_maximum_fusion), channel_id=1, source_target_pairs={{0,7},{1,0},{2,1},{3,2},{4,3},{5,4},{6,5},{7,6},{8,9},{9,10},{10,1... | collective-permute-start | bytes 786440 | tf_op jit(solution)/shard_map/ppermute | solution.py:264
  32.3 1.1 %project.3 = (bf16[256,512]{1,0:T(8,128)(2,1)S(1)}, bf16[256,512]{1,0:T(8,128)(2,1)S(1)}, bf16[256,512]{1,0:T(8,128)(2,1)S(1)}, bf16[128,512]{1,0:T(8,128)(2,1)S(1)}) custom-call(bf16[128,1024]{1,0:T(8,128)(2,1)S(1)} %get-tuple-element.81.own, bf16[128,1024]{1,0:T(8,128)(2,1)S(1)} %collective-permute-done.15.mate, bf16[1024,4096]{1,0:T(8,128)(2,1)S(1)} %bitcast.3), custom_call_target="tpu_custom_call" | custom-call | flops 10000000 | bytes 1024 | tf_op jit(solution)/shard_map/project/pallas_call | solution.py:225
  33.6 4.4 %collective-permute-done.11 = bf16[256,512]{1,0:T(8,128)(2,1)S(1)} collective-permute-done((bf16[256,512]{1,0:T(8,128)(2,1)S(1)}, bf16[256,512]{1,0:T(8,128)(2,1)S(1)}, u32[]{:S(2)}, u32[]{:S(2)}) %collective-permute-start.11) | collective-permute-done | bytes 262176 | tf_op jit(solution)/shard_map/ppermute | solution.py:264
  38.1 2.6 %collective-permute-done.17 = bf16[256,512]{1,0:T(8,128)(2,1)S(1)} collective-permute-done((bf16[256,512]{1,0:T(8,128)(2,1)S(1)}, bf16[256,512]{1,0:T(8,128)(2,1)S(1)}, u32[]{:S(2)}, u32[]{:S(2)}) %collective-permute-start.17) | collective-permute-done | bytes 262176 | tf_op jit(solution)/shard_map/ppermute | solution.py:264
  40.9 3.6 %collective-permute-done.12 = bf16[256,512]{1,0:T(8,128)(2,1)S(1)} collective-permute-done((bf16[256,512]{1,0:T(8,128)(2,1)S(1)}, bf16[256,512]{1,0:T(8,128)(2,1)S(1)}, u32[]{:S(2)}, u32[]{:S(2)}) %collective-permute-start.12) | collective-permute-done | bytes 262176 | tf_op jit(solution)/shard_map/ppermute | solution.py:264
  44.7 2.6 %collective-permute-done.18 = bf16[256,512]{1,0:T(8,128)(2,1)S(1)} collective-permute-done((bf16[256,512]{1,0:T(8,128)(2,1)S(1)}, bf16[256,512]{1,0:T(8,128)(2,1)S(1)}, u32[]{:S(2)}, u32[]{:S(2)}) %collective-permute-start.18) | collective-permute-done | bytes 262176 | tf_op jit(solution)/shard_map/ppermute | solution.py:264
  47.4 0.6 %collective-permute-start.20 = (bf16[128,512]{1,0:T(8,128)(2,1)S(1)}, bf16[128,512]{1,0:T(8,128)(2,1)S(1)}, u32[]{:S(2)}, u32[]{:S(2)}) collective-permute-start(bf16[128,512]{1,0:T(8,128)(2,1)S(1)} %get-tuple-element.87), channel_id=1, source_target_pairs={{0,15},{1,8},{2,9},{3,10},{4,11},{5,12},{6,13},{7,14},{8,1},{9,2},... | collective-permute-start | bytes 393224 | tf_op jit(solution)/shard_map/ppermute | solution.py:264
  48.0 0.6 %collective-permute-start.19 = (bf16[128,512]{1,0:T(8,128)(2,1)S(1)}, bf16[128,512]{1,0:T(8,128)(2,1)S(1)}, u32[]{:S(2)}, u32[]{:S(2)}) collective-permute-start(bf16[128,512]{1,0:T(8,128)(2,1)S(1)} %get-tuple-element.88), channel_id=1, source_target_pairs={{0,7},{1,0},{2,1},{3,2},{4,3},{5,4},{6,5},{7,6},{8,9},{9,10},{10,1... | collective-permute-start | bytes 393224 | tf_op jit(solution)/shard_map/ppermute | solution.py:264
  48.6 2.6 %collective-permute-done.13 = bf16[256,512]{1,0:T(8,128)(2,1)S(1)} collective-permute-done((bf16[256,512]{1,0:T(8,128)(2,1)S(1)}, bf16[256,512]{1,0:T(8,128)(2,1)S(1)}, u32[]{:S(2)}, u32[]{:S(2)}) %collective-permute-start.13) | collective-permute-done | bytes 262176 | tf_op jit(solution)/shard_map/ppermute | solution.py:264
  51.2 2.2 %collective-permute-start.14 = (bf16[128,512]{1,0:T(8,128)(2,1)S(1)}, bf16[128,512]{1,0:T(8,128)(2,1)S(1)}, u32[]{:S(2)}, u32[]{:S(2)}) collective-permute-start(bf16[128,512]{1,0:T(8,128)(2,1)S(1)} %get-tuple-element.91), channel_id=1, source_target_pairs={{0,8},{8,0},{16,24},{24,16},{32,40},{40,32},{48,56},{56,48},{64,72... | collective-permute-start | bytes 393224 | tf_op jit(solution)/shard_map/ppermute | solution.py:248
  53.3 2.4 %collective-permute-done.19.refs_4_ = bf16[128,512]{1,0:T(8,128)(2,1)S(1)} collective-permute-done((bf16[128,512]{1,0:T(8,128)(2,1)S(1)}, bf16[128,512]{1,0:T(8,128)(2,1)S(1)}, u32[]{:S(2)}, u32[]{:S(2)}) %collective-permute-start.19) | collective-permute-done | bytes 131104 | tf_op jit(solution)/shard_map/ppermute | solution.py:264
  55.8 0.8 %finish.1 = bf16[256,512]{1,0:T(8,128)(2,1)} custom-call(bf16[128,512]{1,0:T(8,128)(2,1)S(1)} %get-tuple-element.76.refs_0_, bf16[128,512]{1,0:T(8,128)(2,1)S(1)} %get-tuple-element.92.refs_1_, bf16[128,512]{1,0:T(8,128)(2,1)S(1)} %collective-permute-done.14.refs_2_, bf16[128,512]{1,0:T(8,128)(2,1)S(1)} %get-tuple-element.82.refs_3_, ...), custom_call_target="tpu_custom_call" | custom-call | flops 500000000 | bytes 1024 | tf_op jit(solution)/shard_map/finish/pallas_call | solution.py:225
  (40 shorter events, 1.5 us)
Async XLA Ops:
  0.0 8.0 %copy-start = (bf16[256,1024]{1,0:T(8,128)(2,1)S(1)}, bf16[256,1024]{1,0:T(8,128)(2,1)}, u32[]{:S(2)}) copy-start(bf16[256,1024]{1,0:T(8,128)(2,1)} %queries.1) | copy-start | bytes 1572868
  0.0 8.5 %collective-permute-start = (bf16[256,256]{1,0:T(8,128)(2,1)}, bf16[256,256]{1,0:T(8,128)(2,1)S(1)}, u32[]{:S(2)}, u32[]{:S(2)}) collective-permute-start(bf16[256,256]{1,0:T(8,128)(2,1)} %key_values.1), channel_id=1, source_target_pairs={{0,64},{8,72},{16,80},{24,88},{32,96},{40,104},{48,112},{56,120},{... | collective-permute-start | bytes 393224 | tf_op jit(solution)/shard_map/ppermute | solution.py:252
  2.0 6.4 %collective-permute-start.1 = (s32[1,256]{1,0:T(1,128)}, s32[1,256]{1,0:T(1,128)S(1)}, u32[]{:S(2)}, u32[]{:S(2)}) collective-permute-start(s32[1,256]{1,0:T(1,128)} %bitcast.5), channel_id=1, source_target_pairs={{0,64},{8,72},{16,80},{24,88},{32,96},{40,104},{48,112},{56,120},{... | collective-permute-start | bytes 3080 | tf_op jit(solution)/shard_map/ppermute | solution.py:252
  4.0 0.9 %copy-start.1 = (bf16[256,256]{1,0:T(8,128)(2,1)S(1)}, bf16[256,256]{1,0:T(8,128)(2,1)}, u32[]{:S(2)}) copy-start(bf16[256,256]{1,0:T(8,128)(2,1)} %key_values.1) | copy-start | bytes 393220
  5.0 9.8 %collective-permute-start.5 = (bf16[272,256]{1,0:T(8,128)(2,1)S(1)}, bf16[272,256]{1,0:T(8,128)(2,1)S(1)}, u32[]{:S(2)}, u32[]{:S(2)}) collective-permute-start(bf16[272,256]{1,0:T(8,128)(2,1)S(1)} %get-tuple-element.47.piece.own), channel_id=1, source_target_pairs={{0,32},{8,40},{16,48},{24,56},{32,64},{40,72},{48,80},{56,88},{64,... | collective-permute-start | bytes 417800 | tf_op jit(solution)/shard_map/ppermute | solution.py:252
  8.6 9.0 %collective-permute-start.2 = (bf16[272,256]{1,0:T(8,128)(2,1)S(1)}, bf16[272,256]{1,0:T(8,128)(2,1)S(1)}, u32[]{:S(2)}, u32[]{:S(2)}) collective-permute-start(bf16[272,256]{1,0:T(8,128)(2,1)S(1)} %get-tuple-element.54), channel_id=1, source_target_pairs={{0,16},{8,24},{16,32},{24,40},{32,48},{40,56},{48,0},{56,8},{64,80... | collective-permute-start | bytes 417800 | tf_op jit(solution)/shard_map/ppermute | solution.py:256
  9.1 8.6 %collective-permute-start.3 = (bf16[272,256]{1,0:T(8,128)(2,1)S(1)}, bf16[272,256]{1,0:T(8,128)(2,1)S(1)}, u32[]{:S(2)}, u32[]{:S(2)}) collective-permute-start(bf16[272,256]{1,0:T(8,128)(2,1)S(1)} %get-tuple-element.55), channel_id=1, source_target_pairs={{0,48},{8,56},{16,0},{24,8},{32,16},{40,24},{48,32},{56,40},{64,11... | collective-permute-start | bytes 417800 | tf_op jit(solution)/shard_map/ppermute | solution.py:256
  11.3 3.8 %collective-permute-start.4 = (bf16[272,256]{1,0:T(8,128)(2,1)S(1)}, bf16[272,256]{1,0:T(8,128)(2,1)S(1)}, u32[]{:S(2)}, u32[]{:S(2)}) collective-permute-start(bf16[272,256]{1,0:T(8,128)(2,1)S(1)} %get-tuple-element.56), channel_id=1, source_target_pairs={{0,8},{8,0},{16,24},{24,16},{32,40},{40,32},{48,56},{56,48},{64,72... | collective-permute-start | bytes 417800 | tf_op jit(solution)/shard_map/ppermute | solution.py:248
  13.4 6.1 %slice-start = ((s8[8388608]{0:T(1024)(128)(4,1)}), s8[4194304]{0:T(1024)(128)(4,1)S(1)}, s32[]{:S(2)}) async-start(s8[8388608]{0:T(1024)(128)(4,1)} %bitcast.2), calls=%async_computation | async-start | bytes 8388608
  14.8 4.7 %slice-start.1 = ((s8[8388608]{0:T(1024)(128)(4,1)}), s8[4194304]{0:T(1024)(128)(4,1)S(1)}, s32[]{:S(2)}) async-start(s8[8388608]{0:T(1024)(128)(4,1)} %bitcast.2), calls=%async_computation.1 | async-start | bytes 8388608
  14.8 3.5 %collective-permute-start.8 = (bf16[272,256]{1,0:T(8,128)(2,1)S(1)}, bf16[272,256]{1,0:T(8,128)(2,1)S(1)}, u32[]{:S(2)}, u32[]{:S(2)}) collective-permute-start(bf16[272,256]{1,0:T(8,128)(2,1)S(1)} %collective-permute-done.5.refs_1_), channel_id=1, source_target_pairs={{0,8},{8,0},{16,24},{24,16},{32,40},{40,32},{48,56},{56,48},{64,72... | collective-permute-start | bytes 417800 | tf_op jit(solution)/shard_map/ppermute | solution.py:248
  17.6 1.8 %collective-permute-start.6 = (bf16[272,256]{1,0:T(8,128)(2,1)S(1)}, bf16[272,256]{1,0:T(8,128)(2,1)S(1)}, u32[]{:S(2)}, u32[]{:S(2)}) collective-permute-start(bf16[272,256]{1,0:T(8,128)(2,1)S(1)} %collective-permute-done.2.refs_1_), channel_id=1, source_target_pairs={{0,8},{8,0},{16,24},{24,16},{32,40},{40,32},{48,56},{56,48},{64,72... | collective-permute-start | bytes 417800 | tf_op jit(solution)/shard_map/ppermute | solution.py:248
  18.1 1.4 %collective-permute-start.7 = (bf16[272,256]{1,0:T(8,128)(2,1)S(1)}, bf16[272,256]{1,0:T(8,128)(2,1)S(1)}, u32[]{:S(2)}, u32[]{:S(2)}) collective-permute-start(bf16[272,256]{1,0:T(8,128)(2,1)S(1)} %collective-permute-done.3.refs_2_), channel_id=1, source_target_pairs={{0,8},{8,0},{16,24},{24,16},{32,40},{40,32},{48,56},{56,48},{64,72... | collective-permute-start | bytes 417800 | tf_op jit(solution)/shard_map/ppermute | solution.py:248
  21.1 9.2 %collective-permute-start.9 = (bf16[128,1024]{1,0:T(8,128)(2,1)S(1)}, bf16[128,1024]{1,0:T(8,128)(2,1)S(1)}, u32[]{:S(2)}, u32[]{:S(2)}) collective-permute-start(bf16[128,1024]{1,0:T(8,128)(2,1)S(1)} %get-tuple-element.75.own), channel_id=1, source_target_pairs={{0,8},{8,0},{16,24},{24,16},{32,40},{40,32},{48,56},{56,48},{64,72... | collective-permute-start | bytes 786440 | tf_op jit(solution)/shard_map/ppermute | solution.py:248
  21.4 10.0 %collective-permute-start.10 = (bf16[128,512]{1,0:T(8,128)(2,1)S(1)}, bf16[128,512]{1,0:T(8,128)(2,1)S(1)}, u32[]{:S(2)}, u32[]{:S(2)}) collective-permute-start(bf16[128,512]{1,0:T(8,128)(2,1)S(1)} %get-tuple-element.80), channel_id=1, source_target_pairs={{0,7},{1,0},{2,1},{3,2},{4,3},{5,4},{6,5},{7,6},{8,9},{9,10},{10,1... | collective-permute-start | bytes 393224 | tf_op jit(solution)/shard_map/ppermute | solution.py:264
  24.6 8.7 %collective-permute-start.16 = (bf16[128,512]{1,0:T(8,128)(2,1)S(1)}, bf16[128,512]{1,0:T(8,128)(2,1)S(1)}, u32[]{:S(2)}, u32[]{:S(2)}) collective-permute-start(bf16[128,512]{1,0:T(8,128)(2,1)S(1)} %get-tuple-element.86), channel_id=1, source_target_pairs={{0,7},{1,0},{2,1},{3,2},{4,3},{5,4},{6,5},{7,6},{8,9},{9,10},{10,1... | collective-permute-start | bytes 393224 | tf_op jit(solution)/shard_map/ppermute | solution.py:264
  26.4 5.9 %collective-permute-start.15 = (bf16[128,1024]{1,0:T(8,128)(2,1)S(1)}, bf16[128,1024]{1,0:T(8,128)(2,1)S(1)}, u32[]{:S(2)}, u32[]{:S(2)}) collective-permute-start(bf16[128,1024]{1,0:T(8,128)(2,1)S(1)} %get-tuple-element.81.own), channel_id=1, source_target_pairs={{0,8},{8,0},{16,24},{24,16},{32,40},{40,32},{48,56},{56,48},{64,72... | collective-permute-start | bytes 786440 | tf_op jit(solution)/shard_map/ppermute | solution.py:248
  31.5 6.5 %collective-permute-start.11 = (bf16[256,512]{1,0:T(8,128)(2,1)S(1)}, bf16[256,512]{1,0:T(8,128)(2,1)S(1)}, u32[]{:S(2)}, u32[]{:S(2)}) collective-permute-start(bf16[256,512]{1,0:T(8,128)(2,1)S(1)} %pad_maximum_fusion), channel_id=1, source_target_pairs={{0,7},{1,0},{2,1},{3,2},{4,3},{5,4},{6,5},{7,6},{8,9},{9,10},{10,1... | collective-permute-start | bytes 786440 | tf_op jit(solution)/shard_map/ppermute | solution.py:264
  33.5 7.3 %collective-permute-start.17 = (bf16[256,512]{1,0:T(8,128)(2,1)S(1)}, bf16[256,512]{1,0:T(8,128)(2,1)S(1)}, u32[]{:S(2)}, u32[]{:S(2)}) collective-permute-start(bf16[256,512]{1,0:T(8,128)(2,1)S(1)} %pad_maximum_fusion.1), channel_id=1, source_target_pairs={{0,7},{1,0},{2,1},{3,2},{4,3},{5,4},{6,5},{7,6},{8,9},{9,10},{10,1... | collective-permute-start | bytes 786440 | tf_op jit(solution)/shard_map/ppermute | solution.py:264
  38.0 6.5 %collective-permute-start.12 = (bf16[256,512]{1,0:T(8,128)(2,1)S(1)}, bf16[256,512]{1,0:T(8,128)(2,1)S(1)}, u32[]{:S(2)}, u32[]{:S(2)}) collective-permute-start(bf16[256,512]{1,0:T(8,128)(2,1)S(1)} %add.22), channel_id=1, source_target_pairs={{0,7},{1,0},{2,1},{3,2},{4,3},{5,4},{6,5},{7,6},{8,9},{9,10},{10,1... | collective-permute-start | bytes 786440 | tf_op jit(solution)/shard_map/ppermute | solution.py:264
  40.9 6.5 %collective-permute-start.18 = (bf16[256,512]{1,0:T(8,128)(2,1)S(1)}, bf16[256,512]{1,0:T(8,128)(2,1)S(1)}, u32[]{:S(2)}, u32[]{:S(2)}) collective-permute-start(bf16[256,512]{1,0:T(8,128)(2,1)S(1)} %add.25), channel_id=1, source_target_pairs={{0,7},{1,0},{2,1},{3,2},{4,3},{5,4},{6,5},{7,6},{8,9},{9,10},{10,1... | collective-permute-start | bytes 786440 | tf_op jit(solution)/shard_map/ppermute | solution.py:264
  44.6 6.5 %collective-permute-start.13 = (bf16[256,512]{1,0:T(8,128)(2,1)S(1)}, bf16[256,512]{1,0:T(8,128)(2,1)S(1)}, u32[]{:S(2)}, u32[]{:S(2)}) collective-permute-start(bf16[256,512]{1,0:T(8,128)(2,1)S(1)} %add.23), channel_id=1, source_target_pairs={{0,7},{1,0},{2,1},{3,2},{4,3},{5,4},{6,5},{7,6},{8,9},{9,10},{10,1... | collective-permute-start | bytes 786440 | tf_op jit(solution)/shard_map/ppermute | solution.py:264
  47.4 5.9 %collective-permute-start.20 = (bf16[128,512]{1,0:T(8,128)(2,1)S(1)}, bf16[128,512]{1,0:T(8,128)(2,1)S(1)}, u32[]{:S(2)}, u32[]{:S(2)}) collective-permute-start(bf16[128,512]{1,0:T(8,128)(2,1)S(1)} %get-tuple-element.87), channel_id=1, source_target_pairs={{0,15},{1,8},{2,9},{3,10},{4,11},{5,12},{6,13},{7,14},{8,1},{9,2},... | collective-permute-start | bytes 393224 | tf_op jit(solution)/shard_map/ppermute | solution.py:264
  48.0 7.8 %collective-permute-start.19 = (bf16[128,512]{1,0:T(8,128)(2,1)S(1)}, bf16[128,512]{1,0:T(8,128)(2,1)S(1)}, u32[]{:S(2)}, u32[]{:S(2)}) collective-permute-start(bf16[128,512]{1,0:T(8,128)(2,1)S(1)} %get-tuple-element.88), channel_id=1, source_target_pairs={{0,7},{1,0},{2,1},{3,2},{4,3},{5,4},{6,5},{7,6},{8,9},{9,10},{10,1... | collective-permute-start | bytes 393224 | tf_op jit(solution)/shard_map/ppermute | solution.py:264
  51.2 4.6 %collective-permute-start.14 = (bf16[128,512]{1,0:T(8,128)(2,1)S(1)}, bf16[128,512]{1,0:T(8,128)(2,1)S(1)}, u32[]{:S(2)}, u32[]{:S(2)}) collective-permute-start(bf16[128,512]{1,0:T(8,128)(2,1)S(1)} %get-tuple-element.91), channel_id=1, source_target_pairs={{0,8},{8,0},{16,24},{24,16},{32,40},{40,32},{48,56},{56,48},{64,72... | collective-permute-start | bytes 393224 | tf_op jit(solution)/shard_map/ppermute | solution.py:248
